TPU v7x, 32 devices: a whole 2x2x4 slice. The times are simulated.
32 devices in a mesh: energy: 4 (over y, x), block: 8 (over z, core).
Axes of the slice: x: 2, y: 2, z: 4, core: 2. Of those that a mesh axis runs over, the one named last changes fastest.
Arguments:
- g_less: bfloat16 [128, 8, 128, 128], P('energy', 'block'), may hold values from -6 to 6
- g_great: bfloat16 [128, 8, 128, 128], P('energy', 'block'), may hold values from -6 to 6
- coupling: bfloat16 [8, 3, 128, 128], P('block'), may hold values from -0.3125 to 0.3125
- coupling_mask: int32 [8, 2], P('block'), may hold values 0 or 1
Outputs:
- sigma_less: float32 [128, 8, 128, 128], P('energy', 'block')
All inputs are finite; a program needn't handle non-finite values. No bound on the sum of `coupling_mask` on one device may be relied on, other than what follows from the above.
Results may differ from a plain program's by a relative error of at most 0.009.
Values may be sent and summed in bfloat16 or wider, within the bound.
No kernel may reach another device: no remote copies, remote signals or barrier semaphores. Data moves between devices by JAX's collectives and lax.ppermute only.
A program may use at most 64 MiB of HBM per device.

v0:
```python
import functools
import math

import jax
import jax.numpy as jnp
import numpy as np
from jax import lax
from jax.experimental import pallas as pl
from jax.experimental.pallas import tpu as pltpu
from jax.sharding import PartitionSpec as P

BF16 = jnp.bfloat16
F32 = jnp.float32


def split(table):
    upper = table.astype(BF16)
    lower = (table - upper.astype(np.float32)).astype(BF16)
    return upper, lower


def tables(groups, e_dev):
    total = groups * e_dev
    length = 3 * total // 2
    omega = 2.0 * math.pi / length * (np.arange(length // 2) + 0.5)
    scale = 2.0 / (length * math.sqrt(total))
    energies = np.arange(total)
    lags = energies - total // 2

    def forward(points):
        angle = omega[:, None] * points[None, :]
        table = np.concatenate([np.cos(angle), np.sin(angle)], axis=0).astype(np.float32)
        return np.concatenate(split(table), axis=1)

    def backward(points):
        angle = points[:, None] * omega[None, :]
        table = np.concatenate([np.cos(angle), np.sin(angle)], axis=1) * scale
        return np.concatenate(split(table.astype(np.float32)), axis=0)

    def ordered(me):
        return np.concatenate([np.arange(e_dev) + (me ^ d) * e_dev for d in range(groups)])

    fwd_e = np.stack([forward(energies[ordered(me)]) for me in range(groups)])
    fwd_l = np.stack([forward(lags[ordered(me)]) for me in range(groups)])
    back_l = np.stack([backward(lags[ordered(me)]) for me in range(groups)])
    back_e = np.stack([backward(energies[ordered(me)]) for me in range(groups)])
    return fwd_e, fwd_l, back_l, back_e


def params():
    return pltpu.CompilerParams(vmem_limit_bytes=40 * 1024 * 1024)


def vmem():
    return pl.BlockSpec(memory_space=pltpu.VMEM)


def dot(a, b):
    return jnp.dot(a, b, preferred_element_type=F32)


def less_kernel(groups, me_ref, x_ref, *rest):
    outs, scratch = rest[:groups], rest[groups]
    e_dev, orbitals, _ = x_ref.shape
    rows = orbitals // groups
    me = me_ref[0]
    for d in range(groups):
        start = pl.multiple_of((me ^ d) * rows, rows)
        for e in range(e_dev):
            scratch[pl.ds(d * rows * e_dev + e, rows, stride=e_dev), :] = x_ref[
                e, pl.ds(start, rows), :
            ].astype(F32)
    for d in range(groups):
        outs[d][...] = (
            scratch[d * rows * e_dev : (d + 1) * rows * e_dev, :]
            .astype(BF16)
            .reshape(rows, e_dev, orbitals)
        )


def great_kernel(groups, me_ref, x_ref, *rest):
    outs, scratch = rest[:groups], rest[groups]
    e_dev, orbitals, _ = x_ref.shape
    rows = orbitals // groups
    me = me_ref[0]
    for e in range(e_dev):
        scratch[pl.ds(e, orbitals, stride=e_dev), :] = x_ref[e].astype(F32).T
    for d in range(groups):
        size = rows * e_dev
        start = pl.multiple_of((me ^ d) * size, size)
        outs[d][...] = (
            scratch[pl.ds(start, size), :].astype(BF16).reshape(rows, e_dev, orbitals)
        )


def prepare(kernel, me, x):
    e_dev, orbitals, _ = x.shape
    groups = lax.axis_size("energy")
    rows = orbitals // groups
    return pl.pallas_call(
        functools.partial(kernel, groups),
        out_shape=[jax.ShapeDtypeStruct((rows, e_dev, orbitals), BF16)] * groups,
        in_specs=[pl.BlockSpec(memory_space=pltpu.SMEM), vmem()],
        out_specs=[vmem()] * groups,
        scratch_shapes=[pltpu.VMEM((orbitals * e_dev, orbitals), F32)],
        compiler_params=params(),
    )(me, x)


def gathered(refs, i):
    pair = [
        jnp.concatenate([ref[i + h] for ref in refs], axis=0) for h in range(2)
    ]
    both = jnp.concatenate(pair, axis=1)
    return jnp.concatenate([both, both], axis=0)


def inverse(back, spectrum):
    both = dot(back, spectrum.astype(BF16))
    half = both.shape[0] // 2
    return both[:half] + both[half:]


def pol_kernel(groups, fwd_ref, back_ref, *refs):
    less, great = refs[:groups], refs[groups : 2 * groups]
    outs, scratch = refs[2 * groups : 3 * groups], refs[3 * groups]
    rows, e_dev, orbitals = less[0].shape
    freq = fwd_ref.shape[0] // 2
    fwd, back = fwd_ref[...], back_ref[...]
    total = groups * e_dev
    for i in range(0, rows, 2):
        a = dot(fwd, gathered(less, i))
        b = dot(fwd, gathered(great, i))
        real = a[:freq] * b[:freq] + a[freq:] * b[freq:]
        imag = a[freq:] * b[:freq] - a[:freq] * b[freq:]
        pol = inverse(back, jnp.concatenate([real, imag], axis=0))
        for h in range(2):
            scratch[pl.ds(i + h, total, stride=rows), :] = pol[
                :, h * orbitals : (h + 1) * orbitals
            ]
    for d in range(groups):
        size = e_dev * rows
        outs[d][...] = (
            scratch[d * size : (d + 1) * size, :].astype(BF16).reshape(e_dev, rows, orbitals)
        )


def sigma_kernel(groups, fwd_e_ref, fwd_l_ref, back_ref, *refs):
    less, inter = refs[:groups], refs[groups : 2 * groups]
    outs = refs[2 * groups :]
    rows, e_dev, orbitals = less[0].shape
    freq = fwd_e_ref.shape[0] // 2
    fwd_e, fwd_l, back = fwd_e_ref[...], fwd_l_ref[...], back_ref[...]
    for i in range(0, rows, 2):
        a = dot(fwd_e, gathered(less, i))
        b = dot(fwd_l, gathered(inter, i))
        real = a[:freq] * b[:freq] - a[freq:] * b[freq:]
        imag = a[freq:] * b[:freq] + a[:freq] * b[freq:]
        sigma = inverse(back, jnp.concatenate([real, imag], axis=0)).astype(BF16)
        for h in range(2):
            for d in range(groups):
                outs[d][i + h] = sigma[
                    d * e_dev : (d + 1) * e_dev, h * orbitals : (h + 1) * orbitals
                ]


def assemble_kernel(groups, me_ref, *refs):
    ins, out = refs[:groups], refs[groups]
    rows = ins[0].shape[1]
    me = me_ref[0]
    for d in range(groups):
        start = pl.multiple_of((me ^ d) * rows, rows)
        out[:, pl.ds(start, rows), :] = ins[d][...]


def screen_kernel(groups, me_ref, mask_ref, v_ref, vt_ref, before, own, after, *refs):
    outs, scratch = refs[:groups], refs[groups]
    lags, orbitals, _ = own.shape
    rows = orbitals // groups
    me = me_ref[0]
    left = [v_ref[t] for t in range(3)]
    right = jnp.concatenate(
        [
            vt_ref[0] * mask_ref[0].astype(F32).astype(BF16),
            vt_ref[1],
            vt_ref[2] * mask_ref[1].astype(F32).astype(BF16),
        ],
        axis=0,
    )
    for k in range(0, lags, 2):
        half = [
            dot(left[t], jnp.concatenate([ref[k], ref[k + 1]], axis=1)).astype(BF16)
            for t, ref in enumerate((before, own, after))
        ]
        for h in range(2):
            cols = slice(h * orbitals, (h + 1) * orbitals)
            term = dot(jnp.concatenate([x[:, cols] for x in half], axis=1), right)
            scratch[pl.ds(k + h, orbitals, stride=lags), :] = term
    for d in range(groups):
        size = rows * lags
        start = pl.multiple_of((me ^ d) * size, size)
        outs[d][...] = (
            scratch[pl.ds(start, size), :].astype(BF16).reshape(rows, lags, orbitals)
        )


def final_kernel(groups, me_ref, *refs):
    ins, out = refs[:groups], refs[groups]
    rows, e_dev, orbitals = ins[0].shape
    me = me_ref[0]
    for d in range(groups):
        for i in range(rows):
            out[pl.ds((me ^ d) * rows + i, e_dev, stride=orbitals), :] = ins[d][i].astype(F32)


def exchange(parts):
    groups = lax.axis_size("energy")
    moved = [parts[0]]
    for d in range(1, groups):
        moved.append(lax.ppermute(parts[d], "energy", [(i, i ^ d) for i in range(groups)]))
    return moved


def shards(g_less, g_great, coupling, coupling_mask):
    e_dev, _, orbitals, _ = g_less.shape
    groups = lax.axis_size("energy")
    peers = lax.axis_size("block")
    rows = orbitals // groups
    total = e_dev * groups
    index = lax.axis_index("energy")
    me = index.astype(jnp.int32)[None]
    fwd_e, fwd_l, back_l, back_e = [
        lax.dynamic_index_in_dim(jnp.asarray(t), index, 0, keepdims=False)
        for t in tables(groups, e_dev)
    ]
    smem = pl.BlockSpec(memory_space=pltpu.SMEM)
    less = exchange(prepare(less_kernel, me, g_less.reshape(e_dev, orbitals, orbitals)))
    great = exchange(prepare(great_kernel, me, g_great.reshape(e_dev, orbitals, orbitals)))
    pol = pl.pallas_call(
        functools.partial(pol_kernel, groups),
        out_shape=[jax.ShapeDtypeStruct((e_dev, rows, orbitals), BF16)] * groups,
        in_specs=[vmem()] * (2 + 2 * groups),
        out_specs=[vmem()] * groups,
        scratch_shapes=[pltpu.VMEM((total * rows, orbitals), F32)],
        compiler_params=params(),
    )(fwd_e, back_l, *less, *great)
    pol = exchange(pol)
    own = pl.pallas_call(
        functools.partial(assemble_kernel, groups),
        out_shape=jax.ShapeDtypeStruct((e_dev, orbitals, orbitals), BF16),
        in_specs=[smem] + [vmem()] * groups,
        out_specs=vmem(),
        compiler_params=params(),
    )(me, *pol)
    before = lax.ppermute(own, "block", [(i, i + 1) for i in range(peers - 1)])
    after = lax.ppermute(own, "block", [(i + 1, i) for i in range(peers - 1)])
    v = coupling[0]
    vt = jnp.swapaxes(v, 1, 2)
    inter = pl.pallas_call(
        functools.partial(screen_kernel, groups),
        out_shape=[jax.ShapeDtypeStruct((rows, e_dev, orbitals), BF16)] * groups,
        in_specs=[smem, smem] + [vmem()] * 5,
        out_specs=[vmem()] * groups,
        scratch_shapes=[pltpu.VMEM((orbitals * e_dev, orbitals), F32)],
        compiler_params=params(),
    )(me, coupling_mask[0], v, vt, before, own, after)
    inter = exchange(inter)
    sigma = pl.pallas_call(
        functools.partial(sigma_kernel, groups),
        out_shape=[jax.ShapeDtypeStruct((rows, e_dev, orbitals), BF16)] * groups,
        in_specs=[vmem()] * (3 + 2 * groups),
        out_specs=[vmem()] * groups,
        compiler_params=params(),
    )(fwd_e, fwd_l, back_e, *less, *inter)
    sigma = exchange(sigma)
    out = pl.pallas_call(
        functools.partial(final_kernel, groups),
        out_shape=jax.ShapeDtypeStruct((e_dev * orbitals, orbitals), F32),
        in_specs=[smem] + [vmem()] * groups,
        out_specs=vmem(),
        compiler_params=params(),
    )(me, *sigma)
    return out.reshape(e_dev, 1, orbitals, orbitals)


def solution(mesh):
    return jax.shard_map(
        shards,
        mesh=mesh,
        in_specs=(
            P("energy", "block", None, None),
            P("energy", "block", None, None),
            P("block", None, None, None),
            P("block", None),
        ),
        out_specs=P("energy", "block", None, None),
        check_vma=False,
    )
```

profile of v0, /device:TPU:16, one launch (start us, length us, event | category | flops | bytes accessed | tf_op | source)
XLA Modules:
  0.0 106.2 jit_solution(2044916881984709888)
XLA Ops:
  0.0 1.2 %copy-done = bf16[32,1,128,128]{3,2,1,0:T(8,128)(2,1)S(1)} copy-done((bf16[32,1,128,128]{3,2,1,0:T(8,128)(2,1)S(1)}, bf16[32,1,128,128]{3,2,1,0:T(8,128)(2,1)}, u32[]{:S(2)}) %copy-start) | copy-done | bytes 1048600
  1.2 2.1 %shard_map.82 = (bf16[32,32,128]{2,1,0:T(8,128)(2,1)S(1)}, bf16[32,32,128]{2,1,0:T(8,128)(2,1)S(1)}, bf16[32,32,128]{2,1,0:T(8,128)(2,1)S(1)}, bf16[32,32,128]{2,1,0:T(8,128)(2,1)S(1)}) custom-call(s32[1]{0:T(128)} %bitcast.me_ref, bf16[32,128,128]{2,1,0:T(8,128)(2,1)S(1)} %bitcast.19), custom_call_target="tpu_custom_call" | custom-call | tf_op jit(solution)/shard_map/pallas_call | solution.py:100
  3.3 1.6 %collective-permute-start = (bf16[32,32,128]{2,1,0:T(8,128)(2,1)S(1)}, bf16[32,32,128]{2,1,0:T(8,128)(2,1)S(1)}, u32[]{:S(2)}, u32[]{:S(2)}) collective-permute-start(bf16[32,32,128]{2,1,0:T(8,128)(2,1)S(1)} %get-tuple-element.26), channel_id=1, source_target_pairs={{0,8},{8,0},{16,24},{24,16},{1,9},{9,1},{17,25},{25,17},{2,10},{10... | collective-permute-start | bytes 786440 | tf_op jit(solution)/shard_map/ppermute | solution.py:220
  4.8 1.5 %collective-permute-start.1 = (bf16[32,32,128]{2,1,0:T(8,128)(2,1)S(1)}, bf16[32,32,128]{2,1,0:T(8,128)(2,1)S(1)}, u32[]{:S(2)}, u32[]{:S(2)}) collective-permute-start(bf16[32,32,128]{2,1,0:T(8,128)(2,1)S(1)} %get-tuple-element.27), channel_id=1, source_target_pairs={{0,16},{8,24},{16,0},{24,8},{1,17},{9,25},{17,1},{25,9},{2,18},{10... | collective-permute-start | bytes 786440 | tf_op jit(solution)/shard_map/ppermute | solution.py:220
  6.4 0.5 collective-permute-start.2
  6.8 1.2 %copy-done.1 = bf16[32,1,128,128]{3,2,1,0:T(8,128)(2,1)S(1)} copy-done((bf16[32,1,128,128]{3,2,1,0:T(8,128)(2,1)S(1)}, bf16[32,1,128,128]{3,2,1,0:T(8,128)(2,1)}, u32[]{:S(2)}) %copy-start.1) | copy-done | bytes 1048600
  8.1 1.3 %shard_map.83 = (bf16[32,32,128]{2,1,0:T(8,128)(2,1)S(1)}, bf16[32,32,128]{2,1,0:T(8,128)(2,1)S(1)}, bf16[32,32,128]{2,1,0:T(8,128)(2,1)S(1)}, bf16[32,32,128]{2,1,0:T(8,128)(2,1)S(1)}) custom-call(s32[1]{0:T(128)} %bitcast.me_ref, bf16[32,128,128]{2,1,0:T(8,128)(2,1)S(1)} %bitcast.20), custom_call_target="tpu_custom_call" | custom-call | tf_op jit(solution)/shard_map/pallas_call | solution.py:100
  9.3 1.6 %collective-permute-start.3 = (bf16[32,32,128]{2,1,0:T(8,128)(2,1)S(1)}, bf16[32,32,128]{2,1,0:T(8,128)(2,1)S(1)}, u32[]{:S(2)}, u32[]{:S(2)}) collective-permute-start(bf16[32,32,128]{2,1,0:T(8,128)(2,1)S(1)} %get-tuple-element.30), channel_id=1, source_target_pairs={{0,8},{8,0},{16,24},{24,16},{1,9},{9,1},{17,25},{25,17},{2,10},{10... | collective-permute-start | bytes 786440 | tf_op jit(solution)/shard_map/ppermute | solution.py:220
  10.9 1.5 %collective-permute-start.4 = (bf16[32,32,128]{2,1,0:T(8,128)(2,1)S(1)}, bf16[32,32,128]{2,1,0:T(8,128)(2,1)S(1)}, u32[]{:S(2)}, u32[]{:S(2)}) collective-permute-start(bf16[32,32,128]{2,1,0:T(8,128)(2,1)S(1)} %get-tuple-element.31), channel_id=1, source_target_pairs={{0,16},{8,24},{16,0},{24,8},{1,17},{9,25},{17,1},{25,9},{2,18},{10... | collective-permute-start | bytes 786440 | tf_op jit(solution)/shard_map/ppermute | solution.py:220
  12.4 0.1 collective-permute-done.refs_1_
  12.5 2.4 %collective-permute-start.5 = (bf16[32,32,128]{2,1,0:T(8,128)(2,1)S(1)}, bf16[32,32,128]{2,1,0:T(8,128)(2,1)S(1)}, u32[]{:S(2)}, u32[]{:S(2)}) collective-permute-start(bf16[32,32,128]{2,1,0:T(8,128)(2,1)S(1)} %get-tuple-element.32), channel_id=1, source_target_pairs={{0,24},{8,16},{16,8},{24,0},{1,25},{9,17},{17,9},{25,1},{2,26},{10... | collective-permute-start | bytes 786440 | tf_op jit(solution)/shard_map/ppermute | solution.py:220
  15.0 0.9 dynamic-slice_bitcast_fusion.3.fwd_ref.fwd_e_ref
  15.9 0.9 dynamic-slice_bitcast_fusion.back_ref
  16.8 2.1 %collective-permute-done.1.refs_2_ = bf16[32,32,128]{2,1,0:T(8,128)(2,1)S(1)} collective-permute-done((bf16[32,32,128]{2,1,0:T(8,128)(2,1)S(1)}, bf16[32,32,128]{2,1,0:T(8,128)(2,1)S(1)}, u32[]{:S(2)}, u32[]{:S(2)}) %collective-permute-start.1) | collective-permute-done | bytes 262176 | tf_op jit(solution)/shard_map/ppermute | solution.py:220
  19.0 0.2 collective-permute-done.2.refs_3_
  19.2 4.7 %collective-permute-done.3.refs_5_ = bf16[32,32,128]{2,1,0:T(8,128)(2,1)S(1)} collective-permute-done((bf16[32,32,128]{2,1,0:T(8,128)(2,1)S(1)}, bf16[32,32,128]{2,1,0:T(8,128)(2,1)S(1)}, u32[]{:S(2)}, u32[]{:S(2)}) %collective-permute-start.3) | collective-permute-done | bytes 262176 | tf_op jit(solution)/shard_map/ppermute | solution.py:220
  23.8 5.6 %collective-permute-done.4.refs_6_ = bf16[32,32,128]{2,1,0:T(8,128)(2,1)S(1)} collective-permute-done((bf16[32,32,128]{2,1,0:T(8,128)(2,1)S(1)}, bf16[32,32,128]{2,1,0:T(8,128)(2,1)S(1)}, u32[]{:S(2)}, u32[]{:S(2)}) %collective-permute-start.4) | collective-permute-done | bytes 262176 | tf_op jit(solution)/shard_map/ppermute | solution.py:220
  29.5 0.0 collective-permute-done.5.refs_7_
  29.5 4.9 %shard_map.84 = (bf16[32,32,128]{2,1,0:T(8,128)(2,1)S(1)}, bf16[32,32,128]{2,1,0:T(8,128)(2,1)S(1)}, bf16[32,32,128]{2,1,0:T(8,128)(2,1)S(1)}, bf16[32,32,128]{2,1,0:T(8,128)(2,1)S(1)}) custom-call(bf16[192,256]{1,0:T(8,128)(2,1)S(1)} %dynamic-slice_bitcast_fusion.3.fwd_ref.fwd_e_ref, bf16[256,192]{1,0:T(8,128)(2,1)S(1)} %dynamic-slice_bitcast_fusion.back_ref, ...), custom_call_target="tpu_custom_call" | custom-call | tf_op jit(solution)/shard_map/pallas_call | solution.py:239
  34.4 1.3 %collective-permute-start.6 = (bf16[32,32,128]{2,1,0:T(8,128)(2,1)S(1)}, bf16[32,32,128]{2,1,0:T(8,128)(2,1)S(1)}, u32[]{:S(2)}, u32[]{:S(2)}) collective-permute-start(bf16[32,32,128]{2,1,0:T(8,128)(2,1)S(1)} %get-tuple-element.34), channel_id=1, source_target_pairs={{0,8},{8,0},{16,24},{24,16},{1,9},{9,1},{17,25},{25,17},{2,10},{10... | collective-permute-start | bytes 786440 | tf_op jit(solution)/shard_map/ppermute | solution.py:220
  35.7 0.8 collective-permute-start.7
  36.5 1.4 %collective-permute-start.8 = (bf16[32,32,128]{2,1,0:T(8,128)(2,1)S(1)}, bf16[32,32,128]{2,1,0:T(8,128)(2,1)S(1)}, u32[]{:S(2)}, u32[]{:S(2)}) collective-permute-start(bf16[32,32,128]{2,1,0:T(8,128)(2,1)S(1)} %get-tuple-element.36), channel_id=1, source_target_pairs={{0,24},{8,16},{16,8},{24,0},{1,25},{9,17},{17,9},{25,1},{2,26},{10... | collective-permute-start | bytes 786440 | tf_op jit(solution)/shard_map/ppermute | solution.py:220
  37.9 5.8 %collective-permute-done.6.refs_1_ = bf16[32,32,128]{2,1,0:T(8,128)(2,1)S(1)} collective-permute-done((bf16[32,32,128]{2,1,0:T(8,128)(2,1)S(1)}, bf16[32,32,128]{2,1,0:T(8,128)(2,1)S(1)}, u32[]{:S(2)}, u32[]{:S(2)}) %collective-permute-start.6) | collective-permute-done | bytes 262176 | tf_op jit(solution)/shard_map/ppermute | solution.py:220
  43.7 4.5 %collective-permute-done.7.refs_2_ = bf16[32,32,128]{2,1,0:T(8,128)(2,1)S(1)} collective-permute-done((bf16[32,32,128]{2,1,0:T(8,128)(2,1)S(1)}, bf16[32,32,128]{2,1,0:T(8,128)(2,1)S(1)}, u32[]{:S(2)}, u32[]{:S(2)}) %collective-permute-start.7) | collective-permute-done | bytes 262176 | tf_op jit(solution)/shard_map/ppermute | solution.py:220
  48.2 0.0 collective-permute-done.8.refs_3_
  48.2 0.1 shard_map.85.own
  48.3 1.9 %collective-permute-start.10 = (bf16[32,128,128]{2,1,0:T(8,128)(2,1)S(1)}, bf16[32,128,128]{2,1,0:T(8,128)(2,1)S(1)}, u32[]{:S(2)}, u32[]{:S(2)}) collective-permute-start(bf16[32,128,128]{2,1,0:T(8,128)(2,1)S(1)} %shard_map.85.own), channel_id=1, source_target_pairs={{1,0},{2,1},{3,2},{4,3},{5,4},{6,5},{7,6},{9,8},{10,9},{11,10},{12... | collective-permute-start | bytes 3145736 | tf_op jit(solution)/shard_map/ppermute | solution.py:256
  50.3 2.6 %collective-permute-start.9 = (bf16[32,128,128]{2,1,0:T(8,128)(2,1)S(1)}, bf16[32,128,128]{2,1,0:T(8,128)(2,1)}, u32[]{:S(2)}, u32[]{:S(2)}) collective-permute-start(bf16[32,128,128]{2,1,0:T(8,128)(2,1)S(1)} %shard_map.85.own), channel_id=1, source_target_pairs={{0,1},{1,2},{2,3},{3,4},{4,5},{5,6},{6,7},{8,9},{9,10},{10,11},{11... | collective-permute-start | bytes 3145736 | tf_op jit(solution)/shard_map/ppermute | solution.py:255
  52.9 0.1 copy.9
  53.0 9.6 %collective-permute-done.10.after = bf16[32,128,128]{2,1,0:T(8,128)(2,1)S(1)} collective-permute-done((bf16[32,128,128]{2,1,0:T(8,128)(2,1)S(1)}, bf16[32,128,128]{2,1,0:T(8,128)(2,1)S(1)}, u32[]{:S(2)}, u32[]{:S(2)}) %collective-permute-start.10) | collective-permute-done | bytes 1048608 | tf_op jit(solution)/shard_map/ppermute | solution.py:256
  62.6 3.9 %collective-permute-done.9.before = bf16[32,128,128]{2,1,0:T(8,128)(2,1)} collective-permute-done((bf16[32,128,128]{2,1,0:T(8,128)(2,1)S(1)}, bf16[32,128,128]{2,1,0:T(8,128)(2,1)}, u32[]{:S(2)}, u32[]{:S(2)}) %collective-permute-start.9) | collective-permute-done | bytes 1048608 | tf_op jit(solution)/shard_map/ppermute | solution.py:255
  66.5 6.0 %shard_map.86 = (bf16[32,32,128]{2,1,0:T(8,128)(2,1)S(1)}, bf16[32,32,128]{2,1,0:T(8,128)(2,1)S(1)}, bf16[32,32,128]{2,1,0:T(8,128)(2,1)S(1)}, bf16[32,32,128]{2,1,0:T(8,128)(2,1)S(1)}) custom-call(s32[1]{0:T(128)} %bitcast.me_ref, s32[2]{0:T(128)S(1)} %bitcast.23, bf16[3,128,128]{2,1,0:T(8,128)(2,1)S(1)} %bitcast.21, bf16[3,128,128]{2,1,0:T(8,128)(2,1)S(1)} %bitcast.22, ...), custom_call_target="tpu_custom_call" | custom-call | tf_op jit(solution)/shard_map/pallas_call | solution.py:259
  72.4 0.7 collective-permute-start.11
  73.1 1.2 %collective-permute-start.12 = (bf16[32,32,128]{2,1,0:T(8,128)(2,1)S(1)}, bf16[32,32,128]{2,1,0:T(8,128)(2,1)S(1)}, u32[]{:S(2)}, u32[]{:S(2)}) collective-permute-start(bf16[32,32,128]{2,1,0:T(8,128)(2,1)S(1)} %get-tuple-element.39), channel_id=1, source_target_pairs={{0,16},{8,24},{16,0},{24,8},{1,17},{9,25},{17,1},{25,9},{2,18},{10... | collective-permute-start | bytes 786440 | tf_op jit(solution)/shard_map/ppermute | solution.py:220
  74.3 1.7 %collective-permute-start.13 = (bf16[32,32,128]{2,1,0:T(8,128)(2,1)S(1)}, bf16[32,32,128]{2,1,0:T(8,128)(2,1)S(1)}, u32[]{:S(2)}, u32[]{:S(2)}) collective-permute-start(bf16[32,32,128]{2,1,0:T(8,128)(2,1)S(1)} %get-tuple-element.40), channel_id=1, source_target_pairs={{0,24},{8,16},{16,8},{24,0},{1,25},{9,17},{17,9},{25,1},{2,26},{10... | collective-permute-start | bytes 786440 | tf_op jit(solution)/shard_map/ppermute | solution.py:220
  76.0 0.9 dynamic-slice_bitcast_fusion.2.fwd_l_ref
  76.9 0.9 dynamic-slice_bitcast_fusion.1.back_ref
  77.8 3.9 %collective-permute-done.11.refs_5_ = bf16[32,32,128]{2,1,0:T(8,128)(2,1)S(1)} collective-permute-done((bf16[32,32,128]{2,1,0:T(8,128)(2,1)S(1)}, bf16[32,32,128]{2,1,0:T(8,128)(2,1)S(1)}, u32[]{:S(2)}, u32[]{:S(2)}) %collective-permute-start.11) | collective-permute-done | bytes 262176 | tf_op jit(solution)/shard_map/ppermute | solution.py:220
  81.8 4.0 %collective-permute-done.12.refs_6_ = bf16[32,32,128]{2,1,0:T(8,128)(2,1)S(1)} collective-permute-done((bf16[32,32,128]{2,1,0:T(8,128)(2,1)S(1)}, bf16[32,32,128]{2,1,0:T(8,128)(2,1)S(1)}, u32[]{:S(2)}, u32[]{:S(2)}) %collective-permute-start.12) | collective-permute-done | bytes 262176 | tf_op jit(solution)/shard_map/ppermute | solution.py:220
  85.7 0.0 collective-permute-done.13.refs_7_
  85.8 4.1 %shard_map.87 = (bf16[32,32,128]{2,1,0:T(8,128)(2,1)S(1)}, bf16[32,32,128]{2,1,0:T(8,128)(2,1)S(1)}, bf16[32,32,128]{2,1,0:T(8,128)(2,1)S(1)}, bf16[32,32,128]{2,1,0:T(8,128)(2,1)S(1)}) custom-call(bf16[192,256]{1,0:T(8,128)(2,1)S(1)} %dynamic-slice_bitcast_fusion.3.fwd_ref.fwd_e_ref, bf16[192,256]{1,0:T(8,128)(2,1)S(1)} %dynamic-slice_bitcast_fusion.2.fwd_l_ref, ...), custom_call_target="tpu_custom_call" | custom-call | tf_op jit(solution)/shard_map/pallas_call | solution.py:268
  89.9 1.5 %collective-permute-start.14 = (bf16[32,32,128]{2,1,0:T(8,128)(2,1)S(1)}, bf16[32,32,128]{2,1,0:T(8,128)(2,1)S(1)}, u32[]{:S(2)}, u32[]{:S(2)}) collective-permute-start(bf16[32,32,128]{2,1,0:T(8,128)(2,1)S(1)} %get-tuple-element.42), channel_id=1, source_target_pairs={{0,8},{8,0},{16,24},{24,16},{1,9},{9,1},{17,25},{25,17},{2,10},{10... | collective-permute-start | bytes 786440 | tf_op jit(solution)/shard_map/ppermute | solution.py:220
  91.4 0.6 collective-permute-start.15
  91.9 1.5 %collective-permute-start.16 = (bf16[32,32,128]{2,1,0:T(8,128)(2,1)S(1)}, bf16[32,32,128]{2,1,0:T(8,128)(2,1)S(1)}, u32[]{:S(2)}, u32[]{:S(2)}) collective-permute-start(bf16[32,32,128]{2,1,0:T(8,128)(2,1)S(1)} %get-tuple-element.44), channel_id=1, source_target_pairs={{0,24},{8,16},{16,8},{24,0},{1,25},{9,17},{17,9},{25,1},{2,26},{10... | collective-permute-start | bytes 786440 | tf_op jit(solution)/shard_map/ppermute | solution.py:220
  93.4 5.4 %collective-permute-done.14.refs_1_ = bf16[32,32,128]{2,1,0:T(8,128)(2,1)S(1)} collective-permute-done((bf16[32,32,128]{2,1,0:T(8,128)(2,1)S(1)}, bf16[32,32,128]{2,1,0:T(8,128)(2,1)S(1)}, u32[]{:S(2)}, u32[]{:S(2)}) %collective-permute-start.14) | collective-permute-done | bytes 262176 | tf_op jit(solution)/shard_map/ppermute | solution.py:220
  98.8 4.1 %collective-permute-done.15.refs_2_ = bf16[32,32,128]{2,1,0:T(8,128)(2,1)S(1)} collective-permute-done((bf16[32,32,128]{2,1,0:T(8,128)(2,1)S(1)}, bf16[32,32,128]{2,1,0:T(8,128)(2,1)S(1)}, u32[]{:S(2)}, u32[]{:S(2)}) %collective-permute-start.15) | collective-permute-done | bytes 262176 | tf_op jit(solution)/shard_map/ppermute | solution.py:220
  102.9 0.0 collective-permute-done.16.refs_3_
  102.9 3.3 %shard_map.88 = f32[4096,128]{1,0:T(8,128)} custom-call(s32[1]{0:T(128)} %bitcast.me_ref, bf16[32,32,128]{2,1,0:T(8,128)(2,1)S(1)} %get-tuple-element.41.refs_0_, bf16[32,32,128]{2,1,0:T(8,128)(2,1)S(1)} %collective-permute-done.14.refs_1_, bf16[32,32,128]{2,1,0:T(8,128)(2,1)S(1)} %collective-permute-done.15.refs_2_, ...), custom_call_target="tpu_custom_call" | custom-call | tf_op jit(solution)/shard_map/pallas_call | solution.py:276
  (6 shorter events, 0.0 us)
Async XLA Ops:
  0.0 1.2 %copy-start = (bf16[32,1,128,128]{3,2,1,0:T(8,128)(2,1)S(1)}, bf16[32,1,128,128]{3,2,1,0:T(8,128)(2,1)}, u32[]{:S(2)}) copy-start(bf16[32,1,128,128]{3,2,1,0:T(8,128)(2,1)} %param.8) | copy-start | bytes 3145732
  3.3 9.3 %collective-permute-start = (bf16[32,32,128]{2,1,0:T(8,128)(2,1)S(1)}, bf16[32,32,128]{2,1,0:T(8,128)(2,1)S(1)}, u32[]{:S(2)}, u32[]{:S(2)}) collective-permute-start(bf16[32,32,128]{2,1,0:T(8,128)(2,1)S(1)} %get-tuple-element.26), channel_id=1, source_target_pairs={{0,8},{8,0},{16,24},{24,16},{1,9},{9,1},{17,25},{25,17},{2,10},{10... | collective-permute-start | bytes 786440 | tf_op jit(solution)/shard_map/ppermute | solution.py:220
  4.8 14.1 %collective-permute-start.1 = (bf16[32,32,128]{2,1,0:T(8,128)(2,1)S(1)}, bf16[32,32,128]{2,1,0:T(8,128)(2,1)S(1)}, u32[]{:S(2)}, u32[]{:S(2)}) collective-permute-start(bf16[32,32,128]{2,1,0:T(8,128)(2,1)S(1)} %get-tuple-element.27), channel_id=1, source_target_pairs={{0,16},{8,24},{16,0},{24,8},{1,17},{9,25},{17,1},{25,9},{2,18},{10... | collective-permute-start | bytes 786440 | tf_op jit(solution)/shard_map/ppermute | solution.py:220
  6.4 12.8 %collective-permute-start.2 = (bf16[32,32,128]{2,1,0:T(8,128)(2,1)S(1)}, bf16[32,32,128]{2,1,0:T(8,128)(2,1)S(1)}, u32[]{:S(2)}, u32[]{:S(2)}) collective-permute-start(bf16[32,32,128]{2,1,0:T(8,128)(2,1)S(1)} %get-tuple-element.28), channel_id=1, source_target_pairs={{0,24},{8,16},{16,8},{24,0},{1,25},{9,17},{17,9},{25,1},{2,26},{10... | collective-permute-start | bytes 786440 | tf_op jit(solution)/shard_map/ppermute | solution.py:220
  6.8 1.2 %copy-start.1 = (bf16[32,1,128,128]{3,2,1,0:T(8,128)(2,1)S(1)}, bf16[32,1,128,128]{3,2,1,0:T(8,128)(2,1)}, u32[]{:S(2)}) copy-start(bf16[32,1,128,128]{3,2,1,0:T(8,128)(2,1)} %param.9) | copy-start | bytes 3145732
  9.3 14.5 %collective-permute-start.3 = (bf16[32,32,128]{2,1,0:T(8,128)(2,1)S(1)}, bf16[32,32,128]{2,1,0:T(8,128)(2,1)S(1)}, u32[]{:S(2)}, u32[]{:S(2)}) collective-permute-start(bf16[32,32,128]{2,1,0:T(8,128)(2,1)S(1)} %get-tuple-element.30), channel_id=1, source_target_pairs={{0,8},{8,0},{16,24},{24,16},{1,9},{9,1},{17,25},{25,17},{2,10},{10... | collective-permute-start | bytes 786440 | tf_op jit(solution)/shard_map/ppermute | solution.py:220
  10.9 18.6 %collective-permute-start.4 = (bf16[32,32,128]{2,1,0:T(8,128)(2,1)S(1)}, bf16[32,32,128]{2,1,0:T(8,128)(2,1)S(1)}, u32[]{:S(2)}, u32[]{:S(2)}) collective-permute-start(bf16[32,32,128]{2,1,0:T(8,128)(2,1)S(1)} %get-tuple-element.31), channel_id=1, source_target_pairs={{0,16},{8,24},{16,0},{24,8},{1,17},{9,25},{17,1},{25,9},{2,18},{10... | collective-permute-start | bytes 786440 | tf_op jit(solution)/shard_map/ppermute | solution.py:220
  12.5 16.9 %collective-permute-start.5 = (bf16[32,32,128]{2,1,0:T(8,128)(2,1)S(1)}, bf16[32,32,128]{2,1,0:T(8,128)(2,1)S(1)}, u32[]{:S(2)}, u32[]{:S(2)}) collective-permute-start(bf16[32,32,128]{2,1,0:T(8,128)(2,1)S(1)} %get-tuple-element.32), channel_id=1, source_target_pairs={{0,24},{8,16},{16,8},{24,0},{1,25},{9,17},{17,9},{25,1},{2,26},{10... | collective-permute-start | bytes 786440 | tf_op jit(solution)/shard_map/ppermute | solution.py:220
  29.5 23.4 %copy-start.2 = (bf16[1,3,128,128]{3,2,1,0:T(8,128)(2,1)S(1)}, bf16[1,3,128,128]{3,2,1,0:T(8,128)(2,1)}, u32[]{:S(2)}) copy-start(bf16[1,3,128,128]{3,2,1,0:T(8,128)(2,1)} %param.10) | copy-start | bytes 294916
  29.5 37.0 %copy-start.3 = (s32[1,2]{1,0:T(1,128)S(1)}, s32[1,2]{1,0:T(1,128)}, u32[]{:S(2)}) copy-start(s32[1,2]{1,0:T(1,128)} %param.11) | copy-start | bytes 28
  34.4 9.3 %collective-permute-start.6 = (bf16[32,32,128]{2,1,0:T(8,128)(2,1)S(1)}, bf16[32,32,128]{2,1,0:T(8,128)(2,1)S(1)}, u32[]{:S(2)}, u32[]{:S(2)}) collective-permute-start(bf16[32,32,128]{2,1,0:T(8,128)(2,1)S(1)} %get-tuple-element.34), channel_id=1, source_target_pairs={{0,8},{8,0},{16,24},{24,16},{1,9},{9,1},{17,25},{25,17},{2,10},{10... | collective-permute-start | bytes 786440 | tf_op jit(solution)/shard_map/ppermute | solution.py:220
  35.7 12.5 %collective-permute-start.7 = (bf16[32,32,128]{2,1,0:T(8,128)(2,1)S(1)}, bf16[32,32,128]{2,1,0:T(8,128)(2,1)S(1)}, u32[]{:S(2)}, u32[]{:S(2)}) collective-permute-start(bf16[32,32,128]{2,1,0:T(8,128)(2,1)S(1)} %get-tuple-element.35), channel_id=1, source_target_pairs={{0,16},{8,24},{16,0},{24,8},{1,17},{9,25},{17,1},{25,9},{2,18},{10... | collective-permute-start | bytes 786440 | tf_op jit(solution)/shard_map/ppermute | solution.py:220
  36.5 11.7 %collective-permute-start.8 = (bf16[32,32,128]{2,1,0:T(8,128)(2,1)S(1)}, bf16[32,32,128]{2,1,0:T(8,128)(2,1)S(1)}, u32[]{:S(2)}, u32[]{:S(2)}) collective-permute-start(bf16[32,32,128]{2,1,0:T(8,128)(2,1)S(1)} %get-tuple-element.36), channel_id=1, source_target_pairs={{0,24},{8,16},{16,8},{24,0},{1,25},{9,17},{17,9},{25,1},{2,26},{10... | collective-permute-start | bytes 786440 | tf_op jit(solution)/shard_map/ppermute | solution.py:220
  48.3 14.2 %collective-permute-start.10 = (bf16[32,128,128]{2,1,0:T(8,128)(2,1)S(1)}, bf16[32,128,128]{2,1,0:T(8,128)(2,1)S(1)}, u32[]{:S(2)}, u32[]{:S(2)}) collective-permute-start(bf16[32,128,128]{2,1,0:T(8,128)(2,1)S(1)} %shard_map.85.own), channel_id=1, source_target_pairs={{1,0},{2,1},{3,2},{4,3},{5,4},{6,5},{7,6},{9,8},{10,9},{11,10},{12... | collective-permute-start | bytes 3145736 | tf_op jit(solution)/shard_map/ppermute | solution.py:256
  50.3 16.2 %collective-permute-start.9 = (bf16[32,128,128]{2,1,0:T(8,128)(2,1)S(1)}, bf16[32,128,128]{2,1,0:T(8,128)(2,1)}, u32[]{:S(2)}, u32[]{:S(2)}) collective-permute-start(bf16[32,128,128]{2,1,0:T(8,128)(2,1)S(1)} %shard_map.85.own), channel_id=1, source_target_pairs={{0,1},{1,2},{2,3},{3,4},{4,5},{5,6},{6,7},{8,9},{9,10},{10,11},{11... | collective-permute-start | bytes 3145736 | tf_op jit(solution)/shard_map/ppermute | solution.py:255
  72.4 9.3 %collective-permute-start.11 = (bf16[32,32,128]{2,1,0:T(8,128)(2,1)S(1)}, bf16[32,32,128]{2,1,0:T(8,128)(2,1)S(1)}, u32[]{:S(2)}, u32[]{:S(2)}) collective-permute-start(bf16[32,32,128]{2,1,0:T(8,128)(2,1)S(1)} %get-tuple-element.38), channel_id=1, source_target_pairs={{0,8},{8,0},{16,24},{24,16},{1,9},{9,1},{17,25},{25,17},{2,10},{10... | collective-permute-start | bytes 786440 | tf_op jit(solution)/shard_map/ppermute | solution.py:220
  73.1 12.6 %collective-permute-start.12 = (bf16[32,32,128]{2,1,0:T(8,128)(2,1)S(1)}, bf16[32,32,128]{2,1,0:T(8,128)(2,1)S(1)}, u32[]{:S(2)}, u32[]{:S(2)}) collective-permute-start(bf16[32,32,128]{2,1,0:T(8,128)(2,1)S(1)} %get-tuple-element.39), channel_id=1, source_target_pairs={{0,16},{8,24},{16,0},{24,8},{1,17},{9,25},{17,1},{25,9},{2,18},{10... | collective-permute-start | bytes 786440 | tf_op jit(solution)/shard_map/ppermute | solution.py:220
  74.3 11.5 %collective-permute-start.13 = (bf16[32,32,128]{2,1,0:T(8,128)(2,1)S(1)}, bf16[32,32,128]{2,1,0:T(8,128)(2,1)S(1)}, u32[]{:S(2)}, u32[]{:S(2)}) collective-permute-start(bf16[32,32,128]{2,1,0:T(8,128)(2,1)S(1)} %get-tuple-element.40), channel_id=1, source_target_pairs={{0,24},{8,16},{16,8},{24,0},{1,25},{9,17},{17,9},{25,1},{2,26},{10... | collective-permute-start | bytes 786440 | tf_op jit(solution)/shard_map/ppermute | solution.py:220
  89.9 9.0 %collective-permute-start.14 = (bf16[32,32,128]{2,1,0:T(8,128)(2,1)S(1)}, bf16[32,32,128]{2,1,0:T(8,128)(2,1)S(1)}, u32[]{:S(2)}, u32[]{:S(2)}) collective-permute-start(bf16[32,32,128]{2,1,0:T(8,128)(2,1)S(1)} %get-tuple-element.42), channel_id=1, source_target_pairs={{0,8},{8,0},{16,24},{24,16},{1,9},{9,1},{17,25},{25,17},{2,10},{10... | collective-permute-start | bytes 786440 | tf_op jit(solution)/shard_map/ppermute | solution.py:220
  91.4 11.6 %collective-permute-start.15 = (bf16[32,32,128]{2,1,0:T(8,128)(2,1)S(1)}, bf16[32,32,128]{2,1,0:T(8,128)(2,1)S(1)}, u32[]{:S(2)}, u32[]{:S(2)}) collective-permute-start(bf16[32,32,128]{2,1,0:T(8,128)(2,1)S(1)} %get-tuple-element.43), channel_id=1, source_target_pairs={{0,16},{8,24},{16,0},{24,8},{1,17},{9,25},{17,1},{25,9},{2,18},{10... | collective-permute-start | bytes 786440 | tf_op jit(solution)/shard_map/ppermute | solution.py:220
  91.9 11.0 %collective-permute-start.16 = (bf16[32,32,128]{2,1,0:T(8,128)(2,1)S(1)}, bf16[32,32,128]{2,1,0:T(8,128)(2,1)S(1)}, u32[]{:S(2)}, u32[]{:S(2)}) collective-permute-start(bf16[32,32,128]{2,1,0:T(8,128)(2,1)S(1)} %get-tuple-element.44), channel_id=1, source_target_pairs={{0,24},{8,16},{16,8},{24,0},{1,25},{9,17},{17,9},{25,1},{2,26},{10... | collective-permute-start | bytes 786440 | tf_op jit(solution)/shard_map/ppermute | solution.py:220
where the time goes:
time: 107 us; the launch traced here: 106 us
  waiting for transfers between devices  54 us (50%)
  starting transfers between devices  24.2 us (23%)
  Pallas kernels  21.6 us (20%)
  local copies, waits for them, and re-layouts  6.2 us (6%)
    ppermute x15, waiting for transfers between devices, exchange(): lax.ppermute(parts[d], 'energy', [(i, i ^ d) for i in range(groups)])  40.5 us
    ppermute x15, starting transfers between devices, exchange(): lax.ppermute(parts[d], 'energy', [(i, i ^ d) for i in range(groups)])  19.7 us
    ppermute x1, waiting for transfers between devices, shards(): after = lax.ppermute(own, 'block', [(i + 1, i) for i in range(peers - 1)])  9.56 us
    pallas_call x1, Pallas kernels, shards(): pl.pallas_call(functools.partial(screen_kernel, groups), out_shape=[jax.S...  5.96 us
    pallas_call x1, Pallas kernels, shards(): pl.pallas_call(functools.partial(pol_kernel, groups), out_shape=[jax.Shap...  4.91 us
    pallas_call x1, Pallas kernels, shards(): pl.pallas_call(functools.partial(sigma_kernel, groups), out_shape=[jax.Sh...  4.1 us
    ppermute x1, waiting for transfers between devices, shards(): before = lax.ppermute(own, 'block', [(i, i + 1) for i in range(peers - 1)])  3.93 us
    squeeze x4, local copies, waits for them, and re-layouts, shards(): lax.dynamic_index_in_dim(jnp.asarray(t), index, 0, keepdims=False)  3.62 us
  transfers between devices with their start and end apart: 17, of which 13 were waited for; matrix products, arithmetic and copies ran while one was open for 4% of the time, Pallas kernels for 1%

commit v1 on v0

v1 whole, which is shorter than its diff:
```python
import functools
import math

import jax
import jax.numpy as jnp
import numpy as np
from jax import lax
from jax.experimental import pallas as pl
from jax.experimental.pallas import tpu as pltpu
from jax.sharding import PartitionSpec as P

BF16 = jnp.bfloat16
F32 = jnp.float32
WIDE = 8


def split(table):
    upper = table.astype(BF16)
    lower = (table - upper.astype(np.float32)).astype(BF16)
    return upper, lower


def tables(groups, e_dev):
    total = groups * e_dev
    length = 3 * total // 2
    omega = 2.0 * math.pi / length * (np.arange(length // 2) + 0.5)
    scale = 2.0 / (length * math.sqrt(total))
    energies = np.arange(total)
    lags = energies - total // 2

    def forward(points):
        angle = omega[:, None] * points[None, :]
        table = np.concatenate([np.cos(angle), np.sin(angle)], axis=0).astype(np.float32)
        return np.concatenate(split(table), axis=1)

    def backward(points):
        angle = points[:, None] * omega[None, :]
        table = np.concatenate([np.cos(angle), np.sin(angle)], axis=1) * scale
        return np.concatenate(split(table.astype(np.float32)), axis=0)

    def ordered(me):
        return np.concatenate([np.arange(e_dev) + (me ^ d) * e_dev for d in range(groups)])

    fwd_e = np.stack([forward(energies[ordered(me)]) for me in range(groups)])
    fwd_l = np.stack([forward(lags[ordered(me)]) for me in range(groups)])
    back_l = np.stack([backward(lags[ordered(me)]) for me in range(groups)])
    back_e = np.stack([backward(energies[ordered(me)]) for me in range(groups)])
    return fwd_e, fwd_l, back_l, back_e


def params():
    return pltpu.CompilerParams(vmem_limit_bytes=12 * 1024 * 1024)


def vmem():
    return pl.BlockSpec(memory_space=pltpu.VMEM)


def dot(a, b):
    return jnp.dot(a, b, preferred_element_type=F32)


def prepare_kernel(groups, transposed, me_ref, hbm, *rest):
    outs = rest[:groups]
    x_ref, scratch, sems = rest[groups:]
    e_dev, orbitals, _ = x_ref.shape
    rows = orbitals // groups
    me = me_ref[0]
    span = e_dev // sems.shape[0]
    copies = []
    for p in range(sems.shape[0]):
        part = pl.ds(p * span, span)
        copies.append(pltpu.make_async_copy(hbm.at[part], x_ref.at[part], sems.at[p]))
        copies[p].start()
    for p, copy in enumerate(copies):
        copy.wait()
        for e in range(p * span, (p + 1) * span):
            x = x_ref[e].astype(F32)
            scratch[pl.ds(e, orbitals, stride=e_dev), :] = x.T if transposed else x
    size = rows * e_dev
    for d in range(groups):
        part = scratch[pl.ds(pl.multiple_of((me ^ d) * size, size), size), :]
        outs[d][...] = part.astype(BF16).reshape(rows, e_dev, orbitals)


def gathered(refs, i):
    both = jnp.concatenate(
        [jnp.concatenate([ref[i + h] for ref in refs], axis=0) for h in range(WIDE)], axis=1
    )
    return jnp.concatenate([both, both], axis=0)


def inverse(back, spectrum):
    both = dot(back, spectrum.astype(BF16))
    half = both.shape[0] // 2
    return both[:half] + both[half:]


def spectrum_kernel(fwd_ref, *refs):
    less, out = refs[:-1], refs[-1]
    fwd = fwd_ref[...]
    for n in range(out.shape[0]):
        out[n] = dot(fwd, gathered(less, n * WIDE))


def pol_kernel(groups, halves, fwd_ref, back_ref, less_ref, *refs):
    great, outs, scratch = refs[:groups], refs[groups:-1], refs[-1]
    rows, e_dev, orbitals = great[0].shape
    freq = fwd_ref.shape[0] // 2
    fwd, back = fwd_ref[...], back_ref[...]
    total = groups * e_dev
    for n in range(less_ref.shape[0]):
        a = less_ref[n]
        b = dot(fwd, gathered(great, n * WIDE))
        real = a[:freq] * b[:freq] + a[freq:] * b[freq:]
        imag = a[freq:] * b[:freq] - a[:freq] * b[freq:]
        pol = inverse(back, jnp.concatenate([real, imag], axis=0))
        for h in range(WIDE):
            scratch[pl.ds(n * WIDE + h, total, stride=rows), :] = pol[
                :, h * orbitals : (h + 1) * orbitals
            ]
    lags = e_dev // halves
    size = lags * rows
    for h in range(halves):
        for d in range(groups):
            start = (d * halves + h) * size
            outs[h * groups + d][...] = (
                scratch[start : start + size, :].astype(BF16).reshape(lags, rows, orbitals)
            )


def sigma_kernel(groups, halves, fwd_l_ref, back_ref, less_ref, *refs):
    inter, outs = refs[: groups * halves], refs[groups * halves :]
    count, e_dev, orbitals = outs[0].shape
    inter = [inter[h * groups + d] for d in range(groups) for h in range(halves)]
    freq = fwd_l_ref.shape[0] // 2
    fwd_l, back = fwd_l_ref[...], back_ref[...]
    for n in range(less_ref.shape[0]):
        a = less_ref[n]
        b = dot(fwd_l, gathered(inter, n * WIDE))
        real = a[:freq] * b[:freq] - a[freq:] * b[freq:]
        imag = a[freq:] * b[:freq] + a[:freq] * b[freq:]
        sigma = inverse(back, jnp.concatenate([real, imag], axis=0)).astype(BF16)
        for h in range(WIDE):
            c, i = divmod(n * WIDE + h, count)
            for d in range(groups):
                outs[c * groups + d][i] = sigma[
                    d * e_dev : (d + 1) * e_dev, h * orbitals : (h + 1) * orbitals
                ]


def assemble_kernel(groups, me_ref, *refs):
    ins, out = refs[:groups], refs[groups]
    rows = ins[0].shape[1]
    me = me_ref[0]
    for d in range(groups):
        start = pl.multiple_of((me ^ d) * rows, rows)
        out[:, pl.ds(start, rows), :] = ins[d][...]


def diagonal(a, b):
    zero = jnp.zeros_like(a)
    return jnp.concatenate(
        [jnp.concatenate([a, zero], axis=1), jnp.concatenate([zero, b], axis=1)], axis=0
    )


def setup_kernel(count, me_ref, odd_ref, mask_ref, v_ref, *refs):
    sources, outs = refs[:count], refs[count : 2 * count]
    near_left, near_right, far_left, far_right = refs[2 * count : -1]
    sems = refs[-1]
    copies = [
        pltpu.make_async_copy(src.at[me_ref[0]], dst, sems.at[n])
        for n, (src, dst) in enumerate(zip(sources, outs))
    ]
    for copy in copies:
        copy.start()
    odd = odd_ref[0]
    own, near, far = v_ref[1], v_ref[2 - 2 * odd], v_ref[2 * odd]

    def masked(v, t):
        return (v.astype(F32).T * mask_ref[t].astype(F32)).astype(BF16)

    near_left[...] = jnp.concatenate([own, near], axis=1)
    near_right[...] = diagonal(own.astype(F32).T.astype(BF16), masked(near, 1 - odd))
    far_left[...] = far
    far_right[...] = masked(far, odd)
    for copy in copies:
        copy.wait()


def near_kernel(left, right, own, near, out):
    lags, n, _ = own.shape
    both = jnp.concatenate([own[...].reshape(lags * n, n), near[...].reshape(lags * n, n)], axis=1)
    half = dot(both, right[...]).astype(BF16)
    half = jnp.concatenate(
        [
            jnp.concatenate([half[k * n : k * n + n, :n], half[k * n : k * n + n, n:]], axis=0)
            for k in range(lags)
        ],
        axis=1,
    )
    terms = dot(left[...], half)
    for k in range(lags):
        out[k] = terms[:, k * n : k * n + n]


def far_kernel(groups, me_ref, left, right, partial, far, *refs):
    outs, scratch = refs[:groups], refs[groups]
    lags, n, _ = far.shape
    rows = n // groups
    me = me_ref[0]
    half = dot(far[...].reshape(lags * n, n), right[...]).astype(BF16)
    half = jnp.concatenate([half[k * n : k * n + n] for k in range(lags)], axis=1)
    terms = dot(left[...], half)
    for k in range(lags):
        scratch[pl.ds(k, n, stride=lags), :] = partial[k] + terms[:, k * n : k * n + n]
    size = rows * lags
    for d in range(groups):
        place = pl.ds(pl.multiple_of((me ^ d) * size, size), size)
        outs[d][...] = scratch[place, :].astype(BF16).reshape(rows, lags, n)


def final_kernel(groups, first, me_ref, *refs):
    ins, out, scratch, sems = refs[:groups], refs[-3], refs[-2], refs[-1]
    count, e_dev, orbitals = ins[0].shape
    rows = orbitals // groups
    me = me_ref[0]
    copies = []
    for d in range(groups):
        for i in range(count):
            scratch[d, pl.ds(i, e_dev, stride=count), :] = ins[d][i].astype(F32)
        start = pl.multiple_of((me ^ d) * rows + first, 8)
        copies.append(
            pltpu.make_async_copy(
                scratch.at[d].reshape(e_dev, count, orbitals),
                out.at[:, pl.ds(start, count), :],
                sems.at[d],
            )
        )
        copies[-1].start()
    for copy in copies:
        copy.wait()


def exchange(parts):
    groups = lax.axis_size("energy")
    moved = [parts[0]]
    for d in range(1, groups):
        moved.append(lax.ppermute(parts[d], "energy", [(i, i ^ d) for i in range(groups)]))
    return moved


def call(kernel, out_shape, specs, *args, scratch=(), **kwargs):
    return pl.pallas_call(
        kernel,
        out_shape=out_shape,
        in_specs=specs,
        scratch_shapes=list(scratch),
        compiler_params=params(),
        **kwargs,
    )(*args)


def shards(g_less, g_great, coupling, coupling_mask):
    e_dev, _, orbitals, _ = g_less.shape
    groups = lax.axis_size("energy")
    peers = lax.axis_size("block")
    rows = orbitals // groups
    total = e_dev * groups
    halves = 2 if e_dev % 32 == 0 else 1
    lags = e_dev // halves
    index = lax.axis_index("energy")
    me = index.astype(jnp.int32)[None]
    odd = (lax.axis_index("block") % 2).astype(jnp.int32)[None]
    smem = pl.BlockSpec(memory_space=pltpu.SMEM)
    hbm = pl.BlockSpec(memory_space=pltpu.HBM)

    def shape(*dims, dtype=BF16):
        return jax.ShapeDtypeStruct(dims, dtype)

    less = g_less.reshape(e_dev, orbitals, orbitals)
    great = g_great.reshape(e_dev, orbitals, orbitals)
    less, great = [pltpu.with_memory_space_constraint(x, pltpu.HBM) for x in (less, great)]

    def prepared(x, transposed):
        parts = call(
            functools.partial(prepare_kernel, groups, transposed),
            [shape(rows, e_dev, orbitals)] * groups,
            [smem, hbm],
            me,
            x,
            out_specs=[vmem()] * groups,
            scratch=[
                pltpu.VMEM((e_dev, orbitals, orbitals), BF16),
                pltpu.VMEM((orbitals * e_dev, orbitals), F32),
                pltpu.SemaphoreType.DMA((4,)),
            ],
        )
        return exchange(parts)

    less = prepared(less, False)
    great = prepared(great, True)
    stacks = [pltpu.with_memory_space_constraint(jnp.asarray(t), pltpu.HBM) for t in tables(groups, e_dev)]
    square = (orbitals, orbitals)
    fwd_e, fwd_l, back_l, back_e, near_left, near_right, far_left, far_right = call(
        functools.partial(setup_kernel, len(stacks)),
        [shape(*t.shape[1:]) for t in stacks]
        + [shape(orbitals, 2 * orbitals), shape(2 * orbitals, 2 * orbitals)]
        + [shape(*square), shape(*square)],
        [smem, smem, smem, vmem()] + [hbm] * len(stacks),
        me,
        odd,
        coupling_mask[0],
        coupling[0],
        *stacks,
        out_specs=[vmem()] * (len(stacks) + 4),
        scratch=[pltpu.SemaphoreType.DMA((len(stacks),))],
    )
    less = call(
        spectrum_kernel,
        shape(rows // WIDE, fwd_e.shape[0], WIDE * orbitals, dtype=F32),
        [vmem()] * (1 + groups),
        fwd_e,
        *less,
        out_specs=vmem(),
    )
    pol = call(
        functools.partial(pol_kernel, groups, halves),
        [shape(lags, rows, orbitals)] * (halves * groups),
        [vmem()] * (3 + groups),
        fwd_e,
        back_l,
        less,
        *great,
        out_specs=[vmem()] * (halves * groups),
        scratch=[pltpu.VMEM((total * rows, orbitals), F32)],
    )
    pol = [exchange(pol[h * groups : (h + 1) * groups]) for h in range(halves)]

    near_pairs = [(b, b ^ 1) for b in range(peers) if b ^ 1 < peers]
    far_pairs = [(b, ((b + 1) ^ 1) - 1) for b in range(1, peers) if ((b + 1) ^ 1) - 1 < peers]
    inter = []
    for h in range(halves):
        own = call(
            functools.partial(assemble_kernel, groups),
            shape(lags, orbitals, orbitals),
            [smem] + [vmem()] * groups,
            me,
            *pol[h],
            out_specs=vmem(),
        )
        far = lax.ppermute(own, "block", far_pairs)
        near = lax.ppermute(own, "block", near_pairs)
        partial = call(
            near_kernel,
            shape(lags, orbitals, orbitals, dtype=F32),
            [vmem()] * 4,
            near_left,
            near_right,
            own,
            near,
            out_specs=vmem(),
        )
        parts = call(
            functools.partial(far_kernel, groups),
            [shape(rows, lags, orbitals)] * groups,
            [smem] + [vmem()] * 4,
            me,
            far_left,
            far_right,
            partial,
            far,
            out_specs=[vmem()] * groups,
            scratch=[pltpu.VMEM((orbitals * lags, orbitals), F32)],
        )
        inter += exchange(parts)

    steps = 2 if rows % 32 == 0 else 1
    count = rows // steps
    sigma = call(
        functools.partial(sigma_kernel, groups, halves),
        [shape(count, e_dev, orbitals)] * (groups * steps),
        [vmem()] * (3 + groups * halves),
        fwd_l,
        back_e,
        less,
        *inter,
        out_specs=[vmem()] * (groups * steps),
    )
    sigma = [
        (c * count, count, exchange(sigma[c * groups : (c + 1) * groups])) for c in range(steps)
    ]
    out = []
    for first, count, parts in sigma:
        out = [
            call(
                functools.partial(final_kernel, groups, first),
                shape(e_dev, orbitals, orbitals, dtype=F32),
                [smem] + [vmem()] * groups + [hbm] * len(out),
                me,
                *parts,
                *out,
                out_specs=hbm,
                scratch=[
                    pltpu.VMEM((groups, e_dev * count, orbitals), F32),
                    pltpu.SemaphoreType.DMA((groups,)),
                ],
                input_output_aliases={1 + groups: 0} if out else {},
            )
        ]
    return out[0].reshape(e_dev, 1, orbitals, orbitals)


def solution(mesh):
    return jax.shard_map(
        shards,
        mesh=mesh,
        in_specs=(
            P("energy", "block", None, None),
            P("energy", "block", None, None),
            P("block", None, None, None),
            P("block", None),
        ),
        out_specs=P("energy", "block", None, None),
        check_vma=False,
    )
```

time: 107 us -> 87.8 us (0.82)
  waiting for transfers between devices: 54 us -> 33.7 us
  starting transfers between devices: 24.2 us -> 35.8 us
  local copies, waits for them, and re-layouts: 6.2 us -> 0.01 us
  Pallas kernels: 21.6 us -> 17.8 us
    ppermute x15 -> x24, starting transfers between devices: 19.7 us -> 30.6 us  [exchange(): lax.ppermute(parts[d], 'energy', [(i, i ^ d) for i in range(groups)])]
    ppermute x15 -> x24, waiting for transfers between devices: 40.5 us -> 29.7 us  [exchange(): lax.ppermute(parts[d], 'energy', [(i, i ^ d) for i in range(groups)])]
    ppermute x2 -> x4, waiting for transfers between devices: 13.5 us -> 3.94 us  [the longest x2 3.93 us: shards(): far = lax.ppermute(own, 'block', far_pairs)]
    pallas_call x7 -> x14, Pallas kernels: 21.6 us -> 17.8 us  [call(): pl.pallas_call(kernel, out_shape=out_shape, in_specs=specs, scratch_shape...]
    squeeze x4 -> x0, local copies, waits for them, and re-layouts: 3.62 us -> none  [shards(): lax.dynamic_index_in_dim(jnp.asarray(t), index, 0, keepdims=False)]
    unnamed x9 -> x4, local copies, waits for them, and re-layouts: 2.58 us -> 0.01 us
    ppermute x2 -> x4, starting transfers between devices: 4.51 us -> 5.2 us  [the longest x2 4.87 us: shards(): far = lax.ppermute(own, 'block', far_pairs)]
  transfers between devices with their start and end apart: 17 -> 28, of which waited for: 13 -> 17; matrix products, arithmetic and copies ran while one was open for 4% -> 0% of each run, Pallas kernels for 1% -> 10%
where the time goes in v1:
time: 87.8 us; the launch traced here: 87.6 us
  starting transfers between devices  35.8 us (41%)
  waiting for transfers between devices  33.7 us (38%)
  Pallas kernels  17.8 us (20%)
    ppermute x24, starting transfers between devices, exchange(): lax.ppermute(parts[d], 'energy', [(i, i ^ d) for i in range(groups)])  30.6 us
    ppermute x24, waiting for transfers between devices, exchange(): lax.ppermute(parts[d], 'energy', [(i, i ^ d) for i in range(groups)])  29.7 us
    pallas_call x14, Pallas kernels, call(): pl.pallas_call(kernel, out_shape=out_shape, in_specs=specs, scratch_shape...  17.8 us
    ppermute x2, starting transfers between devices, shards(): far = lax.ppermute(own, 'block', far_pairs)  4.87 us
    ppermute x2, waiting for transfers between devices, shards(): far = lax.ppermute(own, 'block', far_pairs)  3.93 us
  transfers between devices with their start and end apart: 28, of which 17 were waited for; matrix products, arithmetic and copies ran while one was open for 0% of the time, Pallas kernels for 10%

profile of v1, /device:TPU:16, one launch (start us, length us, event | category | flops | bytes accessed | tf_op | source)
XLA Modules:
  0.0 87.6 jit_solution(1096721598064210595)
XLA Ops:
  0.0 3.3 %shard_map.83 = (bf16[32,32,128]{2,1,0:T(8,128)(2,1)S(1)}, bf16[32,32,128]{2,1,0:T(8,128)(2,1)S(1)}, bf16[32,32,128]{2,1,0:T(8,128)(2,1)S(1)}, bf16[32,32,128]{2,1,0:T(8,128)(2,1)S(1)}) custom-call(s32[1]{0:T(128)} %bitcast.me_ref, bf16[32,128,128]{2,1,0:T(8,128)(2,1)} %bitcast.11), custom_call_target="tpu_custom_call" | custom-call | tf_op jit(solution)/shard_map/pallas_call | solution.py:255
  3.3 1.6 %collective-permute-start = (bf16[32,32,128]{2,1,0:T(8,128)(2,1)S(1)}, bf16[32,32,128]{2,1,0:T(8,128)(2,1)S(1)}, u32[]{:S(2)}, u32[]{:S(2)}) collective-permute-start(bf16[32,32,128]{2,1,0:T(8,128)(2,1)S(1)} %get-tuple-element.49), channel_id=1, source_target_pairs={{0,8},{8,0},{16,24},{24,16},{1,9},{9,1},{17,25},{25,17},{2,10},{10... | collective-permute-start | bytes 786440 | tf_op jit(solution)/shard_map/ppermute | solution.py:250
  4.8 1.5 %collective-permute-start.1 = (bf16[32,32,128]{2,1,0:T(8,128)(2,1)S(1)}, bf16[32,32,128]{2,1,0:T(8,128)(2,1)S(1)}, u32[]{:S(2)}, u32[]{:S(2)}) collective-permute-start(bf16[32,32,128]{2,1,0:T(8,128)(2,1)S(1)} %get-tuple-element.50), channel_id=1, source_target_pairs={{0,16},{8,24},{16,0},{24,8},{1,17},{9,25},{17,1},{25,9},{2,18},{10... | collective-permute-start | bytes 786440 | tf_op jit(solution)/shard_map/ppermute | solution.py:250
  6.8 2.5 %shard_map.85 = (bf16[32,32,128]{2,1,0:T(8,128)(2,1)S(1)}, bf16[32,32,128]{2,1,0:T(8,128)(2,1)S(1)}, bf16[32,32,128]{2,1,0:T(8,128)(2,1)S(1)}, bf16[32,32,128]{2,1,0:T(8,128)(2,1)S(1)}) custom-call(s32[1]{0:T(128)} %bitcast.me_ref, bf16[32,128,128]{2,1,0:T(8,128)(2,1)} %bitcast.12), custom_call_target="tpu_custom_call" | custom-call | tf_op jit(solution)/shard_map/pallas_call | solution.py:255
  9.3 1.6 %collective-permute-start.3 = (bf16[32,32,128]{2,1,0:T(8,128)(2,1)S(1)}, bf16[32,32,128]{2,1,0:T(8,128)(2,1)S(1)}, u32[]{:S(2)}, u32[]{:S(2)}) collective-permute-start(bf16[32,32,128]{2,1,0:T(8,128)(2,1)S(1)} %get-tuple-element.58), channel_id=1, source_target_pairs={{0,8},{8,0},{16,24},{24,16},{1,9},{9,1},{17,25},{25,17},{2,10},{10... | collective-permute-start | bytes 786440 | tf_op jit(solution)/shard_map/ppermute | solution.py:250
  10.9 1.5 %collective-permute-start.4 = (bf16[32,32,128]{2,1,0:T(8,128)(2,1)S(1)}, bf16[32,32,128]{2,1,0:T(8,128)(2,1)S(1)}, u32[]{:S(2)}, u32[]{:S(2)}) collective-permute-start(bf16[32,32,128]{2,1,0:T(8,128)(2,1)S(1)} %get-tuple-element.59), channel_id=1, source_target_pairs={{0,16},{8,24},{16,0},{24,8},{1,17},{9,25},{17,1},{25,9},{2,18},{10... | collective-permute-start | bytes 786440 | tf_op jit(solution)/shard_map/ppermute | solution.py:250
  12.5 2.4 %collective-permute-start.5 = (bf16[32,32,128]{2,1,0:T(8,128)(2,1)S(1)}, bf16[32,32,128]{2,1,0:T(8,128)(2,1)S(1)}, u32[]{:S(2)}, u32[]{:S(2)}) collective-permute-start(bf16[32,32,128]{2,1,0:T(8,128)(2,1)S(1)} %get-tuple-element.60), channel_id=1, source_target_pairs={{0,24},{8,16},{16,8},{24,0},{1,25},{9,17},{17,9},{25,1},{2,26},{10... | collective-permute-start | bytes 786440 | tf_op jit(solution)/shard_map/ppermute | solution.py:250
  15.0 1.7 %shard_map.82 = (bf16[192,256]{1,0:T(8,128)(2,1)S(1)}, bf16[192,256]{1,0:T(8,128)(2,1)S(1)}, bf16[256,192]{1,0:T(8,128)(2,1)S(1)}, bf16[256,192]{1,0:T(8,128)(2,...) custom-call(s32[1]{0:T(128)} %bitcast.me_ref, ...), custom_call_target="tpu_custom_call" | custom-call | tf_op jit(solution)/shard_map/pallas_call | solution.py:255
  16.6 2.3 %collective-permute-done.1.refs_2_ = bf16[32,32,128]{2,1,0:T(8,128)(2,1)S(1)} collective-permute-done((bf16[32,32,128]{2,1,0:T(8,128)(2,1)S(1)}, bf16[32,32,128]{2,1,0:T(8,128)(2,1)S(1)}, u32[]{:S(2)}, u32[]{:S(2)}) %collective-permute-start.1) | collective-permute-done | bytes 262176 | tf_op jit(solution)/shard_map/ppermute | solution.py:250
  19.7 4.1 %collective-permute-done.3.refs_1_ = bf16[32,32,128]{2,1,0:T(8,128)(2,1)S(1)} collective-permute-done((bf16[32,32,128]{2,1,0:T(8,128)(2,1)S(1)}, bf16[32,32,128]{2,1,0:T(8,128)(2,1)S(1)}, u32[]{:S(2)}, u32[]{:S(2)}) %collective-permute-start.3) | collective-permute-done | bytes 262176 | tf_op jit(solution)/shard_map/ppermute | solution.py:250
  23.8 5.6 %collective-permute-done.4.refs_2_ = bf16[32,32,128]{2,1,0:T(8,128)(2,1)S(1)} collective-permute-done((bf16[32,32,128]{2,1,0:T(8,128)(2,1)S(1)}, bf16[32,32,128]{2,1,0:T(8,128)(2,1)S(1)}, u32[]{:S(2)}, u32[]{:S(2)}) %collective-permute-start.4) | collective-permute-done | bytes 262176 | tf_op jit(solution)/shard_map/ppermute | solution.py:250
  29.5 2.6 %shard_map.86 = (bf16[16,32,128]{2,1,0:T(8,128)(2,1)S(1)}, bf16[16,32,128]{2,1,0:T(8,128)(2,1)S(1)}, bf16[16,32,128]{2,1,0:T(8,128)(2,1)S(1)}, bf16[16,32,128]{2...) custom-call(bf16[192,256]{1,0:T(8,128)(2,1)S(1)} %get-tuple-element., ...), custom_call_target="tpu_custom_call" | custom-call | tf_op jit(solution)/shard_map/pallas_call | solution.py:255
  32.0 1.3 %collective-permute-start.6 = (bf16[16,32,128]{2,1,0:T(8,128)(2,1)S(1)}, bf16[16,32,128]{2,1,0:T(8,128)(2,1)S(1)}, u32[]{:S(2)}, u32[]{:S(2)}) collective-permute-start(bf16[16,32,128]{2,1,0:T(8,128)(2,1)S(1)} %get-tuple-element.62), channel_id=1, source_target_pairs={{0,8},{8,0},{16,24},{24,16},{1,9},{9,1},{17,25},{25,17},{2,10},{10... | collective-permute-start | bytes 393224 | tf_op jit(solution)/shard_map/ppermute | solution.py:250
  33.4 0.8 collective-permute-start.7
  34.2 1.4 %collective-permute-start.8 = (bf16[16,32,128]{2,1,0:T(8,128)(2,1)S(1)}, bf16[16,32,128]{2,1,0:T(8,128)(2,1)S(1)}, u32[]{:S(2)}, u32[]{:S(2)}) collective-permute-start(bf16[16,32,128]{2,1,0:T(8,128)(2,1)S(1)} %get-tuple-element.64), channel_id=1, source_target_pairs={{0,24},{8,16},{16,8},{24,0},{1,25},{9,17},{17,9},{25,1},{2,26},{10... | collective-permute-start | bytes 393224 | tf_op jit(solution)/shard_map/ppermute | solution.py:250
  35.6 1.3 %collective-permute-start.14 = (bf16[16,32,128]{2,1,0:T(8,128)(2,1)S(1)}, bf16[16,32,128]{2,1,0:T(8,128)(2,1)S(1)}, u32[]{:S(2)}, u32[]{:S(2)}) collective-permute-start(bf16[16,32,128]{2,1,0:T(8,128)(2,1)S(1)} %get-tuple-element.70), channel_id=1, source_target_pairs={{0,8},{8,0},{16,24},{24,16},{1,9},{9,1},{17,25},{25,17},{2,10},{10... | collective-permute-start | bytes 393224 | tf_op jit(solution)/shard_map/ppermute | solution.py:250
  36.9 0.8 collective-permute-start.15
  38.3 1.6 %collective-permute-start.16 = (bf16[16,32,128]{2,1,0:T(8,128)(2,1)S(1)}, bf16[16,32,128]{2,1,0:T(8,128)(2,1)S(1)}, u32[]{:S(2)}, u32[]{:S(2)}) collective-permute-start(bf16[16,32,128]{2,1,0:T(8,128)(2,1)S(1)} %get-tuple-element.72), channel_id=1, source_target_pairs={{0,24},{8,16},{16,8},{24,0},{1,25},{9,17},{17,9},{25,1},{2,26},{10... | collective-permute-start | bytes 393224 | tf_op jit(solution)/shard_map/ppermute | solution.py:250
  39.9 2.4 %collective-permute-done.7.refs_2_ = bf16[16,32,128]{2,1,0:T(8,128)(2,1)S(1)} collective-permute-done((bf16[16,32,128]{2,1,0:T(8,128)(2,1)S(1)}, bf16[16,32,128]{2,1,0:T(8,128)(2,1)S(1)}, u32[]{:S(2)}, u32[]{:S(2)}) %collective-permute-start.7) | collective-permute-done | bytes 131104 | tf_op jit(solution)/shard_map/ppermute | solution.py:250
  42.5 2.4 %collective-permute-start.10 = (bf16[16,128,128]{2,1,0:T(8,128)(2,1)S(1)}, bf16[16,128,128]{2,1,0:T(8,128)(2,1)S(1)}, u32[]{:S(2)}, u32[]{:S(2)}) collective-permute-start(bf16[16,128,128]{2,1,0:T(8,128)(2,1)S(1)} %shard_map.87.own), channel_id=1, source_target_pairs={{1,2},{2,1},{3,4},{4,3},{5,6},{6,5},{9,10},{10,9},{11,12},{12,11},... | collective-permute-start | bytes 1572872 | tf_op jit(solution)/shard_map/ppermute | solution.py:353
  44.9 1.0 %collective-permute-done.15.refs_2_ = bf16[16,32,128]{2,1,0:T(8,128)(2,1)S(1)} collective-permute-done((bf16[16,32,128]{2,1,0:T(8,128)(2,1)S(1)}, bf16[16,32,128]{2,1,0:T(8,128)(2,1)S(1)}, u32[]{:S(2)}, u32[]{:S(2)}) %collective-permute-start.15) | collective-permute-done | bytes 131104 | tf_op jit(solution)/shard_map/ppermute | solution.py:250
  46.2 2.4 %collective-permute-start.18 = (bf16[16,128,128]{2,1,0:T(8,128)(2,1)S(1)}, bf16[16,128,128]{2,1,0:T(8,128)(2,1)S(1)}, u32[]{:S(2)}, u32[]{:S(2)}) collective-permute-start(bf16[16,128,128]{2,1,0:T(8,128)(2,1)S(1)} %shard_map.90.own), channel_id=1, source_target_pairs={{1,2},{2,1},{3,4},{4,3},{5,6},{6,5},{9,10},{10,9},{11,12},{12,11},... | collective-permute-start | bytes 1572872 | tf_op jit(solution)/shard_map/ppermute | solution.py:353
  48.7 0.8 shard_map.88.partial
  49.5 3.5 %collective-permute-done.10.far = bf16[16,128,128]{2,1,0:T(8,128)(2,1)S(1)} collective-permute-done((bf16[16,128,128]{2,1,0:T(8,128)(2,1)S(1)}, bf16[16,128,128]{2,1,0:T(8,128)(2,1)S(1)}, u32[]{:S(2)}, u32[]{:S(2)}) %collective-permute-start.10) | collective-permute-done | bytes 524320 | tf_op jit(solution)/shard_map/ppermute | solution.py:353
  53.0 0.8 shard_map.89
  53.7 1.0 %collective-permute-start.11 = (bf16[32,16,128]{2,1,0:T(8,128)(2,1)S(1)}, bf16[32,16,128]{2,1,0:T(8,128)(2,1)S(1)}, u32[]{:S(2)}, u32[]{:S(2)}) collective-permute-start(bf16[32,16,128]{2,1,0:T(8,128)(2,1)S(1)} %get-tuple-element.66), channel_id=1, source_target_pairs={{0,8},{8,0},{16,24},{24,16},{1,9},{9,1},{17,25},{25,17},{2,10},{10... | collective-permute-start | bytes 393224 | tf_op jit(solution)/shard_map/ppermute | solution.py:250
  54.8 0.7 collective-permute-start.12
  55.5 1.8 %collective-permute-start.13 = (bf16[32,16,128]{2,1,0:T(8,128)(2,1)S(1)}, bf16[32,16,128]{2,1,0:T(8,128)(2,1)S(1)}, u32[]{:S(2)}, u32[]{:S(2)}) collective-permute-start(bf16[32,16,128]{2,1,0:T(8,128)(2,1)S(1)} %get-tuple-element.68), channel_id=1, source_target_pairs={{0,24},{8,16},{16,8},{24,0},{1,25},{9,17},{17,9},{25,1},{2,26},{10... | collective-permute-start | bytes 393224 | tf_op jit(solution)/shard_map/ppermute | solution.py:250
  57.3 0.8 shard_map.91.partial
  58.6 0.8 shard_map.92
  59.4 1.0 %collective-permute-start.19 = (bf16[32,16,128]{2,1,0:T(8,128)(2,1)S(1)}, bf16[32,16,128]{2,1,0:T(8,128)(2,1)S(1)}, u32[]{:S(2)}, u32[]{:S(2)}) collective-permute-start(bf16[32,16,128]{2,1,0:T(8,128)(2,1)S(1)} %get-tuple-element.74), channel_id=1, source_target_pairs={{0,8},{8,0},{16,24},{24,16},{1,9},{9,1},{17,25},{25,17},{2,10},{10... | collective-permute-start | bytes 393224 | tf_op jit(solution)/shard_map/ppermute | solution.py:250
  60.4 0.8 collective-permute-start.20
  61.2 1.8 %collective-permute-start.21 = (bf16[32,16,128]{2,1,0:T(8,128)(2,1)S(1)}, bf16[32,16,128]{2,1,0:T(8,128)(2,1)S(1)}, u32[]{:S(2)}, u32[]{:S(2)}) collective-permute-start(bf16[32,16,128]{2,1,0:T(8,128)(2,1)S(1)} %get-tuple-element.76), channel_id=1, source_target_pairs={{0,24},{8,16},{16,8},{24,0},{1,25},{9,17},{17,9},{25,1},{2,26},{10... | collective-permute-start | bytes 393224 | tf_op jit(solution)/shard_map/ppermute | solution.py:250
  63.5 2.3 %collective-permute-done.19.refs_5_ = bf16[32,16,128]{2,1,0:T(8,128)(2,1)S(1)} collective-permute-done((bf16[32,16,128]{2,1,0:T(8,128)(2,1)S(1)}, bf16[32,16,128]{2,1,0:T(8,128)(2,1)S(1)}, u32[]{:S(2)}, u32[]{:S(2)}) %collective-permute-start.19) | collective-permute-done | bytes 131104 | tf_op jit(solution)/shard_map/ppermute | solution.py:250
  65.8 3.3 %collective-permute-done.20.refs_6_ = bf16[32,16,128]{2,1,0:T(8,128)(2,1)S(1)} collective-permute-done((bf16[32,16,128]{2,1,0:T(8,128)(2,1)S(1)}, bf16[32,16,128]{2,1,0:T(8,128)(2,1)S(1)}, u32[]{:S(2)}, u32[]{:S(2)}) %collective-permute-start.20) | collective-permute-done | bytes 131104 | tf_op jit(solution)/shard_map/ppermute | solution.py:250
  69.1 1.7 %shard_map.93 = (bf16[16,32,128]{2,1,0:T(8,128)(2,1)S(1)}, bf16[16,32,128]{2,1,0:T(8,128)(2,1)S(1)}, bf16[16,32,128]{2,1,0:T(8,128)(2,1)S(1)}, bf16[16,32,128]{2...) custom-call(bf16[192,256]{1,0:T(8,128)(2,1)S(1)} %get-tuple-element., ...), custom_call_target="tpu_custom_call" | custom-call | tf_op jit(solution)/shard_map/pallas_call | solution.py:255
  70.8 1.1 %collective-permute-start.25 = (bf16[16,32,128]{2,1,0:T(8,128)(2,1)S(1)}, bf16[16,32,128]{2,1,0:T(8,128)(2,1)S(1)}, u32[]{:S(2)}, u32[]{:S(2)}) collective-permute-start(bf16[16,32,128]{2,1,0:T(8,128)(2,1)S(1)} %get-tuple-element.82), channel_id=1, source_target_pairs={{0,8},{8,0},{16,24},{24,16},{1,9},{9,1},{17,25},{25,17},{2,10},{10... | collective-permute-start | bytes 393224 | tf_op jit(solution)/shard_map/ppermute | solution.py:250
  71.9 1.0 %collective-permute-start.22 = (bf16[16,32,128]{2,1,0:T(8,128)(2,1)S(1)}, bf16[16,32,128]{2,1,0:T(8,128)(2,1)S(1)}, u32[]{:S(2)}, u32[]{:S(2)}) collective-permute-start(bf16[16,32,128]{2,1,0:T(8,128)(2,1)S(1)} %get-tuple-element.78), channel_id=1, source_target_pairs={{0,8},{8,0},{16,24},{24,16},{1,9},{9,1},{17,25},{25,17},{2,10},{10... | collective-permute-start | bytes 393224 | tf_op jit(solution)/shard_map/ppermute | solution.py:250
  72.9 0.8 collective-permute-start.26
  73.6 1.8 %collective-permute-start.27 = (bf16[16,32,128]{2,1,0:T(8,128)(2,1)S(1)}, bf16[16,32,128]{2,1,0:T(8,128)(2,1)S(1)}, u32[]{:S(2)}, u32[]{:S(2)}) collective-permute-start(bf16[16,32,128]{2,1,0:T(8,128)(2,1)S(1)} %get-tuple-element.84), channel_id=1, source_target_pairs={{0,24},{8,16},{16,8},{24,0},{1,25},{9,17},{17,9},{25,1},{2,26},{10... | collective-permute-start | bytes 393224 | tf_op jit(solution)/shard_map/ppermute | solution.py:250
  75.4 1.1 %collective-permute-start.23 = (bf16[16,32,128]{2,1,0:T(8,128)(2,1)S(1)}, bf16[16,32,128]{2,1,0:T(8,128)(2,1)S(1)}, u32[]{:S(2)}, u32[]{:S(2)}) collective-permute-start(bf16[16,32,128]{2,1,0:T(8,128)(2,1)S(1)} %get-tuple-element.79), channel_id=1, source_target_pairs={{0,16},{8,24},{16,0},{24,8},{1,17},{9,25},{17,1},{25,9},{2,18},{10... | collective-permute-start | bytes 393224 | tf_op jit(solution)/shard_map/ppermute | solution.py:250
  76.5 0.8 collective-permute-done.25.refs_1_
  77.3 1.6 %collective-permute-start.24 = (bf16[16,32,128]{2,1,0:T(8,128)(2,1)S(1)}, bf16[16,32,128]{2,1,0:T(8,128)(2,1)S(1)}, u32[]{:S(2)}, u32[]{:S(2)}) collective-permute-start(bf16[16,32,128]{2,1,0:T(8,128)(2,1)S(1)} %get-tuple-element.80), channel_id=1, source_target_pairs={{0,24},{8,16},{16,8},{24,0},{1,25},{9,17},{17,9},{25,1},{2,26},{10... | collective-permute-start | bytes 393224 | tf_op jit(solution)/shard_map/ppermute | solution.py:250
  78.8 1.3 %collective-permute-done.26.refs_2_ = bf16[16,32,128]{2,1,0:T(8,128)(2,1)S(1)} collective-permute-done((bf16[16,32,128]{2,1,0:T(8,128)(2,1)S(1)}, bf16[16,32,128]{2,1,0:T(8,128)(2,1)S(1)}, u32[]{:S(2)}, u32[]{:S(2)}) %collective-permute-start.26) | collective-permute-done | bytes 131104 | tf_op jit(solution)/shard_map/ppermute | solution.py:250
  80.1 3.0 %collective-permute-done.27.refs_3_ = bf16[16,32,128]{2,1,0:T(8,128)(2,1)S(1)} collective-permute-done((bf16[16,32,128]{2,1,0:T(8,128)(2,1)S(1)}, bf16[16,32,128]{2,1,0:T(8,128)(2,1)S(1)}, u32[]{:S(2)}, u32[]{:S(2)}) %collective-permute-start.27) | collective-permute-done | bytes 131104 | tf_op jit(solution)/shard_map/ppermute | solution.py:250
  83.2 1.2 %shard_map.94.refs_4_ = f32[32,128,128]{2,1,0:T(8,128)} custom-call(s32[1]{0:T(128)} %bitcast.me_ref, bf16[16,32,128]{2,1,0:T(8,128)(2,1)S(1)} %get-tuple-element.81.refs_0_, bf16[16,32,128]{2,1,0:T(8,128)(2,1)S(1)} %collective-permute-done.25.refs_1_, bf16[16,32,128]{2,1,0:T(8,128)(2,1)S(1)} %collective-permute-done.26.refs_2_, ...), custom_call_target="tpu_custom_call" | custom-call | tf_op jit(solution)/shard_map/pallas_call | solution.py:255
  84.3 1.9 %collective-permute-done.23.refs_2_ = bf16[16,32,128]{2,1,0:T(8,128)(2,1)S(1)} collective-permute-done((bf16[16,32,128]{2,1,0:T(8,128)(2,1)S(1)}, bf16[16,32,128]{2,1,0:T(8,128)(2,1)S(1)}, u32[]{:S(2)}, u32[]{:S(2)}) %collective-permute-start.23) | collective-permute-done | bytes 131104 | tf_op jit(solution)/shard_map/ppermute | solution.py:250
  86.3 1.2 %shard_map.95 = f32[32,128,128]{2,1,0:T(8,128)} custom-call(s32[1]{0:T(128)} %bitcast.me_ref, bf16[16,32,128]{2,1,0:T(8,128)(2,1)S(1)} %get-tuple-element.77.refs_0_, bf16[16,32,128]{2,1,0:T(8,128)(2,1)S(1)} %collective-permute-done.22.refs_1_, bf16[16,32,128]{2,1,0:T(8,128)(2,1)S(1)} %collective-permute-done.23.refs_2_, ...), custom_call_target="tpu_custom_call", output_to_operand_aliasing={{}: (5, {})} | custom-call | tf_op jit(solution)/shard_map/pallas_call | solution.py:255
  (26 shorter events, 3.5 us)
Async XLA Ops:
  0.0 15.0 %copy-start.1 = (s32[1,2]{1,0:T(1,128)S(1)}, s32[1,2]{1,0:T(1,128)}, u32[]{:S(2)}) copy-start(s32[1,2]{1,0:T(1,128)} %param.11) | copy-start | bytes 28
  0.0 15.0 %copy-start = (bf16[1,3,128,128]{3,2,1,0:T(8,128)(2,1)S(1)}, bf16[1,3,128,128]{3,2,1,0:T(8,128)(2,1)}, u32[]{:S(2)}) copy-start(bf16[1,3,128,128]{3,2,1,0:T(8,128)(2,1)} %param.10) | copy-start | bytes 294916
  3.3 9.3 %collective-permute-start = (bf16[32,32,128]{2,1,0:T(8,128)(2,1)S(1)}, bf16[32,32,128]{2,1,0:T(8,128)(2,1)S(1)}, u32[]{:S(2)}, u32[]{:S(2)}) collective-permute-start(bf16[32,32,128]{2,1,0:T(8,128)(2,1)S(1)} %get-tuple-element.49), channel_id=1, source_target_pairs={{0,8},{8,0},{16,24},{24,16},{1,9},{9,1},{17,25},{25,17},{2,10},{10... | collective-permute-start | bytes 786440 | tf_op jit(solution)/shard_map/ppermute | solution.py:250
  4.8 14.2 %collective-permute-start.1 = (bf16[32,32,128]{2,1,0:T(8,128)(2,1)S(1)}, bf16[32,32,128]{2,1,0:T(8,128)(2,1)S(1)}, u32[]{:S(2)}, u32[]{:S(2)}) collective-permute-start(bf16[32,32,128]{2,1,0:T(8,128)(2,1)S(1)} %get-tuple-element.50), channel_id=1, source_target_pairs={{0,16},{8,24},{16,0},{24,8},{1,17},{9,25},{17,1},{25,9},{2,18},{10... | collective-permute-start | bytes 786440 | tf_op jit(solution)/shard_map/ppermute | solution.py:250
  6.4 12.8 %collective-permute-start.2 = (bf16[32,32,128]{2,1,0:T(8,128)(2,1)S(1)}, bf16[32,32,128]{2,1,0:T(8,128)(2,1)S(1)}, u32[]{:S(2)}, u32[]{:S(2)}) collective-permute-start(bf16[32,32,128]{2,1,0:T(8,128)(2,1)S(1)} %get-tuple-element.51), channel_id=1, source_target_pairs={{0,24},{8,16},{16,8},{24,0},{1,25},{9,17},{17,9},{25,1},{2,26},{10... | collective-permute-start | bytes 786440 | tf_op jit(solution)/shard_map/ppermute | solution.py:250
  9.3 14.5 %collective-permute-start.3 = (bf16[32,32,128]{2,1,0:T(8,128)(2,1)S(1)}, bf16[32,32,128]{2,1,0:T(8,128)(2,1)S(1)}, u32[]{:S(2)}, u32[]{:S(2)}) collective-permute-start(bf16[32,32,128]{2,1,0:T(8,128)(2,1)S(1)} %get-tuple-element.58), channel_id=1, source_target_pairs={{0,8},{8,0},{16,24},{24,16},{1,9},{9,1},{17,25},{25,17},{2,10},{10... | collective-permute-start | bytes 786440 | tf_op jit(solution)/shard_map/ppermute | solution.py:250
  10.9 18.6 %collective-permute-start.4 = (bf16[32,32,128]{2,1,0:T(8,128)(2,1)S(1)}, bf16[32,32,128]{2,1,0:T(8,128)(2,1)S(1)}, u32[]{:S(2)}, u32[]{:S(2)}) collective-permute-start(bf16[32,32,128]{2,1,0:T(8,128)(2,1)S(1)} %get-tuple-element.59), channel_id=1, source_target_pairs={{0,16},{8,24},{16,0},{24,8},{1,17},{9,25},{17,1},{25,9},{2,18},{10... | collective-permute-start | bytes 786440 | tf_op jit(solution)/shard_map/ppermute | solution.py:250
  12.5 16.9 %collective-permute-start.5 = (bf16[32,32,128]{2,1,0:T(8,128)(2,1)S(1)}, bf16[32,32,128]{2,1,0:T(8,128)(2,1)S(1)}, u32[]{:S(2)}, u32[]{:S(2)}) collective-permute-start(bf16[32,32,128]{2,1,0:T(8,128)(2,1)S(1)} %get-tuple-element.60), channel_id=1, source_target_pairs={{0,24},{8,16},{16,8},{24,0},{1,25},{9,17},{17,9},{25,1},{2,26},{10... | collective-permute-start | bytes 786440 | tf_op jit(solution)/shard_map/ppermute | solution.py:250
  32.0 6.3 %collective-permute-start.6 = (bf16[16,32,128]{2,1,0:T(8,128)(2,1)S(1)}, bf16[16,32,128]{2,1,0:T(8,128)(2,1)S(1)}, u32[]{:S(2)}, u32[]{:S(2)}) collective-permute-start(bf16[16,32,128]{2,1,0:T(8,128)(2,1)S(1)} %get-tuple-element.62), channel_id=1, source_target_pairs={{0,8},{8,0},{16,24},{24,16},{1,9},{9,1},{17,25},{25,17},{2,10},{10... | collective-permute-start | bytes 393224 | tf_op jit(solution)/shard_map/ppermute | solution.py:250
  33.4 8.9 %collective-permute-start.7 = (bf16[16,32,128]{2,1,0:T(8,128)(2,1)S(1)}, bf16[16,32,128]{2,1,0:T(8,128)(2,1)S(1)}, u32[]{:S(2)}, u32[]{:S(2)}) collective-permute-start(bf16[16,32,128]{2,1,0:T(8,128)(2,1)S(1)} %get-tuple-element.63), channel_id=1, source_target_pairs={{0,16},{8,24},{16,0},{24,8},{1,17},{9,25},{17,1},{25,9},{2,18},{10... | collective-permute-start | bytes 393224 | tf_op jit(solution)/shard_map/ppermute | solution.py:250
  34.2 8.2 %collective-permute-start.8 = (bf16[16,32,128]{2,1,0:T(8,128)(2,1)S(1)}, bf16[16,32,128]{2,1,0:T(8,128)(2,1)S(1)}, u32[]{:S(2)}, u32[]{:S(2)}) collective-permute-start(bf16[16,32,128]{2,1,0:T(8,128)(2,1)S(1)} %get-tuple-element.64), channel_id=1, source_target_pairs={{0,24},{8,16},{16,8},{24,0},{1,25},{9,17},{17,9},{25,1},{2,26},{10... | collective-permute-start | bytes 393224 | tf_op jit(solution)/shard_map/ppermute | solution.py:250
  35.6 9.3 %collective-permute-start.14 = (bf16[16,32,128]{2,1,0:T(8,128)(2,1)S(1)}, bf16[16,32,128]{2,1,0:T(8,128)(2,1)S(1)}, u32[]{:S(2)}, u32[]{:S(2)}) collective-permute-start(bf16[16,32,128]{2,1,0:T(8,128)(2,1)S(1)} %get-tuple-element.70), channel_id=1, source_target_pairs={{0,8},{8,0},{16,24},{24,16},{1,9},{9,1},{17,25},{25,17},{2,10},{10... | collective-permute-start | bytes 393224 | tf_op jit(solution)/shard_map/ppermute | solution.py:250
  36.9 9.0 %collective-permute-start.15 = (bf16[16,32,128]{2,1,0:T(8,128)(2,1)S(1)}, bf16[16,32,128]{2,1,0:T(8,128)(2,1)S(1)}, u32[]{:S(2)}, u32[]{:S(2)}) collective-permute-start(bf16[16,32,128]{2,1,0:T(8,128)(2,1)S(1)} %get-tuple-element.71), channel_id=1, source_target_pairs={{0,16},{8,24},{16,0},{24,8},{1,17},{9,25},{17,1},{25,9},{2,18},{10... | collective-permute-start | bytes 393224 | tf_op jit(solution)/shard_map/ppermute | solution.py:250
  38.3 7.6 %collective-permute-start.16 = (bf16[16,32,128]{2,1,0:T(8,128)(2,1)S(1)}, bf16[16,32,128]{2,1,0:T(8,128)(2,1)S(1)}, u32[]{:S(2)}, u32[]{:S(2)}) collective-permute-start(bf16[16,32,128]{2,1,0:T(8,128)(2,1)S(1)} %get-tuple-element.72), channel_id=1, source_target_pairs={{0,24},{8,16},{16,8},{24,0},{1,25},{9,17},{17,9},{25,1},{2,26},{10... | collective-permute-start | bytes 393224 | tf_op jit(solution)/shard_map/ppermute | solution.py:250
  42.4 6.3 %collective-permute-start.9 = (bf16[16,128,128]{2,1,0:T(8,128)(2,1)S(1)}, bf16[16,128,128]{2,1,0:T(8,128)(2,1)S(1)}, u32[]{:S(2)}, u32[]{:S(2)}) collective-permute-start(bf16[16,128,128]{2,1,0:T(8,128)(2,1)S(1)} %shard_map.87.own), channel_id=1, source_target_pairs={{0,1},{1,0},{2,3},{3,2},{4,5},{5,4},{6,7},{7,6},{8,9},{9,8},{10,11... | collective-permute-start | bytes 1572872 | tf_op jit(solution)/shard_map/ppermute | solution.py:354
  42.5 10.5 %collective-permute-start.10 = (bf16[16,128,128]{2,1,0:T(8,128)(2,1)S(1)}, bf16[16,128,128]{2,1,0:T(8,128)(2,1)S(1)}, u32[]{:S(2)}, u32[]{:S(2)}) collective-permute-start(bf16[16,128,128]{2,1,0:T(8,128)(2,1)S(1)} %shard_map.87.own), channel_id=1, source_target_pairs={{1,2},{2,1},{3,4},{4,3},{5,6},{6,5},{9,10},{10,9},{11,12},{12,11},... | collective-permute-start | bytes 1572872 | tf_op jit(solution)/shard_map/ppermute | solution.py:353
  45.9 11.4 %collective-permute-start.17 = (bf16[16,128,128]{2,1,0:T(8,128)(2,1)S(1)}, bf16[16,128,128]{2,1,0:T(8,128)(2,1)S(1)}, u32[]{:S(2)}, u32[]{:S(2)}) collective-permute-start(bf16[16,128,128]{2,1,0:T(8,128)(2,1)S(1)} %shard_map.90.own), channel_id=1, source_target_pairs={{0,1},{1,0},{2,3},{3,2},{4,5},{5,4},{6,7},{7,6},{8,9},{9,8},{10,11... | collective-permute-start | bytes 1572872 | tf_op jit(solution)/shard_map/ppermute | solution.py:354
  46.2 12.4 %collective-permute-start.18 = (bf16[16,128,128]{2,1,0:T(8,128)(2,1)S(1)}, bf16[16,128,128]{2,1,0:T(8,128)(2,1)S(1)}, u32[]{:S(2)}, u32[]{:S(2)}) collective-permute-start(bf16[16,128,128]{2,1,0:T(8,128)(2,1)S(1)} %shard_map.90.own), channel_id=1, source_target_pairs={{1,2},{2,1},{3,4},{4,3},{5,6},{6,5},{9,10},{10,9},{11,12},{12,11},... | collective-permute-start | bytes 1572872 | tf_op jit(solution)/shard_map/ppermute | solution.py:353
  53.7 7.4 %collective-permute-start.11 = (bf16[32,16,128]{2,1,0:T(8,128)(2,1)S(1)}, bf16[32,16,128]{2,1,0:T(8,128)(2,1)S(1)}, u32[]{:S(2)}, u32[]{:S(2)}) collective-permute-start(bf16[32,16,128]{2,1,0:T(8,128)(2,1)S(1)} %get-tuple-element.66), channel_id=1, source_target_pairs={{0,8},{8,0},{16,24},{24,16},{1,9},{9,1},{17,25},{25,17},{2,10},{10... | collective-permute-start | bytes 393224 | tf_op jit(solution)/shard_map/ppermute | solution.py:250
  54.8 8.7 %collective-permute-start.12 = (bf16[32,16,128]{2,1,0:T(8,128)(2,1)S(1)}, bf16[32,16,128]{2,1,0:T(8,128)(2,1)S(1)}, u32[]{:S(2)}, u32[]{:S(2)}) collective-permute-start(bf16[32,16,128]{2,1,0:T(8,128)(2,1)S(1)} %get-tuple-element.67), channel_id=1, source_target_pairs={{0,16},{8,24},{16,0},{24,8},{1,17},{9,25},{17,1},{25,9},{2,18},{10... | collective-permute-start | bytes 393224 | tf_op jit(solution)/shard_map/ppermute | solution.py:250
  55.5 8.0 %collective-permute-start.13 = (bf16[32,16,128]{2,1,0:T(8,128)(2,1)S(1)}, bf16[32,16,128]{2,1,0:T(8,128)(2,1)S(1)}, u32[]{:S(2)}, u32[]{:S(2)}) collective-permute-start(bf16[32,16,128]{2,1,0:T(8,128)(2,1)S(1)} %get-tuple-element.68), channel_id=1, source_target_pairs={{0,24},{8,16},{16,8},{24,0},{1,25},{9,17},{17,9},{25,1},{2,26},{10... | collective-permute-start | bytes 393224 | tf_op jit(solution)/shard_map/ppermute | solution.py:250
  59.4 6.4 %collective-permute-start.19 = (bf16[32,16,128]{2,1,0:T(8,128)(2,1)S(1)}, bf16[32,16,128]{2,1,0:T(8,128)(2,1)S(1)}, u32[]{:S(2)}, u32[]{:S(2)}) collective-permute-start(bf16[32,16,128]{2,1,0:T(8,128)(2,1)S(1)} %get-tuple-element.74), channel_id=1, source_target_pairs={{0,8},{8,0},{16,24},{24,16},{1,9},{9,1},{17,25},{25,17},{2,10},{10... | collective-permute-start | bytes 393224 | tf_op jit(solution)/shard_map/ppermute | solution.py:250
  60.4 8.7 %collective-permute-start.20 = (bf16[32,16,128]{2,1,0:T(8,128)(2,1)S(1)}, bf16[32,16,128]{2,1,0:T(8,128)(2,1)S(1)}, u32[]{:S(2)}, u32[]{:S(2)}) collective-permute-start(bf16[32,16,128]{2,1,0:T(8,128)(2,1)S(1)} %get-tuple-element.75), channel_id=1, source_target_pairs={{0,16},{8,24},{16,0},{24,8},{1,17},{9,25},{17,1},{25,9},{2,18},{10... | collective-permute-start | bytes 393224 | tf_op jit(solution)/shard_map/ppermute | solution.py:250
  61.2 8.0 %collective-permute-start.21 = (bf16[32,16,128]{2,1,0:T(8,128)(2,1)S(1)}, bf16[32,16,128]{2,1,0:T(8,128)(2,1)S(1)}, u32[]{:S(2)}, u32[]{:S(2)}) collective-permute-start(bf16[32,16,128]{2,1,0:T(8,128)(2,1)S(1)} %get-tuple-element.76), channel_id=1, source_target_pairs={{0,24},{8,16},{16,8},{24,0},{1,25},{9,17},{17,9},{25,1},{2,26},{10... | collective-permute-start | bytes 393224 | tf_op jit(solution)/shard_map/ppermute | solution.py:250
  70.8 6.5 %collective-permute-start.25 = (bf16[16,32,128]{2,1,0:T(8,128)(2,1)S(1)}, bf16[16,32,128]{2,1,0:T(8,128)(2,1)S(1)}, u32[]{:S(2)}, u32[]{:S(2)}) collective-permute-start(bf16[16,32,128]{2,1,0:T(8,128)(2,1)S(1)} %get-tuple-element.82), channel_id=1, source_target_pairs={{0,8},{8,0},{16,24},{24,16},{1,9},{9,1},{17,25},{25,17},{2,10},{10... | collective-permute-start | bytes 393224 | tf_op jit(solution)/shard_map/ppermute | solution.py:250
  71.9 12.4 %collective-permute-start.22 = (bf16[16,32,128]{2,1,0:T(8,128)(2,1)S(1)}, bf16[16,32,128]{2,1,0:T(8,128)(2,1)S(1)}, u32[]{:S(2)}, u32[]{:S(2)}) collective-permute-start(bf16[16,32,128]{2,1,0:T(8,128)(2,1)S(1)} %get-tuple-element.78), channel_id=1, source_target_pairs={{0,8},{8,0},{16,24},{24,16},{1,9},{9,1},{17,25},{25,17},{2,10},{10... | collective-permute-start | bytes 393224 | tf_op jit(solution)/shard_map/ppermute | solution.py:250
  72.9 7.2 %collective-permute-start.26 = (bf16[16,32,128]{2,1,0:T(8,128)(2,1)S(1)}, bf16[16,32,128]{2,1,0:T(8,128)(2,1)S(1)}, u32[]{:S(2)}, u32[]{:S(2)}) collective-permute-start(bf16[16,32,128]{2,1,0:T(8,128)(2,1)S(1)} %get-tuple-element.83), channel_id=1, source_target_pairs={{0,16},{8,24},{16,0},{24,8},{1,17},{9,25},{17,1},{25,9},{2,18},{10... | collective-permute-start | bytes 393224 | tf_op jit(solution)/shard_map/ppermute | solution.py:250
  73.6 9.5 %collective-permute-start.27 = (bf16[16,32,128]{2,1,0:T(8,128)(2,1)S(1)}, bf16[16,32,128]{2,1,0:T(8,128)(2,1)S(1)}, u32[]{:S(2)}, u32[]{:S(2)}) collective-permute-start(bf16[16,32,128]{2,1,0:T(8,128)(2,1)S(1)} %get-tuple-element.84), channel_id=1, source_target_pairs={{0,24},{8,16},{16,8},{24,0},{1,25},{9,17},{17,9},{25,1},{2,26},{10... | collective-permute-start | bytes 393224 | tf_op jit(solution)/shard_map/ppermute | solution.py:250
  75.4 10.9 %collective-permute-start.23 = (bf16[16,32,128]{2,1,0:T(8,128)(2,1)S(1)}, bf16[16,32,128]{2,1,0:T(8,128)(2,1)S(1)}, u32[]{:S(2)}, u32[]{:S(2)}) collective-permute-start(bf16[16,32,128]{2,1,0:T(8,128)(2,1)S(1)} %get-tuple-element.79), channel_id=1, source_target_pairs={{0,16},{8,24},{16,0},{24,8},{1,17},{9,25},{17,1},{25,9},{2,18},{10... | collective-permute-start | bytes 393224 | tf_op jit(solution)/shard_map/ppermute | solution.py:250
  77.3 9.0 %collective-permute-start.24 = (bf16[16,32,128]{2,1,0:T(8,128)(2,1)S(1)}, bf16[16,32,128]{2,1,0:T(8,128)(2,1)S(1)}, u32[]{:S(2)}, u32[]{:S(2)}) collective-permute-start(bf16[16,32,128]{2,1,0:T(8,128)(2,1)S(1)} %get-tuple-element.80), channel_id=1, source_target_pairs={{0,24},{8,16},{16,8},{24,0},{1,25},{9,17},{17,9},{25,1},{2,26},{10... | collective-permute-start | bytes 393224 | tf_op jit(solution)/shard_map/ppermute | solution.py:250

commit v2 on v1

--- a/solution.py
+++ b/solution.py
@@ -60,9 +60,21 @@
     return jnp.dot(a, b, preferred_element_type=F32)
 
 
-def prepare_kernel(groups, transposed, me_ref, hbm, *rest):
-    outs = rest[:groups]
-    x_ref, scratch, sems = rest[groups:]
+def slice_kernel(groups, me_ref, hbm, *rest):
+    outs, sems = rest[:groups], rest[groups]
+    rows = outs[0].shape[1]
+    copies = []
+    for d in range(groups):
+        place = pl.ds(pl.multiple_of((me_ref[0] ^ d) * rows, rows), rows)
+        copies.append(pltpu.make_async_copy(hbm.at[:, place], outs[d], sems.at[d]))
+        copies[d].start()
+    for copy in copies:
+        copy.wait()
+
+
+def turn_kernel(groups, counts, me_ref, hbm, *rest):
+    outs = rest[: groups * len(counts)]
+    x_ref, scratch, sems = rest[groups * len(counts) :]
     e_dev, orbitals, _ = x_ref.shape
     rows = orbitals // groups
     me = me_ref[0]
@@ -75,12 +87,14 @@
     for p, copy in enumerate(copies):
         copy.wait()
         for e in range(p * span, (p + 1) * span):
-            x = x_ref[e].astype(F32)
-            scratch[pl.ds(e, orbitals, stride=e_dev), :] = x.T if transposed else x
-    size = rows * e_dev
-    for d in range(groups):
-        part = scratch[pl.ds(pl.multiple_of((me ^ d) * size, size), size), :]
-        outs[d][...] = part.astype(BF16).reshape(rows, e_dev, orbitals)
+            scratch[pl.ds(e, orbitals, stride=e_dev), :] = x_ref[e].astype(F32).T
+    first = 0
+    for c, count in enumerate(counts):
+        for d in range(groups):
+            start = pl.multiple_of(((me ^ d) * rows + first) * e_dev, 8)
+            part = scratch[pl.ds(start, count * e_dev), :]
+            outs[c * groups + d][...] = part.astype(BF16).reshape(count, e_dev, orbitals)
+        first += count
 
 
 def gathered(refs, i):
@@ -97,41 +111,59 @@
 
 
 def spectrum_kernel(fwd_ref, *refs):
-    less, out = refs[:-1], refs[-1]
+    less, out, scratch = refs[:-2], refs[-2], refs[-1]
+    e_dev, rows, orbitals = less[0].shape
+    size = e_dev * rows
+    for d, part in enumerate(less):
+        scratch[d * size : (d + 1) * size, :] = part[...].astype(F32).reshape(size, orbitals)
     fwd = fwd_ref[...]
+    total = e_dev * len(less)
     for n in range(out.shape[0]):
-        out[n] = dot(fwd, gathered(less, n * WIDE))
-
-
-def pol_kernel(groups, halves, fwd_ref, back_ref, less_ref, *refs):
-    great, outs, scratch = refs[:groups], refs[groups:-1], refs[-1]
-    rows, e_dev, orbitals = great[0].shape
+        both = jnp.concatenate(
+            [scratch[pl.ds(n * WIDE + h, total, stride=rows), :] for h in range(WIDE)], axis=1
+        ).astype(BF16)
+        out[n] = dot(fwd, jnp.concatenate([both, both], axis=0))
+
+
+def pol_kernel(groups, halves, first, earlier, fwd_ref, back_ref, less_ref, *refs):
+    great, before = refs[:groups], refs[groups : groups + earlier]
+    outs, scratch = refs[groups + earlier : -1], refs[-1]
+    count, e_dev, orbitals = great[0].shape
     freq = fwd_ref.shape[0] // 2
     fwd, back = fwd_ref[...], back_ref[...]
     total = groups * e_dev
-    for n in range(less_ref.shape[0]):
-        a = less_ref[n]
-        b = dot(fwd, gathered(great, n * WIDE))
+    for i in range(0, count, WIDE):
+        a = less_ref[(first + i) // WIDE]
+        b = dot(fwd, gathered(great, i))
         real = a[:freq] * b[:freq] + a[freq:] * b[freq:]
         imag = a[freq:] * b[:freq] - a[:freq] * b[freq:]
         pol = inverse(back, jnp.concatenate([real, imag], axis=0))
         for h in range(WIDE):
-            scratch[pl.ds(n * WIDE + h, total, stride=rows), :] = pol[
+            scratch[pl.ds(i + h, total, stride=count), :] = pol[
                 :, h * orbitals : (h + 1) * orbitals
             ]
+    if len(outs) == 1:
+        outs[0][...] = scratch[...].astype(BF16).reshape(total, count, orbitals)
+        return
     lags = e_dev // halves
-    size = lags * rows
     for h in range(halves):
         for d in range(groups):
-            start = (d * halves + h) * size
-            outs[h * groups + d][...] = (
-                scratch[start : start + size, :].astype(BF16).reshape(lags, rows, orbitals)
+            out = outs[h * groups + d]
+            start = d * e_dev + h * lags
+            at = 0
+            for ref in before:
+                out[:, at : at + ref.shape[1], :] = ref[start : start + lags]
+                at += ref.shape[1]
+            out[:, first:, :] = (
+                scratch[start * count : (start + lags) * count, :]
+                .astype(BF16)
+                .reshape(lags, count, orbitals)
             )
 
 
 def sigma_kernel(groups, halves, fwd_l_ref, back_ref, less_ref, *refs):
     inter, outs = refs[: groups * halves], refs[groups * halves :]
-    count, e_dev, orbitals = outs[0].shape
+    e_dev, orbitals = outs[0].shape[1:]
     inter = [inter[h * groups + d] for d in range(groups) for h in range(halves)]
     freq = fwd_l_ref.shape[0] // 2
     fwd_l, back = fwd_l_ref[...], back_ref[...]
@@ -142,20 +174,17 @@
         imag = a[freq:] * b[:freq] + a[:freq] * b[freq:]
         sigma = inverse(back, jnp.concatenate([real, imag], axis=0)).astype(BF16)
         for h in range(WIDE):
-            c, i = divmod(n * WIDE + h, count)
             for d in range(groups):
-                outs[c * groups + d][i] = sigma[
+                outs[d][n * WIDE + h] = sigma[
                     d * e_dev : (d + 1) * e_dev, h * orbitals : (h + 1) * orbitals
                 ]
 
 
-def assemble_kernel(groups, me_ref, *refs):
-    ins, out = refs[:groups], refs[groups]
+def assemble_kernel(*refs):
+    ins, out = refs[:-1], refs[-1]
     rows = ins[0].shape[1]
-    me = me_ref[0]
-    for d in range(groups):
-        start = pl.multiple_of((me ^ d) * rows, rows)
-        out[:, pl.ds(start, rows), :] = ins[d][...]
+    for d, part in enumerate(ins):
+        out[:, d * rows : (d + 1) * rows, :] = part[...]
 
 
 def diagonal(a, b):
@@ -165,26 +194,35 @@
     )
 
 
-def setup_kernel(count, me_ref, odd_ref, mask_ref, v_ref, *refs):
+def setup_kernel(groups, count, me_ref, odd_ref, mask_ref, v_ref, *refs):
     sources, outs = refs[:count], refs[count : 2 * count]
-    near_left, near_right, far_left, far_right = refs[2 * count : -1]
-    sems = refs[-1]
+    near_left, near_right, far_left, far_right, scratch, sems = refs[2 * count :]
+    me = me_ref[0]
     copies = [
-        pltpu.make_async_copy(src.at[me_ref[0]], dst, sems.at[n])
+        pltpu.make_async_copy(src.at[me], dst, sems.at[n])
         for n, (src, dst) in enumerate(zip(sources, outs))
     ]
     for copy in copies:
         copy.start()
     odd = odd_ref[0]
-    own, near, far = v_ref[1], v_ref[2 - 2 * odd], v_ref[2 * odd]
-
-    def masked(v, t):
-        return (v.astype(F32).T * mask_ref[t].astype(F32)).astype(BF16)
-
-    near_left[...] = jnp.concatenate([own, near], axis=1)
-    near_right[...] = diagonal(own.astype(F32).T.astype(BF16), masked(near, 1 - odd))
-    far_left[...] = far
-    far_right[...] = masked(far, odd)
+    scratch[0] = v_ref[1].astype(F32).T
+    scratch[1] = v_ref[2 - 2 * odd].astype(F32).T
+    scratch[2] = v_ref[2 * odd].astype(F32).T
+    rows = scratch.shape[1] // groups
+
+    def ordered(n):
+        parts = [
+            scratch[n, pl.ds(pl.multiple_of((me ^ d) * rows, rows), rows), :] for d in range(groups)
+        ]
+        return jnp.concatenate(parts, axis=0).T.astype(BF16)
+
+    def masked(n, t):
+        return (scratch[n] * mask_ref[t].astype(F32)).astype(BF16)
+
+    near_left[...] = jnp.concatenate([ordered(0), ordered(1)], axis=1)
+    near_right[...] = diagonal(scratch[0].astype(BF16), masked(1, 1 - odd))
+    far_left[...] = ordered(2)
+    far_right[...] = masked(2, odd)
     for copy in copies:
         copy.wait()
 
@@ -207,7 +245,7 @@
 
 def far_kernel(groups, me_ref, left, right, partial, far, *refs):
     outs, scratch = refs[:groups], refs[groups]
-    lags, n, _ = far.shape
+    lags, n, _ = partial.shape
     rows = n // groups
     me = me_ref[0]
     half = dot(far[...].reshape(lags * n, n), right[...]).astype(BF16)
@@ -221,21 +259,20 @@
         outs[d][...] = scratch[place, :].astype(BF16).reshape(rows, lags, n)
 
 
-def final_kernel(groups, first, me_ref, *refs):
-    ins, out, scratch, sems = refs[:groups], refs[-3], refs[-2], refs[-1]
-    count, e_dev, orbitals = ins[0].shape
-    rows = orbitals // groups
+def final_kernel(groups, which, me_ref, *refs):
+    ins, out, scratch, sems = refs[: len(which)], refs[-3], refs[-2], refs[-1]
+    rows, e_dev, orbitals = ins[0].shape
     me = me_ref[0]
     copies = []
-    for d in range(groups):
-        for i in range(count):
-            scratch[d, pl.ds(i, e_dev, stride=count), :] = ins[d][i].astype(F32)
-        start = pl.multiple_of((me ^ d) * rows + first, 8)
+    for n, d in enumerate(which):
+        for i in range(rows):
+            scratch[n, pl.ds(i, e_dev, stride=rows), :] = ins[n][i].astype(F32)
+        start = pl.multiple_of((me ^ d) * rows, rows)
         copies.append(
             pltpu.make_async_copy(
-                scratch.at[d].reshape(e_dev, count, orbitals),
-                out.at[:, pl.ds(start, count), :],
-                sems.at[d],
+                scratch.at[n].reshape(e_dev, rows, orbitals),
+                out.at[:, pl.ds(start, rows), :],
+                sems.at[n],
             )
         )
         copies[-1].start()
@@ -283,28 +320,21 @@
     great = g_great.reshape(e_dev, orbitals, orbitals)
     less, great = [pltpu.with_memory_space_constraint(x, pltpu.HBM) for x in (less, great)]
 
-    def prepared(x, transposed):
-        parts = call(
-            functools.partial(prepare_kernel, groups, transposed),
-            [shape(rows, e_dev, orbitals)] * groups,
-            [smem, hbm],
-            me,
-            x,
-            out_specs=[vmem()] * groups,
-            scratch=[
-                pltpu.VMEM((e_dev, orbitals, orbitals), BF16),
-                pltpu.VMEM((orbitals * e_dev, orbitals), F32),
-                pltpu.SemaphoreType.DMA((4,)),
-            ],
-        )
-        return exchange(parts)
-
-    less = prepared(less, False)
-    great = prepared(great, True)
+    parts = [shape(e_dev, rows, orbitals)] * groups
+    less = call(
+        functools.partial(slice_kernel, groups),
+        parts,
+        [smem, hbm],
+        me,
+        less,
+        out_specs=[vmem()] * groups,
+        scratch=[pltpu.SemaphoreType.DMA((groups,))],
+    )
+    less = exchange(less)
     stacks = [pltpu.with_memory_space_constraint(jnp.asarray(t), pltpu.HBM) for t in tables(groups, e_dev)]
     square = (orbitals, orbitals)
     fwd_e, fwd_l, back_l, back_e, near_left, near_right, far_left, far_right = call(
-        functools.partial(setup_kernel, len(stacks)),
+        functools.partial(setup_kernel, groups, len(stacks)),
         [shape(*t.shape[1:]) for t in stacks]
         + [shape(orbitals, 2 * orbitals), shape(2 * orbitals, 2 * orbitals)]
         + [shape(*square), shape(*square)],
@@ -315,8 +345,27 @@
         coupling[0],
         *stacks,
         out_specs=[vmem()] * (len(stacks) + 4),
-        scratch=[pltpu.SemaphoreType.DMA((len(stacks),))],
-    )
+        scratch=[pltpu.VMEM((3, *square), F32), pltpu.SemaphoreType.DMA((len(stacks),))],
+    )
+    counts = [3 * rows // 4, rows // 4] if rows % 32 == 0 else [rows]
+    parts = call(
+        functools.partial(turn_kernel, groups, counts),
+        [shape(count, e_dev, orbitals) for count in counts for _ in range(groups)],
+        [smem, hbm],
+        me,
+        great,
+        out_specs=[vmem()] * (groups * len(counts)),
+        scratch=[
+            pltpu.VMEM((e_dev, orbitals, orbitals), BF16),
+            pltpu.VMEM((orbitals * e_dev, orbitals), F32),
+            pltpu.SemaphoreType.DMA((4,)),
+        ],
+    )
+    great = [exchange(parts[:groups])]
+    if len(counts) > 1:
+        held = lax.optimization_barrier((*parts[groups:], *less, fwd_e))
+        great.append(exchange(held[:groups]))
+        less, fwd_e = held[groups:-1], held[-1]
     less = call(
         spectrum_kernel,
         shape(rows // WIDE, fwd_e.shape[0], WIDE * orbitals, dtype=F32),
@@ -324,18 +373,29 @@
         fwd_e,
         *less,
         out_specs=vmem(),
-    )
-    pol = call(
-        functools.partial(pol_kernel, groups, halves),
-        [shape(lags, rows, orbitals)] * (halves * groups),
-        [vmem()] * (3 + groups),
-        fwd_e,
-        back_l,
-        less,
-        *great,
-        out_specs=[vmem()] * (halves * groups),
         scratch=[pltpu.VMEM((total * rows, orbitals), F32)],
     )
+    pol = []
+    for c, count in enumerate(counts):
+        last = c == len(counts) - 1
+        outs = (
+            [shape(lags, rows, orbitals)] * (halves * groups)
+            if last
+            else [shape(total, count, orbitals)]
+        )
+        pol += call(
+            functools.partial(pol_kernel, groups, halves, sum(counts[:c]), c),
+            outs,
+            [vmem()] * (3 + groups + c),
+            fwd_e,
+            back_l,
+            less,
+            *great[c],
+            *pol,
+            out_specs=[vmem()] * len(outs),
+            scratch=[pltpu.VMEM((total * count, orbitals), F32)],
+        )
+    pol = pol[len(counts) - 1 :]
     pol = [exchange(pol[h * groups : (h + 1) * groups]) for h in range(halves)]
 
     near_pairs = [(b, b ^ 1) for b in range(peers) if b ^ 1 < peers]
@@ -343,10 +403,9 @@
     inter = []
     for h in range(halves):
         own = call(
-            functools.partial(assemble_kernel, groups),
+            assemble_kernel,
             shape(lags, orbitals, orbitals),
-            [smem] + [vmem()] * groups,
-            me,
+            [vmem()] * groups,
             *pol[h],
             out_specs=vmem(),
         )
@@ -376,37 +435,33 @@
         )
         inter += exchange(parts)
 
-    steps = 2 if rows % 32 == 0 else 1
-    count = rows // steps
     sigma = call(
         functools.partial(sigma_kernel, groups, halves),
-        [shape(count, e_dev, orbitals)] * (groups * steps),
+        [shape(rows, e_dev, orbitals)] * groups,
         [vmem()] * (3 + groups * halves),
         fwd_l,
         back_e,
         less,
         *inter,
-        out_specs=[vmem()] * (groups * steps),
-    )
-    sigma = [
-        (c * count, count, exchange(sigma[c * groups : (c + 1) * groups])) for c in range(steps)
-    ]
+        out_specs=[vmem()] * groups,
+    )
+    sigma = exchange(sigma)
     out = []
-    for first, count, parts in sigma:
+    for which in (list(range(groups // 2)), list(range(groups // 2, groups))):
         out = [
             call(
-                functools.partial(final_kernel, groups, first),
+                functools.partial(final_kernel, groups, which),
                 shape(e_dev, orbitals, orbitals, dtype=F32),
-                [smem] + [vmem()] * groups + [hbm] * len(out),
+                [smem] + [vmem()] * len(which) + [hbm] * len(out),
                 me,
-                *parts,
+                *[sigma[d] for d in which],
                 *out,
                 out_specs=hbm,
                 scratch=[
-                    pltpu.VMEM((groups, e_dev * count, orbitals), F32),
-                    pltpu.SemaphoreType.DMA((groups,)),
+                    pltpu.VMEM((len(which), e_dev * rows, orbitals), F32),
+                    pltpu.SemaphoreType.DMA((len(which),)),
                 ],
-                input_output_aliases={1 + groups: 0} if out else {},
+                input_output_aliases={1 + len(which): 0} if out else {},
             )
         ]
     return out[0].reshape(e_dev, 1, orbitals, orbitals)

time: 87.8 us -> 83.7 us (0.953)
  waiting for transfers between devices: 33.7 us -> 28.3 us
  starting transfers between devices: 35.8 us -> 37.3 us
    ppermute x24, waiting for transfers between devices: 29.7 us -> 24.1 us  [exchange(): lax.ppermute(parts[d], 'energy', [(i, i ^ d) for i in range(groups)])]
    ppermute x24, starting transfers between devices: 30.6 us -> 31.7 us  [exchange(): lax.ppermute(parts[d], 'energy', [(i, i ^ d) for i in range(groups)])]
    pallas_call x14 -> x15, Pallas kernels: 17.8 us -> 17.6 us  [call(): pl.pallas_call(kernel, out_shape=out_shape, in_specs=specs, scratch_shape...]
  transfers between devices with their start and end apart: 28 -> 28, of which waited for: 17 -> 16; matrix products, arithmetic and copies ran while one was open for 0% -> 0% of each run, Pallas kernels for 10% -> 15%
where the time goes in v2:
time: 83.7 us; the launch traced here: 83.5 us
  starting transfers between devices  37.3 us (45%)
  waiting for transfers between devices  28.3 us (34%)
  Pallas kernels  17.6 us (21%)
    ppermute x24, starting transfers between devices, exchange(): lax.ppermute(parts[d], 'energy', [(i, i ^ d) for i in range(groups)])  31.7 us
    ppermute x24, waiting for transfers between devices, exchange(): lax.ppermute(parts[d], 'energy', [(i, i ^ d) for i in range(groups)])  24.1 us
    pallas_call x15, Pallas kernels, call(): pl.pallas_call(kernel, out_shape=out_shape, in_specs=specs, scratch_shape...  17.6 us
    ppermute x2, starting transfers between devices, shards(): far = lax.ppermute(own, 'block', far_pairs)  4.6 us
    ppermute x2, waiting for transfers between devices, shards(): far = lax.ppermute(own, 'block', far_pairs)  4.22 us
  transfers between devices with their start and end apart: 28, of which 16 were waited for; matrix products, arithmetic and copies ran while one was open for 0% of the time, Pallas kernels for 15%

profile of v2, /device:TPU:16, one launch (start us, length us, event | category | flops | bytes accessed | tf_op | source)
XLA Modules:
  0.0 83.5 jit_solution(14278657371648027770)
XLA Ops:
  0.0 1.3 %shard_map.84 = (bf16[32,32,128]{2,1,0:T(8,128)(2,1)S(1)}, bf16[32,32,128]{2,1,0:T(8,128)(2,1)S(1)}, bf16[32,32,128]{2,1,0:T(8,128)(2,1)S(1)}, bf16[32,32,128]{2,1,0:T(8,128)(2,1)S(1)}) custom-call(s32[1]{0:T(128)} %bitcast.me_ref, bf16[32,128,128]{2,1,0:T(8,128)(2,1)} %bitcast.11), custom_call_target="tpu_custom_call" | custom-call | tf_op jit(solution)/shard_map/pallas_call | solution.py:292
  1.3 1.6 %collective-permute-start = (bf16[32,32,128]{2,1,0:T(8,128)(2,1)S(1)}, bf16[32,32,128]{2,1,0:T(8,128)(2,1)S(1)}, u32[]{:S(2)}, u32[]{:S(2)}) collective-permute-start(bf16[32,32,128]{2,1,0:T(8,128)(2,1)S(1)} %get-tuple-element.61), channel_id=1, source_target_pairs={{0,8},{8,0},{16,24},{24,16},{1,9},{9,1},{17,25},{25,17},{2,10},{10... | collective-permute-start | bytes 786440 | tf_op jit(solution)/shard_map/ppermute | solution.py:287
  2.8 1.5 %collective-permute-start.1 = (bf16[32,32,128]{2,1,0:T(8,128)(2,1)S(1)}, bf16[32,32,128]{2,1,0:T(8,128)(2,1)S(1)}, u32[]{:S(2)}, u32[]{:S(2)}) collective-permute-start(bf16[32,32,128]{2,1,0:T(8,128)(2,1)S(1)} %get-tuple-element.62), channel_id=1, source_target_pairs={{0,16},{8,24},{16,0},{24,8},{1,17},{9,25},{17,1},{25,9},{2,18},{10... | collective-permute-start | bytes 786440 | tf_op jit(solution)/shard_map/ppermute | solution.py:287
  4.8 2.5 %shard_map.83 = (bf16[24,32,128]{2,1,0:T(8,128)(2,1)S(1)}, bf16[24,32,128]{2,1,0:T(8,128)(2,1)S(1)}, bf16[24,32,128]{2,1,0:T(8,128)(2,1)S(1)}, bf16[24,32,128]{2...) custom-call(s32[1]{0:T(128)} %bitcast.me_ref, ...), custom_call_target="tpu_custom_call" | custom-call | tf_op jit(solution)/shard_map/pallas_call | solution.py:292
  7.3 1.6 %collective-permute-start.6 = (bf16[24,32,128]{2,1,0:T(8,128)(2,1)S(1)}, bf16[24,32,128]{2,1,0:T(8,128)(2,1)S(1)}, u32[]{:S(2)}, u32[]{:S(2)}) collective-permute-start(bf16[24,32,128]{2,1,0:T(8,128)(2,1)S(1)} %get-tuple-element.80), channel_id=1, source_target_pairs={{0,8},{8,0},{16,24},{24,16},{1,9},{9,1},{17,25},{25,17},{2,10},{10... | collective-permute-start | bytes 589832 | tf_op jit(solution)/shard_map/ppermute | solution.py:287
  8.8 1.5 %collective-permute-start.7 = (bf16[24,32,128]{2,1,0:T(8,128)(2,1)S(1)}, bf16[24,32,128]{2,1,0:T(8,128)(2,1)S(1)}, u32[]{:S(2)}, u32[]{:S(2)}) collective-permute-start(bf16[24,32,128]{2,1,0:T(8,128)(2,1)S(1)} %get-tuple-element.81), channel_id=1, source_target_pairs={{0,16},{8,24},{16,0},{24,8},{1,17},{9,25},{17,1},{25,9},{2,18},{10... | collective-permute-start | bytes 589832 | tf_op jit(solution)/shard_map/ppermute | solution.py:287
  10.5 2.4 %collective-permute-start.8 = (bf16[24,32,128]{2,1,0:T(8,128)(2,1)S(1)}, bf16[24,32,128]{2,1,0:T(8,128)(2,1)S(1)}, u32[]{:S(2)}, u32[]{:S(2)}) collective-permute-start(bf16[24,32,128]{2,1,0:T(8,128)(2,1)S(1)} %get-tuple-element.82), channel_id=1, source_target_pairs={{0,24},{8,16},{16,8},{24,0},{1,25},{9,17},{17,9},{25,1},{2,26},{10... | collective-permute-start | bytes 589832 | tf_op jit(solution)/shard_map/ppermute | solution.py:287
  13.0 1.7 %shard_map.82 = (bf16[192,256]{1,0:T(8,128)(2,1)S(1)}, bf16[192,256]{1,0:T(8,128)(2,1)S(1)}, bf16[256,192]{1,0:T(8,128)(2,1)S(1)}, bf16[256,192]{1,0:T(8,128)(2,...) custom-call(s32[1]{0:T(128)} %bitcast.me_ref, ...), custom_call_target="tpu_custom_call" | custom-call | tf_op jit(solution)/shard_map/pallas_call | solution.py:292
  14.7 2.3 %collective-permute-done.1.refs_2_ = bf16[32,32,128]{2,1,0:T(8,128)(2,1)S(1)} collective-permute-done((bf16[32,32,128]{2,1,0:T(8,128)(2,1)S(1)}, bf16[32,32,128]{2,1,0:T(8,128)(2,1)S(1)}, u32[]{:S(2)}, u32[]{:S(2)}) %collective-permute-start.1) | collective-permute-done | bytes 262176 | tf_op jit(solution)/shard_map/ppermute | solution.py:287
  17.2 1.5 %collective-permute-start.3 = (bf16[8,32,128]{2,1,0:T(8,128)(2,1)S(1)}, bf16[8,32,128]{2,1,0:T(8,128)(2,1)S(1)}, u32[]{:S(2)}, u32[]{:S(2)}) collective-permute-start(bf16[8,32,128]{2,1,0:T(8,128)(2,1)S(1)} %get-tuple-element.76), channel_id=1, source_target_pairs={{0,8},{8,0},{16,24},{24,16},{1,9},{9,1},{17,25},{25,17},{2,10},{10... | collective-permute-start | bytes 196616 | tf_op jit(solution)/shard_map/ppermute | solution.py:287
  18.6 0.5 collective-permute-start.4
  19.2 1.3 %collective-permute-done.6.refs_1_ = bf16[24,32,128]{2,1,0:T(8,128)(2,1)S(1)} collective-permute-done((bf16[24,32,128]{2,1,0:T(8,128)(2,1)S(1)}, bf16[24,32,128]{2,1,0:T(8,128)(2,1)S(1)}, u32[]{:S(2)}, u32[]{:S(2)}) %collective-permute-start.6) | collective-permute-done | bytes 196640 | tf_op jit(solution)/shard_map/ppermute | solution.py:287
  20.4 2.4 %collective-permute-start.5 = (bf16[8,32,128]{2,1,0:T(8,128)(2,1)S(1)}, bf16[8,32,128]{2,1,0:T(8,128)(2,1)S(1)}, u32[]{:S(2)}, u32[]{:S(2)}) collective-permute-start(bf16[8,32,128]{2,1,0:T(8,128)(2,1)S(1)} %get-tuple-element.78), channel_id=1, source_target_pairs={{0,24},{8,16},{16,8},{24,0},{1,25},{9,17},{17,9},{25,1},{2,26},{10... | collective-permute-start | bytes 196616 | tf_op jit(solution)/shard_map/ppermute | solution.py:287
  22.9 1.7 %shard_map.85.less_ref = f32[4,192,1024]{2,1,0:T(8,128)S(1)} custom-call(bf16[192,256]{1,0:T(8,128)(2,1)S(1)} %get-tuple-element.65.fwd_ref, bf16[32,32,128]{2,1,0:T(8,128)(2,1)S(1)} %get-tuple-element.66.refs_0_, bf16[32,32,128]{2,1,0:T(8,128)(2,1)S(1)} %collective-permute-done.refs_1_, bf16[32,32,128]{2,1,0:T(8,128)(2,1)S(1)} %collective-permute-done.1.refs_2_, ...), custom_call_target="tpu_custom_call" | custom-call | tf_op jit(solution)/shard_map/pallas_call | solution.py:292
  24.6 1.4 %collective-permute-done.7.refs_2_ = bf16[24,32,128]{2,1,0:T(8,128)(2,1)S(1)} collective-permute-done((bf16[24,32,128]{2,1,0:T(8,128)(2,1)S(1)}, bf16[24,32,128]{2,1,0:T(8,128)(2,1)S(1)}, u32[]{:S(2)}, u32[]{:S(2)}) %collective-permute-start.7) | collective-permute-done | bytes 196640 | tf_op jit(solution)/shard_map/ppermute | solution.py:287
  26.0 1.4 %shard_map.86.refs_4_ = bf16[128,24,128]{2,1,0:T(8,128)(2,1)S(1)} custom-call(bf16[192,256]{1,0:T(8,128)(2,1)S(1)} %get-tuple-element.65.fwd_ref, bf16[256,192]{1,0:T(8,128)(2,1)S(1)} %get-tuple-element.74.back_ref, f32[4,192,1024]{2,1,0:T(8,128)S(1)} %shard_map.85.less_ref, bf16[24,32,128]{2,1,0:T(8,128)(2,1)S(1)} %get-tuple-element.79.refs_0_, ...), custom_call_target="tpu_custom_call" | custom-call | tf_op jit(solution)/shard_map/pallas_call | solution.py:292
  27.5 0.6 shard_map.87
  28.0 1.4 %collective-permute-start.9 = (bf16[16,32,128]{2,1,0:T(8,128)(2,1)S(1)}, bf16[16,32,128]{2,1,0:T(8,128)(2,1)S(1)}, u32[]{:S(2)}, u32[]{:S(2)}) collective-permute-start(bf16[16,32,128]{2,1,0:T(8,128)(2,1)S(1)} %get-tuple-element.84), channel_id=1, source_target_pairs={{0,8},{8,0},{16,24},{24,16},{1,9},{9,1},{17,25},{25,17},{2,10},{10... | collective-permute-start | bytes 393224 | tf_op jit(solution)/shard_map/ppermute | solution.py:287
  29.4 1.0 %collective-permute-start.10 = (bf16[16,32,128]{2,1,0:T(8,128)(2,1)S(1)}, bf16[16,32,128]{2,1,0:T(8,128)(2,1)S(1)}, u32[]{:S(2)}, u32[]{:S(2)}) collective-permute-start(bf16[16,32,128]{2,1,0:T(8,128)(2,1)S(1)} %get-tuple-element.85), channel_id=1, source_target_pairs={{0,16},{8,24},{16,0},{24,8},{1,17},{9,25},{17,1},{25,9},{2,18},{10... | collective-permute-start | bytes 393224 | tf_op jit(solution)/shard_map/ppermute | solution.py:287
  30.4 1.4 %collective-permute-start.11 = (bf16[16,32,128]{2,1,0:T(8,128)(2,1)S(1)}, bf16[16,32,128]{2,1,0:T(8,128)(2,1)S(1)}, u32[]{:S(2)}, u32[]{:S(2)}) collective-permute-start(bf16[16,32,128]{2,1,0:T(8,128)(2,1)S(1)} %get-tuple-element.86), channel_id=1, source_target_pairs={{0,24},{8,16},{16,8},{24,0},{1,25},{9,17},{17,9},{25,1},{2,26},{10... | collective-permute-start | bytes 393224 | tf_op jit(solution)/shard_map/ppermute | solution.py:287
  31.8 1.1 %collective-permute-start.17 = (bf16[16,32,128]{2,1,0:T(8,128)(2,1)S(1)}, bf16[16,32,128]{2,1,0:T(8,128)(2,1)S(1)}, u32[]{:S(2)}, u32[]{:S(2)}) collective-permute-start(bf16[16,32,128]{2,1,0:T(8,128)(2,1)S(1)} %get-tuple-element.92), channel_id=1, source_target_pairs={{0,8},{8,0},{16,24},{24,16},{1,9},{9,1},{17,25},{25,17},{2,10},{10... | collective-permute-start | bytes 393224 | tf_op jit(solution)/shard_map/ppermute | solution.py:287
  32.9 1.0 %collective-permute-start.18 = (bf16[16,32,128]{2,1,0:T(8,128)(2,1)S(1)}, bf16[16,32,128]{2,1,0:T(8,128)(2,1)S(1)}, u32[]{:S(2)}, u32[]{:S(2)}) collective-permute-start(bf16[16,32,128]{2,1,0:T(8,128)(2,1)S(1)} %get-tuple-element.93), channel_id=1, source_target_pairs={{0,16},{8,24},{16,0},{24,8},{1,17},{9,25},{17,1},{25,9},{2,18},{10... | collective-permute-start | bytes 393224 | tf_op jit(solution)/shard_map/ppermute | solution.py:287
  33.9 0.6 collective-permute-done.9.refs_1_
  34.5 1.6 %collective-permute-start.19 = (bf16[16,32,128]{2,1,0:T(8,128)(2,1)S(1)}, bf16[16,32,128]{2,1,0:T(8,128)(2,1)S(1)}, u32[]{:S(2)}, u32[]{:S(2)}) collective-permute-start(bf16[16,32,128]{2,1,0:T(8,128)(2,1)S(1)} %get-tuple-element.94), channel_id=1, source_target_pairs={{0,24},{8,16},{16,8},{24,0},{1,25},{9,17},{17,9},{25,1},{2,26},{10... | collective-permute-start | bytes 393224 | tf_op jit(solution)/shard_map/ppermute | solution.py:287
  36.1 2.6 %collective-permute-done.10.refs_2_ = bf16[16,32,128]{2,1,0:T(8,128)(2,1)S(1)} collective-permute-done((bf16[16,32,128]{2,1,0:T(8,128)(2,1)S(1)}, bf16[16,32,128]{2,1,0:T(8,128)(2,1)S(1)}, u32[]{:S(2)}, u32[]{:S(2)}) %collective-permute-start.10) | collective-permute-done | bytes 131104 | tf_op jit(solution)/shard_map/ppermute | solution.py:287
  38.8 2.4 %collective-permute-start.13 = (bf16[16,128,128]{2,1,0:T(8,128)(2,1)S(1)}, bf16[16,128,128]{2,1,0:T(8,128)(2,1)S(1)}, u32[]{:S(2)}, u32[]{:S(2)}) collective-permute-start(bf16[16,128,128]{2,1,0:T(8,128)(2,1)S(1)} %shard_map.88.own), channel_id=1, source_target_pairs={{1,2},{2,1},{3,4},{4,3},{5,6},{6,5},{9,10},{10,9},{11,12},{12,11},... | collective-permute-start | bytes 1572872 | tf_op jit(solution)/shard_map/ppermute | solution.py:412
  41.7 0.9 %collective-permute-start.20 = (bf16[16,128,128]{2,1,0:T(8,128)(2,1)S(1)}, bf16[16,128,128]{2,1,0:T(8,128)(2,1)S(1)}, u32[]{:S(2)}, u32[]{:S(2)}) collective-permute-start(bf16[16,128,128]{2,1,0:T(8,128)(2,1)S(1)} %shard_map.91.own), channel_id=1, source_target_pairs={{0,1},{1,0},{2,3},{3,2},{4,5},{5,4},{6,7},{7,6},{8,9},{9,8},{10,11... | collective-permute-start | bytes 1572872 | tf_op jit(solution)/shard_map/ppermute | solution.py:413
  42.6 2.2 %collective-permute-start.21 = (bf16[16,128,128]{2,1,0:T(8,128)(2,1)S(1)}, bf16[16,128,128]{2,1,0:T(8,128)(2,1)S(1)}, u32[]{:S(2)}, u32[]{:S(2)}) collective-permute-start(bf16[16,128,128]{2,1,0:T(8,128)(2,1)S(1)} %shard_map.91.own), channel_id=1, source_target_pairs={{1,2},{2,1},{3,4},{4,3},{5,6},{6,5},{9,10},{10,9},{11,12},{12,11},... | collective-permute-start | bytes 1572872 | tf_op jit(solution)/shard_map/ppermute | solution.py:412
  44.8 0.8 shard_map.89.partial
  45.6 3.8 %collective-permute-done.13.far = bf16[16,128,128]{2,1,0:T(8,128)(2,1)S(1)} collective-permute-done((bf16[16,128,128]{2,1,0:T(8,128)(2,1)S(1)}, bf16[16,128,128]{2,1,0:T(8,128)(2,1)S(1)}, u32[]{:S(2)}, u32[]{:S(2)}) %collective-permute-start.13) | collective-permute-done | bytes 524320 | tf_op jit(solution)/shard_map/ppermute | solution.py:412
  49.3 0.8 shard_map.90
  50.1 1.1 %collective-permute-start.14 = (bf16[32,16,128]{2,1,0:T(8,128)(2,1)S(1)}, bf16[32,16,128]{2,1,0:T(8,128)(2,1)S(1)}, u32[]{:S(2)}, u32[]{:S(2)}) collective-permute-start(bf16[32,16,128]{2,1,0:T(8,128)(2,1)S(1)} %get-tuple-element.88), channel_id=1, source_target_pairs={{0,8},{8,0},{16,24},{24,16},{1,9},{9,1},{17,25},{25,17},{2,10},{10... | collective-permute-start | bytes 393224 | tf_op jit(solution)/shard_map/ppermute | solution.py:287
  51.7 2.0 %collective-permute-start.16 = (bf16[32,16,128]{2,1,0:T(8,128)(2,1)S(1)}, bf16[32,16,128]{2,1,0:T(8,128)(2,1)S(1)}, u32[]{:S(2)}, u32[]{:S(2)}) collective-permute-start(bf16[32,16,128]{2,1,0:T(8,128)(2,1)S(1)} %get-tuple-element.90), channel_id=1, source_target_pairs={{0,24},{8,16},{16,8},{24,0},{1,25},{9,17},{17,9},{25,1},{2,26},{10... | collective-permute-start | bytes 393224 | tf_op jit(solution)/shard_map/ppermute | solution.py:287
  53.7 0.8 shard_map.92.partial
  55.0 0.8 shard_map.93
  55.7 1.1 %collective-permute-start.22 = (bf16[32,16,128]{2,1,0:T(8,128)(2,1)S(1)}, bf16[32,16,128]{2,1,0:T(8,128)(2,1)S(1)}, u32[]{:S(2)}, u32[]{:S(2)}) collective-permute-start(bf16[32,16,128]{2,1,0:T(8,128)(2,1)S(1)} %get-tuple-element.96), channel_id=1, source_target_pairs={{0,8},{8,0},{16,24},{24,16},{1,9},{9,1},{17,25},{25,17},{2,10},{10... | collective-permute-start | bytes 393224 | tf_op jit(solution)/shard_map/ppermute | solution.py:287
  57.3 2.0 %collective-permute-start.24 = (bf16[32,16,128]{2,1,0:T(8,128)(2,1)S(1)}, bf16[32,16,128]{2,1,0:T(8,128)(2,1)S(1)}, u32[]{:S(2)}, u32[]{:S(2)}) collective-permute-start(bf16[32,16,128]{2,1,0:T(8,128)(2,1)S(1)} %get-tuple-element.98), channel_id=1, source_target_pairs={{0,24},{8,16},{16,8},{24,0},{1,25},{9,17},{17,9},{25,1},{2,26},{10... | collective-permute-start | bytes 393224 | tf_op jit(solution)/shard_map/ppermute | solution.py:287
  59.3 0.7 collective-permute-done.15.refs_2_
  60.0 2.2 %collective-permute-done.22.refs_5_ = bf16[32,16,128]{2,1,0:T(8,128)(2,1)S(1)} collective-permute-done((bf16[32,16,128]{2,1,0:T(8,128)(2,1)S(1)}, bf16[32,16,128]{2,1,0:T(8,128)(2,1)S(1)}, u32[]{:S(2)}, u32[]{:S(2)}) %collective-permute-start.22) | collective-permute-done | bytes 131104 | tf_op jit(solution)/shard_map/ppermute | solution.py:287
  62.2 3.4 %collective-permute-done.23.refs_6_ = bf16[32,16,128]{2,1,0:T(8,128)(2,1)S(1)} collective-permute-done((bf16[32,16,128]{2,1,0:T(8,128)(2,1)S(1)}, bf16[32,16,128]{2,1,0:T(8,128)(2,1)S(1)}, u32[]{:S(2)}, u32[]{:S(2)}) %collective-permute-start.23) | collective-permute-done | bytes 131104 | tf_op jit(solution)/shard_map/ppermute | solution.py:287
  65.6 1.6 %shard_map.94 = (bf16[32,32,128]{2,1,0:T(8,128)(2,1)S(1)}, bf16[32,32,128]{2,1,0:T(8,128)(2,1)S(1)}, bf16[32,32,128]{2,1,0:T(8,128)(2,1)S(1)}, bf16[32,32,128]{2,1,0:T(8,128)(2,1)S(1)}) custom-call(bf16[192,256]{1,0:T(8,128)(2,1)S(1)} %get-tuple-element.54.fwd_l_ref, bf16[256,192]{1,0:T(8,128)(2,1)S(1)} %get-tuple-element.55.back_ref, ...), custom_call_target="tpu_custom_call" | custom-call | tf_op jit(solution)/shard_map/pallas_call | solution.py:292
  67.2 1.0 %collective-permute-start.27 = (bf16[32,32,128]{2,1,0:T(8,128)(2,1)S(1)}, bf16[32,32,128]{2,1,0:T(8,128)(2,1)S(1)}, u32[]{:S(2)}, u32[]{:S(2)}) collective-permute-start(bf16[32,32,128]{2,1,0:T(8,128)(2,1)S(1)} %get-tuple-element.102), channel_id=1, source_target_pairs={{0,8},{8,0},{16,24},{24,16},{1,9},{9,1},{17,25},{25,17},{2,10},{10... | collective-permute-start | bytes 786440 | tf_op jit(solution)/shard_map/ppermute | solution.py:287
  68.3 0.8 collective-permute-start.25
  69.1 1.8 %collective-permute-start.26 = (bf16[32,32,128]{2,1,0:T(8,128)(2,1)S(1)}, bf16[32,32,128]{2,1,0:T(8,128)(2,1)S(1)}, u32[]{:S(2)}, u32[]{:S(2)}) collective-permute-start(bf16[32,32,128]{2,1,0:T(8,128)(2,1)S(1)} %get-tuple-element.100), channel_id=1, source_target_pairs={{0,24},{8,16},{16,8},{24,0},{1,25},{9,17},{17,9},{25,1},{2,26},{10... | collective-permute-start | bytes 786440 | tf_op jit(solution)/shard_map/ppermute | solution.py:287
  70.8 5.7 %collective-permute-done.27.refs_1_ = bf16[32,32,128]{2,1,0:T(8,128)(2,1)S(1)} collective-permute-done((bf16[32,32,128]{2,1,0:T(8,128)(2,1)S(1)}, bf16[32,32,128]{2,1,0:T(8,128)(2,1)S(1)}, u32[]{:S(2)}, u32[]{:S(2)}) %collective-permute-start.27) | collective-permute-done | bytes 262176 | tf_op jit(solution)/shard_map/ppermute | solution.py:287
  76.5 1.8 %shard_map.95.refs_2_ = f32[32,128,128]{2,1,0:T(8,128)} custom-call(s32[1]{0:T(128)} %bitcast.me_ref, bf16[32,32,128]{2,1,0:T(8,128)(2,1)S(1)} %get-tuple-element.101.refs_0_, bf16[32,32,128]{2,1,0:T(8,128)(2,1)S(1)} %collective-permute-done.27.refs_1_), custom_call_target="tpu_custom_call" | custom-call | tf_op jit(solution)/shard_map/pallas_call | solution.py:292
  78.3 3.2 %collective-permute-done.25.refs_0_ = bf16[32,32,128]{2,1,0:T(8,128)(2,1)S(1)} collective-permute-done((bf16[32,32,128]{2,1,0:T(8,128)(2,1)S(1)}, bf16[32,32,128]{2,1,0:T(8,128)(2,1)S(1)}, u32[]{:S(2)}, u32[]{:S(2)}) %collective-permute-start.25) | collective-permute-done | bytes 262176 | tf_op jit(solution)/shard_map/ppermute | solution.py:287
  81.5 1.8 %shard_map.96 = f32[32,128,128]{2,1,0:T(8,128)} custom-call(s32[1]{0:T(128)} %bitcast.me_ref, bf16[32,32,128]{2,1,0:T(8,128)(2,1)S(1)} %collective-permute-done.25.refs_0_, bf16[32,32,128]{2,1,0:T(8,128)(2,1)S(1)} %collective-permute-done.26.refs_1_, f32[32,128,128]{2,1,0:T(8,128)} %shard_map.95.refs_2_), custom_call_target="tpu_custom_call", output_to_operand_aliasing={{}: (3, {})} | custom-call | tf_op jit(solution)/shard_map/pallas_call | solution.py:292
  (27 shorter events, 2.8 us)
Async XLA Ops:
  0.0 13.0 %copy-start.1 = (s32[1,2]{1,0:T(1,128)S(1)}, s32[1,2]{1,0:T(1,128)}, u32[]{:S(2)}) copy-start(s32[1,2]{1,0:T(1,128)} %param.11) | copy-start | bytes 28
  0.0 13.0 %copy-start = (bf16[1,3,128,128]{3,2,1,0:T(8,128)(2,1)S(1)}, bf16[1,3,128,128]{3,2,1,0:T(8,128)(2,1)}, u32[]{:S(2)}) copy-start(bf16[1,3,128,128]{3,2,1,0:T(8,128)(2,1)} %param.10) | copy-start | bytes 294916
  1.3 9.3 %collective-permute-start = (bf16[32,32,128]{2,1,0:T(8,128)(2,1)S(1)}, bf16[32,32,128]{2,1,0:T(8,128)(2,1)S(1)}, u32[]{:S(2)}, u32[]{:S(2)}) collective-permute-start(bf16[32,32,128]{2,1,0:T(8,128)(2,1)S(1)} %get-tuple-element.61), channel_id=1, source_target_pairs={{0,8},{8,0},{16,24},{24,16},{1,9},{9,1},{17,25},{25,17},{2,10},{10... | collective-permute-start | bytes 786440 | tf_op jit(solution)/shard_map/ppermute | solution.py:287
  2.8 14.2 %collective-permute-start.1 = (bf16[32,32,128]{2,1,0:T(8,128)(2,1)S(1)}, bf16[32,32,128]{2,1,0:T(8,128)(2,1)S(1)}, u32[]{:S(2)}, u32[]{:S(2)}) collective-permute-start(bf16[32,32,128]{2,1,0:T(8,128)(2,1)S(1)} %get-tuple-element.62), channel_id=1, source_target_pairs={{0,16},{8,24},{16,0},{24,8},{1,17},{9,25},{17,1},{25,9},{2,18},{10... | collective-permute-start | bytes 786440 | tf_op jit(solution)/shard_map/ppermute | solution.py:287
  4.3 12.8 %collective-permute-start.2 = (bf16[32,32,128]{2,1,0:T(8,128)(2,1)S(1)}, bf16[32,32,128]{2,1,0:T(8,128)(2,1)S(1)}, u32[]{:S(2)}, u32[]{:S(2)}) collective-permute-start(bf16[32,32,128]{2,1,0:T(8,128)(2,1)S(1)} %get-tuple-element.63), channel_id=1, source_target_pairs={{0,24},{8,16},{16,8},{24,0},{1,25},{9,17},{17,9},{25,1},{2,26},{10... | collective-permute-start | bytes 786440 | tf_op jit(solution)/shard_map/ppermute | solution.py:287
  7.3 13.1 %collective-permute-start.6 = (bf16[24,32,128]{2,1,0:T(8,128)(2,1)S(1)}, bf16[24,32,128]{2,1,0:T(8,128)(2,1)S(1)}, u32[]{:S(2)}, u32[]{:S(2)}) collective-permute-start(bf16[24,32,128]{2,1,0:T(8,128)(2,1)S(1)} %get-tuple-element.80), channel_id=1, source_target_pairs={{0,8},{8,0},{16,24},{24,16},{1,9},{9,1},{17,25},{25,17},{2,10},{10... | collective-permute-start | bytes 589832 | tf_op jit(solution)/shard_map/ppermute | solution.py:287
  8.8 17.1 %collective-permute-start.7 = (bf16[24,32,128]{2,1,0:T(8,128)(2,1)S(1)}, bf16[24,32,128]{2,1,0:T(8,128)(2,1)S(1)}, u32[]{:S(2)}, u32[]{:S(2)}) collective-permute-start(bf16[24,32,128]{2,1,0:T(8,128)(2,1)S(1)} %get-tuple-element.81), channel_id=1, source_target_pairs={{0,16},{8,24},{16,0},{24,8},{1,17},{9,25},{17,1},{25,9},{2,18},{10... | collective-permute-start | bytes 589832 | tf_op jit(solution)/shard_map/ppermute | solution.py:287
  10.5 15.4 %collective-permute-start.8 = (bf16[24,32,128]{2,1,0:T(8,128)(2,1)S(1)}, bf16[24,32,128]{2,1,0:T(8,128)(2,1)S(1)}, u32[]{:S(2)}, u32[]{:S(2)}) collective-permute-start(bf16[24,32,128]{2,1,0:T(8,128)(2,1)S(1)} %get-tuple-element.82), channel_id=1, source_target_pairs={{0,24},{8,16},{16,8},{24,0},{1,25},{9,17},{17,9},{25,1},{2,26},{10... | collective-permute-start | bytes 589832 | tf_op jit(solution)/shard_map/ppermute | solution.py:287
  17.2 10.2 %collective-permute-start.3 = (bf16[8,32,128]{2,1,0:T(8,128)(2,1)S(1)}, bf16[8,32,128]{2,1,0:T(8,128)(2,1)S(1)}, u32[]{:S(2)}, u32[]{:S(2)}) collective-permute-start(bf16[8,32,128]{2,1,0:T(8,128)(2,1)S(1)} %get-tuple-element.76), channel_id=1, source_target_pairs={{0,8},{8,0},{16,24},{24,16},{1,9},{9,1},{17,25},{25,17},{2,10},{10... | collective-permute-start | bytes 196616 | tf_op jit(solution)/shard_map/ppermute | solution.py:287
  18.6 8.8 %collective-permute-start.4 = (bf16[8,32,128]{2,1,0:T(8,128)(2,1)S(1)}, bf16[8,32,128]{2,1,0:T(8,128)(2,1)S(1)}, u32[]{:S(2)}, u32[]{:S(2)}) collective-permute-start(bf16[8,32,128]{2,1,0:T(8,128)(2,1)S(1)} %get-tuple-element.77), channel_id=1, source_target_pairs={{0,16},{8,24},{16,0},{24,8},{1,17},{9,25},{17,1},{25,9},{2,18},{10... | collective-permute-start | bytes 196616 | tf_op jit(solution)/shard_map/ppermute | solution.py:287
  20.4 7.0 %collective-permute-start.5 = (bf16[8,32,128]{2,1,0:T(8,128)(2,1)S(1)}, bf16[8,32,128]{2,1,0:T(8,128)(2,1)S(1)}, u32[]{:S(2)}, u32[]{:S(2)}) collective-permute-start(bf16[8,32,128]{2,1,0:T(8,128)(2,1)S(1)} %get-tuple-element.78), channel_id=1, source_target_pairs={{0,24},{8,16},{16,8},{24,0},{1,25},{9,17},{17,9},{25,1},{2,26},{10... | collective-permute-start | bytes 196616 | tf_op jit(solution)/shard_map/ppermute | solution.py:287
  28.0 6.4 %collective-permute-start.9 = (bf16[16,32,128]{2,1,0:T(8,128)(2,1)S(1)}, bf16[16,32,128]{2,1,0:T(8,128)(2,1)S(1)}, u32[]{:S(2)}, u32[]{:S(2)}) collective-permute-start(bf16[16,32,128]{2,1,0:T(8,128)(2,1)S(1)} %get-tuple-element.84), channel_id=1, source_target_pairs={{0,8},{8,0},{16,24},{24,16},{1,9},{9,1},{17,25},{25,17},{2,10},{10... | collective-permute-start | bytes 393224 | tf_op jit(solution)/shard_map/ppermute | solution.py:287
  29.4 9.3 %collective-permute-start.10 = (bf16[16,32,128]{2,1,0:T(8,128)(2,1)S(1)}, bf16[16,32,128]{2,1,0:T(8,128)(2,1)S(1)}, u32[]{:S(2)}, u32[]{:S(2)}) collective-permute-start(bf16[16,32,128]{2,1,0:T(8,128)(2,1)S(1)} %get-tuple-element.85), channel_id=1, source_target_pairs={{0,16},{8,24},{16,0},{24,8},{1,17},{9,25},{17,1},{25,9},{2,18},{10... | collective-permute-start | bytes 393224 | tf_op jit(solution)/shard_map/ppermute | solution.py:287
  30.4 8.3 %collective-permute-start.11 = (bf16[16,32,128]{2,1,0:T(8,128)(2,1)S(1)}, bf16[16,32,128]{2,1,0:T(8,128)(2,1)S(1)}, u32[]{:S(2)}, u32[]{:S(2)}) collective-permute-start(bf16[16,32,128]{2,1,0:T(8,128)(2,1)S(1)} %get-tuple-element.86), channel_id=1, source_target_pairs={{0,24},{8,16},{16,8},{24,0},{1,25},{9,17},{17,9},{25,1},{2,26},{10... | collective-permute-start | bytes 393224 | tf_op jit(solution)/shard_map/ppermute | solution.py:287
  31.8 9.5 %collective-permute-start.17 = (bf16[16,32,128]{2,1,0:T(8,128)(2,1)S(1)}, bf16[16,32,128]{2,1,0:T(8,128)(2,1)S(1)}, u32[]{:S(2)}, u32[]{:S(2)}) collective-permute-start(bf16[16,32,128]{2,1,0:T(8,128)(2,1)S(1)} %get-tuple-element.92), channel_id=1, source_target_pairs={{0,8},{8,0},{16,24},{24,16},{1,9},{9,1},{17,25},{25,17},{2,10},{10... | collective-permute-start | bytes 393224 | tf_op jit(solution)/shard_map/ppermute | solution.py:287
  32.9 8.7 %collective-permute-start.18 = (bf16[16,32,128]{2,1,0:T(8,128)(2,1)S(1)}, bf16[16,32,128]{2,1,0:T(8,128)(2,1)S(1)}, u32[]{:S(2)}, u32[]{:S(2)}) collective-permute-start(bf16[16,32,128]{2,1,0:T(8,128)(2,1)S(1)} %get-tuple-element.93), channel_id=1, source_target_pairs={{0,16},{8,24},{16,0},{24,8},{1,17},{9,25},{17,1},{25,9},{2,18},{10... | collective-permute-start | bytes 393224 | tf_op jit(solution)/shard_map/ppermute | solution.py:287
  34.5 7.2 %collective-permute-start.19 = (bf16[16,32,128]{2,1,0:T(8,128)(2,1)S(1)}, bf16[16,32,128]{2,1,0:T(8,128)(2,1)S(1)}, u32[]{:S(2)}, u32[]{:S(2)}) collective-permute-start(bf16[16,32,128]{2,1,0:T(8,128)(2,1)S(1)} %get-tuple-element.94), channel_id=1, source_target_pairs={{0,24},{8,16},{16,8},{24,0},{1,25},{9,17},{17,9},{25,1},{2,26},{10... | collective-permute-start | bytes 393224 | tf_op jit(solution)/shard_map/ppermute | solution.py:287
  38.8 6.0 %collective-permute-start.12 = (bf16[16,128,128]{2,1,0:T(8,128)(2,1)S(1)}, bf16[16,128,128]{2,1,0:T(8,128)(2,1)S(1)}, u32[]{:S(2)}, u32[]{:S(2)}) collective-permute-start(bf16[16,128,128]{2,1,0:T(8,128)(2,1)S(1)} %shard_map.88.own), channel_id=1, source_target_pairs={{0,1},{1,0},{2,3},{3,2},{4,5},{5,4},{6,7},{7,6},{8,9},{9,8},{10,11... | collective-permute-start | bytes 1572872 | tf_op jit(solution)/shard_map/ppermute | solution.py:413
  38.8 10.5 %collective-permute-start.13 = (bf16[16,128,128]{2,1,0:T(8,128)(2,1)S(1)}, bf16[16,128,128]{2,1,0:T(8,128)(2,1)S(1)}, u32[]{:S(2)}, u32[]{:S(2)}) collective-permute-start(bf16[16,128,128]{2,1,0:T(8,128)(2,1)S(1)} %shard_map.88.own), channel_id=1, source_target_pairs={{1,2},{2,1},{3,4},{4,3},{5,6},{6,5},{9,10},{10,9},{11,12},{12,11},... | collective-permute-start | bytes 1572872 | tf_op jit(solution)/shard_map/ppermute | solution.py:412
  41.7 12.0 %collective-permute-start.20 = (bf16[16,128,128]{2,1,0:T(8,128)(2,1)S(1)}, bf16[16,128,128]{2,1,0:T(8,128)(2,1)S(1)}, u32[]{:S(2)}, u32[]{:S(2)}) collective-permute-start(bf16[16,128,128]{2,1,0:T(8,128)(2,1)S(1)} %shard_map.91.own), channel_id=1, source_target_pairs={{0,1},{1,0},{2,3},{3,2},{4,5},{5,4},{6,7},{7,6},{8,9},{9,8},{10,11... | collective-permute-start | bytes 1572872 | tf_op jit(solution)/shard_map/ppermute | solution.py:413
  42.6 12.4 %collective-permute-start.21 = (bf16[16,128,128]{2,1,0:T(8,128)(2,1)S(1)}, bf16[16,128,128]{2,1,0:T(8,128)(2,1)S(1)}, u32[]{:S(2)}, u32[]{:S(2)}) collective-permute-start(bf16[16,128,128]{2,1,0:T(8,128)(2,1)S(1)} %shard_map.91.own), channel_id=1, source_target_pairs={{1,2},{2,1},{3,4},{4,3},{5,6},{6,5},{9,10},{10,9},{11,12},{12,11},... | collective-permute-start | bytes 1572872 | tf_op jit(solution)/shard_map/ppermute | solution.py:412
  50.1 7.2 %collective-permute-start.14 = (bf16[32,16,128]{2,1,0:T(8,128)(2,1)S(1)}, bf16[32,16,128]{2,1,0:T(8,128)(2,1)S(1)}, u32[]{:S(2)}, u32[]{:S(2)}) collective-permute-start(bf16[32,16,128]{2,1,0:T(8,128)(2,1)S(1)} %get-tuple-element.88), channel_id=1, source_target_pairs={{0,8},{8,0},{16,24},{24,16},{1,9},{9,1},{17,25},{25,17},{2,10},{10... | collective-permute-start | bytes 393224 | tf_op jit(solution)/shard_map/ppermute | solution.py:287
  51.3 8.7 %collective-permute-start.15 = (bf16[32,16,128]{2,1,0:T(8,128)(2,1)S(1)}, bf16[32,16,128]{2,1,0:T(8,128)(2,1)S(1)}, u32[]{:S(2)}, u32[]{:S(2)}) collective-permute-start(bf16[32,16,128]{2,1,0:T(8,128)(2,1)S(1)} %get-tuple-element.89), channel_id=1, source_target_pairs={{0,16},{8,24},{16,0},{24,8},{1,17},{9,25},{17,1},{25,9},{2,18},{10... | collective-permute-start | bytes 393224 | tf_op jit(solution)/shard_map/ppermute | solution.py:287
  51.7 8.3 %collective-permute-start.16 = (bf16[32,16,128]{2,1,0:T(8,128)(2,1)S(1)}, bf16[32,16,128]{2,1,0:T(8,128)(2,1)S(1)}, u32[]{:S(2)}, u32[]{:S(2)}) collective-permute-start(bf16[32,16,128]{2,1,0:T(8,128)(2,1)S(1)} %get-tuple-element.90), channel_id=1, source_target_pairs={{0,24},{8,16},{16,8},{24,0},{1,25},{9,17},{17,9},{25,1},{2,26},{10... | collective-permute-start | bytes 393224 | tf_op jit(solution)/shard_map/ppermute | solution.py:287
  55.7 6.4 %collective-permute-start.22 = (bf16[32,16,128]{2,1,0:T(8,128)(2,1)S(1)}, bf16[32,16,128]{2,1,0:T(8,128)(2,1)S(1)}, u32[]{:S(2)}, u32[]{:S(2)}) collective-permute-start(bf16[32,16,128]{2,1,0:T(8,128)(2,1)S(1)} %get-tuple-element.96), channel_id=1, source_target_pairs={{0,8},{8,0},{16,24},{24,16},{1,9},{9,1},{17,25},{25,17},{2,10},{10... | collective-permute-start | bytes 393224 | tf_op jit(solution)/shard_map/ppermute | solution.py:287
  56.9 8.7 %collective-permute-start.23 = (bf16[32,16,128]{2,1,0:T(8,128)(2,1)S(1)}, bf16[32,16,128]{2,1,0:T(8,128)(2,1)S(1)}, u32[]{:S(2)}, u32[]{:S(2)}) collective-permute-start(bf16[32,16,128]{2,1,0:T(8,128)(2,1)S(1)} %get-tuple-element.97), channel_id=1, source_target_pairs={{0,16},{8,24},{16,0},{24,8},{1,17},{9,25},{17,1},{25,9},{2,18},{10... | collective-permute-start | bytes 393224 | tf_op jit(solution)/shard_map/ppermute | solution.py:287
  57.3 8.3 %collective-permute-start.24 = (bf16[32,16,128]{2,1,0:T(8,128)(2,1)S(1)}, bf16[32,16,128]{2,1,0:T(8,128)(2,1)S(1)}, u32[]{:S(2)}, u32[]{:S(2)}) collective-permute-start(bf16[32,16,128]{2,1,0:T(8,128)(2,1)S(1)} %get-tuple-element.98), channel_id=1, source_target_pairs={{0,24},{8,16},{16,8},{24,0},{1,25},{9,17},{17,9},{25,1},{2,26},{10... | collective-permute-start | bytes 393224 | tf_op jit(solution)/shard_map/ppermute | solution.py:287
  67.2 9.3 %collective-permute-start.27 = (bf16[32,32,128]{2,1,0:T(8,128)(2,1)S(1)}, bf16[32,32,128]{2,1,0:T(8,128)(2,1)S(1)}, u32[]{:S(2)}, u32[]{:S(2)}) collective-permute-start(bf16[32,32,128]{2,1,0:T(8,128)(2,1)S(1)} %get-tuple-element.102), channel_id=1, source_target_pairs={{0,8},{8,0},{16,24},{24,16},{1,9},{9,1},{17,25},{25,17},{2,10},{10... | collective-permute-start | bytes 786440 | tf_op jit(solution)/shard_map/ppermute | solution.py:287
  68.3 13.3 %collective-permute-start.25 = (bf16[32,32,128]{2,1,0:T(8,128)(2,1)S(1)}, bf16[32,32,128]{2,1,0:T(8,128)(2,1)S(1)}, u32[]{:S(2)}, u32[]{:S(2)}) collective-permute-start(bf16[32,32,128]{2,1,0:T(8,128)(2,1)S(1)} %get-tuple-element.99), channel_id=1, source_target_pairs={{0,16},{8,24},{16,0},{24,8},{1,17},{9,25},{17,1},{25,9},{2,18},{10... | collective-permute-start | bytes 786440 | tf_op jit(solution)/shard_map/ppermute | solution.py:287
  69.1 12.5 %collective-permute-start.26 = (bf16[32,32,128]{2,1,0:T(8,128)(2,1)S(1)}, bf16[32,32,128]{2,1,0:T(8,128)(2,1)S(1)}, u32[]{:S(2)}, u32[]{:S(2)}) collective-permute-start(bf16[32,32,128]{2,1,0:T(8,128)(2,1)S(1)} %get-tuple-element.100), channel_id=1, source_target_pairs={{0,24},{8,16},{16,8},{24,0},{1,25},{9,17},{17,9},{25,1},{2,26},{10... | collective-permute-start | bytes 786440 | tf_op jit(solution)/shard_map/ppermute | solution.py:287

commit v3 on v2

--- a/solution.py
+++ b/solution.py
@@ -161,30 +161,36 @@
             )
 
 
-def sigma_kernel(groups, halves, fwd_l_ref, back_ref, less_ref, *refs):
+def sigma_kernel(groups, first, offsets, fwd_l_ref, back_ref, less_ref, *refs):
+    halves = len(offsets)
     inter, outs = refs[: groups * halves], refs[groups * halves :]
-    e_dev, orbitals = outs[0].shape[1:]
-    inter = [inter[h * groups + d] for d in range(groups) for h in range(halves)]
+    count, e_dev, orbitals = outs[0].shape
     freq = fwd_l_ref.shape[0] // 2
     fwd_l, back = fwd_l_ref[...], back_ref[...]
-    for n in range(less_ref.shape[0]):
-        a = less_ref[n]
-        b = dot(fwd_l, gathered(inter, n * WIDE))
+    inter = [
+        inter[h * groups + d].at[offsets[h] : offsets[h] + count]
+        for d in range(groups)
+        for h in range(halves)
+    ]
+    for i in range(0, count, WIDE):
+        a = less_ref[(first + i) // WIDE]
+        b = dot(fwd_l, gathered(inter, i))
         real = a[:freq] * b[:freq] - a[freq:] * b[freq:]
         imag = a[freq:] * b[:freq] + a[:freq] * b[freq:]
         sigma = inverse(back, jnp.concatenate([real, imag], axis=0)).astype(BF16)
         for h in range(WIDE):
             for d in range(groups):
-                outs[d][n * WIDE + h] = sigma[
+                outs[d][i + h] = sigma[
                     d * e_dev : (d + 1) * e_dev, h * orbitals : (h + 1) * orbitals
                 ]
 
 
 def assemble_kernel(*refs):
     ins, out = refs[:-1], refs[-1]
-    rows = ins[0].shape[1]
-    for d, part in enumerate(ins):
-        out[:, d * rows : (d + 1) * rows, :] = part[...]
+    at = 0
+    for part in ins:
+        out[:, at : at + part.shape[1], :] = part[...]
+        at += part.shape[1]
 
 
 def diagonal(a, b):
@@ -244,7 +250,7 @@
 
 
 def far_kernel(groups, me_ref, left, right, partial, far, *refs):
-    outs, scratch = refs[:groups], refs[groups]
+    outs, scratch = refs[:-1], refs[-1]
     lags, n, _ = partial.shape
     rows = n // groups
     me = me_ref[0]
@@ -253,26 +259,31 @@
     terms = dot(left[...], half)
     for k in range(lags):
         scratch[pl.ds(k, n, stride=lags), :] = partial[k] + terms[:, k * n : k * n + n]
-    size = rows * lags
-    for d in range(groups):
-        place = pl.ds(pl.multiple_of((me ^ d) * size, size), size)
-        outs[d][...] = scratch[place, :].astype(BF16).reshape(rows, lags, n)
-
-
-def final_kernel(groups, which, me_ref, *refs):
-    ins, out, scratch, sems = refs[: len(which)], refs[-3], refs[-2], refs[-1]
-    rows, e_dev, orbitals = ins[0].shape
+    first = 0
+    for c in range(0, len(outs), groups):
+        count = outs[c].shape[0]
+        for d in range(groups):
+            start = pl.multiple_of(((me ^ d) * rows + first) * lags, 8)
+            part = scratch[pl.ds(start, count * lags), :]
+            outs[c + d][...] = part.astype(BF16).reshape(count, lags, n)
+        first += count
+
+
+def final_kernel(groups, first, me_ref, *refs):
+    ins, out, scratch, sems = refs[:groups], refs[-3], refs[-2], refs[-1]
+    count, e_dev, orbitals = ins[0].shape
+    rows = orbitals // groups
     me = me_ref[0]
     copies = []
-    for n, d in enumerate(which):
-        for i in range(rows):
-            scratch[n, pl.ds(i, e_dev, stride=rows), :] = ins[n][i].astype(F32)
-        start = pl.multiple_of((me ^ d) * rows, rows)
+    for d in range(groups):
+        for i in range(count):
+            scratch[d, pl.ds(i, e_dev, stride=count), :] = ins[d][i].astype(F32)
+        start = pl.multiple_of((me ^ d) * rows + first, 8)
         copies.append(
             pltpu.make_async_copy(
-                scratch.at[n].reshape(e_dev, rows, orbitals),
-                out.at[:, pl.ds(start, rows), :],
-                sems.at[n],
+                scratch.at[d].reshape(e_dev, count, orbitals),
+                out.at[:, pl.ds(start, count), :],
+                sems.at[d],
             )
         )
         copies[-1].start()
@@ -402,11 +413,12 @@
     far_pairs = [(b, ((b + 1) ^ 1) - 1) for b in range(1, peers) if ((b + 1) ^ 1) - 1 < peers]
     inter = []
     for h in range(halves):
+        parts = pol[h]
         own = call(
             assemble_kernel,
             shape(lags, orbitals, orbitals),
-            [vmem()] * groups,
-            *pol[h],
+            [vmem()] * len(parts),
+            *parts,
             out_specs=vmem(),
         )
         far = lax.ppermute(own, "block", far_pairs)
@@ -421,47 +433,53 @@
             near,
             out_specs=vmem(),
         )
+        cut = [rows]
         parts = call(
             functools.partial(far_kernel, groups),
-            [shape(rows, lags, orbitals)] * groups,
+            [shape(count, lags, orbitals) for count in cut for _ in range(groups)],
             [smem] + [vmem()] * 4,
             me,
             far_left,
             far_right,
             partial,
             far,
+            out_specs=[vmem()] * (groups * len(cut)),
+            scratch=[pltpu.VMEM((orbitals * lags, orbitals), F32)],
+        )
+        inter.append(
+            [exchange(parts[c * groups : (c + 1) * groups]) for c in range(len(cut))]
+        )
+
+    sigma = []
+    for c, count in enumerate(counts):
+        first = sum(counts[:c])
+        parts = call(
+            functools.partial(sigma_kernel, groups, first, [first] * halves),
+            [shape(count, e_dev, orbitals)] * groups,
+            [vmem()] * (3 + groups * halves),
+            fwd_l,
+            back_e,
+            less,
+            *[part for half in inter for part in half[0]],
             out_specs=[vmem()] * groups,
-            scratch=[pltpu.VMEM((orbitals * lags, orbitals), F32)],
-        )
-        inter += exchange(parts)
-
-    sigma = call(
-        functools.partial(sigma_kernel, groups, halves),
-        [shape(rows, e_dev, orbitals)] * groups,
-        [vmem()] * (3 + groups * halves),
-        fwd_l,
-        back_e,
-        less,
-        *inter,
-        out_specs=[vmem()] * groups,
-    )
-    sigma = exchange(sigma)
+        )
+        sigma.append((first, count, exchange(parts)))
     out = []
-    for which in (list(range(groups // 2)), list(range(groups // 2, groups))):
+    for first, count, parts in sigma:
         out = [
             call(
-                functools.partial(final_kernel, groups, which),
+                functools.partial(final_kernel, groups, first),
                 shape(e_dev, orbitals, orbitals, dtype=F32),
-                [smem] + [vmem()] * len(which) + [hbm] * len(out),
+                [smem] + [vmem()] * groups + [hbm] * len(out),
                 me,
-                *[sigma[d] for d in which],
+                *parts,
                 *out,
                 out_specs=hbm,
                 scratch=[
-                    pltpu.VMEM((len(which), e_dev * rows, orbitals), F32),
-                    pltpu.SemaphoreType.DMA((len(which),)),
+                    pltpu.VMEM((groups, e_dev * count, orbitals), F32),
+                    pltpu.SemaphoreType.DMA((groups,)),
                 ],
-                input_output_aliases={1 + len(which): 0} if out else {},
+                input_output_aliases={1 + groups: 0} if out else {},
             )
         ]
     return out[0].reshape(e_dev, 1, orbitals, orbitals)

time: 83.7 us -> 82.2 us (0.982)
  waiting for transfers between devices: 28.3 us -> 25.5 us
  starting transfers between devices: 37.3 us -> 40 us
  Pallas kernels: 17.6 us -> 16.2 us
    ppermute x24 -> x27, starting transfers between devices: 31.7 us -> 34.6 us  [exchange(): lax.ppermute(parts[d], 'energy', [(i, i ^ d) for i in range(groups)])]
    ppermute x24 -> x27, waiting for transfers between devices: 24.1 us -> 21.2 us  [exchange(): lax.ppermute(parts[d], 'energy', [(i, i ^ d) for i in range(groups)])]
    pallas_call x15 -> x16, Pallas kernels: 17.6 us -> 16.2 us  [call(): pl.pallas_call(kernel, out_shape=out_shape, in_specs=specs, scratch_shape...]
  transfers between devices with their start and end apart: 28 -> 31, of which waited for: 16 -> 17; matrix products, arithmetic and copies ran while one was open for 0% -> 0% of each run, Pallas kernels for 15% -> 15%
where the time goes in v3:
time: 82.2 us; the launch traced here: 82 us
  starting transfers between devices  40 us (49%)
  waiting for transfers between devices  25.5 us (31%)
  Pallas kernels  16.2 us (20%)
    ppermute x27, starting transfers between devices, exchange(): lax.ppermute(parts[d], 'energy', [(i, i ^ d) for i in range(groups)])  34.6 us
    ppermute x27, waiting for transfers between devices, exchange(): lax.ppermute(parts[d], 'energy', [(i, i ^ d) for i in range(groups)])  21.2 us
    pallas_call x16, Pallas kernels, call(): pl.pallas_call(kernel, out_shape=out_shape, in_specs=specs, scratch_shape...  16.2 us
    ppermute x2, starting transfers between devices, shards(): far = lax.ppermute(own, 'block', far_pairs)  4.42 us
    ppermute x2, waiting for transfers between devices, shards(): far = lax.ppermute(own, 'block', far_pairs)  4.39 us
  transfers between devices with their start and end apart: 31, of which 17 were waited for; matrix products, arithmetic and copies ran while one was open for 0% of the time, Pallas kernels for 15%

profile of v3, /device:TPU:16, one launch (start us, length us, event | category | flops | bytes accessed | tf_op | source)
XLA Modules:
  0.0 82.0 jit_solution(2670654514651947336)
XLA Ops:
  0.0 1.3 %shard_map.84 = (bf16[32,32,128]{2,1,0:T(8,128)(2,1)S(1)}, bf16[32,32,128]{2,1,0:T(8,128)(2,1)S(1)}, bf16[32,32,128]{2,1,0:T(8,128)(2,1)S(1)}, bf16[32,32,128]{2,1,0:T(8,128)(2,1)S(1)}) custom-call(s32[1]{0:T(128)} %bitcast.me_ref, bf16[32,128,128]{2,1,0:T(8,128)(2,1)} %bitcast.11), custom_call_target="tpu_custom_call" | custom-call | tf_op jit(solution)/shard_map/pallas_call | solution.py:303
  1.3 1.6 %collective-permute-start = (bf16[32,32,128]{2,1,0:T(8,128)(2,1)S(1)}, bf16[32,32,128]{2,1,0:T(8,128)(2,1)S(1)}, u32[]{:S(2)}, u32[]{:S(2)}) collective-permute-start(bf16[32,32,128]{2,1,0:T(8,128)(2,1)S(1)} %get-tuple-element.65), channel_id=1, source_target_pairs={{0,8},{8,0},{16,24},{24,16},{1,9},{9,1},{17,25},{25,17},{2,10},{10... | collective-permute-start | bytes 786440 | tf_op jit(solution)/shard_map/ppermute | solution.py:298
  2.8 1.5 %collective-permute-start.1 = (bf16[32,32,128]{2,1,0:T(8,128)(2,1)S(1)}, bf16[32,32,128]{2,1,0:T(8,128)(2,1)S(1)}, u32[]{:S(2)}, u32[]{:S(2)}) collective-permute-start(bf16[32,32,128]{2,1,0:T(8,128)(2,1)S(1)} %get-tuple-element.66), channel_id=1, source_target_pairs={{0,16},{8,24},{16,0},{24,8},{1,17},{9,25},{17,1},{25,9},{2,18},{10... | collective-permute-start | bytes 786440 | tf_op jit(solution)/shard_map/ppermute | solution.py:298
  4.8 2.5 %shard_map.83 = (bf16[24,32,128]{2,1,0:T(8,128)(2,1)S(1)}, bf16[24,32,128]{2,1,0:T(8,128)(2,1)S(1)}, bf16[24,32,128]{2,1,0:T(8,128)(2,1)S(1)}, bf16[24,32,128]{2...) custom-call(s32[1]{0:T(128)} %bitcast.me_ref, ...), custom_call_target="tpu_custom_call" | custom-call | tf_op jit(solution)/shard_map/pallas_call | solution.py:303
  7.3 1.6 %collective-permute-start.6 = (bf16[24,32,128]{2,1,0:T(8,128)(2,1)S(1)}, bf16[24,32,128]{2,1,0:T(8,128)(2,1)S(1)}, u32[]{:S(2)}, u32[]{:S(2)}) collective-permute-start(bf16[24,32,128]{2,1,0:T(8,128)(2,1)S(1)} %get-tuple-element.84), channel_id=1, source_target_pairs={{0,8},{8,0},{16,24},{24,16},{1,9},{9,1},{17,25},{25,17},{2,10},{10... | collective-permute-start | bytes 589832 | tf_op jit(solution)/shard_map/ppermute | solution.py:298
  8.8 1.5 %collective-permute-start.7 = (bf16[24,32,128]{2,1,0:T(8,128)(2,1)S(1)}, bf16[24,32,128]{2,1,0:T(8,128)(2,1)S(1)}, u32[]{:S(2)}, u32[]{:S(2)}) collective-permute-start(bf16[24,32,128]{2,1,0:T(8,128)(2,1)S(1)} %get-tuple-element.85), channel_id=1, source_target_pairs={{0,16},{8,24},{16,0},{24,8},{1,17},{9,25},{17,1},{25,9},{2,18},{10... | collective-permute-start | bytes 589832 | tf_op jit(solution)/shard_map/ppermute | solution.py:298
  10.5 2.4 %collective-permute-start.8 = (bf16[24,32,128]{2,1,0:T(8,128)(2,1)S(1)}, bf16[24,32,128]{2,1,0:T(8,128)(2,1)S(1)}, u32[]{:S(2)}, u32[]{:S(2)}) collective-permute-start(bf16[24,32,128]{2,1,0:T(8,128)(2,1)S(1)} %get-tuple-element.86), channel_id=1, source_target_pairs={{0,24},{8,16},{16,8},{24,0},{1,25},{9,17},{17,9},{25,1},{2,26},{10... | collective-permute-start | bytes 589832 | tf_op jit(solution)/shard_map/ppermute | solution.py:298
  13.0 1.7 %shard_map.82 = (bf16[192,256]{1,0:T(8,128)(2,1)S(1)}, bf16[192,256]{1,0:T(8,128)(2,1)S(1)}, bf16[256,192]{1,0:T(8,128)(2,1)S(1)}, bf16[256,192]{1,0:T(8,128)(2,...) custom-call(s32[1]{0:T(128)} %bitcast.me_ref, ...), custom_call_target="tpu_custom_call" | custom-call | tf_op jit(solution)/shard_map/pallas_call | solution.py:303
  14.7 2.3 %collective-permute-done.1.refs_2_ = bf16[32,32,128]{2,1,0:T(8,128)(2,1)S(1)} collective-permute-done((bf16[32,32,128]{2,1,0:T(8,128)(2,1)S(1)}, bf16[32,32,128]{2,1,0:T(8,128)(2,1)S(1)}, u32[]{:S(2)}, u32[]{:S(2)}) %collective-permute-start.1) | collective-permute-done | bytes 262176 | tf_op jit(solution)/shard_map/ppermute | solution.py:298
  17.2 1.5 %collective-permute-start.3 = (bf16[8,32,128]{2,1,0:T(8,128)(2,1)S(1)}, bf16[8,32,128]{2,1,0:T(8,128)(2,1)S(1)}, u32[]{:S(2)}, u32[]{:S(2)}) collective-permute-start(bf16[8,32,128]{2,1,0:T(8,128)(2,1)S(1)} %get-tuple-element.80), channel_id=1, source_target_pairs={{0,8},{8,0},{16,24},{24,16},{1,9},{9,1},{17,25},{25,17},{2,10},{10... | collective-permute-start | bytes 196616 | tf_op jit(solution)/shard_map/ppermute | solution.py:298
  19.2 1.3 %collective-permute-done.6.refs_1_ = bf16[24,32,128]{2,1,0:T(8,128)(2,1)S(1)} collective-permute-done((bf16[24,32,128]{2,1,0:T(8,128)(2,1)S(1)}, bf16[24,32,128]{2,1,0:T(8,128)(2,1)S(1)}, u32[]{:S(2)}, u32[]{:S(2)}) %collective-permute-start.6) | collective-permute-done | bytes 196640 | tf_op jit(solution)/shard_map/ppermute | solution.py:298
  20.4 2.4 %collective-permute-start.5 = (bf16[8,32,128]{2,1,0:T(8,128)(2,1)S(1)}, bf16[8,32,128]{2,1,0:T(8,128)(2,1)S(1)}, u32[]{:S(2)}, u32[]{:S(2)}) collective-permute-start(bf16[8,32,128]{2,1,0:T(8,128)(2,1)S(1)} %get-tuple-element.82), channel_id=1, source_target_pairs={{0,24},{8,16},{16,8},{24,0},{1,25},{9,17},{17,9},{25,1},{2,26},{10... | collective-permute-start | bytes 196616 | tf_op jit(solution)/shard_map/ppermute | solution.py:298
  22.9 1.7 %shard_map.85.less_ref = f32[4,192,1024]{2,1,0:T(8,128)S(1)} custom-call(bf16[192,256]{1,0:T(8,128)(2,1)S(1)} %get-tuple-element.69.fwd_ref, bf16[32,32,128]{2,1,0:T(8,128)(2,1)S(1)} %get-tuple-element.70.refs_0_, bf16[32,32,128]{2,1,0:T(8,128)(2,1)S(1)} %collective-permute-done.refs_1_, bf16[32,32,128]{2,1,0:T(8,128)(2,1)S(1)} %collective-permute-done.1.refs_2_, ...), custom_call_target="tpu_custom_call" | custom-call | tf_op jit(solution)/shard_map/pallas_call | solution.py:303
  24.6 1.4 %collective-permute-done.7.refs_2_ = bf16[24,32,128]{2,1,0:T(8,128)(2,1)S(1)} collective-permute-done((bf16[24,32,128]{2,1,0:T(8,128)(2,1)S(1)}, bf16[24,32,128]{2,1,0:T(8,128)(2,1)S(1)}, u32[]{:S(2)}, u32[]{:S(2)}) %collective-permute-start.7) | collective-permute-done | bytes 196640 | tf_op jit(solution)/shard_map/ppermute | solution.py:298
  26.0 1.4 %shard_map.86.refs_4_ = bf16[128,24,128]{2,1,0:T(8,128)(2,1)S(1)} custom-call(bf16[192,256]{1,0:T(8,128)(2,1)S(1)} %get-tuple-element.69.fwd_ref, bf16[256,192]{1,0:T(8,128)(2,1)S(1)} %get-tuple-element.78.back_ref, f32[4,192,1024]{2,1,0:T(8,128)S(1)} %shard_map.85.less_ref, bf16[24,32,128]{2,1,0:T(8,128)(2,1)S(1)} %get-tuple-element.83.refs_0_, ...), custom_call_target="tpu_custom_call" | custom-call | tf_op jit(solution)/shard_map/pallas_call | solution.py:303
  28.0 1.4 %collective-permute-start.9 = (bf16[16,32,128]{2,1,0:T(8,128)(2,1)S(1)}, bf16[16,32,128]{2,1,0:T(8,128)(2,1)S(1)}, u32[]{:S(2)}, u32[]{:S(2)}) collective-permute-start(bf16[16,32,128]{2,1,0:T(8,128)(2,1)S(1)} %get-tuple-element.88), channel_id=1, source_target_pairs={{0,8},{8,0},{16,24},{24,16},{1,9},{9,1},{17,25},{25,17},{2,10},{10... | collective-permute-start | bytes 393224 | tf_op jit(solution)/shard_map/ppermute | solution.py:298
  29.4 1.0 %collective-permute-start.10 = (bf16[16,32,128]{2,1,0:T(8,128)(2,1)S(1)}, bf16[16,32,128]{2,1,0:T(8,128)(2,1)S(1)}, u32[]{:S(2)}, u32[]{:S(2)}) collective-permute-start(bf16[16,32,128]{2,1,0:T(8,128)(2,1)S(1)} %get-tuple-element.89), channel_id=1, source_target_pairs={{0,16},{8,24},{16,0},{24,8},{1,17},{9,25},{17,1},{25,9},{2,18},{10... | collective-permute-start | bytes 393224 | tf_op jit(solution)/shard_map/ppermute | solution.py:298
  30.4 1.4 %collective-permute-start.11 = (bf16[16,32,128]{2,1,0:T(8,128)(2,1)S(1)}, bf16[16,32,128]{2,1,0:T(8,128)(2,1)S(1)}, u32[]{:S(2)}, u32[]{:S(2)}) collective-permute-start(bf16[16,32,128]{2,1,0:T(8,128)(2,1)S(1)} %get-tuple-element.90), channel_id=1, source_target_pairs={{0,24},{8,16},{16,8},{24,0},{1,25},{9,17},{17,9},{25,1},{2,26},{10... | collective-permute-start | bytes 393224 | tf_op jit(solution)/shard_map/ppermute | solution.py:298
  31.8 1.1 %collective-permute-start.17 = (bf16[16,32,128]{2,1,0:T(8,128)(2,1)S(1)}, bf16[16,32,128]{2,1,0:T(8,128)(2,1)S(1)}, u32[]{:S(2)}, u32[]{:S(2)}) collective-permute-start(bf16[16,32,128]{2,1,0:T(8,128)(2,1)S(1)} %get-tuple-element.96), channel_id=1, source_target_pairs={{0,8},{8,0},{16,24},{24,16},{1,9},{9,1},{17,25},{25,17},{2,10},{10... | collective-permute-start | bytes 393224 | tf_op jit(solution)/shard_map/ppermute | solution.py:298
  32.9 1.0 %collective-permute-start.18 = (bf16[16,32,128]{2,1,0:T(8,128)(2,1)S(1)}, bf16[16,32,128]{2,1,0:T(8,128)(2,1)S(1)}, u32[]{:S(2)}, u32[]{:S(2)}) collective-permute-start(bf16[16,32,128]{2,1,0:T(8,128)(2,1)S(1)} %get-tuple-element.97), channel_id=1, source_target_pairs={{0,16},{8,24},{16,0},{24,8},{1,17},{9,25},{17,1},{25,9},{2,18},{10... | collective-permute-start | bytes 393224 | tf_op jit(solution)/shard_map/ppermute | solution.py:298
  34.5 1.6 %collective-permute-start.19 = (bf16[16,32,128]{2,1,0:T(8,128)(2,1)S(1)}, bf16[16,32,128]{2,1,0:T(8,128)(2,1)S(1)}, u32[]{:S(2)}, u32[]{:S(2)}) collective-permute-start(bf16[16,32,128]{2,1,0:T(8,128)(2,1)S(1)} %get-tuple-element.98), channel_id=1, source_target_pairs={{0,24},{8,16},{16,8},{24,0},{1,25},{9,17},{17,9},{25,1},{2,26},{10... | collective-permute-start | bytes 393224 | tf_op jit(solution)/shard_map/ppermute | solution.py:298
  36.1 2.6 %collective-permute-done.10.refs_2_ = bf16[16,32,128]{2,1,0:T(8,128)(2,1)S(1)} collective-permute-done((bf16[16,32,128]{2,1,0:T(8,128)(2,1)S(1)}, bf16[16,32,128]{2,1,0:T(8,128)(2,1)S(1)}, u32[]{:S(2)}, u32[]{:S(2)}) %collective-permute-start.10) | collective-permute-done | bytes 131104 | tf_op jit(solution)/shard_map/ppermute | solution.py:298
  38.8 2.5 %collective-permute-start.13 = (bf16[16,128,128]{2,1,0:T(8,128)(2,1)S(1)}, bf16[16,128,128]{2,1,0:T(8,128)(2,1)S(1)}, u32[]{:S(2)}, u32[]{:S(2)}) collective-permute-start(bf16[16,128,128]{2,1,0:T(8,128)(2,1)S(1)} %shard_map.88.own), channel_id=1, source_target_pairs={{1,2},{2,1},{3,4},{4,3},{5,6},{6,5},{9,10},{10,9},{11,12},{12,11},... | collective-permute-start | bytes 1572872 | tf_op jit(solution)/shard_map/ppermute | solution.py:424
  41.7 0.9 %collective-permute-start.20 = (bf16[16,128,128]{2,1,0:T(8,128)(2,1)S(1)}, bf16[16,128,128]{2,1,0:T(8,128)(2,1)S(1)}, u32[]{:S(2)}, u32[]{:S(2)}) collective-permute-start(bf16[16,128,128]{2,1,0:T(8,128)(2,1)S(1)} %shard_map.91.own), channel_id=1, source_target_pairs={{0,1},{1,0},{2,3},{3,2},{4,5},{5,4},{6,7},{7,6},{8,9},{9,8},{10,11... | collective-permute-start | bytes 1572872 | tf_op jit(solution)/shard_map/ppermute | solution.py:425
  42.6 2.0 %collective-permute-start.21 = (bf16[16,128,128]{2,1,0:T(8,128)(2,1)S(1)}, bf16[16,128,128]{2,1,0:T(8,128)(2,1)S(1)}, u32[]{:S(2)}, u32[]{:S(2)}) collective-permute-start(bf16[16,128,128]{2,1,0:T(8,128)(2,1)S(1)} %shard_map.91.own), channel_id=1, source_target_pairs={{1,2},{2,1},{3,4},{4,3},{5,6},{6,5},{9,10},{10,9},{11,12},{12,11},... | collective-permute-start | bytes 1572872 | tf_op jit(solution)/shard_map/ppermute | solution.py:424
  44.6 0.8 shard_map.89.partial
  45.4 3.9 %collective-permute-done.13.far = bf16[16,128,128]{2,1,0:T(8,128)(2,1)S(1)} collective-permute-done((bf16[16,128,128]{2,1,0:T(8,128)(2,1)S(1)}, bf16[16,128,128]{2,1,0:T(8,128)(2,1)S(1)}, u32[]{:S(2)}, u32[]{:S(2)}) %collective-permute-start.13) | collective-permute-done | bytes 524320 | tf_op jit(solution)/shard_map/ppermute | solution.py:424
  49.3 0.8 shard_map.90
  50.1 1.2 %collective-permute-start.14 = (bf16[32,16,128]{2,1,0:T(8,128)(2,1)S(1)}, bf16[32,16,128]{2,1,0:T(8,128)(2,1)S(1)}, u32[]{:S(2)}, u32[]{:S(2)}) collective-permute-start(bf16[32,16,128]{2,1,0:T(8,128)(2,1)S(1)} %get-tuple-element.92), channel_id=1, source_target_pairs={{0,8},{8,0},{16,24},{24,16},{1,9},{9,1},{17,25},{25,17},{2,10},{10... | collective-permute-start | bytes 393224 | tf_op jit(solution)/shard_map/ppermute | solution.py:298
  51.7 2.0 %collective-permute-start.16 = (bf16[32,16,128]{2,1,0:T(8,128)(2,1)S(1)}, bf16[32,16,128]{2,1,0:T(8,128)(2,1)S(1)}, u32[]{:S(2)}, u32[]{:S(2)}) collective-permute-start(bf16[32,16,128]{2,1,0:T(8,128)(2,1)S(1)} %get-tuple-element.94), channel_id=1, source_target_pairs={{0,24},{8,16},{16,8},{24,0},{1,25},{9,17},{17,9},{25,1},{2,26},{10... | collective-permute-start | bytes 393224 | tf_op jit(solution)/shard_map/ppermute | solution.py:298
  53.7 0.8 shard_map.92.partial
  55.0 0.8 shard_map.93
  55.7 1.2 %collective-permute-start.22 = (bf16[32,16,128]{2,1,0:T(8,128)(2,1)S(1)}, bf16[32,16,128]{2,1,0:T(8,128)(2,1)S(1)}, u32[]{:S(2)}, u32[]{:S(2)}) collective-permute-start(bf16[32,16,128]{2,1,0:T(8,128)(2,1)S(1)} %get-tuple-element.100), channel_id=1, source_target_pairs={{0,8},{8,0},{16,24},{24,16},{1,9},{9,1},{17,25},{25,17},{2,10},{10... | collective-permute-start | bytes 393224 | tf_op jit(solution)/shard_map/ppermute | solution.py:298
  57.3 2.0 %collective-permute-start.24 = (bf16[32,16,128]{2,1,0:T(8,128)(2,1)S(1)}, bf16[32,16,128]{2,1,0:T(8,128)(2,1)S(1)}, u32[]{:S(2)}, u32[]{:S(2)}) collective-permute-start(bf16[32,16,128]{2,1,0:T(8,128)(2,1)S(1)} %get-tuple-element.102), channel_id=1, source_target_pairs={{0,24},{8,16},{16,8},{24,0},{1,25},{9,17},{17,9},{25,1},{2,26},{10... | collective-permute-start | bytes 393224 | tf_op jit(solution)/shard_map/ppermute | solution.py:298
  59.3 0.7 collective-permute-done.15.refs_2_
  60.0 2.2 %collective-permute-done.22.refs_5_ = bf16[32,16,128]{2,1,0:T(8,128)(2,1)S(1)} collective-permute-done((bf16[32,16,128]{2,1,0:T(8,128)(2,1)S(1)}, bf16[32,16,128]{2,1,0:T(8,128)(2,1)S(1)}, u32[]{:S(2)}, u32[]{:S(2)}) %collective-permute-start.22) | collective-permute-done | bytes 131104 | tf_op jit(solution)/shard_map/ppermute | solution.py:298
  62.2 3.4 %collective-permute-done.23.refs_6_ = bf16[32,16,128]{2,1,0:T(8,128)(2,1)S(1)} collective-permute-done((bf16[32,16,128]{2,1,0:T(8,128)(2,1)S(1)}, bf16[32,16,128]{2,1,0:T(8,128)(2,1)S(1)}, u32[]{:S(2)}, u32[]{:S(2)}) %collective-permute-start.23) | collective-permute-done | bytes 131104 | tf_op jit(solution)/shard_map/ppermute | solution.py:298
  65.6 1.3 %shard_map.95 = (bf16[24,32,128]{2,1,0:T(8,128)(2,1)S(1)}, bf16[24,32,128]{2,1,0:T(8,128)(2,1)S(1)}, bf16[24,32,128]{2,1,0:T(8,128)(2,1)S(1)}, bf16[24,32,128]{2,1,0:T(8,128)(2,1)S(1)}) custom-call(bf16[192,256]{1,0:T(8,128)(2,1)S(1)} %get-tuple-element.58.fwd_l_ref, bf16[256,192]{1,0:T(8,128)(2,1)S(1)} %get-tuple-element.59.back_ref, ...), custom_call_target="tpu_custom_call" | custom-call | tf_op jit(solution)/shard_map/pallas_call | solution.py:303
  66.9 1.0 %collective-permute-start.28 = (bf16[24,32,128]{2,1,0:T(8,128)(2,1)S(1)}, bf16[24,32,128]{2,1,0:T(8,128)(2,1)S(1)}, u32[]{:S(2)}, u32[]{:S(2)}) collective-permute-start(bf16[24,32,128]{2,1,0:T(8,128)(2,1)S(1)} %get-tuple-element.108), channel_id=1, source_target_pairs={{0,8},{8,0},{16,24},{24,16},{1,9},{9,1},{17,25},{25,17},{2,10},{10... | collective-permute-start | bytes 589832 | tf_op jit(solution)/shard_map/ppermute | solution.py:298
  67.9 0.8 collective-permute-start.29
  68.7 1.8 %collective-permute-start.30 = (bf16[24,32,128]{2,1,0:T(8,128)(2,1)S(1)}, bf16[24,32,128]{2,1,0:T(8,128)(2,1)S(1)}, u32[]{:S(2)}, u32[]{:S(2)}) collective-permute-start(bf16[24,32,128]{2,1,0:T(8,128)(2,1)S(1)} %get-tuple-element.110), channel_id=1, source_target_pairs={{0,24},{8,16},{16,8},{24,0},{1,25},{9,17},{17,9},{25,1},{2,26},{10... | collective-permute-start | bytes 589832 | tf_op jit(solution)/shard_map/ppermute | solution.py:298
  71.0 1.0 %collective-permute-start.25 = (bf16[8,32,128]{2,1,0:T(8,128)(2,1)S(1)}, bf16[8,32,128]{2,1,0:T(8,128)(2,1)S(1)}, u32[]{:S(2)}, u32[]{:S(2)}) collective-permute-start(bf16[8,32,128]{2,1,0:T(8,128)(2,1)S(1)} %get-tuple-element.104), channel_id=1, source_target_pairs={{0,8},{8,0},{16,24},{24,16},{1,9},{9,1},{17,25},{25,17},{2,10},{10... | collective-permute-start | bytes 196616 | tf_op jit(solution)/shard_map/ppermute | solution.py:298
  72.0 0.8 collective-permute-start.26
  72.8 2.0 %collective-permute-done.28.refs_1_ = bf16[24,32,128]{2,1,0:T(8,128)(2,1)S(1)} collective-permute-done((bf16[24,32,128]{2,1,0:T(8,128)(2,1)S(1)}, bf16[24,32,128]{2,1,0:T(8,128)(2,1)S(1)}, u32[]{:S(2)}, u32[]{:S(2)}) %collective-permute-start.28) | collective-permute-done | bytes 196640 | tf_op jit(solution)/shard_map/ppermute | solution.py:298
  74.8 1.1 %collective-permute-start.27 = (bf16[8,32,128]{2,1,0:T(8,128)(2,1)S(1)}, bf16[8,32,128]{2,1,0:T(8,128)(2,1)S(1)}, u32[]{:S(2)}, u32[]{:S(2)}) collective-permute-start(bf16[8,32,128]{2,1,0:T(8,128)(2,1)S(1)} %get-tuple-element.106), channel_id=1, source_target_pairs={{0,24},{8,16},{16,8},{24,0},{1,25},{9,17},{17,9},{25,1},{2,26},{10... | collective-permute-start | bytes 196616 | tf_op jit(solution)/shard_map/ppermute | solution.py:298
  75.9 3.8 %collective-permute-done.29.refs_2_ = bf16[24,32,128]{2,1,0:T(8,128)(2,1)S(1)} collective-permute-done((bf16[24,32,128]{2,1,0:T(8,128)(2,1)S(1)}, bf16[24,32,128]{2,1,0:T(8,128)(2,1)S(1)}, u32[]{:S(2)}, u32[]{:S(2)}) %collective-permute-start.29) | collective-permute-done | bytes 196640 | tf_op jit(solution)/shard_map/ppermute | solution.py:298
  79.7 1.2 %shard_map.96.refs_4_ = f32[32,128,128]{2,1,0:T(8,128)} custom-call(s32[1]{0:T(128)} %bitcast.me_ref, bf16[24,32,128]{2,1,0:T(8,128)(2,1)S(1)} %get-tuple-element.107.refs_0_, bf16[24,32,128]{2,1,0:T(8,128)(2,1)S(1)} %collective-permute-done.28.refs_1_, bf16[24,32,128]{2,1,0:T(8,128)(2,1)S(1)} %collective-permute-done.29.refs_2_, ...), custom_call_target="tpu_custom_call" | custom-call | tf_op jit(solution)/shard_map/pallas_call | solution.py:303
  81.2 0.8 %shard_map.97 = f32[32,128,128]{2,1,0:T(8,128)} custom-call(s32[1]{0:T(128)} %bitcast.me_ref, bf16[8,32,128]{2,1,0:T(8,128)(2,1)S(1)} %get-tuple-element.103.refs_0_, bf16[8,32,128]{2,1,0:T(8,128)(2,1)S(1)} %collective-permute-done.25.refs_1_, bf16[8,32,128]{2,1,0:T(8,128)(2,1)S(1)} %collective-permute-done.26.refs_2_, ...), custom_call_target="tpu_custom_call", output_to_operand_aliasing={{}: (5, {})} | custom-call | tf_op jit(solution)/shard_map/pallas_call | solution.py:303
  (34 shorter events, 5.1 us)
Async XLA Ops:
  0.0 13.0 %copy-start.1 = (s32[1,2]{1,0:T(1,128)S(1)}, s32[1,2]{1,0:T(1,128)}, u32[]{:S(2)}) copy-start(s32[1,2]{1,0:T(1,128)} %param.11) | copy-start | bytes 28
  0.0 13.0 %copy-start = (bf16[1,3,128,128]{3,2,1,0:T(8,128)(2,1)S(1)}, bf16[1,3,128,128]{3,2,1,0:T(8,128)(2,1)}, u32[]{:S(2)}) copy-start(bf16[1,3,128,128]{3,2,1,0:T(8,128)(2,1)} %param.10) | copy-start | bytes 294916
  1.3 9.3 %collective-permute-start = (bf16[32,32,128]{2,1,0:T(8,128)(2,1)S(1)}, bf16[32,32,128]{2,1,0:T(8,128)(2,1)S(1)}, u32[]{:S(2)}, u32[]{:S(2)}) collective-permute-start(bf16[32,32,128]{2,1,0:T(8,128)(2,1)S(1)} %get-tuple-element.65), channel_id=1, source_target_pairs={{0,8},{8,0},{16,24},{24,16},{1,9},{9,1},{17,25},{25,17},{2,10},{10... | collective-permute-start | bytes 786440 | tf_op jit(solution)/shard_map/ppermute | solution.py:298
  2.8 14.2 %collective-permute-start.1 = (bf16[32,32,128]{2,1,0:T(8,128)(2,1)S(1)}, bf16[32,32,128]{2,1,0:T(8,128)(2,1)S(1)}, u32[]{:S(2)}, u32[]{:S(2)}) collective-permute-start(bf16[32,32,128]{2,1,0:T(8,128)(2,1)S(1)} %get-tuple-element.66), channel_id=1, source_target_pairs={{0,16},{8,24},{16,0},{24,8},{1,17},{9,25},{17,1},{25,9},{2,18},{10... | collective-permute-start | bytes 786440 | tf_op jit(solution)/shard_map/ppermute | solution.py:298
  4.3 12.8 %collective-permute-start.2 = (bf16[32,32,128]{2,1,0:T(8,128)(2,1)S(1)}, bf16[32,32,128]{2,1,0:T(8,128)(2,1)S(1)}, u32[]{:S(2)}, u32[]{:S(2)}) collective-permute-start(bf16[32,32,128]{2,1,0:T(8,128)(2,1)S(1)} %get-tuple-element.67), channel_id=1, source_target_pairs={{0,24},{8,16},{16,8},{24,0},{1,25},{9,17},{17,9},{25,1},{2,26},{10... | collective-permute-start | bytes 786440 | tf_op jit(solution)/shard_map/ppermute | solution.py:298
  7.3 13.1 %collective-permute-start.6 = (bf16[24,32,128]{2,1,0:T(8,128)(2,1)S(1)}, bf16[24,32,128]{2,1,0:T(8,128)(2,1)S(1)}, u32[]{:S(2)}, u32[]{:S(2)}) collective-permute-start(bf16[24,32,128]{2,1,0:T(8,128)(2,1)S(1)} %get-tuple-element.84), channel_id=1, source_target_pairs={{0,8},{8,0},{16,24},{24,16},{1,9},{9,1},{17,25},{25,17},{2,10},{10... | collective-permute-start | bytes 589832 | tf_op jit(solution)/shard_map/ppermute | solution.py:298
  8.8 17.1 %collective-permute-start.7 = (bf16[24,32,128]{2,1,0:T(8,128)(2,1)S(1)}, bf16[24,32,128]{2,1,0:T(8,128)(2,1)S(1)}, u32[]{:S(2)}, u32[]{:S(2)}) collective-permute-start(bf16[24,32,128]{2,1,0:T(8,128)(2,1)S(1)} %get-tuple-element.85), channel_id=1, source_target_pairs={{0,16},{8,24},{16,0},{24,8},{1,17},{9,25},{17,1},{25,9},{2,18},{10... | collective-permute-start | bytes 589832 | tf_op jit(solution)/shard_map/ppermute | solution.py:298
  10.5 15.4 %collective-permute-start.8 = (bf16[24,32,128]{2,1,0:T(8,128)(2,1)S(1)}, bf16[24,32,128]{2,1,0:T(8,128)(2,1)S(1)}, u32[]{:S(2)}, u32[]{:S(2)}) collective-permute-start(bf16[24,32,128]{2,1,0:T(8,128)(2,1)S(1)} %get-tuple-element.86), channel_id=1, source_target_pairs={{0,24},{8,16},{16,8},{24,0},{1,25},{9,17},{17,9},{25,1},{2,26},{10... | collective-permute-start | bytes 589832 | tf_op jit(solution)/shard_map/ppermute | solution.py:298
  17.2 10.2 %collective-permute-start.3 = (bf16[8,32,128]{2,1,0:T(8,128)(2,1)S(1)}, bf16[8,32,128]{2,1,0:T(8,128)(2,1)S(1)}, u32[]{:S(2)}, u32[]{:S(2)}) collective-permute-start(bf16[8,32,128]{2,1,0:T(8,128)(2,1)S(1)} %get-tuple-element.80), channel_id=1, source_target_pairs={{0,8},{8,0},{16,24},{24,16},{1,9},{9,1},{17,25},{25,17},{2,10},{10... | collective-permute-start | bytes 196616 | tf_op jit(solution)/shard_map/ppermute | solution.py:298
  18.6 8.8 %collective-permute-start.4 = (bf16[8,32,128]{2,1,0:T(8,128)(2,1)S(1)}, bf16[8,32,128]{2,1,0:T(8,128)(2,1)S(1)}, u32[]{:S(2)}, u32[]{:S(2)}) collective-permute-start(bf16[8,32,128]{2,1,0:T(8,128)(2,1)S(1)} %get-tuple-element.81), channel_id=1, source_target_pairs={{0,16},{8,24},{16,0},{24,8},{1,17},{9,25},{17,1},{25,9},{2,18},{10... | collective-permute-start | bytes 196616 | tf_op jit(solution)/shard_map/ppermute | solution.py:298
  20.4 7.0 %collective-permute-start.5 = (bf16[8,32,128]{2,1,0:T(8,128)(2,1)S(1)}, bf16[8,32,128]{2,1,0:T(8,128)(2,1)S(1)}, u32[]{:S(2)}, u32[]{:S(2)}) collective-permute-start(bf16[8,32,128]{2,1,0:T(8,128)(2,1)S(1)} %get-tuple-element.82), channel_id=1, source_target_pairs={{0,24},{8,16},{16,8},{24,0},{1,25},{9,17},{17,9},{25,1},{2,26},{10... | collective-permute-start | bytes 196616 | tf_op jit(solution)/shard_map/ppermute | solution.py:298
  28.0 6.4 %collective-permute-start.9 = (bf16[16,32,128]{2,1,0:T(8,128)(2,1)S(1)}, bf16[16,32,128]{2,1,0:T(8,128)(2,1)S(1)}, u32[]{:S(2)}, u32[]{:S(2)}) collective-permute-start(bf16[16,32,128]{2,1,0:T(8,128)(2,1)S(1)} %get-tuple-element.88), channel_id=1, source_target_pairs={{0,8},{8,0},{16,24},{24,16},{1,9},{9,1},{17,25},{25,17},{2,10},{10... | collective-permute-start | bytes 393224 | tf_op jit(solution)/shard_map/ppermute | solution.py:298
  29.4 9.3 %collective-permute-start.10 = (bf16[16,32,128]{2,1,0:T(8,128)(2,1)S(1)}, bf16[16,32,128]{2,1,0:T(8,128)(2,1)S(1)}, u32[]{:S(2)}, u32[]{:S(2)}) collective-permute-start(bf16[16,32,128]{2,1,0:T(8,128)(2,1)S(1)} %get-tuple-element.89), channel_id=1, source_target_pairs={{0,16},{8,24},{16,0},{24,8},{1,17},{9,25},{17,1},{25,9},{2,18},{10... | collective-permute-start | bytes 393224 | tf_op jit(solution)/shard_map/ppermute | solution.py:298
  30.4 8.3 %collective-permute-start.11 = (bf16[16,32,128]{2,1,0:T(8,128)(2,1)S(1)}, bf16[16,32,128]{2,1,0:T(8,128)(2,1)S(1)}, u32[]{:S(2)}, u32[]{:S(2)}) collective-permute-start(bf16[16,32,128]{2,1,0:T(8,128)(2,1)S(1)} %get-tuple-element.90), channel_id=1, source_target_pairs={{0,24},{8,16},{16,8},{24,0},{1,25},{9,17},{17,9},{25,1},{2,26},{10... | collective-permute-start | bytes 393224 | tf_op jit(solution)/shard_map/ppermute | solution.py:298
  31.8 9.5 %collective-permute-start.17 = (bf16[16,32,128]{2,1,0:T(8,128)(2,1)S(1)}, bf16[16,32,128]{2,1,0:T(8,128)(2,1)S(1)}, u32[]{:S(2)}, u32[]{:S(2)}) collective-permute-start(bf16[16,32,128]{2,1,0:T(8,128)(2,1)S(1)} %get-tuple-element.96), channel_id=1, source_target_pairs={{0,8},{8,0},{16,24},{24,16},{1,9},{9,1},{17,25},{25,17},{2,10},{10... | collective-permute-start | bytes 393224 | tf_op jit(solution)/shard_map/ppermute | solution.py:298
  32.9 8.7 %collective-permute-start.18 = (bf16[16,32,128]{2,1,0:T(8,128)(2,1)S(1)}, bf16[16,32,128]{2,1,0:T(8,128)(2,1)S(1)}, u32[]{:S(2)}, u32[]{:S(2)}) collective-permute-start(bf16[16,32,128]{2,1,0:T(8,128)(2,1)S(1)} %get-tuple-element.97), channel_id=1, source_target_pairs={{0,16},{8,24},{16,0},{24,8},{1,17},{9,25},{17,1},{25,9},{2,18},{10... | collective-permute-start | bytes 393224 | tf_op jit(solution)/shard_map/ppermute | solution.py:298
  34.5 7.2 %collective-permute-start.19 = (bf16[16,32,128]{2,1,0:T(8,128)(2,1)S(1)}, bf16[16,32,128]{2,1,0:T(8,128)(2,1)S(1)}, u32[]{:S(2)}, u32[]{:S(2)}) collective-permute-start(bf16[16,32,128]{2,1,0:T(8,128)(2,1)S(1)} %get-tuple-element.98), channel_id=1, source_target_pairs={{0,24},{8,16},{16,8},{24,0},{1,25},{9,17},{17,9},{25,1},{2,26},{10... | collective-permute-start | bytes 393224 | tf_op jit(solution)/shard_map/ppermute | solution.py:298
  38.8 5.8 %collective-permute-start.12 = (bf16[16,128,128]{2,1,0:T(8,128)(2,1)S(1)}, bf16[16,128,128]{2,1,0:T(8,128)(2,1)S(1)}, u32[]{:S(2)}, u32[]{:S(2)}) collective-permute-start(bf16[16,128,128]{2,1,0:T(8,128)(2,1)S(1)} %shard_map.88.own), channel_id=1, source_target_pairs={{0,1},{1,0},{2,3},{3,2},{4,5},{5,4},{6,7},{7,6},{8,9},{9,8},{10,11... | collective-permute-start | bytes 1572872 | tf_op jit(solution)/shard_map/ppermute | solution.py:425
  38.8 10.5 %collective-permute-start.13 = (bf16[16,128,128]{2,1,0:T(8,128)(2,1)S(1)}, bf16[16,128,128]{2,1,0:T(8,128)(2,1)S(1)}, u32[]{:S(2)}, u32[]{:S(2)}) collective-permute-start(bf16[16,128,128]{2,1,0:T(8,128)(2,1)S(1)} %shard_map.88.own), channel_id=1, source_target_pairs={{1,2},{2,1},{3,4},{4,3},{5,6},{6,5},{9,10},{10,9},{11,12},{12,11},... | collective-permute-start | bytes 1572872 | tf_op jit(solution)/shard_map/ppermute | solution.py:424
  41.7 12.0 %collective-permute-start.20 = (bf16[16,128,128]{2,1,0:T(8,128)(2,1)S(1)}, bf16[16,128,128]{2,1,0:T(8,128)(2,1)S(1)}, u32[]{:S(2)}, u32[]{:S(2)}) collective-permute-start(bf16[16,128,128]{2,1,0:T(8,128)(2,1)S(1)} %shard_map.91.own), channel_id=1, source_target_pairs={{0,1},{1,0},{2,3},{3,2},{4,5},{5,4},{6,7},{7,6},{8,9},{9,8},{10,11... | collective-permute-start | bytes 1572872 | tf_op jit(solution)/shard_map/ppermute | solution.py:425
  42.6 12.4 %collective-permute-start.21 = (bf16[16,128,128]{2,1,0:T(8,128)(2,1)S(1)}, bf16[16,128,128]{2,1,0:T(8,128)(2,1)S(1)}, u32[]{:S(2)}, u32[]{:S(2)}) collective-permute-start(bf16[16,128,128]{2,1,0:T(8,128)(2,1)S(1)} %shard_map.91.own), channel_id=1, source_target_pairs={{1,2},{2,1},{3,4},{4,3},{5,6},{6,5},{9,10},{10,9},{11,12},{12,11},... | collective-permute-start | bytes 1572872 | tf_op jit(solution)/shard_map/ppermute | solution.py:424
  50.1 7.2 %collective-permute-start.14 = (bf16[32,16,128]{2,1,0:T(8,128)(2,1)S(1)}, bf16[32,16,128]{2,1,0:T(8,128)(2,1)S(1)}, u32[]{:S(2)}, u32[]{:S(2)}) collective-permute-start(bf16[32,16,128]{2,1,0:T(8,128)(2,1)S(1)} %get-tuple-element.92), channel_id=1, source_target_pairs={{0,8},{8,0},{16,24},{24,16},{1,9},{9,1},{17,25},{25,17},{2,10},{10... | collective-permute-start | bytes 393224 | tf_op jit(solution)/shard_map/ppermute | solution.py:298
  51.3 8.7 %collective-permute-start.15 = (bf16[32,16,128]{2,1,0:T(8,128)(2,1)S(1)}, bf16[32,16,128]{2,1,0:T(8,128)(2,1)S(1)}, u32[]{:S(2)}, u32[]{:S(2)}) collective-permute-start(bf16[32,16,128]{2,1,0:T(8,128)(2,1)S(1)} %get-tuple-element.93), channel_id=1, source_target_pairs={{0,16},{8,24},{16,0},{24,8},{1,17},{9,25},{17,1},{25,9},{2,18},{10... | collective-permute-start | bytes 393224 | tf_op jit(solution)/shard_map/ppermute | solution.py:298
  51.7 8.3 %collective-permute-start.16 = (bf16[32,16,128]{2,1,0:T(8,128)(2,1)S(1)}, bf16[32,16,128]{2,1,0:T(8,128)(2,1)S(1)}, u32[]{:S(2)}, u32[]{:S(2)}) collective-permute-start(bf16[32,16,128]{2,1,0:T(8,128)(2,1)S(1)} %get-tuple-element.94), channel_id=1, source_target_pairs={{0,24},{8,16},{16,8},{24,0},{1,25},{9,17},{17,9},{25,1},{2,26},{10... | collective-permute-start | bytes 393224 | tf_op jit(solution)/shard_map/ppermute | solution.py:298
  55.7 6.4 %collective-permute-start.22 = (bf16[32,16,128]{2,1,0:T(8,128)(2,1)S(1)}, bf16[32,16,128]{2,1,0:T(8,128)(2,1)S(1)}, u32[]{:S(2)}, u32[]{:S(2)}) collective-permute-start(bf16[32,16,128]{2,1,0:T(8,128)(2,1)S(1)} %get-tuple-element.100), channel_id=1, source_target_pairs={{0,8},{8,0},{16,24},{24,16},{1,9},{9,1},{17,25},{25,17},{2,10},{10... | collective-permute-start | bytes 393224 | tf_op jit(solution)/shard_map/ppermute | solution.py:298
  56.9 8.7 %collective-permute-start.23 = (bf16[32,16,128]{2,1,0:T(8,128)(2,1)S(1)}, bf16[32,16,128]{2,1,0:T(8,128)(2,1)S(1)}, u32[]{:S(2)}, u32[]{:S(2)}) collective-permute-start(bf16[32,16,128]{2,1,0:T(8,128)(2,1)S(1)} %get-tuple-element.101), channel_id=1, source_target_pairs={{0,16},{8,24},{16,0},{24,8},{1,17},{9,25},{17,1},{25,9},{2,18},{10... | collective-permute-start | bytes 393224 | tf_op jit(solution)/shard_map/ppermute | solution.py:298
  57.3 8.3 %collective-permute-start.24 = (bf16[32,16,128]{2,1,0:T(8,128)(2,1)S(1)}, bf16[32,16,128]{2,1,0:T(8,128)(2,1)S(1)}, u32[]{:S(2)}, u32[]{:S(2)}) collective-permute-start(bf16[32,16,128]{2,1,0:T(8,128)(2,1)S(1)} %get-tuple-element.102), channel_id=1, source_target_pairs={{0,24},{8,16},{16,8},{24,0},{1,25},{9,17},{17,9},{25,1},{2,26},{10... | collective-permute-start | bytes 393224 | tf_op jit(solution)/shard_map/ppermute | solution.py:298
  66.9 7.9 %collective-permute-start.28 = (bf16[24,32,128]{2,1,0:T(8,128)(2,1)S(1)}, bf16[24,32,128]{2,1,0:T(8,128)(2,1)S(1)}, u32[]{:S(2)}, u32[]{:S(2)}) collective-permute-start(bf16[24,32,128]{2,1,0:T(8,128)(2,1)S(1)} %get-tuple-element.108), channel_id=1, source_target_pairs={{0,8},{8,0},{16,24},{24,16},{1,9},{9,1},{17,25},{25,17},{2,10},{10... | collective-permute-start | bytes 589832 | tf_op jit(solution)/shard_map/ppermute | solution.py:298
  67.9 11.8 %collective-permute-start.29 = (bf16[24,32,128]{2,1,0:T(8,128)(2,1)S(1)}, bf16[24,32,128]{2,1,0:T(8,128)(2,1)S(1)}, u32[]{:S(2)}, u32[]{:S(2)}) collective-permute-start(bf16[24,32,128]{2,1,0:T(8,128)(2,1)S(1)} %get-tuple-element.109), channel_id=1, source_target_pairs={{0,16},{8,24},{16,0},{24,8},{1,17},{9,25},{17,1},{25,9},{2,18},{10... | collective-permute-start | bytes 589832 | tf_op jit(solution)/shard_map/ppermute | solution.py:298
  68.7 11.0 %collective-permute-start.30 = (bf16[24,32,128]{2,1,0:T(8,128)(2,1)S(1)}, bf16[24,32,128]{2,1,0:T(8,128)(2,1)S(1)}, u32[]{:S(2)}, u32[]{:S(2)}) collective-permute-start(bf16[24,32,128]{2,1,0:T(8,128)(2,1)S(1)} %get-tuple-element.110), channel_id=1, source_target_pairs={{0,24},{8,16},{16,8},{24,0},{1,25},{9,17},{17,9},{25,1},{2,26},{10... | collective-permute-start | bytes 589832 | tf_op jit(solution)/shard_map/ppermute | solution.py:298
  71.0 10.0 %collective-permute-start.25 = (bf16[8,32,128]{2,1,0:T(8,128)(2,1)S(1)}, bf16[8,32,128]{2,1,0:T(8,128)(2,1)S(1)}, u32[]{:S(2)}, u32[]{:S(2)}) collective-permute-start(bf16[8,32,128]{2,1,0:T(8,128)(2,1)S(1)} %get-tuple-element.104), channel_id=1, source_target_pairs={{0,8},{8,0},{16,24},{24,16},{1,9},{9,1},{17,25},{25,17},{2,10},{10... | collective-permute-start | bytes 196616 | tf_op jit(solution)/shard_map/ppermute | solution.py:298
  72.0 9.2 %collective-permute-start.26 = (bf16[8,32,128]{2,1,0:T(8,128)(2,1)S(1)}, bf16[8,32,128]{2,1,0:T(8,128)(2,1)S(1)}, u32[]{:S(2)}, u32[]{:S(2)}) collective-permute-start(bf16[8,32,128]{2,1,0:T(8,128)(2,1)S(1)} %get-tuple-element.105), channel_id=1, source_target_pairs={{0,16},{8,24},{16,0},{24,8},{1,17},{9,25},{17,1},{25,9},{2,18},{10... | collective-permute-start | bytes 196616 | tf_op jit(solution)/shard_map/ppermute | solution.py:298
  74.8 6.4 %collective-permute-start.27 = (bf16[8,32,128]{2,1,0:T(8,128)(2,1)S(1)}, bf16[8,32,128]{2,1,0:T(8,128)(2,1)S(1)}, u32[]{:S(2)}, u32[]{:S(2)}) collective-permute-start(bf16[8,32,128]{2,1,0:T(8,128)(2,1)S(1)} %get-tuple-element.106), channel_id=1, source_target_pairs={{0,24},{8,16},{16,8},{24,0},{1,25},{9,17},{17,9},{25,1},{2,26},{10... | collective-permute-start | bytes 196616 | tf_op jit(solution)/shard_map/ppermute | solution.py:298

commit v4 on v3

--- a/solution.py
+++ b/solution.py
@@ -142,23 +142,21 @@
             scratch[pl.ds(i + h, total, stride=count), :] = pol[
                 :, h * orbitals : (h + 1) * orbitals
             ]
-    if len(outs) == 1:
-        outs[0][...] = scratch[...].astype(BF16).reshape(total, count, orbitals)
-        return
     lags = e_dev // halves
-    for h in range(halves):
-        for d in range(groups):
+
+    def part(d, h):
+        start = (d * halves + h) * lags * count
+        return scratch[start : start + lags * count, :].astype(BF16).reshape(lags, count, orbitals)
+
+    for d in range(groups):
+        outs[d][...] = part(d, 0)
+        for h in range(1, halves):
             out = outs[h * groups + d]
-            start = d * e_dev + h * lags
             at = 0
-            for ref in before:
-                out[:, at : at + ref.shape[1], :] = ref[start : start + lags]
+            for ref in before[(h - 1) * groups + d :: (halves - 1) * groups]:
+                out[:, at : at + ref.shape[1], :] = ref[...]
                 at += ref.shape[1]
-            out[:, first:, :] = (
-                scratch[start * count : (start + lags) * count, :]
-                .astype(BF16)
-                .reshape(lags, count, orbitals)
-            )
+            out[:, at:, :] = part(d, h)
 
 
 def sigma_kernel(groups, first, offsets, fwd_l_ref, back_ref, less_ref, *refs):
@@ -358,7 +356,7 @@
         out_specs=[vmem()] * (len(stacks) + 4),
         scratch=[pltpu.VMEM((3, *square), F32), pltpu.SemaphoreType.DMA((len(stacks),))],
     )
-    counts = [3 * rows // 4, rows // 4] if rows % 32 == 0 else [rows]
+    counts = [rows // 2, rows // 2] if rows % 32 == 0 else [rows]
     parts = call(
         functools.partial(turn_kernel, groups, counts),
         [shape(count, e_dev, orbitals) for count in counts for _ in range(groups)],
@@ -373,10 +371,7 @@
         ],
     )
     great = [exchange(parts[:groups])]
-    if len(counts) > 1:
-        held = lax.optimization_barrier((*parts[groups:], *less, fwd_e))
-        great.append(exchange(held[:groups]))
-        less, fwd_e = held[groups:-1], held[-1]
+    rest = parts[groups:]
     less = call(
         spectrum_kernel,
         shape(rows // WIDE, fwd_e.shape[0], WIDE * orbitals, dtype=F32),
@@ -386,34 +381,37 @@
         out_specs=vmem(),
         scratch=[pltpu.VMEM((total * rows, orbitals), F32)],
     )
-    pol = []
+    if len(counts) > 1:
+        *rest, less = lax.optimization_barrier((*rest, less))
+        great.append(exchange(rest))
+    pol = [[] for _ in range(halves)]
+    later = []
     for c, count in enumerate(counts):
-        last = c == len(counts) - 1
-        outs = (
-            [shape(lags, rows, orbitals)] * (halves * groups)
-            if last
-            else [shape(total, count, orbitals)]
-        )
-        pol += call(
-            functools.partial(pol_kernel, groups, halves, sum(counts[:c]), c),
-            outs,
-            [vmem()] * (3 + groups + c),
+        width = rows if c == len(counts) - 1 else count
+        parts = call(
+            functools.partial(pol_kernel, groups, halves, sum(counts[:c]), len(later)),
+            [shape(lags, count, orbitals)] * groups
+            + [shape(lags, width, orbitals)] * ((halves - 1) * groups),
+            [vmem()] * (3 + groups + len(later)),
             fwd_e,
             back_l,
             less,
             *great[c],
-            *pol,
-            out_specs=[vmem()] * len(outs),
+            *later,
+            out_specs=[vmem()] * (halves * groups),
             scratch=[pltpu.VMEM((total * count, orbitals), F32)],
         )
-    pol = pol[len(counts) - 1 :]
-    pol = [exchange(pol[h * groups : (h + 1) * groups]) for h in range(halves)]
+        pol[0].append(exchange(parts[:groups]))
+        later += parts[groups:]
+    for h in range(1, halves):
+        last = len(later) - (halves - h) * groups
+        pol[h].append(exchange(later[last : last + groups]))
 
     near_pairs = [(b, b ^ 1) for b in range(peers) if b ^ 1 < peers]
     far_pairs = [(b, ((b + 1) ^ 1) - 1) for b in range(1, peers) if ((b + 1) ^ 1) - 1 < peers]
     inter = []
     for h in range(halves):
-        parts = pol[h]
+        parts = [chunk[d] for d in range(groups) for chunk in pol[h]]
         own = call(
             assemble_kernel,
             shape(lags, orbitals, orbitals),
@@ -450,6 +448,7 @@
             [exchange(parts[c * groups : (c + 1) * groups]) for c in range(len(cut))]
         )
 
+    counts = [3 * rows // 4, rows // 4] if rows % 32 == 0 else [rows]
     sigma = []
     for c, count in enumerate(counts):
         first = sum(counts[:c])

time: 82.2 us -> 80.9 us (0.984)
  waiting for transfers between devices: 25.5 us -> 19.9 us
  starting transfers between devices: 40 us -> 44 us
    ppermute x27 -> x30, waiting for transfers between devices: 21.2 us -> 16.6 us  [exchange(): lax.ppermute(parts[d], 'energy', [(i, i ^ d) for i in range(groups)])]
    ppermute x27 -> x30, starting transfers between devices: 34.6 us -> 38.7 us  [exchange(): lax.ppermute(parts[d], 'energy', [(i, i ^ d) for i in range(groups)])]
    ppermute x2, waiting for transfers between devices: 4.39 us -> 3.3 us  [shards(): far = lax.ppermute(own, 'block', far_pairs)]
    ppermute x2, starting transfers between devices: 0.98 us -> 0.14 us  [shards(): near = lax.ppermute(own, 'block', near_pairs)]
  transfers between devices with their start and end apart: 31 -> 34, of which waited for: 17 -> 15; matrix products, arithmetic and copies ran while one was open for 0% -> 0% of each run, Pallas kernels for 15% -> 16%
where the time goes in v4:
time: 80.9 us; the launch traced here: 80.7 us
  starting transfers between devices  44 us (54%)
  waiting for transfers between devices  19.9 us (25%)
  Pallas kernels  16.4 us (20%)
    ppermute x30, starting transfers between devices, exchange(): lax.ppermute(parts[d], 'energy', [(i, i ^ d) for i in range(groups)])  38.7 us
    ppermute x30, waiting for transfers between devices, exchange(): lax.ppermute(parts[d], 'energy', [(i, i ^ d) for i in range(groups)])  16.6 us
    pallas_call x16, Pallas kernels, call(): pl.pallas_call(kernel, out_shape=out_shape, in_specs=specs, scratch_shape...  16.4 us
    ppermute x2, starting transfers between devices, shards(): far = lax.ppermute(own, 'block', far_pairs)  5.08 us
    ppermute x2, waiting for transfers between devices, shards(): far = lax.ppermute(own, 'block', far_pairs)  3.3 us
  transfers between devices with their start and end apart: 34, of which 15 were waited for; matrix products, arithmetic and copies ran while one was open for 0% of the time, Pallas kernels for 16%

profile of v4, /device:TPU:16, one launch (start us, length us, event | category | flops | bytes accessed | tf_op | source)
XLA Modules:
  0.0 80.7 jit_solution(17972368978961828090)
XLA Ops:
  0.0 1.3 %shard_map.84 = (bf16[32,32,128]{2,1,0:T(8,128)(2,1)S(1)}, bf16[32,32,128]{2,1,0:T(8,128)(2,1)S(1)}, bf16[32,32,128]{2,1,0:T(8,128)(2,1)S(1)}, bf16[32,32,128]{2,1,0:T(8,128)(2,1)S(1)}) custom-call(s32[1]{0:T(128)} %bitcast.me_ref, bf16[32,128,128]{2,1,0:T(8,128)(2,1)} %bitcast.11), custom_call_target="tpu_custom_call" | custom-call | tf_op jit(solution)/shard_map/pallas_call | solution.py:301
  1.3 1.6 %collective-permute-start = (bf16[32,32,128]{2,1,0:T(8,128)(2,1)S(1)}, bf16[32,32,128]{2,1,0:T(8,128)(2,1)S(1)}, u32[]{:S(2)}, u32[]{:S(2)}) collective-permute-start(bf16[32,32,128]{2,1,0:T(8,128)(2,1)S(1)} %get-tuple-element.70), channel_id=1, source_target_pairs={{0,8},{8,0},{16,24},{24,16},{1,9},{9,1},{17,25},{25,17},{2,10},{10... | collective-permute-start | bytes 786440 | tf_op jit(solution)/shard_map/ppermute | solution.py:296
  2.8 1.5 %collective-permute-start.1 = (bf16[32,32,128]{2,1,0:T(8,128)(2,1)S(1)}, bf16[32,32,128]{2,1,0:T(8,128)(2,1)S(1)}, u32[]{:S(2)}, u32[]{:S(2)}) collective-permute-start(bf16[32,32,128]{2,1,0:T(8,128)(2,1)S(1)} %get-tuple-element.71), channel_id=1, source_target_pairs={{0,16},{8,24},{16,0},{24,8},{1,17},{9,25},{17,1},{25,9},{2,18},{10... | collective-permute-start | bytes 786440 | tf_op jit(solution)/shard_map/ppermute | solution.py:296
  4.8 2.5 %shard_map.83 = (bf16[16,32,128]{2,1,0:T(8,128)(2,1)S(1)}, bf16[16,32,128]{2,1,0:T(8,128)(2,1)S(1)}, bf16[16,32,128]{2,1,0:T(8,128)(2,1)S(1)}, bf16[16,32,128]{2...) custom-call(s32[1]{0:T(128)} %bitcast.me_ref, ...), custom_call_target="tpu_custom_call" | custom-call | tf_op jit(solution)/shard_map/pallas_call | solution.py:301
  7.3 1.6 %collective-permute-start.3 = (bf16[16,32,128]{2,1,0:T(8,128)(2,1)S(1)}, bf16[16,32,128]{2,1,0:T(8,128)(2,1)S(1)}, u32[]{:S(2)}, u32[]{:S(2)}) collective-permute-start(bf16[16,32,128]{2,1,0:T(8,128)(2,1)S(1)} %get-tuple-element.80), channel_id=1, source_target_pairs={{0,8},{8,0},{16,24},{24,16},{1,9},{9,1},{17,25},{25,17},{2,10},{10... | collective-permute-start | bytes 393224 | tf_op jit(solution)/shard_map/ppermute | solution.py:296
  8.8 1.5 %collective-permute-start.4 = (bf16[16,32,128]{2,1,0:T(8,128)(2,1)S(1)}, bf16[16,32,128]{2,1,0:T(8,128)(2,1)S(1)}, u32[]{:S(2)}, u32[]{:S(2)}) collective-permute-start(bf16[16,32,128]{2,1,0:T(8,128)(2,1)S(1)} %get-tuple-element.81), channel_id=1, source_target_pairs={{0,16},{8,24},{16,0},{24,8},{1,17},{9,25},{17,1},{25,9},{2,18},{10... | collective-permute-start | bytes 393224 | tf_op jit(solution)/shard_map/ppermute | solution.py:296
  10.5 2.4 %collective-permute-start.5 = (bf16[16,32,128]{2,1,0:T(8,128)(2,1)S(1)}, bf16[16,32,128]{2,1,0:T(8,128)(2,1)S(1)}, u32[]{:S(2)}, u32[]{:S(2)}) collective-permute-start(bf16[16,32,128]{2,1,0:T(8,128)(2,1)S(1)} %get-tuple-element.82), channel_id=1, source_target_pairs={{0,24},{8,16},{16,8},{24,0},{1,25},{9,17},{17,9},{25,1},{2,26},{10... | collective-permute-start | bytes 393224 | tf_op jit(solution)/shard_map/ppermute | solution.py:296
  13.0 1.7 %shard_map.82 = (bf16[192,256]{1,0:T(8,128)(2,1)S(1)}, bf16[192,256]{1,0:T(8,128)(2,1)S(1)}, bf16[256,192]{1,0:T(8,128)(2,1)S(1)}, bf16[256,192]{1,0:T(8,128)(2,...) custom-call(s32[1]{0:T(128)} %bitcast.me_ref, ...), custom_call_target="tpu_custom_call" | custom-call | tf_op jit(solution)/shard_map/pallas_call | solution.py:301
  14.7 2.3 %collective-permute-done.1.refs_2_ = bf16[32,32,128]{2,1,0:T(8,128)(2,1)S(1)} collective-permute-done((bf16[32,32,128]{2,1,0:T(8,128)(2,1)S(1)}, bf16[32,32,128]{2,1,0:T(8,128)(2,1)S(1)}, u32[]{:S(2)}, u32[]{:S(2)}) %collective-permute-start.1) | collective-permute-done | bytes 262176 | tf_op jit(solution)/shard_map/ppermute | solution.py:296
  17.2 1.7 %shard_map.85.less_ref = f32[4,192,1024]{2,1,0:T(8,128)S(1)} custom-call(bf16[192,256]{1,0:T(8,128)(2,1)S(1)} %get-tuple-element.68.fwd_ref, bf16[32,32,128]{2,1,0:T(8,128)(2,1)S(1)} %get-tuple-element.69.refs_0_, bf16[32,32,128]{2,1,0:T(8,128)(2,1)S(1)} %collective-permute-done.refs_1_, bf16[32,32,128]{2,1,0:T(8,128)(2,1)S(1)} %collective-permute-done.1.refs_2_, ...), custom_call_target="tpu_custom_call" | custom-call | tf_op jit(solution)/shard_map/pallas_call | solution.py:301
  18.9 1.6 %collective-permute-start.6 = (bf16[16,32,128]{2,1,0:T(8,128)(2,1)S(1)}, bf16[16,32,128]{2,1,0:T(8,128)(2,1)S(1)}, u32[]{:S(2)}, u32[]{:S(2)}) collective-permute-start(bf16[16,32,128]{2,1,0:T(8,128)(2,1)S(1)} %get-tuple-element.85), channel_id=1, source_target_pairs={{0,8},{8,0},{16,24},{24,16},{1,9},{9,1},{17,25},{25,17},{2,10},{10... | collective-permute-start | bytes 393224 | tf_op jit(solution)/shard_map/ppermute | solution.py:296
  20.4 1.5 %collective-permute-start.7 = (bf16[16,32,128]{2,1,0:T(8,128)(2,1)S(1)}, bf16[16,32,128]{2,1,0:T(8,128)(2,1)S(1)}, u32[]{:S(2)}, u32[]{:S(2)}) collective-permute-start(bf16[16,32,128]{2,1,0:T(8,128)(2,1)S(1)} %get-tuple-element.86), channel_id=1, source_target_pairs={{0,16},{8,24},{16,0},{24,8},{1,17},{9,25},{17,1},{25,9},{2,18},{10... | collective-permute-start | bytes 393224 | tf_op jit(solution)/shard_map/ppermute | solution.py:296
  21.9 1.4 %collective-permute-start.8 = (bf16[16,32,128]{2,1,0:T(8,128)(2,1)S(1)}, bf16[16,32,128]{2,1,0:T(8,128)(2,1)S(1)}, u32[]{:S(2)}, u32[]{:S(2)}) collective-permute-start(bf16[16,32,128]{2,1,0:T(8,128)(2,1)S(1)} %get-tuple-element.87), channel_id=1, source_target_pairs={{0,24},{8,16},{16,8},{24,0},{1,25},{9,17},{17,9},{25,1},{2,26},{10... | collective-permute-start | bytes 393224 | tf_op jit(solution)/shard_map/ppermute | solution.py:296
  23.3 1.0 %shard_map.86 = (bf16[16,16,128]{2,1,0:T(8,128)(2,1)S(1)}, bf16[16,16,128]{2,1,0:T(8,128)(2,1)S(1)}, bf16[16,16,128]{2,1,0:T(8,128)(2,1)S(1)}, bf16[16,16,128]{2...) custom-call(bf16[192,256]{1,0:T(8,128)(2,1)S(1)} %get-tuple-element., ...), custom_call_target="tpu_custom_call" | custom-call | tf_op jit(solution)/shard_map/pallas_call | solution.py:301
  24.4 1.0 %collective-permute-start.9 = (bf16[16,16,128]{2,1,0:T(8,128)(2,1)S(1)}, bf16[16,16,128]{2,1,0:T(8,128)(2,1)S(1)}, u32[]{:S(2)}, u32[]{:S(2)}) collective-permute-start(bf16[16,16,128]{2,1,0:T(8,128)(2,1)S(1)} %get-tuple-element.93), channel_id=1, source_target_pairs={{0,8},{8,0},{16,24},{24,16},{1,9},{9,1},{17,25},{25,17},{2,10},{10... | collective-permute-start | bytes 196616 | tf_op jit(solution)/shard_map/ppermute | solution.py:296
  25.4 1.6 %collective-permute-start.11 = (bf16[16,16,128]{2,1,0:T(8,128)(2,1)S(1)}, bf16[16,16,128]{2,1,0:T(8,128)(2,1)S(1)}, u32[]{:S(2)}, u32[]{:S(2)}) collective-permute-start(bf16[16,16,128]{2,1,0:T(8,128)(2,1)S(1)} %get-tuple-element.95), channel_id=1, source_target_pairs={{0,16},{8,24},{16,0},{24,8},{1,17},{9,25},{17,1},{25,9},{2,18},{10... | collective-permute-start | bytes 196616 | tf_op jit(solution)/shard_map/ppermute | solution.py:296
  27.0 1.4 %collective-permute-start.13 = (bf16[16,16,128]{2,1,0:T(8,128)(2,1)S(1)}, bf16[16,16,128]{2,1,0:T(8,128)(2,1)S(1)}, u32[]{:S(2)}, u32[]{:S(2)}) collective-permute-start(bf16[16,16,128]{2,1,0:T(8,128)(2,1)S(1)} %get-tuple-element.97), channel_id=1, source_target_pairs={{0,24},{8,16},{16,8},{24,0},{1,25},{9,17},{17,9},{25,1},{2,26},{10... | collective-permute-start | bytes 196616 | tf_op jit(solution)/shard_map/ppermute | solution.py:296
  28.7 1.1 %shard_map.87 = (bf16[16,16,128]{2,1,0:T(8,128)(2,1)S(1)}, bf16[16,16,128]{2,1,0:T(8,128)(2,1)S(1)}, bf16[16,16,128]{2,1,0:T(8,128)(2,1)S(1)}, bf16[16,16,128]{2...) custom-call(bf16[192,256]{1,0:T(8,128)(2,1)S(1)} %get-tuple-element., ...), custom_call_target="tpu_custom_call" | custom-call | tf_op jit(solution)/shard_map/pallas_call | solution.py:301
  29.8 1.7 %collective-permute-start.10 = (bf16[16,16,128]{2,1,0:T(8,128)(2,1)S(1)}, bf16[16,16,128]{2,1,0:T(8,128)(2,1)S(1)}, u32[]{:S(2)}, u32[]{:S(2)}) collective-permute-start(bf16[16,16,128]{2,1,0:T(8,128)(2,1)S(1)} %get-tuple-element.94), channel_id=1, source_target_pairs={{0,8},{8,0},{16,24},{24,16},{1,9},{9,1},{17,25},{25,17},{2,10},{10... | collective-permute-start | bytes 196616 | tf_op jit(solution)/shard_map/ppermute | solution.py:296
  32.3 1.1 %collective-permute-start.14 = (bf16[16,16,128]{2,1,0:T(8,128)(2,1)S(1)}, bf16[16,16,128]{2,1,0:T(8,128)(2,1)S(1)}, u32[]{:S(2)}, u32[]{:S(2)}) collective-permute-start(bf16[16,16,128]{2,1,0:T(8,128)(2,1)S(1)} %get-tuple-element.98), channel_id=1, source_target_pairs={{0,24},{8,16},{16,8},{24,0},{1,25},{9,17},{17,9},{25,1},{2,26},{10... | collective-permute-start | bytes 196616 | tf_op jit(solution)/shard_map/ppermute | solution.py:296
  33.4 1.7 %collective-permute-start.20 = (bf16[16,32,128]{2,1,0:T(8,128)(2,1)S(1)}, bf16[16,32,128]{2,1,0:T(8,128)(2,1)S(1)}, u32[]{:S(2)}, u32[]{:S(2)}) collective-permute-start(bf16[16,32,128]{2,1,0:T(8,128)(2,1)S(1)} %get-tuple-element.104), channel_id=1, source_target_pairs={{0,8},{8,0},{16,24},{24,16},{1,9},{9,1},{17,25},{25,17},{2,10},{10... | collective-permute-start | bytes 393224 | tf_op jit(solution)/shard_map/ppermute | solution.py:296
  35.8 1.1 %collective-permute-start.22 = (bf16[16,32,128]{2,1,0:T(8,128)(2,1)S(1)}, bf16[16,32,128]{2,1,0:T(8,128)(2,1)S(1)}, u32[]{:S(2)}, u32[]{:S(2)}) collective-permute-start(bf16[16,32,128]{2,1,0:T(8,128)(2,1)S(1)} %get-tuple-element.106), channel_id=1, source_target_pairs={{0,24},{8,16},{16,8},{24,0},{1,25},{9,17},{17,9},{25,1},{2,26},{10... | collective-permute-start | bytes 393224 | tf_op jit(solution)/shard_map/ppermute | solution.py:296
  37.6 2.4 %collective-permute-start.16 = (bf16[16,128,128]{2,1,0:T(8,128)(2,1)S(1)}, bf16[16,128,128]{2,1,0:T(8,128)(2,1)S(1)}, u32[]{:S(2)}, u32[]{:S(2)}) collective-permute-start(bf16[16,128,128]{2,1,0:T(8,128)(2,1)S(1)} %shard_map.88.own), channel_id=1, source_target_pairs={{1,2},{2,1},{3,4},{4,3},{5,6},{6,5},{9,10},{10,9},{11,12},{12,11},... | collective-permute-start | bytes 1572872 | tf_op jit(solution)/shard_map/ppermute | solution.py:422
  40.1 1.6 %collective-permute-done.22.refs_3_ = bf16[16,32,128]{2,1,0:T(8,128)(2,1)S(1)} collective-permute-done((bf16[16,32,128]{2,1,0:T(8,128)(2,1)S(1)}, bf16[16,32,128]{2,1,0:T(8,128)(2,1)S(1)}, u32[]{:S(2)}, u32[]{:S(2)}) %collective-permute-start.22) | collective-permute-done | bytes 131104 | tf_op jit(solution)/shard_map/ppermute | solution.py:296
  41.8 2.6 %collective-permute-start.24 = (bf16[16,128,128]{2,1,0:T(8,128)(2,1)S(1)}, bf16[16,128,128]{2,1,0:T(8,128)(2,1)S(1)}, u32[]{:S(2)}, u32[]{:S(2)}) collective-permute-start(bf16[16,128,128]{2,1,0:T(8,128)(2,1)S(1)} %shard_map.91.own), channel_id=1, source_target_pairs={{1,2},{2,1},{3,4},{4,3},{5,6},{6,5},{9,10},{10,9},{11,12},{12,11},... | collective-permute-start | bytes 1572872 | tf_op jit(solution)/shard_map/ppermute | solution.py:422
  44.4 0.8 %shard_map.89.partial = f32[16,128,128]{2,1,0:T(8,128)S(1)} custom-call(bf16[128,256]{1,0:T(8,128)(2,1)S(1)} %get-tuple-element.76.left, bf16[256,256]{1,0:T(8,128)(2,1)S(1)} %get-tuple-element.77.right, bf16[16,128,128]{2,1,0:T(8,128)(2,1)S(1)} %shard_map.88.own, bf16[16,128,128]{2,1,0:T(8,128)(2,1)S(1)} %collective-permute-done.15.near), custom_call_target="tpu_custom_call" | custom-call | tf_op jit(solution)/shard_map/pallas_call | solution.py:301
  45.2 2.8 %collective-permute-done.16.far = bf16[16,128,128]{2,1,0:T(8,128)(2,1)S(1)} collective-permute-done((bf16[16,128,128]{2,1,0:T(8,128)(2,1)S(1)}, bf16[16,128,128]{2,1,0:T(8,128)(2,1)S(1)}, u32[]{:S(2)}, u32[]{:S(2)}) %collective-permute-start.16) | collective-permute-done | bytes 524320 | tf_op jit(solution)/shard_map/ppermute | solution.py:422
  48.1 0.8 shard_map.90
  48.9 1.3 %collective-permute-start.17 = (bf16[32,16,128]{2,1,0:T(8,128)(2,1)S(1)}, bf16[32,16,128]{2,1,0:T(8,128)(2,1)S(1)}, u32[]{:S(2)}, u32[]{:S(2)}) collective-permute-start(bf16[32,16,128]{2,1,0:T(8,128)(2,1)S(1)} %get-tuple-element.100), channel_id=1, source_target_pairs={{0,8},{8,0},{16,24},{24,16},{1,9},{9,1},{17,25},{25,17},{2,10},{10... | collective-permute-start | bytes 393224 | tf_op jit(solution)/shard_map/ppermute | solution.py:296
  50.8 1.7 %collective-permute-start.19 = (bf16[32,16,128]{2,1,0:T(8,128)(2,1)S(1)}, bf16[32,16,128]{2,1,0:T(8,128)(2,1)S(1)}, u32[]{:S(2)}, u32[]{:S(2)}) collective-permute-start(bf16[32,16,128]{2,1,0:T(8,128)(2,1)S(1)} %get-tuple-element.102), channel_id=1, source_target_pairs={{0,24},{8,16},{16,8},{24,0},{1,25},{9,17},{17,9},{25,1},{2,26},{10... | collective-permute-start | bytes 393224 | tf_op jit(solution)/shard_map/ppermute | solution.py:296
  52.4 0.8 %shard_map.92.partial = f32[16,128,128]{2,1,0:T(8,128)S(1)} custom-call(bf16[128,256]{1,0:T(8,128)(2,1)S(1)} %get-tuple-element.76.left, bf16[256,256]{1,0:T(8,128)(2,1)S(1)} %get-tuple-element.77.right, bf16[16,128,128]{2,1,0:T(8,128)(2,1)S(1)} %shard_map.91.own, bf16[16,128,128]{2,1,0:T(8,128)(2,1)S(1)} %collective-permute-done.23.near), custom_call_target="tpu_custom_call" | custom-call | tf_op jit(solution)/shard_map/pallas_call | solution.py:301
  53.7 0.8 shard_map.93
  54.5 1.3 %collective-permute-start.25 = (bf16[32,16,128]{2,1,0:T(8,128)(2,1)S(1)}, bf16[32,16,128]{2,1,0:T(8,128)(2,1)S(1)}, u32[]{:S(2)}, u32[]{:S(2)}) collective-permute-start(bf16[32,16,128]{2,1,0:T(8,128)(2,1)S(1)} %get-tuple-element.108), channel_id=1, source_target_pairs={{0,8},{8,0},{16,24},{24,16},{1,9},{9,1},{17,25},{25,17},{2,10},{10... | collective-permute-start | bytes 393224 | tf_op jit(solution)/shard_map/ppermute | solution.py:296
  56.4 1.7 %collective-permute-start.27 = (bf16[32,16,128]{2,1,0:T(8,128)(2,1)S(1)}, bf16[32,16,128]{2,1,0:T(8,128)(2,1)S(1)}, u32[]{:S(2)}, u32[]{:S(2)}) collective-permute-start(bf16[32,16,128]{2,1,0:T(8,128)(2,1)S(1)} %get-tuple-element.110), channel_id=1, source_target_pairs={{0,24},{8,16},{16,8},{24,0},{1,25},{9,17},{17,9},{25,1},{2,26},{10... | collective-permute-start | bytes 393224 | tf_op jit(solution)/shard_map/ppermute | solution.py:296
  58.0 0.9 %collective-permute-done.18.refs_2_ = bf16[32,16,128]{2,1,0:T(8,128)(2,1)S(1)} collective-permute-done((bf16[32,16,128]{2,1,0:T(8,128)(2,1)S(1)}, bf16[32,16,128]{2,1,0:T(8,128)(2,1)S(1)}, u32[]{:S(2)}, u32[]{:S(2)}) %collective-permute-start.18) | collective-permute-done | bytes 131104 | tf_op jit(solution)/shard_map/ppermute | solution.py:296
  58.9 2.0 %collective-permute-done.25.refs_5_ = bf16[32,16,128]{2,1,0:T(8,128)(2,1)S(1)} collective-permute-done((bf16[32,16,128]{2,1,0:T(8,128)(2,1)S(1)}, bf16[32,16,128]{2,1,0:T(8,128)(2,1)S(1)}, u32[]{:S(2)}, u32[]{:S(2)}) %collective-permute-start.25) | collective-permute-done | bytes 131104 | tf_op jit(solution)/shard_map/ppermute | solution.py:296
  60.9 3.6 %collective-permute-done.26.refs_6_ = bf16[32,16,128]{2,1,0:T(8,128)(2,1)S(1)} collective-permute-done((bf16[32,16,128]{2,1,0:T(8,128)(2,1)S(1)}, bf16[32,16,128]{2,1,0:T(8,128)(2,1)S(1)}, u32[]{:S(2)}, u32[]{:S(2)}) %collective-permute-start.26) | collective-permute-done | bytes 131104 | tf_op jit(solution)/shard_map/ppermute | solution.py:296
  64.5 1.3 %shard_map.95 = (bf16[24,32,128]{2,1,0:T(8,128)(2,1)S(1)}, bf16[24,32,128]{2,1,0:T(8,128)(2,1)S(1)}, bf16[24,32,128]{2,1,0:T(8,128)(2,1)S(1)}, bf16[24,32,128]{2,1,0:T(8,128)(2,1)S(1)}) custom-call(bf16[192,256]{1,0:T(8,128)(2,1)S(1)} %get-tuple-element.62.fwd_l_ref, bf16[256,192]{1,0:T(8,128)(2,1)S(1)} %get-tuple-element.63.back_ref, ...), custom_call_target="tpu_custom_call" | custom-call | tf_op jit(solution)/shard_map/pallas_call | solution.py:301
  65.8 0.8 %collective-permute-start.31 = (bf16[24,32,128]{2,1,0:T(8,128)(2,1)S(1)}, bf16[24,32,128]{2,1,0:T(8,128)(2,1)S(1)}, u32[]{:S(2)}, u32[]{:S(2)}) collective-permute-start(bf16[24,32,128]{2,1,0:T(8,128)(2,1)S(1)} %get-tuple-element.116), channel_id=1, source_target_pairs={{0,8},{8,0},{16,24},{24,16},{1,9},{9,1},{17,25},{25,17},{2,10},{10... | collective-permute-start | bytes 589832 | tf_op jit(solution)/shard_map/ppermute | solution.py:296
  66.6 1.3 %collective-permute-start.32 = (bf16[24,32,128]{2,1,0:T(8,128)(2,1)S(1)}, bf16[24,32,128]{2,1,0:T(8,128)(2,1)S(1)}, u32[]{:S(2)}, u32[]{:S(2)}) collective-permute-start(bf16[24,32,128]{2,1,0:T(8,128)(2,1)S(1)} %get-tuple-element.117), channel_id=1, source_target_pairs={{0,16},{8,24},{16,0},{24,8},{1,17},{9,25},{17,1},{25,9},{2,18},{10... | collective-permute-start | bytes 589832 | tf_op jit(solution)/shard_map/ppermute | solution.py:296
  67.9 1.5 %collective-permute-start.33 = (bf16[24,32,128]{2,1,0:T(8,128)(2,1)S(1)}, bf16[24,32,128]{2,1,0:T(8,128)(2,1)S(1)}, u32[]{:S(2)}, u32[]{:S(2)}) collective-permute-start(bf16[24,32,128]{2,1,0:T(8,128)(2,1)S(1)} %get-tuple-element.118), channel_id=1, source_target_pairs={{0,24},{8,16},{16,8},{24,0},{1,25},{9,17},{17,9},{25,1},{2,26},{10... | collective-permute-start | bytes 589832 | tf_op jit(solution)/shard_map/ppermute | solution.py:296
  69.9 0.8 %collective-permute-start.28 = (bf16[8,32,128]{2,1,0:T(8,128)(2,1)S(1)}, bf16[8,32,128]{2,1,0:T(8,128)(2,1)S(1)}, u32[]{:S(2)}, u32[]{:S(2)}) collective-permute-start(bf16[8,32,128]{2,1,0:T(8,128)(2,1)S(1)} %get-tuple-element.112), channel_id=1, source_target_pairs={{0,8},{8,0},{16,24},{24,16},{1,9},{9,1},{17,25},{25,17},{2,10},{10... | collective-permute-start | bytes 196616 | tf_op jit(solution)/shard_map/ppermute | solution.py:296
  70.7 1.3 %collective-permute-start.29 = (bf16[8,32,128]{2,1,0:T(8,128)(2,1)S(1)}, bf16[8,32,128]{2,1,0:T(8,128)(2,1)S(1)}, u32[]{:S(2)}, u32[]{:S(2)}) collective-permute-start(bf16[8,32,128]{2,1,0:T(8,128)(2,1)S(1)} %get-tuple-element.113), channel_id=1, source_target_pairs={{0,16},{8,24},{16,0},{24,8},{1,17},{9,25},{17,1},{25,9},{2,18},{10... | collective-permute-start | bytes 196616 | tf_op jit(solution)/shard_map/ppermute | solution.py:296
  72.0 1.7 %collective-permute-done.31.refs_1_ = bf16[24,32,128]{2,1,0:T(8,128)(2,1)S(1)} collective-permute-done((bf16[24,32,128]{2,1,0:T(8,128)(2,1)S(1)}, bf16[24,32,128]{2,1,0:T(8,128)(2,1)S(1)}, u32[]{:S(2)}, u32[]{:S(2)}) %collective-permute-start.31) | collective-permute-done | bytes 196640 | tf_op jit(solution)/shard_map/ppermute | solution.py:296
  73.7 1.5 %collective-permute-start.30 = (bf16[8,32,128]{2,1,0:T(8,128)(2,1)S(1)}, bf16[8,32,128]{2,1,0:T(8,128)(2,1)S(1)}, u32[]{:S(2)}, u32[]{:S(2)}) collective-permute-start(bf16[8,32,128]{2,1,0:T(8,128)(2,1)S(1)} %get-tuple-element.114), channel_id=1, source_target_pairs={{0,24},{8,16},{16,8},{24,0},{1,25},{9,17},{17,9},{25,1},{2,26},{10... | collective-permute-start | bytes 196616 | tf_op jit(solution)/shard_map/ppermute | solution.py:296
  75.2 2.1 %collective-permute-done.32.refs_2_ = bf16[24,32,128]{2,1,0:T(8,128)(2,1)S(1)} collective-permute-done((bf16[24,32,128]{2,1,0:T(8,128)(2,1)S(1)}, bf16[24,32,128]{2,1,0:T(8,128)(2,1)S(1)}, u32[]{:S(2)}, u32[]{:S(2)}) %collective-permute-start.32) | collective-permute-done | bytes 196640 | tf_op jit(solution)/shard_map/ppermute | solution.py:296
  78.0 1.2 %shard_map.96.refs_4_ = f32[32,128,128]{2,1,0:T(8,128)} custom-call(s32[1]{0:T(128)} %bitcast.me_ref, bf16[24,32,128]{2,1,0:T(8,128)(2,1)S(1)} %get-tuple-element.115.refs_0_, bf16[24,32,128]{2,1,0:T(8,128)(2,1)S(1)} %collective-permute-done.31.refs_1_, bf16[24,32,128]{2,1,0:T(8,128)(2,1)S(1)} %collective-permute-done.32.refs_2_, ...), custom_call_target="tpu_custom_call" | custom-call | tf_op jit(solution)/shard_map/pallas_call | solution.py:301
  79.7 0.8 %shard_map.97 = f32[32,128,128]{2,1,0:T(8,128)} custom-call(s32[1]{0:T(128)} %bitcast.me_ref, bf16[8,32,128]{2,1,0:T(8,128)(2,1)S(1)} %get-tuple-element.111.refs_0_, bf16[8,32,128]{2,1,0:T(8,128)(2,1)S(1)} %collective-permute-done.28.refs_1_, bf16[8,32,128]{2,1,0:T(8,128)(2,1)S(1)} %collective-permute-done.29.refs_2_, ...), custom_call_target="tpu_custom_call", output_to_operand_aliasing={{}: (5, {})} | custom-call | tf_op jit(solution)/shard_map/pallas_call | solution.py:301
  (40 shorter events, 6.7 us)
Async XLA Ops:
  0.0 13.0 %copy-start.1 = (s32[1,2]{1,0:T(1,128)S(1)}, s32[1,2]{1,0:T(1,128)}, u32[]{:S(2)}) copy-start(s32[1,2]{1,0:T(1,128)} %param.11) | copy-start | bytes 28
  0.0 13.0 %copy-start = (bf16[1,3,128,128]{3,2,1,0:T(8,128)(2,1)S(1)}, bf16[1,3,128,128]{3,2,1,0:T(8,128)(2,1)}, u32[]{:S(2)}) copy-start(bf16[1,3,128,128]{3,2,1,0:T(8,128)(2,1)} %param.10) | copy-start | bytes 294916
  1.3 9.3 %collective-permute-start = (bf16[32,32,128]{2,1,0:T(8,128)(2,1)S(1)}, bf16[32,32,128]{2,1,0:T(8,128)(2,1)S(1)}, u32[]{:S(2)}, u32[]{:S(2)}) collective-permute-start(bf16[32,32,128]{2,1,0:T(8,128)(2,1)S(1)} %get-tuple-element.70), channel_id=1, source_target_pairs={{0,8},{8,0},{16,24},{24,16},{1,9},{9,1},{17,25},{25,17},{2,10},{10... | collective-permute-start | bytes 786440 | tf_op jit(solution)/shard_map/ppermute | solution.py:296
  2.8 14.2 %collective-permute-start.1 = (bf16[32,32,128]{2,1,0:T(8,128)(2,1)S(1)}, bf16[32,32,128]{2,1,0:T(8,128)(2,1)S(1)}, u32[]{:S(2)}, u32[]{:S(2)}) collective-permute-start(bf16[32,32,128]{2,1,0:T(8,128)(2,1)S(1)} %get-tuple-element.71), channel_id=1, source_target_pairs={{0,16},{8,24},{16,0},{24,8},{1,17},{9,25},{17,1},{25,9},{2,18},{10... | collective-permute-start | bytes 786440 | tf_op jit(solution)/shard_map/ppermute | solution.py:296
  4.3 12.8 %collective-permute-start.2 = (bf16[32,32,128]{2,1,0:T(8,128)(2,1)S(1)}, bf16[32,32,128]{2,1,0:T(8,128)(2,1)S(1)}, u32[]{:S(2)}, u32[]{:S(2)}) collective-permute-start(bf16[32,32,128]{2,1,0:T(8,128)(2,1)S(1)} %get-tuple-element.72), channel_id=1, source_target_pairs={{0,24},{8,16},{16,8},{24,0},{1,25},{9,17},{17,9},{25,1},{2,26},{10... | collective-permute-start | bytes 786440 | tf_op jit(solution)/shard_map/ppermute | solution.py:296
  7.3 14.6 %collective-permute-start.3 = (bf16[16,32,128]{2,1,0:T(8,128)(2,1)S(1)}, bf16[16,32,128]{2,1,0:T(8,128)(2,1)S(1)}, u32[]{:S(2)}, u32[]{:S(2)}) collective-permute-start(bf16[16,32,128]{2,1,0:T(8,128)(2,1)S(1)} %get-tuple-element.80), channel_id=1, source_target_pairs={{0,8},{8,0},{16,24},{24,16},{1,9},{9,1},{17,25},{25,17},{2,10},{10... | collective-permute-start | bytes 393224 | tf_op jit(solution)/shard_map/ppermute | solution.py:296
  8.8 14.5 %collective-permute-start.4 = (bf16[16,32,128]{2,1,0:T(8,128)(2,1)S(1)}, bf16[16,32,128]{2,1,0:T(8,128)(2,1)S(1)}, u32[]{:S(2)}, u32[]{:S(2)}) collective-permute-start(bf16[16,32,128]{2,1,0:T(8,128)(2,1)S(1)} %get-tuple-element.81), channel_id=1, source_target_pairs={{0,16},{8,24},{16,0},{24,8},{1,17},{9,25},{17,1},{25,9},{2,18},{10... | collective-permute-start | bytes 393224 | tf_op jit(solution)/shard_map/ppermute | solution.py:296
  10.5 12.8 %collective-permute-start.5 = (bf16[16,32,128]{2,1,0:T(8,128)(2,1)S(1)}, bf16[16,32,128]{2,1,0:T(8,128)(2,1)S(1)}, u32[]{:S(2)}, u32[]{:S(2)}) collective-permute-start(bf16[16,32,128]{2,1,0:T(8,128)(2,1)S(1)} %get-tuple-element.82), channel_id=1, source_target_pairs={{0,24},{8,16},{16,8},{24,0},{1,25},{9,17},{17,9},{25,1},{2,26},{10... | collective-permute-start | bytes 393224 | tf_op jit(solution)/shard_map/ppermute | solution.py:296
  18.9 8.1 %collective-permute-start.6 = (bf16[16,32,128]{2,1,0:T(8,128)(2,1)S(1)}, bf16[16,32,128]{2,1,0:T(8,128)(2,1)S(1)}, u32[]{:S(2)}, u32[]{:S(2)}) collective-permute-start(bf16[16,32,128]{2,1,0:T(8,128)(2,1)S(1)} %get-tuple-element.85), channel_id=1, source_target_pairs={{0,8},{8,0},{16,24},{24,16},{1,9},{9,1},{17,25},{25,17},{2,10},{10... | collective-permute-start | bytes 393224 | tf_op jit(solution)/shard_map/ppermute | solution.py:296
  20.4 7.9 %collective-permute-start.7 = (bf16[16,32,128]{2,1,0:T(8,128)(2,1)S(1)}, bf16[16,32,128]{2,1,0:T(8,128)(2,1)S(1)}, u32[]{:S(2)}, u32[]{:S(2)}) collective-permute-start(bf16[16,32,128]{2,1,0:T(8,128)(2,1)S(1)} %get-tuple-element.86), channel_id=1, source_target_pairs={{0,16},{8,24},{16,0},{24,8},{1,17},{9,25},{17,1},{25,9},{2,18},{10... | collective-permute-start | bytes 393224 | tf_op jit(solution)/shard_map/ppermute | solution.py:296
  21.9 6.8 %collective-permute-start.8 = (bf16[16,32,128]{2,1,0:T(8,128)(2,1)S(1)}, bf16[16,32,128]{2,1,0:T(8,128)(2,1)S(1)}, u32[]{:S(2)}, u32[]{:S(2)}) collective-permute-start(bf16[16,32,128]{2,1,0:T(8,128)(2,1)S(1)} %get-tuple-element.87), channel_id=1, source_target_pairs={{0,24},{8,16},{16,8},{24,0},{1,25},{9,17},{17,9},{25,1},{2,26},{10... | collective-permute-start | bytes 393224 | tf_op jit(solution)/shard_map/ppermute | solution.py:296
  24.4 7.9 %collective-permute-start.9 = (bf16[16,16,128]{2,1,0:T(8,128)(2,1)S(1)}, bf16[16,16,128]{2,1,0:T(8,128)(2,1)S(1)}, u32[]{:S(2)}, u32[]{:S(2)}) collective-permute-start(bf16[16,16,128]{2,1,0:T(8,128)(2,1)S(1)} %get-tuple-element.93), channel_id=1, source_target_pairs={{0,8},{8,0},{16,24},{24,16},{1,9},{9,1},{17,25},{25,17},{2,10},{10... | collective-permute-start | bytes 196616 | tf_op jit(solution)/shard_map/ppermute | solution.py:296
  25.4 8.0 %collective-permute-start.11 = (bf16[16,16,128]{2,1,0:T(8,128)(2,1)S(1)}, bf16[16,16,128]{2,1,0:T(8,128)(2,1)S(1)}, u32[]{:S(2)}, u32[]{:S(2)}) collective-permute-start(bf16[16,16,128]{2,1,0:T(8,128)(2,1)S(1)} %get-tuple-element.95), channel_id=1, source_target_pairs={{0,16},{8,24},{16,0},{24,8},{1,17},{9,25},{17,1},{25,9},{2,18},{10... | collective-permute-start | bytes 196616 | tf_op jit(solution)/shard_map/ppermute | solution.py:296
  27.0 8.0 %collective-permute-start.13 = (bf16[16,16,128]{2,1,0:T(8,128)(2,1)S(1)}, bf16[16,16,128]{2,1,0:T(8,128)(2,1)S(1)}, u32[]{:S(2)}, u32[]{:S(2)}) collective-permute-start(bf16[16,16,128]{2,1,0:T(8,128)(2,1)S(1)} %get-tuple-element.97), channel_id=1, source_target_pairs={{0,24},{8,16},{16,8},{24,0},{1,25},{9,17},{17,9},{25,1},{2,26},{10... | collective-permute-start | bytes 196616 | tf_op jit(solution)/shard_map/ppermute | solution.py:296
  29.8 6.0 %collective-permute-start.10 = (bf16[16,16,128]{2,1,0:T(8,128)(2,1)S(1)}, bf16[16,16,128]{2,1,0:T(8,128)(2,1)S(1)}, u32[]{:S(2)}, u32[]{:S(2)}) collective-permute-start(bf16[16,16,128]{2,1,0:T(8,128)(2,1)S(1)} %get-tuple-element.94), channel_id=1, source_target_pairs={{0,8},{8,0},{16,24},{24,16},{1,9},{9,1},{17,25},{25,17},{2,10},{10... | collective-permute-start | bytes 196616 | tf_op jit(solution)/shard_map/ppermute | solution.py:296
  31.5 5.3 %collective-permute-start.12 = (bf16[16,16,128]{2,1,0:T(8,128)(2,1)S(1)}, bf16[16,16,128]{2,1,0:T(8,128)(2,1)S(1)}, u32[]{:S(2)}, u32[]{:S(2)}) collective-permute-start(bf16[16,16,128]{2,1,0:T(8,128)(2,1)S(1)} %get-tuple-element.96), channel_id=1, source_target_pairs={{0,16},{8,24},{16,0},{24,8},{1,17},{9,25},{17,1},{25,9},{2,18},{10... | collective-permute-start | bytes 196616 | tf_op jit(solution)/shard_map/ppermute | solution.py:296
  32.3 5.2 %collective-permute-start.14 = (bf16[16,16,128]{2,1,0:T(8,128)(2,1)S(1)}, bf16[16,16,128]{2,1,0:T(8,128)(2,1)S(1)}, u32[]{:S(2)}, u32[]{:S(2)}) collective-permute-start(bf16[16,16,128]{2,1,0:T(8,128)(2,1)S(1)} %get-tuple-element.98), channel_id=1, source_target_pairs={{0,24},{8,16},{16,8},{24,0},{1,25},{9,17},{17,9},{25,1},{2,26},{10... | collective-permute-start | bytes 196616 | tf_op jit(solution)/shard_map/ppermute | solution.py:296
  33.4 6.7 %collective-permute-start.20 = (bf16[16,32,128]{2,1,0:T(8,128)(2,1)S(1)}, bf16[16,32,128]{2,1,0:T(8,128)(2,1)S(1)}, u32[]{:S(2)}, u32[]{:S(2)}) collective-permute-start(bf16[16,32,128]{2,1,0:T(8,128)(2,1)S(1)} %get-tuple-element.104), channel_id=1, source_target_pairs={{0,8},{8,0},{16,24},{24,16},{1,9},{9,1},{17,25},{25,17},{2,10},{10... | collective-permute-start | bytes 393224 | tf_op jit(solution)/shard_map/ppermute | solution.py:296
  35.0 5.0 %collective-permute-start.21 = (bf16[16,32,128]{2,1,0:T(8,128)(2,1)S(1)}, bf16[16,32,128]{2,1,0:T(8,128)(2,1)S(1)}, u32[]{:S(2)}, u32[]{:S(2)}) collective-permute-start(bf16[16,32,128]{2,1,0:T(8,128)(2,1)S(1)} %get-tuple-element.105), channel_id=1, source_target_pairs={{0,16},{8,24},{16,0},{24,8},{1,17},{9,25},{17,1},{25,9},{2,18},{10... | collective-permute-start | bytes 393224 | tf_op jit(solution)/shard_map/ppermute | solution.py:296
  35.8 5.9 %collective-permute-start.22 = (bf16[16,32,128]{2,1,0:T(8,128)(2,1)S(1)}, bf16[16,32,128]{2,1,0:T(8,128)(2,1)S(1)}, u32[]{:S(2)}, u32[]{:S(2)}) collective-permute-start(bf16[16,32,128]{2,1,0:T(8,128)(2,1)S(1)} %get-tuple-element.106), channel_id=1, source_target_pairs={{0,24},{8,16},{16,8},{24,0},{1,25},{9,17},{17,9},{25,1},{2,26},{10... | collective-permute-start | bytes 393224 | tf_op jit(solution)/shard_map/ppermute | solution.py:296
  37.5 6.9 %collective-permute-start.15 = (bf16[16,128,128]{2,1,0:T(8,128)(2,1)S(1)}, bf16[16,128,128]{2,1,0:T(8,128)(2,1)S(1)}, u32[]{:S(2)}, u32[]{:S(2)}) collective-permute-start(bf16[16,128,128]{2,1,0:T(8,128)(2,1)S(1)} %shard_map.88.own), channel_id=1, source_target_pairs={{0,1},{1,0},{2,3},{3,2},{4,5},{5,4},{6,7},{7,6},{8,9},{9,8},{10,11... | collective-permute-start | bytes 1572872 | tf_op jit(solution)/shard_map/ppermute | solution.py:423
  37.6 10.5 %collective-permute-start.16 = (bf16[16,128,128]{2,1,0:T(8,128)(2,1)S(1)}, bf16[16,128,128]{2,1,0:T(8,128)(2,1)S(1)}, u32[]{:S(2)}, u32[]{:S(2)}) collective-permute-start(bf16[16,128,128]{2,1,0:T(8,128)(2,1)S(1)} %shard_map.88.own), channel_id=1, source_target_pairs={{1,2},{2,1},{3,4},{4,3},{5,6},{6,5},{9,10},{10,9},{11,12},{12,11},... | collective-permute-start | bytes 1572872 | tf_op jit(solution)/shard_map/ppermute | solution.py:422
  41.7 10.7 %collective-permute-start.23 = (bf16[16,128,128]{2,1,0:T(8,128)(2,1)S(1)}, bf16[16,128,128]{2,1,0:T(8,128)(2,1)S(1)}, u32[]{:S(2)}, u32[]{:S(2)}) collective-permute-start(bf16[16,128,128]{2,1,0:T(8,128)(2,1)S(1)} %shard_map.91.own), channel_id=1, source_target_pairs={{0,1},{1,0},{2,3},{3,2},{4,5},{5,4},{6,7},{7,6},{8,9},{9,8},{10,11... | collective-permute-start | bytes 1572872 | tf_op jit(solution)/shard_map/ppermute | solution.py:423
  41.8 11.9 %collective-permute-start.24 = (bf16[16,128,128]{2,1,0:T(8,128)(2,1)S(1)}, bf16[16,128,128]{2,1,0:T(8,128)(2,1)S(1)}, u32[]{:S(2)}, u32[]{:S(2)}) collective-permute-start(bf16[16,128,128]{2,1,0:T(8,128)(2,1)S(1)} %shard_map.91.own), channel_id=1, source_target_pairs={{1,2},{2,1},{3,4},{4,3},{5,6},{6,5},{9,10},{10,9},{11,12},{12,11},... | collective-permute-start | bytes 1572872 | tf_op jit(solution)/shard_map/ppermute | solution.py:422
  48.9 7.5 %collective-permute-start.17 = (bf16[32,16,128]{2,1,0:T(8,128)(2,1)S(1)}, bf16[32,16,128]{2,1,0:T(8,128)(2,1)S(1)}, u32[]{:S(2)}, u32[]{:S(2)}) collective-permute-start(bf16[32,16,128]{2,1,0:T(8,128)(2,1)S(1)} %get-tuple-element.100), channel_id=1, source_target_pairs={{0,8},{8,0},{16,24},{24,16},{1,9},{9,1},{17,25},{25,17},{2,10},{10... | collective-permute-start | bytes 393224 | tf_op jit(solution)/shard_map/ppermute | solution.py:296
  50.2 8.7 %collective-permute-start.18 = (bf16[32,16,128]{2,1,0:T(8,128)(2,1)S(1)}, bf16[32,16,128]{2,1,0:T(8,128)(2,1)S(1)}, u32[]{:S(2)}, u32[]{:S(2)}) collective-permute-start(bf16[32,16,128]{2,1,0:T(8,128)(2,1)S(1)} %get-tuple-element.101), channel_id=1, source_target_pairs={{0,16},{8,24},{16,0},{24,8},{1,17},{9,25},{17,1},{25,9},{2,18},{10... | collective-permute-start | bytes 393224 | tf_op jit(solution)/shard_map/ppermute | solution.py:296
  50.8 8.2 %collective-permute-start.19 = (bf16[32,16,128]{2,1,0:T(8,128)(2,1)S(1)}, bf16[32,16,128]{2,1,0:T(8,128)(2,1)S(1)}, u32[]{:S(2)}, u32[]{:S(2)}) collective-permute-start(bf16[32,16,128]{2,1,0:T(8,128)(2,1)S(1)} %get-tuple-element.102), channel_id=1, source_target_pairs={{0,24},{8,16},{16,8},{24,0},{1,25},{9,17},{17,9},{25,1},{2,26},{10... | collective-permute-start | bytes 393224 | tf_op jit(solution)/shard_map/ppermute | solution.py:296
  54.5 6.4 %collective-permute-start.25 = (bf16[32,16,128]{2,1,0:T(8,128)(2,1)S(1)}, bf16[32,16,128]{2,1,0:T(8,128)(2,1)S(1)}, u32[]{:S(2)}, u32[]{:S(2)}) collective-permute-start(bf16[32,16,128]{2,1,0:T(8,128)(2,1)S(1)} %get-tuple-element.108), channel_id=1, source_target_pairs={{0,8},{8,0},{16,24},{24,16},{1,9},{9,1},{17,25},{25,17},{2,10},{10... | collective-permute-start | bytes 393224 | tf_op jit(solution)/shard_map/ppermute | solution.py:296
  55.8 8.7 %collective-permute-start.26 = (bf16[32,16,128]{2,1,0:T(8,128)(2,1)S(1)}, bf16[32,16,128]{2,1,0:T(8,128)(2,1)S(1)}, u32[]{:S(2)}, u32[]{:S(2)}) collective-permute-start(bf16[32,16,128]{2,1,0:T(8,128)(2,1)S(1)} %get-tuple-element.109), channel_id=1, source_target_pairs={{0,16},{8,24},{16,0},{24,8},{1,17},{9,25},{17,1},{25,9},{2,18},{10... | collective-permute-start | bytes 393224 | tf_op jit(solution)/shard_map/ppermute | solution.py:296
  56.4 8.2 %collective-permute-start.27 = (bf16[32,16,128]{2,1,0:T(8,128)(2,1)S(1)}, bf16[32,16,128]{2,1,0:T(8,128)(2,1)S(1)}, u32[]{:S(2)}, u32[]{:S(2)}) collective-permute-start(bf16[32,16,128]{2,1,0:T(8,128)(2,1)S(1)} %get-tuple-element.110), channel_id=1, source_target_pairs={{0,24},{8,16},{16,8},{24,0},{1,25},{9,17},{17,9},{25,1},{2,26},{10... | collective-permute-start | bytes 393224 | tf_op jit(solution)/shard_map/ppermute | solution.py:296
  65.8 7.9 %collective-permute-start.31 = (bf16[24,32,128]{2,1,0:T(8,128)(2,1)S(1)}, bf16[24,32,128]{2,1,0:T(8,128)(2,1)S(1)}, u32[]{:S(2)}, u32[]{:S(2)}) collective-permute-start(bf16[24,32,128]{2,1,0:T(8,128)(2,1)S(1)} %get-tuple-element.116), channel_id=1, source_target_pairs={{0,8},{8,0},{16,24},{24,16},{1,9},{9,1},{17,25},{25,17},{2,10},{10... | collective-permute-start | bytes 589832 | tf_op jit(solution)/shard_map/ppermute | solution.py:296
  66.6 10.7 %collective-permute-start.32 = (bf16[24,32,128]{2,1,0:T(8,128)(2,1)S(1)}, bf16[24,32,128]{2,1,0:T(8,128)(2,1)S(1)}, u32[]{:S(2)}, u32[]{:S(2)}) collective-permute-start(bf16[24,32,128]{2,1,0:T(8,128)(2,1)S(1)} %get-tuple-element.117), channel_id=1, source_target_pairs={{0,16},{8,24},{16,0},{24,8},{1,17},{9,25},{17,1},{25,9},{2,18},{10... | collective-permute-start | bytes 589832 | tf_op jit(solution)/shard_map/ppermute | solution.py:296
  67.9 10.1 %collective-permute-start.33 = (bf16[24,32,128]{2,1,0:T(8,128)(2,1)S(1)}, bf16[24,32,128]{2,1,0:T(8,128)(2,1)S(1)}, u32[]{:S(2)}, u32[]{:S(2)}) collective-permute-start(bf16[24,32,128]{2,1,0:T(8,128)(2,1)S(1)} %get-tuple-element.118), channel_id=1, source_target_pairs={{0,24},{8,16},{16,8},{24,0},{1,25},{9,17},{17,9},{25,1},{2,26},{10... | collective-permute-start | bytes 589832 | tf_op jit(solution)/shard_map/ppermute | solution.py:296
  69.9 9.3 %collective-permute-start.28 = (bf16[8,32,128]{2,1,0:T(8,128)(2,1)S(1)}, bf16[8,32,128]{2,1,0:T(8,128)(2,1)S(1)}, u32[]{:S(2)}, u32[]{:S(2)}) collective-permute-start(bf16[8,32,128]{2,1,0:T(8,128)(2,1)S(1)} %get-tuple-element.112), channel_id=1, source_target_pairs={{0,8},{8,0},{16,24},{24,16},{1,9},{9,1},{17,25},{25,17},{2,10},{10... | collective-permute-start | bytes 196616 | tf_op jit(solution)/shard_map/ppermute | solution.py:296
  70.7 8.5 %collective-permute-start.29 = (bf16[8,32,128]{2,1,0:T(8,128)(2,1)S(1)}, bf16[8,32,128]{2,1,0:T(8,128)(2,1)S(1)}, u32[]{:S(2)}, u32[]{:S(2)}) collective-permute-start(bf16[8,32,128]{2,1,0:T(8,128)(2,1)S(1)} %get-tuple-element.113), channel_id=1, source_target_pairs={{0,16},{8,24},{16,0},{24,8},{1,17},{9,25},{17,1},{25,9},{2,18},{10... | collective-permute-start | bytes 196616 | tf_op jit(solution)/shard_map/ppermute | solution.py:296
  73.7 6.0 %collective-permute-start.30 = (bf16[8,32,128]{2,1,0:T(8,128)(2,1)S(1)}, bf16[8,32,128]{2,1,0:T(8,128)(2,1)S(1)}, u32[]{:S(2)}, u32[]{:S(2)}) collective-permute-start(bf16[8,32,128]{2,1,0:T(8,128)(2,1)S(1)} %get-tuple-element.114), channel_id=1, source_target_pairs={{0,24},{8,16},{16,8},{24,0},{1,25},{9,17},{17,9},{25,1},{2,26},{10... | collective-permute-start | bytes 196616 | tf_op jit(solution)/shard_map/ppermute | solution.py:296

commit v5 on v4

--- a/solution.py
+++ b/solution.py
@@ -11,7 +11,6 @@
 
 BF16 = jnp.bfloat16
 F32 = jnp.float32
-WIDE = 8
 
 
 def split(table):
@@ -97,9 +96,9 @@
         first += count
 
 
-def gathered(refs, i):
+def gathered(refs, i, wide):
     both = jnp.concatenate(
-        [jnp.concatenate([ref[i + h] for ref in refs], axis=0) for h in range(WIDE)], axis=1
+        [jnp.concatenate([ref[i + h] for ref in refs], axis=0) for h in range(wide)], axis=1
     )
     return jnp.concatenate([both, both], axis=0)
 
@@ -116,13 +115,11 @@
     size = e_dev * rows
     for d, part in enumerate(less):
         scratch[d * size : (d + 1) * size, :] = part[...].astype(F32).reshape(size, orbitals)
-    fwd = fwd_ref[...]
     total = e_dev * len(less)
-    for n in range(out.shape[0]):
-        both = jnp.concatenate(
-            [scratch[pl.ds(n * WIDE + h, total, stride=rows), :] for h in range(WIDE)], axis=1
-        ).astype(BF16)
-        out[n] = dot(fwd, jnp.concatenate([both, both], axis=0))
+    both = jnp.concatenate(
+        [scratch[pl.ds(i, total, stride=rows), :] for i in range(rows)], axis=1
+    ).astype(BF16)
+    out[...] = dot(fwd_ref[...], jnp.concatenate([both, both], axis=0))
 
 
 def pol_kernel(groups, halves, first, earlier, fwd_ref, back_ref, less_ref, *refs):
@@ -132,13 +129,14 @@
     freq = fwd_ref.shape[0] // 2
     fwd, back = fwd_ref[...], back_ref[...]
     total = groups * e_dev
-    for i in range(0, count, WIDE):
-        a = less_ref[(first + i) // WIDE]
-        b = dot(fwd, gathered(great, i))
+    wide = count
+    for i in range(0, count, wide):
+        a = less_ref[:, (first + i) * orbitals : (first + i + wide) * orbitals]
+        b = dot(fwd, gathered(great, i, wide))
         real = a[:freq] * b[:freq] + a[freq:] * b[freq:]
         imag = a[freq:] * b[:freq] - a[:freq] * b[freq:]
         pol = inverse(back, jnp.concatenate([real, imag], axis=0))
-        for h in range(WIDE):
+        for h in range(wide):
             scratch[pl.ds(i + h, total, stride=count), :] = pol[
                 :, h * orbitals : (h + 1) * orbitals
             ]
@@ -170,13 +168,14 @@
         for d in range(groups)
         for h in range(halves)
     ]
-    for i in range(0, count, WIDE):
-        a = less_ref[(first + i) // WIDE]
-        b = dot(fwd_l, gathered(inter, i))
+    wide = count
+    for i in range(0, count, wide):
+        a = less_ref[:, (first + i) * orbitals : (first + i + wide) * orbitals]
+        b = dot(fwd_l, gathered(inter, i, wide))
         real = a[:freq] * b[:freq] - a[freq:] * b[freq:]
         imag = a[freq:] * b[:freq] + a[:freq] * b[freq:]
         sigma = inverse(back, jnp.concatenate([real, imag], axis=0)).astype(BF16)
-        for h in range(WIDE):
+        for h in range(wide):
             for d in range(groups):
                 outs[d][i + h] = sigma[
                     d * e_dev : (d + 1) * e_dev, h * orbitals : (h + 1) * orbitals
@@ -257,6 +256,41 @@
     terms = dot(left[...], half)
     for k in range(lags):
         scratch[pl.ds(k, n, stride=lags), :] = partial[k] + terms[:, k * n : k * n + n]
+    first = 0
+    for c in range(0, len(outs), groups):
+        count = outs[c].shape[0]
+        for d in range(groups):
+            start = pl.multiple_of(((me ^ d) * rows + first) * lags, 8)
+            part = scratch[pl.ds(start, count * lags), :]
+            outs[c + d][...] = part.astype(BF16).reshape(count, lags, n)
+        first += count
+
+
+def all_kernel(groups, me_ref, near_left, near_right, far_left, far_right, own, near, far, *refs):
+    outs, scratch = refs[:-1], refs[-1]
+    lags, n, _ = far.shape
+    rows = n // groups
+    me = me_ref[0]
+    both = jnp.concatenate([own[...].reshape(lags * n, n), near[...].reshape(lags * n, n)], axis=1)
+    half = dot(both, near_right[...]).astype(BF16)
+    other = dot(far[...].reshape(lags * n, n), far_right[...]).astype(BF16)
+    half = jnp.concatenate(
+        [
+            jnp.concatenate(
+                [
+                    half[k * n : k * n + n, :n],
+                    half[k * n : k * n + n, n:],
+                    other[k * n : k * n + n],
+                ],
+                axis=0,
+            )
+            for k in range(lags)
+        ],
+        axis=1,
+    )
+    terms = dot(jnp.concatenate([near_left[...], far_left[...]], axis=1), half)
+    for k in range(lags):
+        scratch[pl.ds(k, n, stride=lags), :] = terms[:, k * n : k * n + n]
     first = 0
     for c in range(0, len(outs), groups):
         count = outs[c].shape[0]
@@ -374,7 +408,7 @@
     rest = parts[groups:]
     less = call(
         spectrum_kernel,
-        shape(rows // WIDE, fwd_e.shape[0], WIDE * orbitals, dtype=F32),
+        shape(fwd_e.shape[0], rows * orbitals, dtype=F32),
         [vmem()] * (1 + groups),
         fwd_e,
         *less,
@@ -421,29 +455,47 @@
         )
         far = lax.ppermute(own, "block", far_pairs)
         near = lax.ppermute(own, "block", near_pairs)
-        partial = call(
-            near_kernel,
-            shape(lags, orbitals, orbitals, dtype=F32),
-            [vmem()] * 4,
-            near_left,
-            near_right,
-            own,
-            near,
-            out_specs=vmem(),
-        )
-        cut = [rows]
-        parts = call(
-            functools.partial(far_kernel, groups),
-            [shape(count, lags, orbitals) for count in cut for _ in range(groups)],
-            [smem] + [vmem()] * 4,
-            me,
-            far_left,
-            far_right,
-            partial,
-            far,
-            out_specs=[vmem()] * (groups * len(cut)),
-            scratch=[pltpu.VMEM((orbitals * lags, orbitals), F32)],
-        )
+        if h < halves - 1:
+            partial = call(
+                near_kernel,
+                shape(lags, orbitals, orbitals, dtype=F32),
+                [vmem()] * 4,
+                near_left,
+                near_right,
+                own,
+                near,
+                out_specs=vmem(),
+            )
+            cut = [rows]
+            parts = call(
+                functools.partial(far_kernel, groups),
+                [shape(count, lags, orbitals) for count in cut for _ in range(groups)],
+                [smem] + [vmem()] * 4,
+                me,
+                far_left,
+                far_right,
+                partial,
+                far,
+                out_specs=[vmem()] * (groups * len(cut)),
+                scratch=[pltpu.VMEM((orbitals * lags, orbitals), F32)],
+            )
+        else:
+            cut = [rows]
+            parts = call(
+                functools.partial(all_kernel, groups),
+                [shape(rows, lags, orbitals)] * groups,
+                [smem] + [vmem()] * 7,
+                me,
+                near_left,
+                near_right,
+                far_left,
+                far_right,
+                own,
+                near,
+                far,
+                out_specs=[vmem()] * groups,
+                scratch=[pltpu.VMEM((orbitals * lags, orbitals), F32)],
+            )
         inter.append(
             [exchange(parts[c * groups : (c + 1) * groups]) for c in range(len(cut))]
         )

time: 80.9 us -> 80.7 us (level)
  waiting for transfers between devices: 19.9 us -> 20.9 us
  Pallas kernels: 16.4 us -> 15.4 us
    ppermute x2, waiting for transfers between devices: 3.3 us -> 4.3 us  [shards(): far = lax.ppermute(own, 'block', far_pairs)]
    pallas_call x16 -> x15, Pallas kernels: 16.4 us -> 15.4 us  [call(): pl.pallas_call(kernel, out_shape=out_shape, in_specs=specs, scratch_shape...]
  transfers between devices with their start and end apart: 34 -> 34, of which waited for: 15 -> 15; matrix products, arithmetic and copies ran while one was open for 0% -> 0% of each run, Pallas kernels for 16% -> 15%
where the time goes in v5:
time: 80.7 us; the launch traced here: 80.4 us
  starting transfers between devices  43.8 us (54%)
  waiting for transfers between devices  20.9 us (26%)
  Pallas kernels  15.4 us (19%)
    ppermute x30, starting transfers between devices, exchange(): lax.ppermute(parts[d], 'energy', [(i, i ^ d) for i in range(groups)])  38.8 us
    ppermute x30, waiting for transfers between devices, exchange(): lax.ppermute(parts[d], 'energy', [(i, i ^ d) for i in range(groups)])  16.6 us
    pallas_call x15, Pallas kernels, call(): pl.pallas_call(kernel, out_shape=out_shape, in_specs=specs, scratch_shape...  15.4 us
    ppermute x2, starting transfers between devices, shards(): far = lax.ppermute(own, 'block', far_pairs)  4.89 us
    ppermute x2, waiting for transfers between devices, shards(): far = lax.ppermute(own, 'block', far_pairs)  4.3 us
  transfers between devices with their start and end apart: 34, of which 15 were waited for; matrix products, arithmetic and copies ran while one was open for 0% of the time, Pallas kernels for 15%

profile of v5, /device:TPU:16, one launch (start us, length us, event | category | flops | bytes accessed | tf_op | source)
XLA Modules:
  0.0 80.4 jit_solution(2673584536305322540)
XLA Ops:
  0.0 1.3 %shard_map.84 = (bf16[32,32,128]{2,1,0:T(8,128)(2,1)S(1)}, bf16[32,32,128]{2,1,0:T(8,128)(2,1)S(1)}, bf16[32,32,128]{2,1,0:T(8,128)(2,1)S(1)}, bf16[32,32,128]{2,1,0:T(8,128)(2,1)S(1)}) custom-call(s32[1]{0:T(128)} %bitcast.me_ref, bf16[32,128,128]{2,1,0:T(8,128)(2,1)} %bitcast.11), custom_call_target="tpu_custom_call" | custom-call | tf_op jit(solution)/shard_map/pallas_call | solution.py:335
  1.3 1.6 %collective-permute-start = (bf16[32,32,128]{2,1,0:T(8,128)(2,1)S(1)}, bf16[32,32,128]{2,1,0:T(8,128)(2,1)S(1)}, u32[]{:S(2)}, u32[]{:S(2)}) collective-permute-start(bf16[32,32,128]{2,1,0:T(8,128)(2,1)S(1)} %get-tuple-element.70), channel_id=1, source_target_pairs={{0,8},{8,0},{16,24},{24,16},{1,9},{9,1},{17,25},{25,17},{2,10},{10... | collective-permute-start | bytes 786440 | tf_op jit(solution)/shard_map/ppermute | solution.py:330
  2.8 1.5 %collective-permute-start.1 = (bf16[32,32,128]{2,1,0:T(8,128)(2,1)S(1)}, bf16[32,32,128]{2,1,0:T(8,128)(2,1)S(1)}, u32[]{:S(2)}, u32[]{:S(2)}) collective-permute-start(bf16[32,32,128]{2,1,0:T(8,128)(2,1)S(1)} %get-tuple-element.71), channel_id=1, source_target_pairs={{0,16},{8,24},{16,0},{24,8},{1,17},{9,25},{17,1},{25,9},{2,18},{10... | collective-permute-start | bytes 786440 | tf_op jit(solution)/shard_map/ppermute | solution.py:330
  4.8 2.5 %shard_map.83 = (bf16[16,32,128]{2,1,0:T(8,128)(2,1)S(1)}, bf16[16,32,128]{2,1,0:T(8,128)(2,1)S(1)}, bf16[16,32,128]{2,1,0:T(8,128)(2,1)S(1)}, bf16[16,32,128]{2...) custom-call(s32[1]{0:T(128)} %bitcast.me_ref, ...), custom_call_target="tpu_custom_call" | custom-call | tf_op jit(solution)/shard_map/pallas_call | solution.py:335
  7.3 1.6 %collective-permute-start.3 = (bf16[16,32,128]{2,1,0:T(8,128)(2,1)S(1)}, bf16[16,32,128]{2,1,0:T(8,128)(2,1)S(1)}, u32[]{:S(2)}, u32[]{:S(2)}) collective-permute-start(bf16[16,32,128]{2,1,0:T(8,128)(2,1)S(1)} %get-tuple-element.80), channel_id=1, source_target_pairs={{0,8},{8,0},{16,24},{24,16},{1,9},{9,1},{17,25},{25,17},{2,10},{10... | collective-permute-start | bytes 393224 | tf_op jit(solution)/shard_map/ppermute | solution.py:330
  8.8 1.5 %collective-permute-start.4 = (bf16[16,32,128]{2,1,0:T(8,128)(2,1)S(1)}, bf16[16,32,128]{2,1,0:T(8,128)(2,1)S(1)}, u32[]{:S(2)}, u32[]{:S(2)}) collective-permute-start(bf16[16,32,128]{2,1,0:T(8,128)(2,1)S(1)} %get-tuple-element.81), channel_id=1, source_target_pairs={{0,16},{8,24},{16,0},{24,8},{1,17},{9,25},{17,1},{25,9},{2,18},{10... | collective-permute-start | bytes 393224 | tf_op jit(solution)/shard_map/ppermute | solution.py:330
  10.5 2.4 %collective-permute-start.5 = (bf16[16,32,128]{2,1,0:T(8,128)(2,1)S(1)}, bf16[16,32,128]{2,1,0:T(8,128)(2,1)S(1)}, u32[]{:S(2)}, u32[]{:S(2)}) collective-permute-start(bf16[16,32,128]{2,1,0:T(8,128)(2,1)S(1)} %get-tuple-element.82), channel_id=1, source_target_pairs={{0,24},{8,16},{16,8},{24,0},{1,25},{9,17},{17,9},{25,1},{2,26},{10... | collective-permute-start | bytes 393224 | tf_op jit(solution)/shard_map/ppermute | solution.py:330
  13.0 1.7 %shard_map.82 = (bf16[192,256]{1,0:T(8,128)(2,1)S(1)}, bf16[192,256]{1,0:T(8,128)(2,1)S(1)}, bf16[256,192]{1,0:T(8,128)(2,1)S(1)}, bf16[256,192]{1,0:T(8,128)(2,...) custom-call(s32[1]{0:T(128)} %bitcast.me_ref, ...), custom_call_target="tpu_custom_call" | custom-call | tf_op jit(solution)/shard_map/pallas_call | solution.py:335
  14.7 2.3 %collective-permute-done.1.refs_2_ = bf16[32,32,128]{2,1,0:T(8,128)(2,1)S(1)} collective-permute-done((bf16[32,32,128]{2,1,0:T(8,128)(2,1)S(1)}, bf16[32,32,128]{2,1,0:T(8,128)(2,1)S(1)}, u32[]{:S(2)}, u32[]{:S(2)}) %collective-permute-start.1) | collective-permute-done | bytes 262176 | tf_op jit(solution)/shard_map/ppermute | solution.py:330
  17.2 1.7 %shard_map.85.less_ref = f32[192,4096]{1,0:T(8,128)S(1)} custom-call(bf16[192,256]{1,0:T(8,128)(2,1)S(1)} %get-tuple-element.68.fwd_ref, bf16[32,32,128]{2,1,0:T(8,128)(2,1)S(1)} %get-tuple-element.69.refs_0_, bf16[32,32,128]{2,1,0:T(8,128)(2,1)S(1)} %collective-permute-done.refs_1_, bf16[32,32,128]{2,1,0:T(8,128)(2,1)S(1)} %collective-permute-done.1.refs_2_, ...), custom_call_target="tpu_custom_call" | custom-call | tf_op jit(solution)/shard_map/pallas_call | solution.py:335
  18.9 1.6 %collective-permute-start.6 = (bf16[16,32,128]{2,1,0:T(8,128)(2,1)S(1)}, bf16[16,32,128]{2,1,0:T(8,128)(2,1)S(1)}, u32[]{:S(2)}, u32[]{:S(2)}) collective-permute-start(bf16[16,32,128]{2,1,0:T(8,128)(2,1)S(1)} %get-tuple-element.85), channel_id=1, source_target_pairs={{0,8},{8,0},{16,24},{24,16},{1,9},{9,1},{17,25},{25,17},{2,10},{10... | collective-permute-start | bytes 393224 | tf_op jit(solution)/shard_map/ppermute | solution.py:330
  20.4 1.5 %collective-permute-start.7 = (bf16[16,32,128]{2,1,0:T(8,128)(2,1)S(1)}, bf16[16,32,128]{2,1,0:T(8,128)(2,1)S(1)}, u32[]{:S(2)}, u32[]{:S(2)}) collective-permute-start(bf16[16,32,128]{2,1,0:T(8,128)(2,1)S(1)} %get-tuple-element.86), channel_id=1, source_target_pairs={{0,16},{8,24},{16,0},{24,8},{1,17},{9,25},{17,1},{25,9},{2,18},{10... | collective-permute-start | bytes 393224 | tf_op jit(solution)/shard_map/ppermute | solution.py:330
  21.9 1.4 %collective-permute-start.8 = (bf16[16,32,128]{2,1,0:T(8,128)(2,1)S(1)}, bf16[16,32,128]{2,1,0:T(8,128)(2,1)S(1)}, u32[]{:S(2)}, u32[]{:S(2)}) collective-permute-start(bf16[16,32,128]{2,1,0:T(8,128)(2,1)S(1)} %get-tuple-element.87), channel_id=1, source_target_pairs={{0,24},{8,16},{16,8},{24,0},{1,25},{9,17},{17,9},{25,1},{2,26},{10... | collective-permute-start | bytes 393224 | tf_op jit(solution)/shard_map/ppermute | solution.py:330
  23.3 0.9 %shard_map.86 = (bf16[16,16,128]{2,1,0:T(8,128)(2,1)S(1)}, bf16[16,16,128]{2,1,0:T(8,128)(2,1)S(1)}, bf16[16,16,128]{2,1,0:T(8,128)(2,1)S(1)}, bf16[16,16,128]{2...) custom-call(bf16[192,256]{1,0:T(8,128)(2,1)S(1)} %get-tuple-element., ...), custom_call_target="tpu_custom_call" | custom-call | tf_op jit(solution)/shard_map/pallas_call | solution.py:335
  24.2 1.0 %collective-permute-start.9 = (bf16[16,16,128]{2,1,0:T(8,128)(2,1)S(1)}, bf16[16,16,128]{2,1,0:T(8,128)(2,1)S(1)}, u32[]{:S(2)}, u32[]{:S(2)}) collective-permute-start(bf16[16,16,128]{2,1,0:T(8,128)(2,1)S(1)} %get-tuple-element.93), channel_id=1, source_target_pairs={{0,8},{8,0},{16,24},{24,16},{1,9},{9,1},{17,25},{25,17},{2,10},{10... | collective-permute-start | bytes 196616 | tf_op jit(solution)/shard_map/ppermute | solution.py:330
  25.2 1.6 %collective-permute-start.11 = (bf16[16,16,128]{2,1,0:T(8,128)(2,1)S(1)}, bf16[16,16,128]{2,1,0:T(8,128)(2,1)S(1)}, u32[]{:S(2)}, u32[]{:S(2)}) collective-permute-start(bf16[16,16,128]{2,1,0:T(8,128)(2,1)S(1)} %get-tuple-element.95), channel_id=1, source_target_pairs={{0,16},{8,24},{16,0},{24,8},{1,17},{9,25},{17,1},{25,9},{2,18},{10... | collective-permute-start | bytes 196616 | tf_op jit(solution)/shard_map/ppermute | solution.py:330
  26.9 1.4 %collective-permute-start.13 = (bf16[16,16,128]{2,1,0:T(8,128)(2,1)S(1)}, bf16[16,16,128]{2,1,0:T(8,128)(2,1)S(1)}, u32[]{:S(2)}, u32[]{:S(2)}) collective-permute-start(bf16[16,16,128]{2,1,0:T(8,128)(2,1)S(1)} %get-tuple-element.97), channel_id=1, source_target_pairs={{0,24},{8,16},{16,8},{24,0},{1,25},{9,17},{17,9},{25,1},{2,26},{10... | collective-permute-start | bytes 196616 | tf_op jit(solution)/shard_map/ppermute | solution.py:330
  28.8 0.9 %shard_map.87 = (bf16[16,16,128]{2,1,0:T(8,128)(2,1)S(1)}, bf16[16,16,128]{2,1,0:T(8,128)(2,1)S(1)}, bf16[16,16,128]{2,1,0:T(8,128)(2,1)S(1)}, bf16[16,16,128]{2...) custom-call(bf16[192,256]{1,0:T(8,128)(2,1)S(1)} %get-tuple-element., ...), custom_call_target="tpu_custom_call" | custom-call | tf_op jit(solution)/shard_map/pallas_call | solution.py:335
  29.7 1.7 %collective-permute-start.10 = (bf16[16,16,128]{2,1,0:T(8,128)(2,1)S(1)}, bf16[16,16,128]{2,1,0:T(8,128)(2,1)S(1)}, u32[]{:S(2)}, u32[]{:S(2)}) collective-permute-start(bf16[16,16,128]{2,1,0:T(8,128)(2,1)S(1)} %get-tuple-element.94), channel_id=1, source_target_pairs={{0,8},{8,0},{16,24},{24,16},{1,9},{9,1},{17,25},{25,17},{2,10},{10... | collective-permute-start | bytes 196616 | tf_op jit(solution)/shard_map/ppermute | solution.py:330
  32.1 1.2 %collective-permute-start.14 = (bf16[16,16,128]{2,1,0:T(8,128)(2,1)S(1)}, bf16[16,16,128]{2,1,0:T(8,128)(2,1)S(1)}, u32[]{:S(2)}, u32[]{:S(2)}) collective-permute-start(bf16[16,16,128]{2,1,0:T(8,128)(2,1)S(1)} %get-tuple-element.98), channel_id=1, source_target_pairs={{0,24},{8,16},{16,8},{24,0},{1,25},{9,17},{17,9},{25,1},{2,26},{10... | collective-permute-start | bytes 196616 | tf_op jit(solution)/shard_map/ppermute | solution.py:330
  33.3 1.6 %collective-permute-start.20 = (bf16[16,32,128]{2,1,0:T(8,128)(2,1)S(1)}, bf16[16,32,128]{2,1,0:T(8,128)(2,1)S(1)}, u32[]{:S(2)}, u32[]{:S(2)}) collective-permute-start(bf16[16,32,128]{2,1,0:T(8,128)(2,1)S(1)} %get-tuple-element.104), channel_id=1, source_target_pairs={{0,8},{8,0},{16,24},{24,16},{1,9},{9,1},{17,25},{25,17},{2,10},{10... | collective-permute-start | bytes 393224 | tf_op jit(solution)/shard_map/ppermute | solution.py:330
  35.6 1.2 %collective-permute-start.22 = (bf16[16,32,128]{2,1,0:T(8,128)(2,1)S(1)}, bf16[16,32,128]{2,1,0:T(8,128)(2,1)S(1)}, u32[]{:S(2)}, u32[]{:S(2)}) collective-permute-start(bf16[16,32,128]{2,1,0:T(8,128)(2,1)S(1)} %get-tuple-element.106), channel_id=1, source_target_pairs={{0,24},{8,16},{16,8},{24,0},{1,25},{9,17},{17,9},{25,1},{2,26},{10... | collective-permute-start | bytes 393224 | tf_op jit(solution)/shard_map/ppermute | solution.py:330
  37.4 2.4 %collective-permute-start.16 = (bf16[16,128,128]{2,1,0:T(8,128)(2,1)S(1)}, bf16[16,128,128]{2,1,0:T(8,128)(2,1)S(1)}, u32[]{:S(2)}, u32[]{:S(2)}) collective-permute-start(bf16[16,128,128]{2,1,0:T(8,128)(2,1)S(1)} %shard_map.88.own), channel_id=1, source_target_pairs={{1,2},{2,1},{3,4},{4,3},{5,6},{6,5},{9,10},{10,9},{11,12},{12,11},... | collective-permute-start | bytes 1572872 | tf_op jit(solution)/shard_map/ppermute | solution.py:456
  39.9 1.6 %collective-permute-done.22.refs_3_ = bf16[16,32,128]{2,1,0:T(8,128)(2,1)S(1)} collective-permute-done((bf16[16,32,128]{2,1,0:T(8,128)(2,1)S(1)}, bf16[16,32,128]{2,1,0:T(8,128)(2,1)S(1)}, u32[]{:S(2)}, u32[]{:S(2)}) %collective-permute-start.22) | collective-permute-done | bytes 131104 | tf_op jit(solution)/shard_map/ppermute | solution.py:330
  41.6 2.4 %collective-permute-start.24 = (bf16[16,128,128]{2,1,0:T(8,128)(2,1)S(1)}, bf16[16,128,128]{2,1,0:T(8,128)(2,1)S(1)}, u32[]{:S(2)}, u32[]{:S(2)}) collective-permute-start(bf16[16,128,128]{2,1,0:T(8,128)(2,1)S(1)} %shard_map.91.own), channel_id=1, source_target_pairs={{1,2},{2,1},{3,4},{4,3},{5,6},{6,5},{9,10},{10,9},{11,12},{12,11},... | collective-permute-start | bytes 1572872 | tf_op jit(solution)/shard_map/ppermute | solution.py:456
  44.0 0.8 %shard_map.89.partial = f32[16,128,128]{2,1,0:T(8,128)S(1)} custom-call(bf16[128,256]{1,0:T(8,128)(2,1)S(1)} %get-tuple-element.76.left.near_left, bf16[256,256]{1,0:T(8,128)(2,1)S(1)} %get-tuple-element.77.right.near_right, bf16[16,128,128]{2,1,0:T(8,128)(2,1)S(1)} %shard_map.88.own, bf16[16,128,128]{2,1,0:T(8,128)(2,1)S(1)} %collective-permute-done.15.near), custom_call_target="tpu_custom_call" | custom-call | tf_op jit(solution)/shard_map/pallas_call | solution.py:335
  44.9 3.0 %collective-permute-done.16.far = bf16[16,128,128]{2,1,0:T(8,128)(2,1)S(1)} collective-permute-done((bf16[16,128,128]{2,1,0:T(8,128)(2,1)S(1)}, bf16[16,128,128]{2,1,0:T(8,128)(2,1)S(1)}, u32[]{:S(2)}, u32[]{:S(2)}) %collective-permute-start.16) | collective-permute-done | bytes 524320 | tf_op jit(solution)/shard_map/ppermute | solution.py:456
  47.9 0.8 shard_map.90
  48.7 1.4 %collective-permute-start.17 = (bf16[32,16,128]{2,1,0:T(8,128)(2,1)S(1)}, bf16[32,16,128]{2,1,0:T(8,128)(2,1)S(1)}, u32[]{:S(2)}, u32[]{:S(2)}) collective-permute-start(bf16[32,16,128]{2,1,0:T(8,128)(2,1)S(1)} %get-tuple-element.100), channel_id=1, source_target_pairs={{0,8},{8,0},{16,24},{24,16},{1,9},{9,1},{17,25},{25,17},{2,10},{10... | collective-permute-start | bytes 393224 | tf_op jit(solution)/shard_map/ppermute | solution.py:330
  50.6 1.7 %collective-permute-start.19 = (bf16[32,16,128]{2,1,0:T(8,128)(2,1)S(1)}, bf16[32,16,128]{2,1,0:T(8,128)(2,1)S(1)}, u32[]{:S(2)}, u32[]{:S(2)}) collective-permute-start(bf16[32,16,128]{2,1,0:T(8,128)(2,1)S(1)} %get-tuple-element.102), channel_id=1, source_target_pairs={{0,24},{8,16},{16,8},{24,0},{1,25},{9,17},{17,9},{25,1},{2,26},{10... | collective-permute-start | bytes 393224 | tf_op jit(solution)/shard_map/ppermute | solution.py:330
  52.2 1.3 %collective-permute-done.24.far = bf16[16,128,128]{2,1,0:T(8,128)(2,1)S(1)} collective-permute-done((bf16[16,128,128]{2,1,0:T(8,128)(2,1)S(1)}, bf16[16,128,128]{2,1,0:T(8,128)(2,1)S(1)}, u32[]{:S(2)}, u32[]{:S(2)}) %collective-permute-start.24) | collective-permute-done | bytes 524320 | tf_op jit(solution)/shard_map/ppermute | solution.py:456
  53.5 1.0 %shard_map.92 = (bf16[32,16,128]{2,1,0:T(8,128)(2,1)S(1)}, bf16[32,16,128]{2,1,0:T(8,128)(2,1)S(1)}, bf16[32,16,128]{2,1,0:T(8,128)(2,1)S(1)}, bf16[32,16,128]{2,1,0:T(8,128)(2,1)S(1)}) custom-call(s32[1]{0:T(128)} %bitcast.me_ref, bf16[128,256]{1,0:T(8,128)(2,1)S(1)} %get-tuple-element.76.left.near_left, ...), custom_call_target="tpu_custom_call" | custom-call | tf_op jit(solution)/shard_map/pallas_call | solution.py:335
  54.5 1.4 %collective-permute-start.25 = (bf16[32,16,128]{2,1,0:T(8,128)(2,1)S(1)}, bf16[32,16,128]{2,1,0:T(8,128)(2,1)S(1)}, u32[]{:S(2)}, u32[]{:S(2)}) collective-permute-start(bf16[32,16,128]{2,1,0:T(8,128)(2,1)S(1)} %get-tuple-element.108), channel_id=1, source_target_pairs={{0,8},{8,0},{16,24},{24,16},{1,9},{9,1},{17,25},{25,17},{2,10},{10... | collective-permute-start | bytes 393224 | tf_op jit(solution)/shard_map/ppermute | solution.py:330
  56.4 1.7 %collective-permute-start.27 = (bf16[32,16,128]{2,1,0:T(8,128)(2,1)S(1)}, bf16[32,16,128]{2,1,0:T(8,128)(2,1)S(1)}, u32[]{:S(2)}, u32[]{:S(2)}) collective-permute-start(bf16[32,16,128]{2,1,0:T(8,128)(2,1)S(1)} %get-tuple-element.110), channel_id=1, source_target_pairs={{0,24},{8,16},{16,8},{24,0},{1,25},{9,17},{17,9},{25,1},{2,26},{10... | collective-permute-start | bytes 393224 | tf_op jit(solution)/shard_map/ppermute | solution.py:330
  58.8 2.2 %collective-permute-done.25.refs_5_ = bf16[32,16,128]{2,1,0:T(8,128)(2,1)S(1)} collective-permute-done((bf16[32,16,128]{2,1,0:T(8,128)(2,1)S(1)}, bf16[32,16,128]{2,1,0:T(8,128)(2,1)S(1)}, u32[]{:S(2)}, u32[]{:S(2)}) %collective-permute-start.25) | collective-permute-done | bytes 131104 | tf_op jit(solution)/shard_map/ppermute | solution.py:330
  61.0 3.7 %collective-permute-done.26.refs_6_ = bf16[32,16,128]{2,1,0:T(8,128)(2,1)S(1)} collective-permute-done((bf16[32,16,128]{2,1,0:T(8,128)(2,1)S(1)}, bf16[32,16,128]{2,1,0:T(8,128)(2,1)S(1)}, u32[]{:S(2)}, u32[]{:S(2)}) %collective-permute-start.26) | collective-permute-done | bytes 131104 | tf_op jit(solution)/shard_map/ppermute | solution.py:330
  64.6 1.1 %shard_map.94 = (bf16[24,32,128]{2,1,0:T(8,128)(2,1)S(1)}, bf16[24,32,128]{2,1,0:T(8,128)(2,1)S(1)}, bf16[24,32,128]{2,1,0:T(8,128)(2,1)S(1)}, bf16[24,32,128]{2,1,0:T(8,128)(2,1)S(1)}) custom-call(bf16[192,256]{1,0:T(8,128)(2,1)S(1)} %get-tuple-element.62.fwd_l_ref, bf16[256,192]{1,0:T(8,128)(2,1)S(1)} %get-tuple-element.63.back_ref, ...), custom_call_target="tpu_custom_call" | custom-call | tf_op jit(solution)/shard_map/pallas_call | solution.py:335
  65.8 0.8 collective-permute-start.31
  66.6 1.3 %collective-permute-start.32 = (bf16[24,32,128]{2,1,0:T(8,128)(2,1)S(1)}, bf16[24,32,128]{2,1,0:T(8,128)(2,1)S(1)}, u32[]{:S(2)}, u32[]{:S(2)}) collective-permute-start(bf16[24,32,128]{2,1,0:T(8,128)(2,1)S(1)} %get-tuple-element.117), channel_id=1, source_target_pairs={{0,16},{8,24},{16,0},{24,8},{1,17},{9,25},{17,1},{25,9},{2,18},{10... | collective-permute-start | bytes 589832 | tf_op jit(solution)/shard_map/ppermute | solution.py:330
  67.9 1.4 %collective-permute-start.33 = (bf16[24,32,128]{2,1,0:T(8,128)(2,1)S(1)}, bf16[24,32,128]{2,1,0:T(8,128)(2,1)S(1)}, u32[]{:S(2)}, u32[]{:S(2)}) collective-permute-start(bf16[24,32,128]{2,1,0:T(8,128)(2,1)S(1)} %get-tuple-element.118), channel_id=1, source_target_pairs={{0,24},{8,16},{16,8},{24,0},{1,25},{9,17},{17,9},{25,1},{2,26},{10... | collective-permute-start | bytes 589832 | tf_op jit(solution)/shard_map/ppermute | solution.py:330
  69.9 0.8 collective-permute-start.28
  70.6 1.3 %collective-permute-start.29 = (bf16[8,32,128]{2,1,0:T(8,128)(2,1)S(1)}, bf16[8,32,128]{2,1,0:T(8,128)(2,1)S(1)}, u32[]{:S(2)}, u32[]{:S(2)}) collective-permute-start(bf16[8,32,128]{2,1,0:T(8,128)(2,1)S(1)} %get-tuple-element.113), channel_id=1, source_target_pairs={{0,16},{8,24},{16,0},{24,8},{1,17},{9,25},{17,1},{25,9},{2,18},{10... | collective-permute-start | bytes 196616 | tf_op jit(solution)/shard_map/ppermute | solution.py:330
  72.0 1.7 %collective-permute-done.31.refs_1_ = bf16[24,32,128]{2,1,0:T(8,128)(2,1)S(1)} collective-permute-done((bf16[24,32,128]{2,1,0:T(8,128)(2,1)S(1)}, bf16[24,32,128]{2,1,0:T(8,128)(2,1)S(1)}, u32[]{:S(2)}, u32[]{:S(2)}) %collective-permute-start.31) | collective-permute-done | bytes 196640 | tf_op jit(solution)/shard_map/ppermute | solution.py:330
  73.7 1.5 %collective-permute-start.30 = (bf16[8,32,128]{2,1,0:T(8,128)(2,1)S(1)}, bf16[8,32,128]{2,1,0:T(8,128)(2,1)S(1)}, u32[]{:S(2)}, u32[]{:S(2)}) collective-permute-start(bf16[8,32,128]{2,1,0:T(8,128)(2,1)S(1)} %get-tuple-element.114), channel_id=1, source_target_pairs={{0,24},{8,16},{16,8},{24,0},{1,25},{9,17},{17,9},{25,1},{2,26},{10... | collective-permute-start | bytes 196616 | tf_op jit(solution)/shard_map/ppermute | solution.py:330
  75.1 1.7 %collective-permute-done.32.refs_2_ = bf16[24,32,128]{2,1,0:T(8,128)(2,1)S(1)} collective-permute-done((bf16[24,32,128]{2,1,0:T(8,128)(2,1)S(1)}, bf16[24,32,128]{2,1,0:T(8,128)(2,1)S(1)}, u32[]{:S(2)}, u32[]{:S(2)}) %collective-permute-start.32) | collective-permute-done | bytes 196640 | tf_op jit(solution)/shard_map/ppermute | solution.py:330
  76.8 1.1 %collective-permute-done.33.refs_3_ = bf16[24,32,128]{2,1,0:T(8,128)(2,1)S(1)} collective-permute-done((bf16[24,32,128]{2,1,0:T(8,128)(2,1)S(1)}, bf16[24,32,128]{2,1,0:T(8,128)(2,1)S(1)}, u32[]{:S(2)}, u32[]{:S(2)}) %collective-permute-start.33) | collective-permute-done | bytes 196640 | tf_op jit(solution)/shard_map/ppermute | solution.py:330
  77.9 1.2 %shard_map.95.refs_4_ = f32[32,128,128]{2,1,0:T(8,128)} custom-call(s32[1]{0:T(128)} %bitcast.me_ref, bf16[24,32,128]{2,1,0:T(8,128)(2,1)S(1)} %get-tuple-element.115.refs_0_, bf16[24,32,128]{2,1,0:T(8,128)(2,1)S(1)} %collective-permute-done.31.refs_1_, bf16[24,32,128]{2,1,0:T(8,128)(2,1)S(1)} %collective-permute-done.32.refs_2_, ...), custom_call_target="tpu_custom_call" | custom-call | tf_op jit(solution)/shard_map/pallas_call | solution.py:335
  79.5 0.8 %shard_map.96 = f32[32,128,128]{2,1,0:T(8,128)} custom-call(s32[1]{0:T(128)} %bitcast.me_ref, bf16[8,32,128]{2,1,0:T(8,128)(2,1)S(1)} %get-tuple-element.111.refs_0_, bf16[8,32,128]{2,1,0:T(8,128)(2,1)S(1)} %collective-permute-done.28.refs_1_, bf16[8,32,128]{2,1,0:T(8,128)(2,1)S(1)} %collective-permute-done.29.refs_2_, ...), custom_call_target="tpu_custom_call", output_to_operand_aliasing={{}: (5, {})} | custom-call | tf_op jit(solution)/shard_map/pallas_call | solution.py:335
  (39 shorter events, 6.1 us)
Async XLA Ops:
  0.0 13.0 %copy-start.1 = (s32[1,2]{1,0:T(1,128)S(1)}, s32[1,2]{1,0:T(1,128)}, u32[]{:S(2)}) copy-start(s32[1,2]{1,0:T(1,128)} %param.11) | copy-start | bytes 28
  0.0 13.0 %copy-start = (bf16[1,3,128,128]{3,2,1,0:T(8,128)(2,1)S(1)}, bf16[1,3,128,128]{3,2,1,0:T(8,128)(2,1)}, u32[]{:S(2)}) copy-start(bf16[1,3,128,128]{3,2,1,0:T(8,128)(2,1)} %param.10) | copy-start | bytes 294916
  1.3 9.3 %collective-permute-start = (bf16[32,32,128]{2,1,0:T(8,128)(2,1)S(1)}, bf16[32,32,128]{2,1,0:T(8,128)(2,1)S(1)}, u32[]{:S(2)}, u32[]{:S(2)}) collective-permute-start(bf16[32,32,128]{2,1,0:T(8,128)(2,1)S(1)} %get-tuple-element.70), channel_id=1, source_target_pairs={{0,8},{8,0},{16,24},{24,16},{1,9},{9,1},{17,25},{25,17},{2,10},{10... | collective-permute-start | bytes 786440 | tf_op jit(solution)/shard_map/ppermute | solution.py:330
  2.8 14.2 %collective-permute-start.1 = (bf16[32,32,128]{2,1,0:T(8,128)(2,1)S(1)}, bf16[32,32,128]{2,1,0:T(8,128)(2,1)S(1)}, u32[]{:S(2)}, u32[]{:S(2)}) collective-permute-start(bf16[32,32,128]{2,1,0:T(8,128)(2,1)S(1)} %get-tuple-element.71), channel_id=1, source_target_pairs={{0,16},{8,24},{16,0},{24,8},{1,17},{9,25},{17,1},{25,9},{2,18},{10... | collective-permute-start | bytes 786440 | tf_op jit(solution)/shard_map/ppermute | solution.py:330
  4.3 12.8 %collective-permute-start.2 = (bf16[32,32,128]{2,1,0:T(8,128)(2,1)S(1)}, bf16[32,32,128]{2,1,0:T(8,128)(2,1)S(1)}, u32[]{:S(2)}, u32[]{:S(2)}) collective-permute-start(bf16[32,32,128]{2,1,0:T(8,128)(2,1)S(1)} %get-tuple-element.72), channel_id=1, source_target_pairs={{0,24},{8,16},{16,8},{24,0},{1,25},{9,17},{17,9},{25,1},{2,26},{10... | collective-permute-start | bytes 786440 | tf_op jit(solution)/shard_map/ppermute | solution.py:330
  7.3 14.6 %collective-permute-start.3 = (bf16[16,32,128]{2,1,0:T(8,128)(2,1)S(1)}, bf16[16,32,128]{2,1,0:T(8,128)(2,1)S(1)}, u32[]{:S(2)}, u32[]{:S(2)}) collective-permute-start(bf16[16,32,128]{2,1,0:T(8,128)(2,1)S(1)} %get-tuple-element.80), channel_id=1, source_target_pairs={{0,8},{8,0},{16,24},{24,16},{1,9},{9,1},{17,25},{25,17},{2,10},{10... | collective-permute-start | bytes 393224 | tf_op jit(solution)/shard_map/ppermute | solution.py:330
  8.8 14.4 %collective-permute-start.4 = (bf16[16,32,128]{2,1,0:T(8,128)(2,1)S(1)}, bf16[16,32,128]{2,1,0:T(8,128)(2,1)S(1)}, u32[]{:S(2)}, u32[]{:S(2)}) collective-permute-start(bf16[16,32,128]{2,1,0:T(8,128)(2,1)S(1)} %get-tuple-element.81), channel_id=1, source_target_pairs={{0,16},{8,24},{16,0},{24,8},{1,17},{9,25},{17,1},{25,9},{2,18},{10... | collective-permute-start | bytes 393224 | tf_op jit(solution)/shard_map/ppermute | solution.py:330
  10.5 12.8 %collective-permute-start.5 = (bf16[16,32,128]{2,1,0:T(8,128)(2,1)S(1)}, bf16[16,32,128]{2,1,0:T(8,128)(2,1)S(1)}, u32[]{:S(2)}, u32[]{:S(2)}) collective-permute-start(bf16[16,32,128]{2,1,0:T(8,128)(2,1)S(1)} %get-tuple-element.82), channel_id=1, source_target_pairs={{0,24},{8,16},{16,8},{24,0},{1,25},{9,17},{17,9},{25,1},{2,26},{10... | collective-permute-start | bytes 393224 | tf_op jit(solution)/shard_map/ppermute | solution.py:330
  18.9 8.0 %collective-permute-start.6 = (bf16[16,32,128]{2,1,0:T(8,128)(2,1)S(1)}, bf16[16,32,128]{2,1,0:T(8,128)(2,1)S(1)}, u32[]{:S(2)}, u32[]{:S(2)}) collective-permute-start(bf16[16,32,128]{2,1,0:T(8,128)(2,1)S(1)} %get-tuple-element.85), channel_id=1, source_target_pairs={{0,8},{8,0},{16,24},{24,16},{1,9},{9,1},{17,25},{25,17},{2,10},{10... | collective-permute-start | bytes 393224 | tf_op jit(solution)/shard_map/ppermute | solution.py:330
  20.4 8.3 %collective-permute-start.7 = (bf16[16,32,128]{2,1,0:T(8,128)(2,1)S(1)}, bf16[16,32,128]{2,1,0:T(8,128)(2,1)S(1)}, u32[]{:S(2)}, u32[]{:S(2)}) collective-permute-start(bf16[16,32,128]{2,1,0:T(8,128)(2,1)S(1)} %get-tuple-element.86), channel_id=1, source_target_pairs={{0,16},{8,24},{16,0},{24,8},{1,17},{9,25},{17,1},{25,9},{2,18},{10... | collective-permute-start | bytes 393224 | tf_op jit(solution)/shard_map/ppermute | solution.py:330
  21.9 6.9 %collective-permute-start.8 = (bf16[16,32,128]{2,1,0:T(8,128)(2,1)S(1)}, bf16[16,32,128]{2,1,0:T(8,128)(2,1)S(1)}, u32[]{:S(2)}, u32[]{:S(2)}) collective-permute-start(bf16[16,32,128]{2,1,0:T(8,128)(2,1)S(1)} %get-tuple-element.87), channel_id=1, source_target_pairs={{0,24},{8,16},{16,8},{24,0},{1,25},{9,17},{17,9},{25,1},{2,26},{10... | collective-permute-start | bytes 393224 | tf_op jit(solution)/shard_map/ppermute | solution.py:330
  24.2 7.9 %collective-permute-start.9 = (bf16[16,16,128]{2,1,0:T(8,128)(2,1)S(1)}, bf16[16,16,128]{2,1,0:T(8,128)(2,1)S(1)}, u32[]{:S(2)}, u32[]{:S(2)}) collective-permute-start(bf16[16,16,128]{2,1,0:T(8,128)(2,1)S(1)} %get-tuple-element.93), channel_id=1, source_target_pairs={{0,8},{8,0},{16,24},{24,16},{1,9},{9,1},{17,25},{25,17},{2,10},{10... | collective-permute-start | bytes 196616 | tf_op jit(solution)/shard_map/ppermute | solution.py:330
  25.2 8.0 %collective-permute-start.11 = (bf16[16,16,128]{2,1,0:T(8,128)(2,1)S(1)}, bf16[16,16,128]{2,1,0:T(8,128)(2,1)S(1)}, u32[]{:S(2)}, u32[]{:S(2)}) collective-permute-start(bf16[16,16,128]{2,1,0:T(8,128)(2,1)S(1)} %get-tuple-element.95), channel_id=1, source_target_pairs={{0,16},{8,24},{16,0},{24,8},{1,17},{9,25},{17,1},{25,9},{2,18},{10... | collective-permute-start | bytes 196616 | tf_op jit(solution)/shard_map/ppermute | solution.py:330
  26.9 8.0 %collective-permute-start.13 = (bf16[16,16,128]{2,1,0:T(8,128)(2,1)S(1)}, bf16[16,16,128]{2,1,0:T(8,128)(2,1)S(1)}, u32[]{:S(2)}, u32[]{:S(2)}) collective-permute-start(bf16[16,16,128]{2,1,0:T(8,128)(2,1)S(1)} %get-tuple-element.97), channel_id=1, source_target_pairs={{0,24},{8,16},{16,8},{24,0},{1,25},{9,17},{17,9},{25,1},{2,26},{10... | collective-permute-start | bytes 196616 | tf_op jit(solution)/shard_map/ppermute | solution.py:330
  29.7 5.9 %collective-permute-start.10 = (bf16[16,16,128]{2,1,0:T(8,128)(2,1)S(1)}, bf16[16,16,128]{2,1,0:T(8,128)(2,1)S(1)}, u32[]{:S(2)}, u32[]{:S(2)}) collective-permute-start(bf16[16,16,128]{2,1,0:T(8,128)(2,1)S(1)} %get-tuple-element.94), channel_id=1, source_target_pairs={{0,8},{8,0},{16,24},{24,16},{1,9},{9,1},{17,25},{25,17},{2,10},{10... | collective-permute-start | bytes 196616 | tf_op jit(solution)/shard_map/ppermute | solution.py:330
  31.4 5.4 %collective-permute-start.12 = (bf16[16,16,128]{2,1,0:T(8,128)(2,1)S(1)}, bf16[16,16,128]{2,1,0:T(8,128)(2,1)S(1)}, u32[]{:S(2)}, u32[]{:S(2)}) collective-permute-start(bf16[16,16,128]{2,1,0:T(8,128)(2,1)S(1)} %get-tuple-element.96), channel_id=1, source_target_pairs={{0,16},{8,24},{16,0},{24,8},{1,17},{9,25},{17,1},{25,9},{2,18},{10... | collective-permute-start | bytes 196616 | tf_op jit(solution)/shard_map/ppermute | solution.py:330
  32.1 5.2 %collective-permute-start.14 = (bf16[16,16,128]{2,1,0:T(8,128)(2,1)S(1)}, bf16[16,16,128]{2,1,0:T(8,128)(2,1)S(1)}, u32[]{:S(2)}, u32[]{:S(2)}) collective-permute-start(bf16[16,16,128]{2,1,0:T(8,128)(2,1)S(1)} %get-tuple-element.98), channel_id=1, source_target_pairs={{0,24},{8,16},{16,8},{24,0},{1,25},{9,17},{17,9},{25,1},{2,26},{10... | collective-permute-start | bytes 196616 | tf_op jit(solution)/shard_map/ppermute | solution.py:330
  33.3 6.6 %collective-permute-start.20 = (bf16[16,32,128]{2,1,0:T(8,128)(2,1)S(1)}, bf16[16,32,128]{2,1,0:T(8,128)(2,1)S(1)}, u32[]{:S(2)}, u32[]{:S(2)}) collective-permute-start(bf16[16,32,128]{2,1,0:T(8,128)(2,1)S(1)} %get-tuple-element.104), channel_id=1, source_target_pairs={{0,8},{8,0},{16,24},{24,16},{1,9},{9,1},{17,25},{25,17},{2,10},{10... | collective-permute-start | bytes 393224 | tf_op jit(solution)/shard_map/ppermute | solution.py:330
  34.9 5.0 %collective-permute-start.21 = (bf16[16,32,128]{2,1,0:T(8,128)(2,1)S(1)}, bf16[16,32,128]{2,1,0:T(8,128)(2,1)S(1)}, u32[]{:S(2)}, u32[]{:S(2)}) collective-permute-start(bf16[16,32,128]{2,1,0:T(8,128)(2,1)S(1)} %get-tuple-element.105), channel_id=1, source_target_pairs={{0,16},{8,24},{16,0},{24,8},{1,17},{9,25},{17,1},{25,9},{2,18},{10... | collective-permute-start | bytes 393224 | tf_op jit(solution)/shard_map/ppermute | solution.py:330
  35.6 5.9 %collective-permute-start.22 = (bf16[16,32,128]{2,1,0:T(8,128)(2,1)S(1)}, bf16[16,32,128]{2,1,0:T(8,128)(2,1)S(1)}, u32[]{:S(2)}, u32[]{:S(2)}) collective-permute-start(bf16[16,32,128]{2,1,0:T(8,128)(2,1)S(1)} %get-tuple-element.106), channel_id=1, source_target_pairs={{0,24},{8,16},{16,8},{24,0},{1,25},{9,17},{17,9},{25,1},{2,26},{10... | collective-permute-start | bytes 393224 | tf_op jit(solution)/shard_map/ppermute | solution.py:330
  37.3 6.7 %collective-permute-start.15 = (bf16[16,128,128]{2,1,0:T(8,128)(2,1)S(1)}, bf16[16,128,128]{2,1,0:T(8,128)(2,1)S(1)}, u32[]{:S(2)}, u32[]{:S(2)}) collective-permute-start(bf16[16,128,128]{2,1,0:T(8,128)(2,1)S(1)} %shard_map.88.own), channel_id=1, source_target_pairs={{0,1},{1,0},{2,3},{3,2},{4,5},{5,4},{6,7},{7,6},{8,9},{9,8},{10,11... | collective-permute-start | bytes 1572872 | tf_op jit(solution)/shard_map/ppermute | solution.py:457
  37.4 10.5 %collective-permute-start.16 = (bf16[16,128,128]{2,1,0:T(8,128)(2,1)S(1)}, bf16[16,128,128]{2,1,0:T(8,128)(2,1)S(1)}, u32[]{:S(2)}, u32[]{:S(2)}) collective-permute-start(bf16[16,128,128]{2,1,0:T(8,128)(2,1)S(1)} %shard_map.88.own), channel_id=1, source_target_pairs={{1,2},{2,1},{3,4},{4,3},{5,6},{6,5},{9,10},{10,9},{11,12},{12,11},... | collective-permute-start | bytes 1572872 | tf_op jit(solution)/shard_map/ppermute | solution.py:456
  41.5 10.7 %collective-permute-start.23 = (bf16[16,128,128]{2,1,0:T(8,128)(2,1)S(1)}, bf16[16,128,128]{2,1,0:T(8,128)(2,1)S(1)}, u32[]{:S(2)}, u32[]{:S(2)}) collective-permute-start(bf16[16,128,128]{2,1,0:T(8,128)(2,1)S(1)} %shard_map.91.own), channel_id=1, source_target_pairs={{0,1},{1,0},{2,3},{3,2},{4,5},{5,4},{6,7},{7,6},{8,9},{9,8},{10,11... | collective-permute-start | bytes 1572872 | tf_op jit(solution)/shard_map/ppermute | solution.py:457
  41.6 11.9 %collective-permute-start.24 = (bf16[16,128,128]{2,1,0:T(8,128)(2,1)S(1)}, bf16[16,128,128]{2,1,0:T(8,128)(2,1)S(1)}, u32[]{:S(2)}, u32[]{:S(2)}) collective-permute-start(bf16[16,128,128]{2,1,0:T(8,128)(2,1)S(1)} %shard_map.91.own), channel_id=1, source_target_pairs={{1,2},{2,1},{3,4},{4,3},{5,6},{6,5},{9,10},{10,9},{11,12},{12,11},... | collective-permute-start | bytes 1572872 | tf_op jit(solution)/shard_map/ppermute | solution.py:456
  48.7 7.8 %collective-permute-start.17 = (bf16[32,16,128]{2,1,0:T(8,128)(2,1)S(1)}, bf16[32,16,128]{2,1,0:T(8,128)(2,1)S(1)}, u32[]{:S(2)}, u32[]{:S(2)}) collective-permute-start(bf16[32,16,128]{2,1,0:T(8,128)(2,1)S(1)} %get-tuple-element.100), channel_id=1, source_target_pairs={{0,8},{8,0},{16,24},{24,16},{1,9},{9,1},{17,25},{25,17},{2,10},{10... | collective-permute-start | bytes 393224 | tf_op jit(solution)/shard_map/ppermute | solution.py:330
  50.0 8.7 %collective-permute-start.18 = (bf16[32,16,128]{2,1,0:T(8,128)(2,1)S(1)}, bf16[32,16,128]{2,1,0:T(8,128)(2,1)S(1)}, u32[]{:S(2)}, u32[]{:S(2)}) collective-permute-start(bf16[32,16,128]{2,1,0:T(8,128)(2,1)S(1)} %get-tuple-element.101), channel_id=1, source_target_pairs={{0,16},{8,24},{16,0},{24,8},{1,17},{9,25},{17,1},{25,9},{2,18},{10... | collective-permute-start | bytes 393224 | tf_op jit(solution)/shard_map/ppermute | solution.py:330
  50.6 8.2 %collective-permute-start.19 = (bf16[32,16,128]{2,1,0:T(8,128)(2,1)S(1)}, bf16[32,16,128]{2,1,0:T(8,128)(2,1)S(1)}, u32[]{:S(2)}, u32[]{:S(2)}) collective-permute-start(bf16[32,16,128]{2,1,0:T(8,128)(2,1)S(1)} %get-tuple-element.102), channel_id=1, source_target_pairs={{0,24},{8,16},{16,8},{24,0},{1,25},{9,17},{17,9},{25,1},{2,26},{10... | collective-permute-start | bytes 393224 | tf_op jit(solution)/shard_map/ppermute | solution.py:330
  54.5 6.4 %collective-permute-start.25 = (bf16[32,16,128]{2,1,0:T(8,128)(2,1)S(1)}, bf16[32,16,128]{2,1,0:T(8,128)(2,1)S(1)}, u32[]{:S(2)}, u32[]{:S(2)}) collective-permute-start(bf16[32,16,128]{2,1,0:T(8,128)(2,1)S(1)} %get-tuple-element.108), channel_id=1, source_target_pairs={{0,8},{8,0},{16,24},{24,16},{1,9},{9,1},{17,25},{25,17},{2,10},{10... | collective-permute-start | bytes 393224 | tf_op jit(solution)/shard_map/ppermute | solution.py:330
  55.9 8.7 %collective-permute-start.26 = (bf16[32,16,128]{2,1,0:T(8,128)(2,1)S(1)}, bf16[32,16,128]{2,1,0:T(8,128)(2,1)S(1)}, u32[]{:S(2)}, u32[]{:S(2)}) collective-permute-start(bf16[32,16,128]{2,1,0:T(8,128)(2,1)S(1)} %get-tuple-element.109), channel_id=1, source_target_pairs={{0,16},{8,24},{16,0},{24,8},{1,17},{9,25},{17,1},{25,9},{2,18},{10... | collective-permute-start | bytes 393224 | tf_op jit(solution)/shard_map/ppermute | solution.py:330
  56.4 8.2 %collective-permute-start.27 = (bf16[32,16,128]{2,1,0:T(8,128)(2,1)S(1)}, bf16[32,16,128]{2,1,0:T(8,128)(2,1)S(1)}, u32[]{:S(2)}, u32[]{:S(2)}) collective-permute-start(bf16[32,16,128]{2,1,0:T(8,128)(2,1)S(1)} %get-tuple-element.110), channel_id=1, source_target_pairs={{0,24},{8,16},{16,8},{24,0},{1,25},{9,17},{17,9},{25,1},{2,26},{10... | collective-permute-start | bytes 393224 | tf_op jit(solution)/shard_map/ppermute | solution.py:330
  65.8 7.9 %collective-permute-start.31 = (bf16[24,32,128]{2,1,0:T(8,128)(2,1)S(1)}, bf16[24,32,128]{2,1,0:T(8,128)(2,1)S(1)}, u32[]{:S(2)}, u32[]{:S(2)}) collective-permute-start(bf16[24,32,128]{2,1,0:T(8,128)(2,1)S(1)} %get-tuple-element.116), channel_id=1, source_target_pairs={{0,8},{8,0},{16,24},{24,16},{1,9},{9,1},{17,25},{25,17},{2,10},{10... | collective-permute-start | bytes 589832 | tf_op jit(solution)/shard_map/ppermute | solution.py:330
  66.6 10.3 %collective-permute-start.32 = (bf16[24,32,128]{2,1,0:T(8,128)(2,1)S(1)}, bf16[24,32,128]{2,1,0:T(8,128)(2,1)S(1)}, u32[]{:S(2)}, u32[]{:S(2)}) collective-permute-start(bf16[24,32,128]{2,1,0:T(8,128)(2,1)S(1)} %get-tuple-element.117), channel_id=1, source_target_pairs={{0,16},{8,24},{16,0},{24,8},{1,17},{9,25},{17,1},{25,9},{2,18},{10... | collective-permute-start | bytes 589832 | tf_op jit(solution)/shard_map/ppermute | solution.py:330
  67.9 10.0 %collective-permute-start.33 = (bf16[24,32,128]{2,1,0:T(8,128)(2,1)S(1)}, bf16[24,32,128]{2,1,0:T(8,128)(2,1)S(1)}, u32[]{:S(2)}, u32[]{:S(2)}) collective-permute-start(bf16[24,32,128]{2,1,0:T(8,128)(2,1)S(1)} %get-tuple-element.118), channel_id=1, source_target_pairs={{0,24},{8,16},{16,8},{24,0},{1,25},{9,17},{17,9},{25,1},{2,26},{10... | collective-permute-start | bytes 589832 | tf_op jit(solution)/shard_map/ppermute | solution.py:330
  69.9 9.3 %collective-permute-start.28 = (bf16[8,32,128]{2,1,0:T(8,128)(2,1)S(1)}, bf16[8,32,128]{2,1,0:T(8,128)(2,1)S(1)}, u32[]{:S(2)}, u32[]{:S(2)}) collective-permute-start(bf16[8,32,128]{2,1,0:T(8,128)(2,1)S(1)} %get-tuple-element.112), channel_id=1, source_target_pairs={{0,8},{8,0},{16,24},{24,16},{1,9},{9,1},{17,25},{25,17},{2,10},{10... | collective-permute-start | bytes 196616 | tf_op jit(solution)/shard_map/ppermute | solution.py:330
  70.6 8.5 %collective-permute-start.29 = (bf16[8,32,128]{2,1,0:T(8,128)(2,1)S(1)}, bf16[8,32,128]{2,1,0:T(8,128)(2,1)S(1)}, u32[]{:S(2)}, u32[]{:S(2)}) collective-permute-start(bf16[8,32,128]{2,1,0:T(8,128)(2,1)S(1)} %get-tuple-element.113), channel_id=1, source_target_pairs={{0,16},{8,24},{16,0},{24,8},{1,17},{9,25},{17,1},{25,9},{2,18},{10... | collective-permute-start | bytes 196616 | tf_op jit(solution)/shard_map/ppermute | solution.py:330
  73.7 5.9 %collective-permute-start.30 = (bf16[8,32,128]{2,1,0:T(8,128)(2,1)S(1)}, bf16[8,32,128]{2,1,0:T(8,128)(2,1)S(1)}, u32[]{:S(2)}, u32[]{:S(2)}) collective-permute-start(bf16[8,32,128]{2,1,0:T(8,128)(2,1)S(1)} %get-tuple-element.114), channel_id=1, source_target_pairs={{0,24},{8,16},{16,8},{24,0},{1,25},{9,17},{17,9},{25,1},{2,26},{10... | collective-permute-start | bytes 196616 | tf_op jit(solution)/shard_map/ppermute | solution.py:330

commit v6 on v5

--- a/solution.py
+++ b/solution.py
@@ -199,7 +199,7 @@
 
 def setup_kernel(groups, count, me_ref, odd_ref, mask_ref, v_ref, *refs):
     sources, outs = refs[:count], refs[count : 2 * count]
-    near_left, near_right, far_left, far_right, scratch, sems = refs[2 * count :]
+    left, pair_right, far_right, scratch, sems = refs[2 * count :]
     me = me_ref[0]
     copies = [
         pltpu.make_async_copy(src.at[me], dst, sems.at[n])
@@ -222,57 +222,20 @@
     def masked(n, t):
         return (scratch[n] * mask_ref[t].astype(F32)).astype(BF16)
 
-    near_left[...] = jnp.concatenate([ordered(0), ordered(1)], axis=1)
-    near_right[...] = diagonal(scratch[0].astype(BF16), masked(1, 1 - odd))
-    far_left[...] = ordered(2)
+    left[...] = jnp.concatenate([ordered(0), ordered(1), ordered(2)], axis=1)
+    pair_right[...] = diagonal(scratch[0].astype(BF16), masked(1, 1 - odd))
     far_right[...] = masked(2, odd)
     for copy in copies:
         copy.wait()
 
 
-def near_kernel(left, right, own, near, out):
-    lags, n, _ = own.shape
-    both = jnp.concatenate([own[...].reshape(lags * n, n), near[...].reshape(lags * n, n)], axis=1)
-    half = dot(both, right[...]).astype(BF16)
-    half = jnp.concatenate(
-        [
-            jnp.concatenate([half[k * n : k * n + n, :n], half[k * n : k * n + n, n:]], axis=0)
-            for k in range(lags)
-        ],
-        axis=1,
-    )
-    terms = dot(left[...], half)
-    for k in range(lags):
-        out[k] = terms[:, k * n : k * n + n]
-
-
-def far_kernel(groups, me_ref, left, right, partial, far, *refs):
-    outs, scratch = refs[:-1], refs[-1]
-    lags, n, _ = partial.shape
-    rows = n // groups
-    me = me_ref[0]
-    half = dot(far[...].reshape(lags * n, n), right[...]).astype(BF16)
-    half = jnp.concatenate([half[k * n : k * n + n] for k in range(lags)], axis=1)
-    terms = dot(left[...], half)
-    for k in range(lags):
-        scratch[pl.ds(k, n, stride=lags), :] = partial[k] + terms[:, k * n : k * n + n]
-    first = 0
-    for c in range(0, len(outs), groups):
-        count = outs[c].shape[0]
-        for d in range(groups):
-            start = pl.multiple_of(((me ^ d) * rows + first) * lags, 8)
-            part = scratch[pl.ds(start, count * lags), :]
-            outs[c + d][...] = part.astype(BF16).reshape(count, lags, n)
-        first += count
-
-
-def all_kernel(groups, me_ref, near_left, near_right, far_left, far_right, own, near, far, *refs):
+def screen_kernel(groups, me_ref, left, pair_right, far_right, own, near, far, *refs):
     outs, scratch = refs[:-1], refs[-1]
     lags, n, _ = far.shape
     rows = n // groups
     me = me_ref[0]
     both = jnp.concatenate([own[...].reshape(lags * n, n), near[...].reshape(lags * n, n)], axis=1)
-    half = dot(both, near_right[...]).astype(BF16)
+    half = dot(both, pair_right[...]).astype(BF16)
     other = dot(far[...].reshape(lags * n, n), far_right[...]).astype(BF16)
     half = jnp.concatenate(
         [
@@ -288,7 +251,7 @@
         ],
         axis=1,
     )
-    terms = dot(jnp.concatenate([near_left[...], far_left[...]], axis=1), half)
+    terms = dot(left[...], half)
     for k in range(lags):
         scratch[pl.ds(k, n, stride=lags), :] = terms[:, k * n : k * n + n]
     first = 0
@@ -376,18 +339,17 @@
     less = exchange(less)
     stacks = [pltpu.with_memory_space_constraint(jnp.asarray(t), pltpu.HBM) for t in tables(groups, e_dev)]
     square = (orbitals, orbitals)
-    fwd_e, fwd_l, back_l, back_e, near_left, near_right, far_left, far_right = call(
+    fwd_e, fwd_l, back_l, back_e, left, pair_right, far_right = call(
         functools.partial(setup_kernel, groups, len(stacks)),
         [shape(*t.shape[1:]) for t in stacks]
-        + [shape(orbitals, 2 * orbitals), shape(2 * orbitals, 2 * orbitals)]
-        + [shape(*square), shape(*square)],
+        + [shape(orbitals, 3 * orbitals), shape(2 * orbitals, 2 * orbitals), shape(*square)],
         [smem, smem, smem, vmem()] + [hbm] * len(stacks),
         me,
         odd,
         coupling_mask[0],
         coupling[0],
         *stacks,
-        out_specs=[vmem()] * (len(stacks) + 4),
+        out_specs=[vmem()] * (len(stacks) + 3),
         scratch=[pltpu.VMEM((3, *square), F32), pltpu.SemaphoreType.DMA((len(stacks),))],
     )
     counts = [rows // 2, rows // 2] if rows % 32 == 0 else [rows]
@@ -455,50 +417,21 @@
         )
         far = lax.ppermute(own, "block", far_pairs)
         near = lax.ppermute(own, "block", near_pairs)
-        if h < halves - 1:
-            partial = call(
-                near_kernel,
-                shape(lags, orbitals, orbitals, dtype=F32),
-                [vmem()] * 4,
-                near_left,
-                near_right,
-                own,
-                near,
-                out_specs=vmem(),
-            )
-            cut = [rows]
-            parts = call(
-                functools.partial(far_kernel, groups),
-                [shape(count, lags, orbitals) for count in cut for _ in range(groups)],
-                [smem] + [vmem()] * 4,
-                me,
-                far_left,
-                far_right,
-                partial,
-                far,
-                out_specs=[vmem()] * (groups * len(cut)),
-                scratch=[pltpu.VMEM((orbitals * lags, orbitals), F32)],
-            )
-        else:
-            cut = [rows]
-            parts = call(
-                functools.partial(all_kernel, groups),
-                [shape(rows, lags, orbitals)] * groups,
-                [smem] + [vmem()] * 7,
-                me,
-                near_left,
-                near_right,
-                far_left,
-                far_right,
-                own,
-                near,
-                far,
-                out_specs=[vmem()] * groups,
-                scratch=[pltpu.VMEM((orbitals * lags, orbitals), F32)],
-            )
-        inter.append(
-            [exchange(parts[c * groups : (c + 1) * groups]) for c in range(len(cut))]
+        parts = call(
+            functools.partial(screen_kernel, groups),
+            [shape(rows, lags, orbitals)] * groups,
+            [smem] + [vmem()] * 6,
+            me,
+            left,
+            pair_right,
+            far_right,
+            own,
+            near,
+            far,
+            out_specs=[vmem()] * groups,
+            scratch=[pltpu.VMEM((orbitals * lags, orbitals), F32)],
         )
+        inter.append(exchange(parts))
 
     counts = [3 * rows // 4, rows // 4] if rows % 32 == 0 else [rows]
     sigma = []
@@ -511,7 +444,7 @@
             fwd_l,
             back_e,
             less,
-            *[part for half in inter for part in half[0]],
+            *[part for half in inter for part in half],
             out_specs=[vmem()] * groups,
         )
         sigma.append((first, count, exchange(parts)))

time: 80.7 us -> 80 us (level)
  waiting for transfers between devices: 20.9 us -> 18.3 us
  starting transfers between devices: 43.8 us -> 46.1 us
    ppermute x2, starting transfers between devices: 0.14 us -> 3.49 us  [shards(): near = lax.ppermute(own, 'block', near_pairs)]
    ppermute x30, waiting for transfers between devices: 16.6 us -> 14.7 us  [exchange(): lax.ppermute(parts[d], 'energy', [(i, i ^ d) for i in range(groups)])]
    ppermute x2, starting transfers between devices: 4.89 us -> 3.84 us  [shards(): far = lax.ppermute(own, 'block', far_pairs)]
    pallas_call x15 -> x14, Pallas kernels: 15.4 us -> 14.9 us  [call(): pl.pallas_call(kernel, out_shape=out_shape, in_specs=specs, scratch_shape...]
  transfers between devices with their start and end apart: 34 -> 34, of which waited for: 15 -> 14; matrix products, arithmetic and copies ran while one was open for 0% -> 0% of each run, Pallas kernels for 15% -> 15%
where the time goes in v6:
time: 80 us; the launch traced here: 79.5 us
  starting transfers between devices  46.1 us (58%)
  waiting for transfers between devices  18.3 us (23%)
  Pallas kernels  14.9 us (19%)
    ppermute x30, starting transfers between devices, exchange(): lax.ppermute(parts[d], 'energy', [(i, i ^ d) for i in range(groups)])  38.8 us
    pallas_call x14, Pallas kernels, call(): pl.pallas_call(kernel, out_shape=out_shape, in_specs=specs, scratch_shape...  14.9 us
    ppermute x30, waiting for transfers between devices, exchange(): lax.ppermute(parts[d], 'energy', [(i, i ^ d) for i in range(groups)])  14.7 us
    ppermute x2, starting transfers between devices, shards(): far = lax.ppermute(own, 'block', far_pairs)  3.84 us
    ppermute x2, waiting for transfers between devices, shards(): far = lax.ppermute(own, 'block', far_pairs)  3.67 us
    ppermute x2, starting transfers between devices, shards(): near = lax.ppermute(own, 'block', near_pairs)  3.49 us
  transfers between devices with their start and end apart: 34, of which 14 were waited for; matrix products, arithmetic and copies ran while one was open for 0% of the time, Pallas kernels for 15%

profile of v6, /device:TPU:16, one launch (start us, length us, event | category | flops | bytes accessed | tf_op | source)
XLA Modules:
  0.0 79.5 jit_solution(9276762761094546784)
XLA Ops:
  0.0 1.3 %shard_map.84 = (bf16[32,32,128]{2,1,0:T(8,128)(2,1)S(1)}, bf16[32,32,128]{2,1,0:T(8,128)(2,1)S(1)}, bf16[32,32,128]{2,1,0:T(8,128)(2,1)S(1)}, bf16[32,32,128]{2,1,0:T(8,128)(2,1)S(1)}) custom-call(s32[1]{0:T(128)} %bitcast.me_ref, bf16[32,128,128]{2,1,0:T(8,128)(2,1)} %bitcast.11), custom_call_target="tpu_custom_call" | custom-call | tf_op jit(solution)/shard_map/pallas_call | solution.py:298
  1.3 1.6 %collective-permute-start = (bf16[32,32,128]{2,1,0:T(8,128)(2,1)S(1)}, bf16[32,32,128]{2,1,0:T(8,128)(2,1)S(1)}, u32[]{:S(2)}, u32[]{:S(2)}) collective-permute-start(bf16[32,32,128]{2,1,0:T(8,128)(2,1)S(1)} %get-tuple-element.69), channel_id=1, source_target_pairs={{0,8},{8,0},{16,24},{24,16},{1,9},{9,1},{17,25},{25,17},{2,10},{10... | collective-permute-start | bytes 786440 | tf_op jit(solution)/shard_map/ppermute | solution.py:293
  2.8 1.5 %collective-permute-start.1 = (bf16[32,32,128]{2,1,0:T(8,128)(2,1)S(1)}, bf16[32,32,128]{2,1,0:T(8,128)(2,1)S(1)}, u32[]{:S(2)}, u32[]{:S(2)}) collective-permute-start(bf16[32,32,128]{2,1,0:T(8,128)(2,1)S(1)} %get-tuple-element.70), channel_id=1, source_target_pairs={{0,16},{8,24},{16,0},{24,8},{1,17},{9,25},{17,1},{25,9},{2,18},{10... | collective-permute-start | bytes 786440 | tf_op jit(solution)/shard_map/ppermute | solution.py:293
  4.8 2.5 %shard_map.83 = (bf16[16,32,128]{2,1,0:T(8,128)(2,1)S(1)}, bf16[16,32,128]{2,1,0:T(8,128)(2,1)S(1)}, bf16[16,32,128]{2,1,0:T(8,128)(2,1)S(1)}, bf16[16,32,128]{2...) custom-call(s32[1]{0:T(128)} %bitcast.me_ref, ...), custom_call_target="tpu_custom_call" | custom-call | tf_op jit(solution)/shard_map/pallas_call | solution.py:298
  7.3 1.6 %collective-permute-start.3 = (bf16[16,32,128]{2,1,0:T(8,128)(2,1)S(1)}, bf16[16,32,128]{2,1,0:T(8,128)(2,1)S(1)}, u32[]{:S(2)}, u32[]{:S(2)}) collective-permute-start(bf16[16,32,128]{2,1,0:T(8,128)(2,1)S(1)} %get-tuple-element.78), channel_id=1, source_target_pairs={{0,8},{8,0},{16,24},{24,16},{1,9},{9,1},{17,25},{25,17},{2,10},{10... | collective-permute-start | bytes 393224 | tf_op jit(solution)/shard_map/ppermute | solution.py:293
  8.8 1.5 %collective-permute-start.4 = (bf16[16,32,128]{2,1,0:T(8,128)(2,1)S(1)}, bf16[16,32,128]{2,1,0:T(8,128)(2,1)S(1)}, u32[]{:S(2)}, u32[]{:S(2)}) collective-permute-start(bf16[16,32,128]{2,1,0:T(8,128)(2,1)S(1)} %get-tuple-element.79), channel_id=1, source_target_pairs={{0,16},{8,24},{16,0},{24,8},{1,17},{9,25},{17,1},{25,9},{2,18},{10... | collective-permute-start | bytes 393224 | tf_op jit(solution)/shard_map/ppermute | solution.py:293
  10.5 2.4 %collective-permute-start.5 = (bf16[16,32,128]{2,1,0:T(8,128)(2,1)S(1)}, bf16[16,32,128]{2,1,0:T(8,128)(2,1)S(1)}, u32[]{:S(2)}, u32[]{:S(2)}) collective-permute-start(bf16[16,32,128]{2,1,0:T(8,128)(2,1)S(1)} %get-tuple-element.80), channel_id=1, source_target_pairs={{0,24},{8,16},{16,8},{24,0},{1,25},{9,17},{17,9},{25,1},{2,26},{10... | collective-permute-start | bytes 393224 | tf_op jit(solution)/shard_map/ppermute | solution.py:293
  13.0 1.8 %shard_map.82 = (bf16[192,256]{1,0:T(8,128)(2,1)S(1)}, bf16[192,256]{1,0:T(8,128)(2,1)S(1)}, bf16[256,192]{1,0:T(8,128)(2,1)S(1)}, bf16[256,192]{1,0:T(8,128)(2,...) custom-call(s32[1]{0:T(128)} %bitcast.me_ref, s32[1]{0:T(128)} %bitcast.1.odd_ref, ...), custom_call_target="tpu_custom_call" | custom-call | tf_op jit(solution)/shard_map/pallas_call | solution.py:298
  14.7 2.3 %collective-permute-done.1.refs_2_ = bf16[32,32,128]{2,1,0:T(8,128)(2,1)S(1)} collective-permute-done((bf16[32,32,128]{2,1,0:T(8,128)(2,1)S(1)}, bf16[32,32,128]{2,1,0:T(8,128)(2,1)S(1)}, u32[]{:S(2)}, u32[]{:S(2)}) %collective-permute-start.1) | collective-permute-done | bytes 262176 | tf_op jit(solution)/shard_map/ppermute | solution.py:293
  17.2 1.7 %shard_map.85.less_ref = f32[192,4096]{1,0:T(8,128)S(1)} custom-call(bf16[192,256]{1,0:T(8,128)(2,1)S(1)} %get-tuple-element.67.fwd_ref, bf16[32,32,128]{2,1,0:T(8,128)(2,1)S(1)} %get-tuple-element.68.refs_0_, bf16[32,32,128]{2,1,0:T(8,128)(2,1)S(1)} %collective-permute-done.refs_1_, bf16[32,32,128]{2,1,0:T(8,128)(2,1)S(1)} %collective-permute-done.1.refs_2_, ...), custom_call_target="tpu_custom_call" | custom-call | tf_op jit(solution)/shard_map/pallas_call | solution.py:298
  18.9 1.6 %collective-permute-start.6 = (bf16[16,32,128]{2,1,0:T(8,128)(2,1)S(1)}, bf16[16,32,128]{2,1,0:T(8,128)(2,1)S(1)}, u32[]{:S(2)}, u32[]{:S(2)}) collective-permute-start(bf16[16,32,128]{2,1,0:T(8,128)(2,1)S(1)} %get-tuple-element.83), channel_id=1, source_target_pairs={{0,8},{8,0},{16,24},{24,16},{1,9},{9,1},{17,25},{25,17},{2,10},{10... | collective-permute-start | bytes 393224 | tf_op jit(solution)/shard_map/ppermute | solution.py:293
  20.4 1.5 %collective-permute-start.7 = (bf16[16,32,128]{2,1,0:T(8,128)(2,1)S(1)}, bf16[16,32,128]{2,1,0:T(8,128)(2,1)S(1)}, u32[]{:S(2)}, u32[]{:S(2)}) collective-permute-start(bf16[16,32,128]{2,1,0:T(8,128)(2,1)S(1)} %get-tuple-element.84), channel_id=1, source_target_pairs={{0,16},{8,24},{16,0},{24,8},{1,17},{9,25},{17,1},{25,9},{2,18},{10... | collective-permute-start | bytes 393224 | tf_op jit(solution)/shard_map/ppermute | solution.py:293
  21.9 1.4 %collective-permute-start.8 = (bf16[16,32,128]{2,1,0:T(8,128)(2,1)S(1)}, bf16[16,32,128]{2,1,0:T(8,128)(2,1)S(1)}, u32[]{:S(2)}, u32[]{:S(2)}) collective-permute-start(bf16[16,32,128]{2,1,0:T(8,128)(2,1)S(1)} %get-tuple-element.85), channel_id=1, source_target_pairs={{0,24},{8,16},{16,8},{24,0},{1,25},{9,17},{17,9},{25,1},{2,26},{10... | collective-permute-start | bytes 393224 | tf_op jit(solution)/shard_map/ppermute | solution.py:293
  23.3 0.9 %shard_map.86 = (bf16[16,16,128]{2,1,0:T(8,128)(2,1)S(1)}, bf16[16,16,128]{2,1,0:T(8,128)(2,1)S(1)}, bf16[16,16,128]{2,1,0:T(8,128)(2,1)S(1)}, bf16[16,16,128]{2...) custom-call(bf16[192,256]{1,0:T(8,128)(2,1)S(1)} %get-tuple-element., ...), custom_call_target="tpu_custom_call" | custom-call | tf_op jit(solution)/shard_map/pallas_call | solution.py:298
  24.2 1.0 %collective-permute-start.9 = (bf16[16,16,128]{2,1,0:T(8,128)(2,1)S(1)}, bf16[16,16,128]{2,1,0:T(8,128)(2,1)S(1)}, u32[]{:S(2)}, u32[]{:S(2)}) collective-permute-start(bf16[16,16,128]{2,1,0:T(8,128)(2,1)S(1)} %get-tuple-element.91), channel_id=1, source_target_pairs={{0,8},{8,0},{16,24},{24,16},{1,9},{9,1},{17,25},{25,17},{2,10},{10... | collective-permute-start | bytes 196616 | tf_op jit(solution)/shard_map/ppermute | solution.py:293
  25.2 1.6 %collective-permute-start.11 = (bf16[16,16,128]{2,1,0:T(8,128)(2,1)S(1)}, bf16[16,16,128]{2,1,0:T(8,128)(2,1)S(1)}, u32[]{:S(2)}, u32[]{:S(2)}) collective-permute-start(bf16[16,16,128]{2,1,0:T(8,128)(2,1)S(1)} %get-tuple-element.93), channel_id=1, source_target_pairs={{0,16},{8,24},{16,0},{24,8},{1,17},{9,25},{17,1},{25,9},{2,18},{10... | collective-permute-start | bytes 196616 | tf_op jit(solution)/shard_map/ppermute | solution.py:293
  26.9 1.4 %collective-permute-start.13 = (bf16[16,16,128]{2,1,0:T(8,128)(2,1)S(1)}, bf16[16,16,128]{2,1,0:T(8,128)(2,1)S(1)}, u32[]{:S(2)}, u32[]{:S(2)}) collective-permute-start(bf16[16,16,128]{2,1,0:T(8,128)(2,1)S(1)} %get-tuple-element.95), channel_id=1, source_target_pairs={{0,24},{8,16},{16,8},{24,0},{1,25},{9,17},{17,9},{25,1},{2,26},{10... | collective-permute-start | bytes 196616 | tf_op jit(solution)/shard_map/ppermute | solution.py:293
  28.8 0.9 %shard_map.87 = (bf16[16,16,128]{2,1,0:T(8,128)(2,1)S(1)}, bf16[16,16,128]{2,1,0:T(8,128)(2,1)S(1)}, bf16[16,16,128]{2,1,0:T(8,128)(2,1)S(1)}, bf16[16,16,128]{2...) custom-call(bf16[192,256]{1,0:T(8,128)(2,1)S(1)} %get-tuple-element., ...), custom_call_target="tpu_custom_call" | custom-call | tf_op jit(solution)/shard_map/pallas_call | solution.py:298
  29.7 1.7 %collective-permute-start.10 = (bf16[16,16,128]{2,1,0:T(8,128)(2,1)S(1)}, bf16[16,16,128]{2,1,0:T(8,128)(2,1)S(1)}, u32[]{:S(2)}, u32[]{:S(2)}) collective-permute-start(bf16[16,16,128]{2,1,0:T(8,128)(2,1)S(1)} %get-tuple-element.92), channel_id=1, source_target_pairs={{0,8},{8,0},{16,24},{24,16},{1,9},{9,1},{17,25},{25,17},{2,10},{10... | collective-permute-start | bytes 196616 | tf_op jit(solution)/shard_map/ppermute | solution.py:293
  32.1 1.2 %collective-permute-start.14 = (bf16[16,16,128]{2,1,0:T(8,128)(2,1)S(1)}, bf16[16,16,128]{2,1,0:T(8,128)(2,1)S(1)}, u32[]{:S(2)}, u32[]{:S(2)}) collective-permute-start(bf16[16,16,128]{2,1,0:T(8,128)(2,1)S(1)} %get-tuple-element.96), channel_id=1, source_target_pairs={{0,24},{8,16},{16,8},{24,0},{1,25},{9,17},{17,9},{25,1},{2,26},{10... | collective-permute-start | bytes 196616 | tf_op jit(solution)/shard_map/ppermute | solution.py:293
  33.3 1.6 %collective-permute-start.20 = (bf16[16,32,128]{2,1,0:T(8,128)(2,1)S(1)}, bf16[16,32,128]{2,1,0:T(8,128)(2,1)S(1)}, u32[]{:S(2)}, u32[]{:S(2)}) collective-permute-start(bf16[16,32,128]{2,1,0:T(8,128)(2,1)S(1)} %get-tuple-element.102), channel_id=1, source_target_pairs={{0,8},{8,0},{16,24},{24,16},{1,9},{9,1},{17,25},{25,17},{2,10},{10... | collective-permute-start | bytes 393224 | tf_op jit(solution)/shard_map/ppermute | solution.py:293
  34.9 0.7 collective-permute-start.21
  35.6 1.2 %collective-permute-start.22 = (bf16[16,32,128]{2,1,0:T(8,128)(2,1)S(1)}, bf16[16,32,128]{2,1,0:T(8,128)(2,1)S(1)}, u32[]{:S(2)}, u32[]{:S(2)}) collective-permute-start(bf16[16,32,128]{2,1,0:T(8,128)(2,1)S(1)} %get-tuple-element.104), channel_id=1, source_target_pairs={{0,24},{8,16},{16,8},{24,0},{1,25},{9,17},{17,9},{25,1},{2,26},{10... | collective-permute-start | bytes 393224 | tf_op jit(solution)/shard_map/ppermute | solution.py:293
  37.3 1.9 %collective-permute-start.16 = (bf16[16,128,128]{2,1,0:T(8,128)(2,1)S(1)}, bf16[16,128,128]{2,1,0:T(8,128)(2,1)S(1)}, u32[]{:S(2)}, u32[]{:S(2)}) collective-permute-start(bf16[16,128,128]{2,1,0:T(8,128)(2,1)S(1)} %shard_map.88.own), channel_id=1, source_target_pairs={{1,2},{2,1},{3,4},{4,3},{5,6},{6,5},{9,10},{10,9},{11,12},{12,11},... | collective-permute-start | bytes 1572872 | tf_op jit(solution)/shard_map/ppermute | solution.py:418
  39.2 1.7 %collective-permute-start.15 = (bf16[16,128,128]{2,1,0:T(8,128)(2,1)S(1)}, bf16[16,128,128]{2,1,0:T(8,128)(2,1)S(1)}, u32[]{:S(2)}, u32[]{:S(2)}) collective-permute-start(bf16[16,128,128]{2,1,0:T(8,128)(2,1)S(1)} %shard_map.88.own), channel_id=1, source_target_pairs={{0,1},{1,0},{2,3},{3,2},{4,5},{5,4},{6,7},{7,6},{8,9},{9,8},{10,11... | collective-permute-start | bytes 1572872 | tf_op jit(solution)/shard_map/ppermute | solution.py:419
  41.5 1.9 %collective-permute-start.24 = (bf16[16,128,128]{2,1,0:T(8,128)(2,1)S(1)}, bf16[16,128,128]{2,1,0:T(8,128)(2,1)S(1)}, u32[]{:S(2)}, u32[]{:S(2)}) collective-permute-start(bf16[16,128,128]{2,1,0:T(8,128)(2,1)S(1)} %shard_map.90.own), channel_id=1, source_target_pairs={{1,2},{2,1},{3,4},{4,3},{5,6},{6,5},{9,10},{10,9},{11,12},{12,11},... | collective-permute-start | bytes 1572872 | tf_op jit(solution)/shard_map/ppermute | solution.py:418
  43.4 1.7 %collective-permute-start.23 = (bf16[16,128,128]{2,1,0:T(8,128)(2,1)S(1)}, bf16[16,128,128]{2,1,0:T(8,128)(2,1)S(1)}, u32[]{:S(2)}, u32[]{:S(2)}) collective-permute-start(bf16[16,128,128]{2,1,0:T(8,128)(2,1)S(1)} %shard_map.90.own), channel_id=1, source_target_pairs={{0,1},{1,0},{2,3},{3,2},{4,5},{5,4},{6,7},{7,6},{8,9},{9,8},{10,11... | collective-permute-start | bytes 1572872 | tf_op jit(solution)/shard_map/ppermute | solution.py:419
  45.2 2.6 %collective-permute-done.16.far = bf16[16,128,128]{2,1,0:T(8,128)(2,1)S(1)} collective-permute-done((bf16[16,128,128]{2,1,0:T(8,128)(2,1)S(1)}, bf16[16,128,128]{2,1,0:T(8,128)(2,1)S(1)}, u32[]{:S(2)}, u32[]{:S(2)}) %collective-permute-start.16) | collective-permute-done | bytes 524320 | tf_op jit(solution)/shard_map/ppermute | solution.py:418
  47.8 1.0 %shard_map.89 = (bf16[32,16,128]{2,1,0:T(8,128)(2,1)S(1)}, bf16[32,16,128]{2,1,0:T(8,128)(2,1)S(1)}, bf16[32,16,128]{2,1,0:T(8,128)(2,1)S(1)}, bf16[32,16,128]{2,1,0:T(8,128)(2,1)S(1)}) custom-call(s32[1]{0:T(128)} %bitcast.me_ref, bf16[128,384]{1,0:T(8,128)(2,1)S(1)} %get-tuple-element.73.left, bf16[256,256]{1,0:T(8,128)(2,1)S(1)} %get-tuple-element.74.pair_right, ...), custom_call_target="tpu_custom_call" | custom-call | tf_op jit(solution)/shard_map/pallas_call | solution.py:298
  48.8 1.4 %collective-permute-start.17 = (bf16[32,16,128]{2,1,0:T(8,128)(2,1)S(1)}, bf16[32,16,128]{2,1,0:T(8,128)(2,1)S(1)}, u32[]{:S(2)}, u32[]{:S(2)}) collective-permute-start(bf16[32,16,128]{2,1,0:T(8,128)(2,1)S(1)} %get-tuple-element.98), channel_id=1, source_target_pairs={{0,8},{8,0},{16,24},{24,16},{1,9},{9,1},{17,25},{25,17},{2,10},{10... | collective-permute-start | bytes 393224 | tf_op jit(solution)/shard_map/ppermute | solution.py:293
  50.7 1.7 %collective-permute-start.19 = (bf16[32,16,128]{2,1,0:T(8,128)(2,1)S(1)}, bf16[32,16,128]{2,1,0:T(8,128)(2,1)S(1)}, u32[]{:S(2)}, u32[]{:S(2)}) collective-permute-start(bf16[32,16,128]{2,1,0:T(8,128)(2,1)S(1)} %get-tuple-element.100), channel_id=1, source_target_pairs={{0,24},{8,16},{16,8},{24,0},{1,25},{9,17},{17,9},{25,1},{2,26},{10... | collective-permute-start | bytes 393224 | tf_op jit(solution)/shard_map/ppermute | solution.py:293
  52.4 1.0 %collective-permute-done.24.far = bf16[16,128,128]{2,1,0:T(8,128)(2,1)S(1)} collective-permute-done((bf16[16,128,128]{2,1,0:T(8,128)(2,1)S(1)}, bf16[16,128,128]{2,1,0:T(8,128)(2,1)S(1)}, u32[]{:S(2)}, u32[]{:S(2)}) %collective-permute-start.24) | collective-permute-done | bytes 524320 | tf_op jit(solution)/shard_map/ppermute | solution.py:418
  53.4 1.0 %shard_map.91 = (bf16[32,16,128]{2,1,0:T(8,128)(2,1)S(1)}, bf16[32,16,128]{2,1,0:T(8,128)(2,1)S(1)}, bf16[32,16,128]{2,1,0:T(8,128)(2,1)S(1)}, bf16[32,16,128]{2,1,0:T(8,128)(2,1)S(1)}) custom-call(s32[1]{0:T(128)} %bitcast.me_ref, bf16[128,384]{1,0:T(8,128)(2,1)S(1)} %get-tuple-element.73.left, bf16[256,256]{1,0:T(8,128)(2,1)S(1)} %get-tuple-element.74.pair_right, ...), custom_call_target="tpu_custom_call" | custom-call | tf_op jit(solution)/shard_map/pallas_call | solution.py:298
  54.5 1.4 %collective-permute-start.25 = (bf16[32,16,128]{2,1,0:T(8,128)(2,1)S(1)}, bf16[32,16,128]{2,1,0:T(8,128)(2,1)S(1)}, u32[]{:S(2)}, u32[]{:S(2)}) collective-permute-start(bf16[32,16,128]{2,1,0:T(8,128)(2,1)S(1)} %get-tuple-element.106), channel_id=1, source_target_pairs={{0,8},{8,0},{16,24},{24,16},{1,9},{9,1},{17,25},{25,17},{2,10},{10... | collective-permute-start | bytes 393224 | tf_op jit(solution)/shard_map/ppermute | solution.py:293
  56.4 1.7 %collective-permute-start.27 = (bf16[32,16,128]{2,1,0:T(8,128)(2,1)S(1)}, bf16[32,16,128]{2,1,0:T(8,128)(2,1)S(1)}, u32[]{:S(2)}, u32[]{:S(2)}) collective-permute-start(bf16[32,16,128]{2,1,0:T(8,128)(2,1)S(1)} %get-tuple-element.108), channel_id=1, source_target_pairs={{0,24},{8,16},{16,8},{24,0},{1,25},{9,17},{17,9},{25,1},{2,26},{10... | collective-permute-start | bytes 393224 | tf_op jit(solution)/shard_map/ppermute | solution.py:293
  58.4 2.4 %collective-permute-done.25.refs_5_ = bf16[32,16,128]{2,1,0:T(8,128)(2,1)S(1)} collective-permute-done((bf16[32,16,128]{2,1,0:T(8,128)(2,1)S(1)}, bf16[32,16,128]{2,1,0:T(8,128)(2,1)S(1)}, u32[]{:S(2)}, u32[]{:S(2)}) %collective-permute-start.25) | collective-permute-done | bytes 131104 | tf_op jit(solution)/shard_map/ppermute | solution.py:293
  60.8 3.2 %collective-permute-done.26.refs_6_ = bf16[32,16,128]{2,1,0:T(8,128)(2,1)S(1)} collective-permute-done((bf16[32,16,128]{2,1,0:T(8,128)(2,1)S(1)}, bf16[32,16,128]{2,1,0:T(8,128)(2,1)S(1)}, u32[]{:S(2)}, u32[]{:S(2)}) %collective-permute-start.26) | collective-permute-done | bytes 131104 | tf_op jit(solution)/shard_map/ppermute | solution.py:293
  64.0 1.1 %shard_map.93 = (bf16[24,32,128]{2,1,0:T(8,128)(2,1)S(1)}, bf16[24,32,128]{2,1,0:T(8,128)(2,1)S(1)}, bf16[24,32,128]{2,1,0:T(8,128)(2,1)S(1)}, bf16[24,32,128]{2,1,0:T(8,128)(2,1)S(1)}) custom-call(bf16[192,256]{1,0:T(8,128)(2,1)S(1)} %get-tuple-element.61.fwd_l_ref, bf16[256,192]{1,0:T(8,128)(2,1)S(1)} %get-tuple-element.62.back_ref, ...), custom_call_target="tpu_custom_call" | custom-call | tf_op jit(solution)/shard_map/pallas_call | solution.py:298
  65.2 0.8 collective-permute-start.31
  65.9 1.3 %collective-permute-start.32 = (bf16[24,32,128]{2,1,0:T(8,128)(2,1)S(1)}, bf16[24,32,128]{2,1,0:T(8,128)(2,1)S(1)}, u32[]{:S(2)}, u32[]{:S(2)}) collective-permute-start(bf16[24,32,128]{2,1,0:T(8,128)(2,1)S(1)} %get-tuple-element.115), channel_id=1, source_target_pairs={{0,16},{8,24},{16,0},{24,8},{1,17},{9,25},{17,1},{25,9},{2,18},{10... | collective-permute-start | bytes 589832 | tf_op jit(solution)/shard_map/ppermute | solution.py:293
  67.3 1.5 %collective-permute-start.33 = (bf16[24,32,128]{2,1,0:T(8,128)(2,1)S(1)}, bf16[24,32,128]{2,1,0:T(8,128)(2,1)S(1)}, u32[]{:S(2)}, u32[]{:S(2)}) collective-permute-start(bf16[24,32,128]{2,1,0:T(8,128)(2,1)S(1)} %get-tuple-element.116), channel_id=1, source_target_pairs={{0,24},{8,16},{16,8},{24,0},{1,25},{9,17},{17,9},{25,1},{2,26},{10... | collective-permute-start | bytes 589832 | tf_op jit(solution)/shard_map/ppermute | solution.py:293
  69.3 0.8 collective-permute-start.28
  70.0 1.3 %collective-permute-start.29 = (bf16[8,32,128]{2,1,0:T(8,128)(2,1)S(1)}, bf16[8,32,128]{2,1,0:T(8,128)(2,1)S(1)}, u32[]{:S(2)}, u32[]{:S(2)}) collective-permute-start(bf16[8,32,128]{2,1,0:T(8,128)(2,1)S(1)} %get-tuple-element.111), channel_id=1, source_target_pairs={{0,16},{8,24},{16,0},{24,8},{1,17},{9,25},{17,1},{25,9},{2,18},{10... | collective-permute-start | bytes 196616 | tf_op jit(solution)/shard_map/ppermute | solution.py:293
  71.4 1.7 %collective-permute-done.31.refs_1_ = bf16[24,32,128]{2,1,0:T(8,128)(2,1)S(1)} collective-permute-done((bf16[24,32,128]{2,1,0:T(8,128)(2,1)S(1)}, bf16[24,32,128]{2,1,0:T(8,128)(2,1)S(1)}, u32[]{:S(2)}, u32[]{:S(2)}) %collective-permute-start.31) | collective-permute-done | bytes 196640 | tf_op jit(solution)/shard_map/ppermute | solution.py:293
  73.1 1.5 %collective-permute-start.30 = (bf16[8,32,128]{2,1,0:T(8,128)(2,1)S(1)}, bf16[8,32,128]{2,1,0:T(8,128)(2,1)S(1)}, u32[]{:S(2)}, u32[]{:S(2)}) collective-permute-start(bf16[8,32,128]{2,1,0:T(8,128)(2,1)S(1)} %get-tuple-element.112), channel_id=1, source_target_pairs={{0,24},{8,16},{16,8},{24,0},{1,25},{9,17},{17,9},{25,1},{2,26},{10... | collective-permute-start | bytes 196616 | tf_op jit(solution)/shard_map/ppermute | solution.py:293
  74.5 2.7 %collective-permute-done.32.refs_2_ = bf16[24,32,128]{2,1,0:T(8,128)(2,1)S(1)} collective-permute-done((bf16[24,32,128]{2,1,0:T(8,128)(2,1)S(1)}, bf16[24,32,128]{2,1,0:T(8,128)(2,1)S(1)}, u32[]{:S(2)}, u32[]{:S(2)}) %collective-permute-start.32) | collective-permute-done | bytes 196640 | tf_op jit(solution)/shard_map/ppermute | solution.py:293
  77.2 1.2 %shard_map.94.refs_4_ = f32[32,128,128]{2,1,0:T(8,128)} custom-call(s32[1]{0:T(128)} %bitcast.me_ref, bf16[24,32,128]{2,1,0:T(8,128)(2,1)S(1)} %get-tuple-element.113.refs_0_, bf16[24,32,128]{2,1,0:T(8,128)(2,1)S(1)} %collective-permute-done.31.refs_1_, bf16[24,32,128]{2,1,0:T(8,128)(2,1)S(1)} %collective-permute-done.32.refs_2_, ...), custom_call_target="tpu_custom_call" | custom-call | tf_op jit(solution)/shard_map/pallas_call | solution.py:298
  78.6 0.8 %shard_map.95 = f32[32,128,128]{2,1,0:T(8,128)} custom-call(s32[1]{0:T(128)} %bitcast.me_ref, bf16[8,32,128]{2,1,0:T(8,128)(2,1)S(1)} %get-tuple-element.109.refs_0_, bf16[8,32,128]{2,1,0:T(8,128)(2,1)S(1)} %collective-permute-done.28.refs_1_, bf16[8,32,128]{2,1,0:T(8,128)(2,1)S(1)} %collective-permute-done.29.refs_2_, ...), custom_call_target="tpu_custom_call", output_to_operand_aliasing={{}: (5, {})} | custom-call | tf_op jit(solution)/shard_map/pallas_call | solution.py:298
  (38 shorter events, 5.2 us)
Async XLA Ops:
  0.0 13.0 %copy-start.1 = (s32[1,2]{1,0:T(1,128)S(1)}, s32[1,2]{1,0:T(1,128)}, u32[]{:S(2)}) copy-start(s32[1,2]{1,0:T(1,128)} %param.11) | copy-start | bytes 28
  0.0 13.0 %copy-start = (bf16[1,3,128,128]{3,2,1,0:T(8,128)(2,1)S(1)}, bf16[1,3,128,128]{3,2,1,0:T(8,128)(2,1)}, u32[]{:S(2)}) copy-start(bf16[1,3,128,128]{3,2,1,0:T(8,128)(2,1)} %param.10) | copy-start | bytes 294916
  1.3 9.3 %collective-permute-start = (bf16[32,32,128]{2,1,0:T(8,128)(2,1)S(1)}, bf16[32,32,128]{2,1,0:T(8,128)(2,1)S(1)}, u32[]{:S(2)}, u32[]{:S(2)}) collective-permute-start(bf16[32,32,128]{2,1,0:T(8,128)(2,1)S(1)} %get-tuple-element.69), channel_id=1, source_target_pairs={{0,8},{8,0},{16,24},{24,16},{1,9},{9,1},{17,25},{25,17},{2,10},{10... | collective-permute-start | bytes 786440 | tf_op jit(solution)/shard_map/ppermute | solution.py:293
  2.8 14.2 %collective-permute-start.1 = (bf16[32,32,128]{2,1,0:T(8,128)(2,1)S(1)}, bf16[32,32,128]{2,1,0:T(8,128)(2,1)S(1)}, u32[]{:S(2)}, u32[]{:S(2)}) collective-permute-start(bf16[32,32,128]{2,1,0:T(8,128)(2,1)S(1)} %get-tuple-element.70), channel_id=1, source_target_pairs={{0,16},{8,24},{16,0},{24,8},{1,17},{9,25},{17,1},{25,9},{2,18},{10... | collective-permute-start | bytes 786440 | tf_op jit(solution)/shard_map/ppermute | solution.py:293
  4.3 12.8 %collective-permute-start.2 = (bf16[32,32,128]{2,1,0:T(8,128)(2,1)S(1)}, bf16[32,32,128]{2,1,0:T(8,128)(2,1)S(1)}, u32[]{:S(2)}, u32[]{:S(2)}) collective-permute-start(bf16[32,32,128]{2,1,0:T(8,128)(2,1)S(1)} %get-tuple-element.71), channel_id=1, source_target_pairs={{0,24},{8,16},{16,8},{24,0},{1,25},{9,17},{17,9},{25,1},{2,26},{10... | collective-permute-start | bytes 786440 | tf_op jit(solution)/shard_map/ppermute | solution.py:293
  7.3 14.6 %collective-permute-start.3 = (bf16[16,32,128]{2,1,0:T(8,128)(2,1)S(1)}, bf16[16,32,128]{2,1,0:T(8,128)(2,1)S(1)}, u32[]{:S(2)}, u32[]{:S(2)}) collective-permute-start(bf16[16,32,128]{2,1,0:T(8,128)(2,1)S(1)} %get-tuple-element.78), channel_id=1, source_target_pairs={{0,8},{8,0},{16,24},{24,16},{1,9},{9,1},{17,25},{25,17},{2,10},{10... | collective-permute-start | bytes 393224 | tf_op jit(solution)/shard_map/ppermute | solution.py:293
  8.8 14.4 %collective-permute-start.4 = (bf16[16,32,128]{2,1,0:T(8,128)(2,1)S(1)}, bf16[16,32,128]{2,1,0:T(8,128)(2,1)S(1)}, u32[]{:S(2)}, u32[]{:S(2)}) collective-permute-start(bf16[16,32,128]{2,1,0:T(8,128)(2,1)S(1)} %get-tuple-element.79), channel_id=1, source_target_pairs={{0,16},{8,24},{16,0},{24,8},{1,17},{9,25},{17,1},{25,9},{2,18},{10... | collective-permute-start | bytes 393224 | tf_op jit(solution)/shard_map/ppermute | solution.py:293
  10.5 12.8 %collective-permute-start.5 = (bf16[16,32,128]{2,1,0:T(8,128)(2,1)S(1)}, bf16[16,32,128]{2,1,0:T(8,128)(2,1)S(1)}, u32[]{:S(2)}, u32[]{:S(2)}) collective-permute-start(bf16[16,32,128]{2,1,0:T(8,128)(2,1)S(1)} %get-tuple-element.80), channel_id=1, source_target_pairs={{0,24},{8,16},{16,8},{24,0},{1,25},{9,17},{17,9},{25,1},{2,26},{10... | collective-permute-start | bytes 393224 | tf_op jit(solution)/shard_map/ppermute | solution.py:293
  18.9 8.0 %collective-permute-start.6 = (bf16[16,32,128]{2,1,0:T(8,128)(2,1)S(1)}, bf16[16,32,128]{2,1,0:T(8,128)(2,1)S(1)}, u32[]{:S(2)}, u32[]{:S(2)}) collective-permute-start(bf16[16,32,128]{2,1,0:T(8,128)(2,1)S(1)} %get-tuple-element.83), channel_id=1, source_target_pairs={{0,8},{8,0},{16,24},{24,16},{1,9},{9,1},{17,25},{25,17},{2,10},{10... | collective-permute-start | bytes 393224 | tf_op jit(solution)/shard_map/ppermute | solution.py:293
  20.4 8.3 %collective-permute-start.7 = (bf16[16,32,128]{2,1,0:T(8,128)(2,1)S(1)}, bf16[16,32,128]{2,1,0:T(8,128)(2,1)S(1)}, u32[]{:S(2)}, u32[]{:S(2)}) collective-permute-start(bf16[16,32,128]{2,1,0:T(8,128)(2,1)S(1)} %get-tuple-element.84), channel_id=1, source_target_pairs={{0,16},{8,24},{16,0},{24,8},{1,17},{9,25},{17,1},{25,9},{2,18},{10... | collective-permute-start | bytes 393224 | tf_op jit(solution)/shard_map/ppermute | solution.py:293
  21.9 6.9 %collective-permute-start.8 = (bf16[16,32,128]{2,1,0:T(8,128)(2,1)S(1)}, bf16[16,32,128]{2,1,0:T(8,128)(2,1)S(1)}, u32[]{:S(2)}, u32[]{:S(2)}) collective-permute-start(bf16[16,32,128]{2,1,0:T(8,128)(2,1)S(1)} %get-tuple-element.85), channel_id=1, source_target_pairs={{0,24},{8,16},{16,8},{24,0},{1,25},{9,17},{17,9},{25,1},{2,26},{10... | collective-permute-start | bytes 393224 | tf_op jit(solution)/shard_map/ppermute | solution.py:293
  24.2 7.9 %collective-permute-start.9 = (bf16[16,16,128]{2,1,0:T(8,128)(2,1)S(1)}, bf16[16,16,128]{2,1,0:T(8,128)(2,1)S(1)}, u32[]{:S(2)}, u32[]{:S(2)}) collective-permute-start(bf16[16,16,128]{2,1,0:T(8,128)(2,1)S(1)} %get-tuple-element.91), channel_id=1, source_target_pairs={{0,8},{8,0},{16,24},{24,16},{1,9},{9,1},{17,25},{25,17},{2,10},{10... | collective-permute-start | bytes 196616 | tf_op jit(solution)/shard_map/ppermute | solution.py:293
  25.2 8.0 %collective-permute-start.11 = (bf16[16,16,128]{2,1,0:T(8,128)(2,1)S(1)}, bf16[16,16,128]{2,1,0:T(8,128)(2,1)S(1)}, u32[]{:S(2)}, u32[]{:S(2)}) collective-permute-start(bf16[16,16,128]{2,1,0:T(8,128)(2,1)S(1)} %get-tuple-element.93), channel_id=1, source_target_pairs={{0,16},{8,24},{16,0},{24,8},{1,17},{9,25},{17,1},{25,9},{2,18},{10... | collective-permute-start | bytes 196616 | tf_op jit(solution)/shard_map/ppermute | solution.py:293
  26.9 8.0 %collective-permute-start.13 = (bf16[16,16,128]{2,1,0:T(8,128)(2,1)S(1)}, bf16[16,16,128]{2,1,0:T(8,128)(2,1)S(1)}, u32[]{:S(2)}, u32[]{:S(2)}) collective-permute-start(bf16[16,16,128]{2,1,0:T(8,128)(2,1)S(1)} %get-tuple-element.95), channel_id=1, source_target_pairs={{0,24},{8,16},{16,8},{24,0},{1,25},{9,17},{17,9},{25,1},{2,26},{10... | collective-permute-start | bytes 196616 | tf_op jit(solution)/shard_map/ppermute | solution.py:293
  29.7 5.9 %collective-permute-start.10 = (bf16[16,16,128]{2,1,0:T(8,128)(2,1)S(1)}, bf16[16,16,128]{2,1,0:T(8,128)(2,1)S(1)}, u32[]{:S(2)}, u32[]{:S(2)}) collective-permute-start(bf16[16,16,128]{2,1,0:T(8,128)(2,1)S(1)} %get-tuple-element.92), channel_id=1, source_target_pairs={{0,8},{8,0},{16,24},{24,16},{1,9},{9,1},{17,25},{25,17},{2,10},{10... | collective-permute-start | bytes 196616 | tf_op jit(solution)/shard_map/ppermute | solution.py:293
  31.4 5.4 %collective-permute-start.12 = (bf16[16,16,128]{2,1,0:T(8,128)(2,1)S(1)}, bf16[16,16,128]{2,1,0:T(8,128)(2,1)S(1)}, u32[]{:S(2)}, u32[]{:S(2)}) collective-permute-start(bf16[16,16,128]{2,1,0:T(8,128)(2,1)S(1)} %get-tuple-element.94), channel_id=1, source_target_pairs={{0,16},{8,24},{16,0},{24,8},{1,17},{9,25},{17,1},{25,9},{2,18},{10... | collective-permute-start | bytes 196616 | tf_op jit(solution)/shard_map/ppermute | solution.py:293
  32.1 5.2 %collective-permute-start.14 = (bf16[16,16,128]{2,1,0:T(8,128)(2,1)S(1)}, bf16[16,16,128]{2,1,0:T(8,128)(2,1)S(1)}, u32[]{:S(2)}, u32[]{:S(2)}) collective-permute-start(bf16[16,16,128]{2,1,0:T(8,128)(2,1)S(1)} %get-tuple-element.96), channel_id=1, source_target_pairs={{0,24},{8,16},{16,8},{24,0},{1,25},{9,17},{17,9},{25,1},{2,26},{10... | collective-permute-start | bytes 196616 | tf_op jit(solution)/shard_map/ppermute | solution.py:293
  33.3 7.7 %collective-permute-start.20 = (bf16[16,32,128]{2,1,0:T(8,128)(2,1)S(1)}, bf16[16,32,128]{2,1,0:T(8,128)(2,1)S(1)}, u32[]{:S(2)}, u32[]{:S(2)}) collective-permute-start(bf16[16,32,128]{2,1,0:T(8,128)(2,1)S(1)} %get-tuple-element.102), channel_id=1, source_target_pairs={{0,8},{8,0},{16,24},{24,16},{1,9},{9,1},{17,25},{25,17},{2,10},{10... | collective-permute-start | bytes 393224 | tf_op jit(solution)/shard_map/ppermute | solution.py:293
  34.9 6.1 %collective-permute-start.21 = (bf16[16,32,128]{2,1,0:T(8,128)(2,1)S(1)}, bf16[16,32,128]{2,1,0:T(8,128)(2,1)S(1)}, u32[]{:S(2)}, u32[]{:S(2)}) collective-permute-start(bf16[16,32,128]{2,1,0:T(8,128)(2,1)S(1)} %get-tuple-element.103), channel_id=1, source_target_pairs={{0,16},{8,24},{16,0},{24,8},{1,17},{9,25},{17,1},{25,9},{2,18},{10... | collective-permute-start | bytes 393224 | tf_op jit(solution)/shard_map/ppermute | solution.py:293
  35.6 5.9 %collective-permute-start.22 = (bf16[16,32,128]{2,1,0:T(8,128)(2,1)S(1)}, bf16[16,32,128]{2,1,0:T(8,128)(2,1)S(1)}, u32[]{:S(2)}, u32[]{:S(2)}) collective-permute-start(bf16[16,32,128]{2,1,0:T(8,128)(2,1)S(1)} %get-tuple-element.104), channel_id=1, source_target_pairs={{0,24},{8,16},{16,8},{24,0},{1,25},{9,17},{17,9},{25,1},{2,26},{10... | collective-permute-start | bytes 393224 | tf_op jit(solution)/shard_map/ppermute | solution.py:293
  37.3 10.5 %collective-permute-start.16 = (bf16[16,128,128]{2,1,0:T(8,128)(2,1)S(1)}, bf16[16,128,128]{2,1,0:T(8,128)(2,1)S(1)}, u32[]{:S(2)}, u32[]{:S(2)}) collective-permute-start(bf16[16,128,128]{2,1,0:T(8,128)(2,1)S(1)} %shard_map.88.own), channel_id=1, source_target_pairs={{1,2},{2,1},{3,4},{4,3},{5,6},{6,5},{9,10},{10,9},{11,12},{12,11},... | collective-permute-start | bytes 1572872 | tf_op jit(solution)/shard_map/ppermute | solution.py:418
  39.2 8.6 %collective-permute-start.15 = (bf16[16,128,128]{2,1,0:T(8,128)(2,1)S(1)}, bf16[16,128,128]{2,1,0:T(8,128)(2,1)S(1)}, u32[]{:S(2)}, u32[]{:S(2)}) collective-permute-start(bf16[16,128,128]{2,1,0:T(8,128)(2,1)S(1)} %shard_map.88.own), channel_id=1, source_target_pairs={{0,1},{1,0},{2,3},{3,2},{4,5},{5,4},{6,7},{7,6},{8,9},{9,8},{10,11... | collective-permute-start | bytes 1572872 | tf_op jit(solution)/shard_map/ppermute | solution.py:419
  41.5 11.9 %collective-permute-start.24 = (bf16[16,128,128]{2,1,0:T(8,128)(2,1)S(1)}, bf16[16,128,128]{2,1,0:T(8,128)(2,1)S(1)}, u32[]{:S(2)}, u32[]{:S(2)}) collective-permute-start(bf16[16,128,128]{2,1,0:T(8,128)(2,1)S(1)} %shard_map.90.own), channel_id=1, source_target_pairs={{1,2},{2,1},{3,4},{4,3},{5,6},{6,5},{9,10},{10,9},{11,12},{12,11},... | collective-permute-start | bytes 1572872 | tf_op jit(solution)/shard_map/ppermute | solution.py:418
  43.4 10.0 %collective-permute-start.23 = (bf16[16,128,128]{2,1,0:T(8,128)(2,1)S(1)}, bf16[16,128,128]{2,1,0:T(8,128)(2,1)S(1)}, u32[]{:S(2)}, u32[]{:S(2)}) collective-permute-start(bf16[16,128,128]{2,1,0:T(8,128)(2,1)S(1)} %shard_map.90.own), channel_id=1, source_target_pairs={{0,1},{1,0},{2,3},{3,2},{4,5},{5,4},{6,7},{7,6},{8,9},{9,8},{10,11... | collective-permute-start | bytes 1572872 | tf_op jit(solution)/shard_map/ppermute | solution.py:419
  48.8 7.5 %collective-permute-start.17 = (bf16[32,16,128]{2,1,0:T(8,128)(2,1)S(1)}, bf16[32,16,128]{2,1,0:T(8,128)(2,1)S(1)}, u32[]{:S(2)}, u32[]{:S(2)}) collective-permute-start(bf16[32,16,128]{2,1,0:T(8,128)(2,1)S(1)} %get-tuple-element.98), channel_id=1, source_target_pairs={{0,8},{8,0},{16,24},{24,16},{1,9},{9,1},{17,25},{25,17},{2,10},{10... | collective-permute-start | bytes 393224 | tf_op jit(solution)/shard_map/ppermute | solution.py:293
  50.2 8.2 %collective-permute-start.18 = (bf16[32,16,128]{2,1,0:T(8,128)(2,1)S(1)}, bf16[32,16,128]{2,1,0:T(8,128)(2,1)S(1)}, u32[]{:S(2)}, u32[]{:S(2)}) collective-permute-start(bf16[32,16,128]{2,1,0:T(8,128)(2,1)S(1)} %get-tuple-element.99), channel_id=1, source_target_pairs={{0,16},{8,24},{16,0},{24,8},{1,17},{9,25},{17,1},{25,9},{2,18},{10... | collective-permute-start | bytes 393224 | tf_op jit(solution)/shard_map/ppermute | solution.py:293
  50.7 7.7 %collective-permute-start.19 = (bf16[32,16,128]{2,1,0:T(8,128)(2,1)S(1)}, bf16[32,16,128]{2,1,0:T(8,128)(2,1)S(1)}, u32[]{:S(2)}, u32[]{:S(2)}) collective-permute-start(bf16[32,16,128]{2,1,0:T(8,128)(2,1)S(1)} %get-tuple-element.100), channel_id=1, source_target_pairs={{0,24},{8,16},{16,8},{24,0},{1,25},{9,17},{17,9},{25,1},{2,26},{10... | collective-permute-start | bytes 393224 | tf_op jit(solution)/shard_map/ppermute | solution.py:293
  54.5 6.3 %collective-permute-start.25 = (bf16[32,16,128]{2,1,0:T(8,128)(2,1)S(1)}, bf16[32,16,128]{2,1,0:T(8,128)(2,1)S(1)}, u32[]{:S(2)}, u32[]{:S(2)}) collective-permute-start(bf16[32,16,128]{2,1,0:T(8,128)(2,1)S(1)} %get-tuple-element.106), channel_id=1, source_target_pairs={{0,8},{8,0},{16,24},{24,16},{1,9},{9,1},{17,25},{25,17},{2,10},{10... | collective-permute-start | bytes 393224 | tf_op jit(solution)/shard_map/ppermute | solution.py:293
  55.8 8.2 %collective-permute-start.26 = (bf16[32,16,128]{2,1,0:T(8,128)(2,1)S(1)}, bf16[32,16,128]{2,1,0:T(8,128)(2,1)S(1)}, u32[]{:S(2)}, u32[]{:S(2)}) collective-permute-start(bf16[32,16,128]{2,1,0:T(8,128)(2,1)S(1)} %get-tuple-element.107), channel_id=1, source_target_pairs={{0,16},{8,24},{16,0},{24,8},{1,17},{9,25},{17,1},{25,9},{2,18},{10... | collective-permute-start | bytes 393224 | tf_op jit(solution)/shard_map/ppermute | solution.py:293
  56.4 7.7 %collective-permute-start.27 = (bf16[32,16,128]{2,1,0:T(8,128)(2,1)S(1)}, bf16[32,16,128]{2,1,0:T(8,128)(2,1)S(1)}, u32[]{:S(2)}, u32[]{:S(2)}) collective-permute-start(bf16[32,16,128]{2,1,0:T(8,128)(2,1)S(1)} %get-tuple-element.108), channel_id=1, source_target_pairs={{0,24},{8,16},{16,8},{24,0},{1,25},{9,17},{17,9},{25,1},{2,26},{10... | collective-permute-start | bytes 393224 | tf_op jit(solution)/shard_map/ppermute | solution.py:293
  65.2 7.9 %collective-permute-start.31 = (bf16[24,32,128]{2,1,0:T(8,128)(2,1)S(1)}, bf16[24,32,128]{2,1,0:T(8,128)(2,1)S(1)}, u32[]{:S(2)}, u32[]{:S(2)}) collective-permute-start(bf16[24,32,128]{2,1,0:T(8,128)(2,1)S(1)} %get-tuple-element.114), channel_id=1, source_target_pairs={{0,8},{8,0},{16,24},{24,16},{1,9},{9,1},{17,25},{25,17},{2,10},{10... | collective-permute-start | bytes 589832 | tf_op jit(solution)/shard_map/ppermute | solution.py:293
  65.9 11.3 %collective-permute-start.32 = (bf16[24,32,128]{2,1,0:T(8,128)(2,1)S(1)}, bf16[24,32,128]{2,1,0:T(8,128)(2,1)S(1)}, u32[]{:S(2)}, u32[]{:S(2)}) collective-permute-start(bf16[24,32,128]{2,1,0:T(8,128)(2,1)S(1)} %get-tuple-element.115), channel_id=1, source_target_pairs={{0,16},{8,24},{16,0},{24,8},{1,17},{9,25},{17,1},{25,9},{2,18},{10... | collective-permute-start | bytes 589832 | tf_op jit(solution)/shard_map/ppermute | solution.py:293
  67.3 10.0 %collective-permute-start.33 = (bf16[24,32,128]{2,1,0:T(8,128)(2,1)S(1)}, bf16[24,32,128]{2,1,0:T(8,128)(2,1)S(1)}, u32[]{:S(2)}, u32[]{:S(2)}) collective-permute-start(bf16[24,32,128]{2,1,0:T(8,128)(2,1)S(1)} %get-tuple-element.116), channel_id=1, source_target_pairs={{0,24},{8,16},{16,8},{24,0},{1,25},{9,17},{17,9},{25,1},{2,26},{10... | collective-permute-start | bytes 589832 | tf_op jit(solution)/shard_map/ppermute | solution.py:293
  69.3 9.2 %collective-permute-start.28 = (bf16[8,32,128]{2,1,0:T(8,128)(2,1)S(1)}, bf16[8,32,128]{2,1,0:T(8,128)(2,1)S(1)}, u32[]{:S(2)}, u32[]{:S(2)}) collective-permute-start(bf16[8,32,128]{2,1,0:T(8,128)(2,1)S(1)} %get-tuple-element.110), channel_id=1, source_target_pairs={{0,8},{8,0},{16,24},{24,16},{1,9},{9,1},{17,25},{25,17},{2,10},{10... | collective-permute-start | bytes 196616 | tf_op jit(solution)/shard_map/ppermute | solution.py:293
  70.0 8.6 %collective-permute-start.29 = (bf16[8,32,128]{2,1,0:T(8,128)(2,1)S(1)}, bf16[8,32,128]{2,1,0:T(8,128)(2,1)S(1)}, u32[]{:S(2)}, u32[]{:S(2)}) collective-permute-start(bf16[8,32,128]{2,1,0:T(8,128)(2,1)S(1)} %get-tuple-element.111), channel_id=1, source_target_pairs={{0,16},{8,24},{16,0},{24,8},{1,17},{9,25},{17,1},{25,9},{2,18},{10... | collective-permute-start | bytes 196616 | tf_op jit(solution)/shard_map/ppermute | solution.py:293
  73.1 5.6 %collective-permute-start.30 = (bf16[8,32,128]{2,1,0:T(8,128)(2,1)S(1)}, bf16[8,32,128]{2,1,0:T(8,128)(2,1)S(1)}, u32[]{:S(2)}, u32[]{:S(2)}) collective-permute-start(bf16[8,32,128]{2,1,0:T(8,128)(2,1)S(1)} %get-tuple-element.112), channel_id=1, source_target_pairs={{0,24},{8,16},{16,8},{24,0},{1,25},{9,17},{17,9},{25,1},{2,26},{10... | collective-permute-start | bytes 196616 | tf_op jit(solution)/shard_map/ppermute | solution.py:293

commit v7 on v6

--- a/solution.py
+++ b/solution.py
@@ -182,8 +182,9 @@
                 ]
 
 
-def assemble_kernel(*refs):
-    ins, out = refs[:-1], refs[-1]
+def assemble_kernel(groups, *refs):
+    out = refs[-1]
+    ins = [part for d in range(groups) for part in refs[d:-1:groups]]
     at = 0
     for part in ins:
         out[:, at : at + part.shape[1], :] = part[...]
@@ -264,21 +265,22 @@
         first += count
 
 
-def final_kernel(groups, first, me_ref, *refs):
-    ins, out, scratch, sems = refs[:groups], refs[-3], refs[-2], refs[-1]
-    count, e_dev, orbitals = ins[0].shape
-    rows = orbitals // groups
+def final_kernel(groups, pieces, me_ref, *refs):
+    ins, out = refs[: len(pieces)], refs[-len(pieces) - 2]
+    scratch, sems = refs[-len(pieces) - 1 : -1], refs[-1]
     me = me_ref[0]
     copies = []
-    for d in range(groups):
+    for n, (d, first) in enumerate(pieces):
+        count, e_dev, orbitals = ins[n].shape
+        rows = orbitals // groups
         for i in range(count):
-            scratch[d, pl.ds(i, e_dev, stride=count), :] = ins[d][i].astype(F32)
+            scratch[n][pl.ds(i, e_dev, stride=count), :] = ins[n][i].astype(F32)
         start = pl.multiple_of((me ^ d) * rows + first, 8)
         copies.append(
             pltpu.make_async_copy(
-                scratch.at[d].reshape(e_dev, count, orbitals),
+                scratch[n].reshape(e_dev, count, orbitals),
                 out.at[:, pl.ds(start, count), :],
-                sems.at[d],
+                sems.at[n],
             )
         )
         copies[-1].start()
@@ -407,9 +409,9 @@
     far_pairs = [(b, ((b + 1) ^ 1) - 1) for b in range(1, peers) if ((b + 1) ^ 1) - 1 < peers]
     inter = []
     for h in range(halves):
-        parts = [chunk[d] for d in range(groups) for chunk in pol[h]]
+        parts = [part for chunk in pol[h] for part in chunk]
         own = call(
-            assemble_kernel,
+            functools.partial(assemble_kernel, groups),
             shape(lags, orbitals, orbitals),
             [vmem()] * len(parts),
             *parts,
@@ -448,22 +450,25 @@
             out_specs=[vmem()] * groups,
         )
         sigma.append((first, count, exchange(parts)))
+    pieces = [[(d, first, part) for d, part in enumerate(parts)] for first, _, parts in sigma]
+    if len(pieces) > 1:
+        pieces[-2].append(pieces[-1].pop(0))
     out = []
-    for first, count, parts in sigma:
+    for group in pieces:
         out = [
             call(
-                functools.partial(final_kernel, groups, first),
+                functools.partial(final_kernel, groups, [(d, first) for d, first, _ in group]),
                 shape(e_dev, orbitals, orbitals, dtype=F32),
-                [smem] + [vmem()] * groups + [hbm] * len(out),
+                [smem] + [vmem()] * len(group) + [hbm] * len(out),
                 me,
-                *parts,
+                *[part for _, _, part in group],
                 *out,
                 out_specs=hbm,
                 scratch=[
-                    pltpu.VMEM((groups, e_dev * count, orbitals), F32),
-                    pltpu.SemaphoreType.DMA((groups,)),
-                ],
-                input_output_aliases={1 + groups: 0} if out else {},
+                    pltpu.VMEM((e_dev * part.shape[0], orbitals), F32) for _, _, part in group
+                ]
+                + [pltpu.SemaphoreType.DMA((len(group),))],
+                input_output_aliases={1 + len(group): 0} if out else {},
             )
         ]
     return out[0].reshape(e_dev, 1, orbitals, orbitals)

time: 80 us -> 79.9 us (level)
  no operation moved by 1% of the time
where the time goes in v7:
time: 79.9 us; the launch traced here: 79.4 us
  starting transfers between devices  46.1 us (58%)
  waiting for transfers between devices  18.3 us (23%)
  Pallas kernels  14.9 us (19%)
    ppermute x30, starting transfers between devices, exchange(): lax.ppermute(parts[d], 'energy', [(i, i ^ d) for i in range(groups)])  38.8 us
    pallas_call x14, Pallas kernels, call(): pl.pallas_call(kernel, out_shape=out_shape, in_specs=specs, scratch_shape...  14.9 us
    ppermute x30, waiting for transfers between devices, exchange(): lax.ppermute(parts[d], 'energy', [(i, i ^ d) for i in range(groups)])  14.6 us
    ppermute x2, starting transfers between devices, shards(): far = lax.ppermute(own, 'block', far_pairs)  3.84 us
    ppermute x2, waiting for transfers between devices, shards(): far = lax.ppermute(own, 'block', far_pairs)  3.67 us
    ppermute x2, starting transfers between devices, shards(): near = lax.ppermute(own, 'block', near_pairs)  3.49 us
  transfers between devices with their start and end apart: 34, of which 14 were waited for; matrix products, arithmetic and copies ran while one was open for 0% of the time, Pallas kernels for 15%

profile of v7, /device:TPU:16, one launch (start us, length us, event | category | flops | bytes accessed | tf_op | source)
XLA Modules:
  0.0 79.4 jit_solution(13656070909014113068)
XLA Ops:
  0.0 1.3 %shard_map.84 = (bf16[32,32,128]{2,1,0:T(8,128)(2,1)S(1)}, bf16[32,32,128]{2,1,0:T(8,128)(2,1)S(1)}, bf16[32,32,128]{2,1,0:T(8,128)(2,1)S(1)}, bf16[32,32,128]{2,1,0:T(8,128)(2,1)S(1)}) custom-call(s32[1]{0:T(128)} %bitcast.me_ref, bf16[32,128,128]{2,1,0:T(8,128)(2,1)} %bitcast.11), custom_call_target="tpu_custom_call" | custom-call | tf_op jit(solution)/shard_map/pallas_call | solution.py:300
  1.3 1.6 %collective-permute-start = (bf16[32,32,128]{2,1,0:T(8,128)(2,1)S(1)}, bf16[32,32,128]{2,1,0:T(8,128)(2,1)S(1)}, u32[]{:S(2)}, u32[]{:S(2)}) collective-permute-start(bf16[32,32,128]{2,1,0:T(8,128)(2,1)S(1)} %get-tuple-element.69), channel_id=1, source_target_pairs={{0,8},{8,0},{16,24},{24,16},{1,9},{9,1},{17,25},{25,17},{2,10},{10... | collective-permute-start | bytes 786440 | tf_op jit(solution)/shard_map/ppermute | solution.py:295
  2.8 1.5 %collective-permute-start.1 = (bf16[32,32,128]{2,1,0:T(8,128)(2,1)S(1)}, bf16[32,32,128]{2,1,0:T(8,128)(2,1)S(1)}, u32[]{:S(2)}, u32[]{:S(2)}) collective-permute-start(bf16[32,32,128]{2,1,0:T(8,128)(2,1)S(1)} %get-tuple-element.70), channel_id=1, source_target_pairs={{0,16},{8,24},{16,0},{24,8},{1,17},{9,25},{17,1},{25,9},{2,18},{10... | collective-permute-start | bytes 786440 | tf_op jit(solution)/shard_map/ppermute | solution.py:295
  4.8 2.5 %shard_map.83 = (bf16[16,32,128]{2,1,0:T(8,128)(2,1)S(1)}, bf16[16,32,128]{2,1,0:T(8,128)(2,1)S(1)}, bf16[16,32,128]{2,1,0:T(8,128)(2,1)S(1)}, bf16[16,32,128]{2...) custom-call(s32[1]{0:T(128)} %bitcast.me_ref, ...), custom_call_target="tpu_custom_call" | custom-call | tf_op jit(solution)/shard_map/pallas_call | solution.py:300
  7.3 1.6 %collective-permute-start.3 = (bf16[16,32,128]{2,1,0:T(8,128)(2,1)S(1)}, bf16[16,32,128]{2,1,0:T(8,128)(2,1)S(1)}, u32[]{:S(2)}, u32[]{:S(2)}) collective-permute-start(bf16[16,32,128]{2,1,0:T(8,128)(2,1)S(1)} %get-tuple-element.78), channel_id=1, source_target_pairs={{0,8},{8,0},{16,24},{24,16},{1,9},{9,1},{17,25},{25,17},{2,10},{10... | collective-permute-start | bytes 393224 | tf_op jit(solution)/shard_map/ppermute | solution.py:295
  8.8 1.5 %collective-permute-start.4 = (bf16[16,32,128]{2,1,0:T(8,128)(2,1)S(1)}, bf16[16,32,128]{2,1,0:T(8,128)(2,1)S(1)}, u32[]{:S(2)}, u32[]{:S(2)}) collective-permute-start(bf16[16,32,128]{2,1,0:T(8,128)(2,1)S(1)} %get-tuple-element.79), channel_id=1, source_target_pairs={{0,16},{8,24},{16,0},{24,8},{1,17},{9,25},{17,1},{25,9},{2,18},{10... | collective-permute-start | bytes 393224 | tf_op jit(solution)/shard_map/ppermute | solution.py:295
  10.5 2.4 %collective-permute-start.5 = (bf16[16,32,128]{2,1,0:T(8,128)(2,1)S(1)}, bf16[16,32,128]{2,1,0:T(8,128)(2,1)S(1)}, u32[]{:S(2)}, u32[]{:S(2)}) collective-permute-start(bf16[16,32,128]{2,1,0:T(8,128)(2,1)S(1)} %get-tuple-element.80), channel_id=1, source_target_pairs={{0,24},{8,16},{16,8},{24,0},{1,25},{9,17},{17,9},{25,1},{2,26},{10... | collective-permute-start | bytes 393224 | tf_op jit(solution)/shard_map/ppermute | solution.py:295
  13.0 1.8 %shard_map.82 = (bf16[192,256]{1,0:T(8,128)(2,1)S(1)}, bf16[192,256]{1,0:T(8,128)(2,1)S(1)}, bf16[256,192]{1,0:T(8,128)(2,1)S(1)}, bf16[256,192]{1,0:T(8,128)(2,...) custom-call(s32[1]{0:T(128)} %bitcast.me_ref, s32[1]{0:T(128)} %bitcast.1.odd_ref, ...), custom_call_target="tpu_custom_call" | custom-call | tf_op jit(solution)/shard_map/pallas_call | solution.py:300
  14.7 2.3 %collective-permute-done.1.refs_2_ = bf16[32,32,128]{2,1,0:T(8,128)(2,1)S(1)} collective-permute-done((bf16[32,32,128]{2,1,0:T(8,128)(2,1)S(1)}, bf16[32,32,128]{2,1,0:T(8,128)(2,1)S(1)}, u32[]{:S(2)}, u32[]{:S(2)}) %collective-permute-start.1) | collective-permute-done | bytes 262176 | tf_op jit(solution)/shard_map/ppermute | solution.py:295
  17.2 1.7 %shard_map.85.less_ref = f32[192,4096]{1,0:T(8,128)S(1)} custom-call(bf16[192,256]{1,0:T(8,128)(2,1)S(1)} %get-tuple-element.67.fwd_ref, bf16[32,32,128]{2,1,0:T(8,128)(2,1)S(1)} %get-tuple-element.68.refs_0_, bf16[32,32,128]{2,1,0:T(8,128)(2,1)S(1)} %collective-permute-done.refs_1_, bf16[32,32,128]{2,1,0:T(8,128)(2,1)S(1)} %collective-permute-done.1.refs_2_, ...), custom_call_target="tpu_custom_call" | custom-call | tf_op jit(solution)/shard_map/pallas_call | solution.py:300
  18.9 1.6 %collective-permute-start.9 = (bf16[16,32,128]{2,1,0:T(8,128)(2,1)S(1)}, bf16[16,32,128]{2,1,0:T(8,128)(2,1)S(1)}, u32[]{:S(2)}, u32[]{:S(2)}) collective-permute-start(bf16[16,32,128]{2,1,0:T(8,128)(2,1)S(1)} %get-tuple-element.86), channel_id=1, source_target_pairs={{0,8},{8,0},{16,24},{24,16},{1,9},{9,1},{17,25},{25,17},{2,10},{10... | collective-permute-start | bytes 393224 | tf_op jit(solution)/shard_map/ppermute | solution.py:295
  20.4 1.5 %collective-permute-start.10 = (bf16[16,32,128]{2,1,0:T(8,128)(2,1)S(1)}, bf16[16,32,128]{2,1,0:T(8,128)(2,1)S(1)}, u32[]{:S(2)}, u32[]{:S(2)}) collective-permute-start(bf16[16,32,128]{2,1,0:T(8,128)(2,1)S(1)} %get-tuple-element.87), channel_id=1, source_target_pairs={{0,16},{8,24},{16,0},{24,8},{1,17},{9,25},{17,1},{25,9},{2,18},{10... | collective-permute-start | bytes 393224 | tf_op jit(solution)/shard_map/ppermute | solution.py:295
  21.9 1.4 %collective-permute-start.11 = (bf16[16,32,128]{2,1,0:T(8,128)(2,1)S(1)}, bf16[16,32,128]{2,1,0:T(8,128)(2,1)S(1)}, u32[]{:S(2)}, u32[]{:S(2)}) collective-permute-start(bf16[16,32,128]{2,1,0:T(8,128)(2,1)S(1)} %get-tuple-element.88), channel_id=1, source_target_pairs={{0,24},{8,16},{16,8},{24,0},{1,25},{9,17},{17,9},{25,1},{2,26},{10... | collective-permute-start | bytes 393224 | tf_op jit(solution)/shard_map/ppermute | solution.py:295
  23.3 0.9 %shard_map.86 = (bf16[16,16,128]{2,1,0:T(8,128)(2,1)S(1)}, bf16[16,16,128]{2,1,0:T(8,128)(2,1)S(1)}, bf16[16,16,128]{2,1,0:T(8,128)(2,1)S(1)}, bf16[16,16,128]{2...) custom-call(bf16[192,256]{1,0:T(8,128)(2,1)S(1)} %get-tuple-element., ...), custom_call_target="tpu_custom_call" | custom-call | tf_op jit(solution)/shard_map/pallas_call | solution.py:300
  24.2 1.0 %collective-permute-start.6 = (bf16[16,16,128]{2,1,0:T(8,128)(2,1)S(1)}, bf16[16,16,128]{2,1,0:T(8,128)(2,1)S(1)}, u32[]{:S(2)}, u32[]{:S(2)}) collective-permute-start(bf16[16,16,128]{2,1,0:T(8,128)(2,1)S(1)} %get-tuple-element.82), channel_id=1, source_target_pairs={{0,8},{8,0},{16,24},{24,16},{1,9},{9,1},{17,25},{25,17},{2,10},{10... | collective-permute-start | bytes 196616 | tf_op jit(solution)/shard_map/ppermute | solution.py:295
  25.2 1.6 %collective-permute-start.7 = (bf16[16,16,128]{2,1,0:T(8,128)(2,1)S(1)}, bf16[16,16,128]{2,1,0:T(8,128)(2,1)S(1)}, u32[]{:S(2)}, u32[]{:S(2)}) collective-permute-start(bf16[16,16,128]{2,1,0:T(8,128)(2,1)S(1)} %get-tuple-element.83), channel_id=1, source_target_pairs={{0,16},{8,24},{16,0},{24,8},{1,17},{9,25},{17,1},{25,9},{2,18},{10... | collective-permute-start | bytes 196616 | tf_op jit(solution)/shard_map/ppermute | solution.py:295
  26.9 1.4 %collective-permute-start.8 = (bf16[16,16,128]{2,1,0:T(8,128)(2,1)S(1)}, bf16[16,16,128]{2,1,0:T(8,128)(2,1)S(1)}, u32[]{:S(2)}, u32[]{:S(2)}) collective-permute-start(bf16[16,16,128]{2,1,0:T(8,128)(2,1)S(1)} %get-tuple-element.84), channel_id=1, source_target_pairs={{0,24},{8,16},{16,8},{24,0},{1,25},{9,17},{17,9},{25,1},{2,26},{10... | collective-permute-start | bytes 196616 | tf_op jit(solution)/shard_map/ppermute | solution.py:295
  28.8 0.9 %shard_map.87 = (bf16[16,16,128]{2,1,0:T(8,128)(2,1)S(1)}, bf16[16,16,128]{2,1,0:T(8,128)(2,1)S(1)}, bf16[16,16,128]{2,1,0:T(8,128)(2,1)S(1)}, bf16[16,16,128]{2...) custom-call(bf16[192,256]{1,0:T(8,128)(2,1)S(1)} %get-tuple-element., ...), custom_call_target="tpu_custom_call" | custom-call | tf_op jit(solution)/shard_map/pallas_call | solution.py:300
  29.7 1.7 %collective-permute-start.12 = (bf16[16,16,128]{2,1,0:T(8,128)(2,1)S(1)}, bf16[16,16,128]{2,1,0:T(8,128)(2,1)S(1)}, u32[]{:S(2)}, u32[]{:S(2)}) collective-permute-start(bf16[16,16,128]{2,1,0:T(8,128)(2,1)S(1)} %get-tuple-element.94), channel_id=1, source_target_pairs={{0,8},{8,0},{16,24},{24,16},{1,9},{9,1},{17,25},{25,17},{2,10},{10... | collective-permute-start | bytes 196616 | tf_op jit(solution)/shard_map/ppermute | solution.py:295
  32.1 1.2 %collective-permute-start.14 = (bf16[16,16,128]{2,1,0:T(8,128)(2,1)S(1)}, bf16[16,16,128]{2,1,0:T(8,128)(2,1)S(1)}, u32[]{:S(2)}, u32[]{:S(2)}) collective-permute-start(bf16[16,16,128]{2,1,0:T(8,128)(2,1)S(1)} %get-tuple-element.96), channel_id=1, source_target_pairs={{0,24},{8,16},{16,8},{24,0},{1,25},{9,17},{17,9},{25,1},{2,26},{10... | collective-permute-start | bytes 196616 | tf_op jit(solution)/shard_map/ppermute | solution.py:295
  33.3 1.6 %collective-permute-start.20 = (bf16[16,32,128]{2,1,0:T(8,128)(2,1)S(1)}, bf16[16,32,128]{2,1,0:T(8,128)(2,1)S(1)}, u32[]{:S(2)}, u32[]{:S(2)}) collective-permute-start(bf16[16,32,128]{2,1,0:T(8,128)(2,1)S(1)} %get-tuple-element.102), channel_id=1, source_target_pairs={{0,8},{8,0},{16,24},{24,16},{1,9},{9,1},{17,25},{25,17},{2,10},{10... | collective-permute-start | bytes 393224 | tf_op jit(solution)/shard_map/ppermute | solution.py:295
  34.9 0.7 collective-permute-start.21
  35.6 1.2 %collective-permute-start.22 = (bf16[16,32,128]{2,1,0:T(8,128)(2,1)S(1)}, bf16[16,32,128]{2,1,0:T(8,128)(2,1)S(1)}, u32[]{:S(2)}, u32[]{:S(2)}) collective-permute-start(bf16[16,32,128]{2,1,0:T(8,128)(2,1)S(1)} %get-tuple-element.104), channel_id=1, source_target_pairs={{0,24},{8,16},{16,8},{24,0},{1,25},{9,17},{17,9},{25,1},{2,26},{10... | collective-permute-start | bytes 393224 | tf_op jit(solution)/shard_map/ppermute | solution.py:295
  37.3 1.9 %collective-permute-start.16 = (bf16[16,128,128]{2,1,0:T(8,128)(2,1)S(1)}, bf16[16,128,128]{2,1,0:T(8,128)(2,1)S(1)}, u32[]{:S(2)}, u32[]{:S(2)}) collective-permute-start(bf16[16,128,128]{2,1,0:T(8,128)(2,1)S(1)} %shard_map.88.own), channel_id=1, source_target_pairs={{1,2},{2,1},{3,4},{4,3},{5,6},{6,5},{9,10},{10,9},{11,12},{12,11},... | collective-permute-start | bytes 1572872 | tf_op jit(solution)/shard_map/ppermute | solution.py:420
  39.2 1.7 %collective-permute-start.15 = (bf16[16,128,128]{2,1,0:T(8,128)(2,1)S(1)}, bf16[16,128,128]{2,1,0:T(8,128)(2,1)S(1)}, u32[]{:S(2)}, u32[]{:S(2)}) collective-permute-start(bf16[16,128,128]{2,1,0:T(8,128)(2,1)S(1)} %shard_map.88.own), channel_id=1, source_target_pairs={{0,1},{1,0},{2,3},{3,2},{4,5},{5,4},{6,7},{7,6},{8,9},{9,8},{10,11... | collective-permute-start | bytes 1572872 | tf_op jit(solution)/shard_map/ppermute | solution.py:421
  41.5 1.9 %collective-permute-start.24 = (bf16[16,128,128]{2,1,0:T(8,128)(2,1)S(1)}, bf16[16,128,128]{2,1,0:T(8,128)(2,1)S(1)}, u32[]{:S(2)}, u32[]{:S(2)}) collective-permute-start(bf16[16,128,128]{2,1,0:T(8,128)(2,1)S(1)} %shard_map.90.own), channel_id=1, source_target_pairs={{1,2},{2,1},{3,4},{4,3},{5,6},{6,5},{9,10},{10,9},{11,12},{12,11},... | collective-permute-start | bytes 1572872 | tf_op jit(solution)/shard_map/ppermute | solution.py:420
  43.4 1.7 %collective-permute-start.23 = (bf16[16,128,128]{2,1,0:T(8,128)(2,1)S(1)}, bf16[16,128,128]{2,1,0:T(8,128)(2,1)S(1)}, u32[]{:S(2)}, u32[]{:S(2)}) collective-permute-start(bf16[16,128,128]{2,1,0:T(8,128)(2,1)S(1)} %shard_map.90.own), channel_id=1, source_target_pairs={{0,1},{1,0},{2,3},{3,2},{4,5},{5,4},{6,7},{7,6},{8,9},{9,8},{10,11... | collective-permute-start | bytes 1572872 | tf_op jit(solution)/shard_map/ppermute | solution.py:421
  45.2 2.6 %collective-permute-done.16.far = bf16[16,128,128]{2,1,0:T(8,128)(2,1)S(1)} collective-permute-done((bf16[16,128,128]{2,1,0:T(8,128)(2,1)S(1)}, bf16[16,128,128]{2,1,0:T(8,128)(2,1)S(1)}, u32[]{:S(2)}, u32[]{:S(2)}) %collective-permute-start.16) | collective-permute-done | bytes 524320 | tf_op jit(solution)/shard_map/ppermute | solution.py:420
  47.8 1.0 %shard_map.89 = (bf16[32,16,128]{2,1,0:T(8,128)(2,1)S(1)}, bf16[32,16,128]{2,1,0:T(8,128)(2,1)S(1)}, bf16[32,16,128]{2,1,0:T(8,128)(2,1)S(1)}, bf16[32,16,128]{2,1,0:T(8,128)(2,1)S(1)}) custom-call(s32[1]{0:T(128)} %bitcast.me_ref, bf16[128,384]{1,0:T(8,128)(2,1)S(1)} %get-tuple-element.73.left, bf16[256,256]{1,0:T(8,128)(2,1)S(1)} %get-tuple-element.74.pair_right, ...), custom_call_target="tpu_custom_call" | custom-call | tf_op jit(solution)/shard_map/pallas_call | solution.py:300
  48.8 1.4 %collective-permute-start.17 = (bf16[32,16,128]{2,1,0:T(8,128)(2,1)S(1)}, bf16[32,16,128]{2,1,0:T(8,128)(2,1)S(1)}, u32[]{:S(2)}, u32[]{:S(2)}) collective-permute-start(bf16[32,16,128]{2,1,0:T(8,128)(2,1)S(1)} %get-tuple-element.98), channel_id=1, source_target_pairs={{0,8},{8,0},{16,24},{24,16},{1,9},{9,1},{17,25},{25,17},{2,10},{10... | collective-permute-start | bytes 393224 | tf_op jit(solution)/shard_map/ppermute | solution.py:295
  50.7 1.7 %collective-permute-start.19 = (bf16[32,16,128]{2,1,0:T(8,128)(2,1)S(1)}, bf16[32,16,128]{2,1,0:T(8,128)(2,1)S(1)}, u32[]{:S(2)}, u32[]{:S(2)}) collective-permute-start(bf16[32,16,128]{2,1,0:T(8,128)(2,1)S(1)} %get-tuple-element.100), channel_id=1, source_target_pairs={{0,24},{8,16},{16,8},{24,0},{1,25},{9,17},{17,9},{25,1},{2,26},{10... | collective-permute-start | bytes 393224 | tf_op jit(solution)/shard_map/ppermute | solution.py:295
  52.4 1.0 %collective-permute-done.24.far = bf16[16,128,128]{2,1,0:T(8,128)(2,1)S(1)} collective-permute-done((bf16[16,128,128]{2,1,0:T(8,128)(2,1)S(1)}, bf16[16,128,128]{2,1,0:T(8,128)(2,1)S(1)}, u32[]{:S(2)}, u32[]{:S(2)}) %collective-permute-start.24) | collective-permute-done | bytes 524320 | tf_op jit(solution)/shard_map/ppermute | solution.py:420
  53.4 1.0 %shard_map.91 = (bf16[32,16,128]{2,1,0:T(8,128)(2,1)S(1)}, bf16[32,16,128]{2,1,0:T(8,128)(2,1)S(1)}, bf16[32,16,128]{2,1,0:T(8,128)(2,1)S(1)}, bf16[32,16,128]{2,1,0:T(8,128)(2,1)S(1)}) custom-call(s32[1]{0:T(128)} %bitcast.me_ref, bf16[128,384]{1,0:T(8,128)(2,1)S(1)} %get-tuple-element.73.left, bf16[256,256]{1,0:T(8,128)(2,1)S(1)} %get-tuple-element.74.pair_right, ...), custom_call_target="tpu_custom_call" | custom-call | tf_op jit(solution)/shard_map/pallas_call | solution.py:300
  54.5 1.4 %collective-permute-start.25 = (bf16[32,16,128]{2,1,0:T(8,128)(2,1)S(1)}, bf16[32,16,128]{2,1,0:T(8,128)(2,1)S(1)}, u32[]{:S(2)}, u32[]{:S(2)}) collective-permute-start(bf16[32,16,128]{2,1,0:T(8,128)(2,1)S(1)} %get-tuple-element.106), channel_id=1, source_target_pairs={{0,8},{8,0},{16,24},{24,16},{1,9},{9,1},{17,25},{25,17},{2,10},{10... | collective-permute-start | bytes 393224 | tf_op jit(solution)/shard_map/ppermute | solution.py:295
  56.4 1.7 %collective-permute-start.27 = (bf16[32,16,128]{2,1,0:T(8,128)(2,1)S(1)}, bf16[32,16,128]{2,1,0:T(8,128)(2,1)S(1)}, u32[]{:S(2)}, u32[]{:S(2)}) collective-permute-start(bf16[32,16,128]{2,1,0:T(8,128)(2,1)S(1)} %get-tuple-element.108), channel_id=1, source_target_pairs={{0,24},{8,16},{16,8},{24,0},{1,25},{9,17},{17,9},{25,1},{2,26},{10... | collective-permute-start | bytes 393224 | tf_op jit(solution)/shard_map/ppermute | solution.py:295
  58.4 2.4 %collective-permute-done.25.refs_5_ = bf16[32,16,128]{2,1,0:T(8,128)(2,1)S(1)} collective-permute-done((bf16[32,16,128]{2,1,0:T(8,128)(2,1)S(1)}, bf16[32,16,128]{2,1,0:T(8,128)(2,1)S(1)}, u32[]{:S(2)}, u32[]{:S(2)}) %collective-permute-start.25) | collective-permute-done | bytes 131104 | tf_op jit(solution)/shard_map/ppermute | solution.py:295
  60.8 3.2 %collective-permute-done.26.refs_6_ = bf16[32,16,128]{2,1,0:T(8,128)(2,1)S(1)} collective-permute-done((bf16[32,16,128]{2,1,0:T(8,128)(2,1)S(1)}, bf16[32,16,128]{2,1,0:T(8,128)(2,1)S(1)}, u32[]{:S(2)}, u32[]{:S(2)}) %collective-permute-start.26) | collective-permute-done | bytes 131104 | tf_op jit(solution)/shard_map/ppermute | solution.py:295
  64.0 1.1 %shard_map.93 = (bf16[24,32,128]{2,1,0:T(8,128)(2,1)S(1)}, bf16[24,32,128]{2,1,0:T(8,128)(2,1)S(1)}, bf16[24,32,128]{2,1,0:T(8,128)(2,1)S(1)}, bf16[24,32,128]{2,1,0:T(8,128)(2,1)S(1)}) custom-call(bf16[192,256]{1,0:T(8,128)(2,1)S(1)} %get-tuple-element.61.fwd_l_ref, bf16[256,192]{1,0:T(8,128)(2,1)S(1)} %get-tuple-element.62.back_ref, ...), custom_call_target="tpu_custom_call" | custom-call | tf_op jit(solution)/shard_map/pallas_call | solution.py:300
  65.2 0.8 collective-permute-start.31
  65.9 1.3 %collective-permute-start.32 = (bf16[24,32,128]{2,1,0:T(8,128)(2,1)S(1)}, bf16[24,32,128]{2,1,0:T(8,128)(2,1)S(1)}, u32[]{:S(2)}, u32[]{:S(2)}) collective-permute-start(bf16[24,32,128]{2,1,0:T(8,128)(2,1)S(1)} %get-tuple-element.114), channel_id=1, source_target_pairs={{0,16},{8,24},{16,0},{24,8},{1,17},{9,25},{17,1},{25,9},{2,18},{10... | collective-permute-start | bytes 589832 | tf_op jit(solution)/shard_map/ppermute | solution.py:295
  67.3 1.5 %collective-permute-start.33 = (bf16[24,32,128]{2,1,0:T(8,128)(2,1)S(1)}, bf16[24,32,128]{2,1,0:T(8,128)(2,1)S(1)}, u32[]{:S(2)}, u32[]{:S(2)}) collective-permute-start(bf16[24,32,128]{2,1,0:T(8,128)(2,1)S(1)} %get-tuple-element.115), channel_id=1, source_target_pairs={{0,24},{8,16},{16,8},{24,0},{1,25},{9,17},{17,9},{25,1},{2,26},{10... | collective-permute-start | bytes 589832 | tf_op jit(solution)/shard_map/ppermute | solution.py:295
  69.3 0.8 collective-permute-start.28
  70.0 1.3 %collective-permute-start.29 = (bf16[8,32,128]{2,1,0:T(8,128)(2,1)S(1)}, bf16[8,32,128]{2,1,0:T(8,128)(2,1)S(1)}, u32[]{:S(2)}, u32[]{:S(2)}) collective-permute-start(bf16[8,32,128]{2,1,0:T(8,128)(2,1)S(1)} %get-tuple-element.110), channel_id=1, source_target_pairs={{0,16},{8,24},{16,0},{24,8},{1,17},{9,25},{17,1},{25,9},{2,18},{10... | collective-permute-start | bytes 196616 | tf_op jit(solution)/shard_map/ppermute | solution.py:295
  71.4 1.7 %collective-permute-done.31.refs_1_ = bf16[24,32,128]{2,1,0:T(8,128)(2,1)S(1)} collective-permute-done((bf16[24,32,128]{2,1,0:T(8,128)(2,1)S(1)}, bf16[24,32,128]{2,1,0:T(8,128)(2,1)S(1)}, u32[]{:S(2)}, u32[]{:S(2)}) %collective-permute-start.31) | collective-permute-done | bytes 196640 | tf_op jit(solution)/shard_map/ppermute | solution.py:295
  73.1 1.5 %collective-permute-start.30 = (bf16[8,32,128]{2,1,0:T(8,128)(2,1)S(1)}, bf16[8,32,128]{2,1,0:T(8,128)(2,1)S(1)}, u32[]{:S(2)}, u32[]{:S(2)}) collective-permute-start(bf16[8,32,128]{2,1,0:T(8,128)(2,1)S(1)} %get-tuple-element.111), channel_id=1, source_target_pairs={{0,24},{8,16},{16,8},{24,0},{1,25},{9,17},{17,9},{25,1},{2,26},{10... | collective-permute-start | bytes 196616 | tf_op jit(solution)/shard_map/ppermute | solution.py:295
  74.5 2.7 %collective-permute-done.32.refs_2_ = bf16[24,32,128]{2,1,0:T(8,128)(2,1)S(1)} collective-permute-done((bf16[24,32,128]{2,1,0:T(8,128)(2,1)S(1)}, bf16[24,32,128]{2,1,0:T(8,128)(2,1)S(1)}, u32[]{:S(2)}, u32[]{:S(2)}) %collective-permute-start.32) | collective-permute-done | bytes 196640 | tf_op jit(solution)/shard_map/ppermute | solution.py:295
  77.2 1.3 %shard_map.94.refs_3_ = f32[32,128,128]{2,1,0:T(8,128)} custom-call(s32[1]{0:T(128)} %bitcast.me_ref, bf16[24,32,128]{2,1,0:T(8,128)(2,1)S(1)} %get-tuple-element.112.refs_0_, bf16[24,32,128]{2,1,0:T(8,128)(2,1)S(1)} %collective-permute-done.31.refs_1_, bf16[24,32,128]{2,1,0:T(8,128)(2,1)S(1)} %collective-permute-done.32.refs_2_, ...), custom_call_target="tpu_custom_call" | custom-call | tf_op jit(solution)/shard_map/pallas_call | solution.py:300
  78.6 0.8 shard_map.95
  (38 shorter events, 5.1 us)
Async XLA Ops:
  0.0 13.0 %copy-start.1 = (s32[1,2]{1,0:T(1,128)S(1)}, s32[1,2]{1,0:T(1,128)}, u32[]{:S(2)}) copy-start(s32[1,2]{1,0:T(1,128)} %param.11) | copy-start | bytes 28
  0.0 13.0 %copy-start = (bf16[1,3,128,128]{3,2,1,0:T(8,128)(2,1)S(1)}, bf16[1,3,128,128]{3,2,1,0:T(8,128)(2,1)}, u32[]{:S(2)}) copy-start(bf16[1,3,128,128]{3,2,1,0:T(8,128)(2,1)} %param.10) | copy-start | bytes 294916
  1.3 9.3 %collective-permute-start = (bf16[32,32,128]{2,1,0:T(8,128)(2,1)S(1)}, bf16[32,32,128]{2,1,0:T(8,128)(2,1)S(1)}, u32[]{:S(2)}, u32[]{:S(2)}) collective-permute-start(bf16[32,32,128]{2,1,0:T(8,128)(2,1)S(1)} %get-tuple-element.69), channel_id=1, source_target_pairs={{0,8},{8,0},{16,24},{24,16},{1,9},{9,1},{17,25},{25,17},{2,10},{10... | collective-permute-start | bytes 786440 | tf_op jit(solution)/shard_map/ppermute | solution.py:295
  2.8 14.2 %collective-permute-start.1 = (bf16[32,32,128]{2,1,0:T(8,128)(2,1)S(1)}, bf16[32,32,128]{2,1,0:T(8,128)(2,1)S(1)}, u32[]{:S(2)}, u32[]{:S(2)}) collective-permute-start(bf16[32,32,128]{2,1,0:T(8,128)(2,1)S(1)} %get-tuple-element.70), channel_id=1, source_target_pairs={{0,16},{8,24},{16,0},{24,8},{1,17},{9,25},{17,1},{25,9},{2,18},{10... | collective-permute-start | bytes 786440 | tf_op jit(solution)/shard_map/ppermute | solution.py:295
  4.3 12.8 %collective-permute-start.2 = (bf16[32,32,128]{2,1,0:T(8,128)(2,1)S(1)}, bf16[32,32,128]{2,1,0:T(8,128)(2,1)S(1)}, u32[]{:S(2)}, u32[]{:S(2)}) collective-permute-start(bf16[32,32,128]{2,1,0:T(8,128)(2,1)S(1)} %get-tuple-element.71), channel_id=1, source_target_pairs={{0,24},{8,16},{16,8},{24,0},{1,25},{9,17},{17,9},{25,1},{2,26},{10... | collective-permute-start | bytes 786440 | tf_op jit(solution)/shard_map/ppermute | solution.py:295
  7.3 14.6 %collective-permute-start.3 = (bf16[16,32,128]{2,1,0:T(8,128)(2,1)S(1)}, bf16[16,32,128]{2,1,0:T(8,128)(2,1)S(1)}, u32[]{:S(2)}, u32[]{:S(2)}) collective-permute-start(bf16[16,32,128]{2,1,0:T(8,128)(2,1)S(1)} %get-tuple-element.78), channel_id=1, source_target_pairs={{0,8},{8,0},{16,24},{24,16},{1,9},{9,1},{17,25},{25,17},{2,10},{10... | collective-permute-start | bytes 393224 | tf_op jit(solution)/shard_map/ppermute | solution.py:295
  8.8 14.4 %collective-permute-start.4 = (bf16[16,32,128]{2,1,0:T(8,128)(2,1)S(1)}, bf16[16,32,128]{2,1,0:T(8,128)(2,1)S(1)}, u32[]{:S(2)}, u32[]{:S(2)}) collective-permute-start(bf16[16,32,128]{2,1,0:T(8,128)(2,1)S(1)} %get-tuple-element.79), channel_id=1, source_target_pairs={{0,16},{8,24},{16,0},{24,8},{1,17},{9,25},{17,1},{25,9},{2,18},{10... | collective-permute-start | bytes 393224 | tf_op jit(solution)/shard_map/ppermute | solution.py:295
  10.5 12.8 %collective-permute-start.5 = (bf16[16,32,128]{2,1,0:T(8,128)(2,1)S(1)}, bf16[16,32,128]{2,1,0:T(8,128)(2,1)S(1)}, u32[]{:S(2)}, u32[]{:S(2)}) collective-permute-start(bf16[16,32,128]{2,1,0:T(8,128)(2,1)S(1)} %get-tuple-element.80), channel_id=1, source_target_pairs={{0,24},{8,16},{16,8},{24,0},{1,25},{9,17},{17,9},{25,1},{2,26},{10... | collective-permute-start | bytes 393224 | tf_op jit(solution)/shard_map/ppermute | solution.py:295
  18.9 8.0 %collective-permute-start.9 = (bf16[16,32,128]{2,1,0:T(8,128)(2,1)S(1)}, bf16[16,32,128]{2,1,0:T(8,128)(2,1)S(1)}, u32[]{:S(2)}, u32[]{:S(2)}) collective-permute-start(bf16[16,32,128]{2,1,0:T(8,128)(2,1)S(1)} %get-tuple-element.86), channel_id=1, source_target_pairs={{0,8},{8,0},{16,24},{24,16},{1,9},{9,1},{17,25},{25,17},{2,10},{10... | collective-permute-start | bytes 393224 | tf_op jit(solution)/shard_map/ppermute | solution.py:295
  20.4 8.3 %collective-permute-start.10 = (bf16[16,32,128]{2,1,0:T(8,128)(2,1)S(1)}, bf16[16,32,128]{2,1,0:T(8,128)(2,1)S(1)}, u32[]{:S(2)}, u32[]{:S(2)}) collective-permute-start(bf16[16,32,128]{2,1,0:T(8,128)(2,1)S(1)} %get-tuple-element.87), channel_id=1, source_target_pairs={{0,16},{8,24},{16,0},{24,8},{1,17},{9,25},{17,1},{25,9},{2,18},{10... | collective-permute-start | bytes 393224 | tf_op jit(solution)/shard_map/ppermute | solution.py:295
  21.9 6.9 %collective-permute-start.11 = (bf16[16,32,128]{2,1,0:T(8,128)(2,1)S(1)}, bf16[16,32,128]{2,1,0:T(8,128)(2,1)S(1)}, u32[]{:S(2)}, u32[]{:S(2)}) collective-permute-start(bf16[16,32,128]{2,1,0:T(8,128)(2,1)S(1)} %get-tuple-element.88), channel_id=1, source_target_pairs={{0,24},{8,16},{16,8},{24,0},{1,25},{9,17},{17,9},{25,1},{2,26},{10... | collective-permute-start | bytes 393224 | tf_op jit(solution)/shard_map/ppermute | solution.py:295
  24.2 7.9 %collective-permute-start.6 = (bf16[16,16,128]{2,1,0:T(8,128)(2,1)S(1)}, bf16[16,16,128]{2,1,0:T(8,128)(2,1)S(1)}, u32[]{:S(2)}, u32[]{:S(2)}) collective-permute-start(bf16[16,16,128]{2,1,0:T(8,128)(2,1)S(1)} %get-tuple-element.82), channel_id=1, source_target_pairs={{0,8},{8,0},{16,24},{24,16},{1,9},{9,1},{17,25},{25,17},{2,10},{10... | collective-permute-start | bytes 196616 | tf_op jit(solution)/shard_map/ppermute | solution.py:295
  25.2 8.0 %collective-permute-start.7 = (bf16[16,16,128]{2,1,0:T(8,128)(2,1)S(1)}, bf16[16,16,128]{2,1,0:T(8,128)(2,1)S(1)}, u32[]{:S(2)}, u32[]{:S(2)}) collective-permute-start(bf16[16,16,128]{2,1,0:T(8,128)(2,1)S(1)} %get-tuple-element.83), channel_id=1, source_target_pairs={{0,16},{8,24},{16,0},{24,8},{1,17},{9,25},{17,1},{25,9},{2,18},{10... | collective-permute-start | bytes 196616 | tf_op jit(solution)/shard_map/ppermute | solution.py:295
  26.9 8.0 %collective-permute-start.8 = (bf16[16,16,128]{2,1,0:T(8,128)(2,1)S(1)}, bf16[16,16,128]{2,1,0:T(8,128)(2,1)S(1)}, u32[]{:S(2)}, u32[]{:S(2)}) collective-permute-start(bf16[16,16,128]{2,1,0:T(8,128)(2,1)S(1)} %get-tuple-element.84), channel_id=1, source_target_pairs={{0,24},{8,16},{16,8},{24,0},{1,25},{9,17},{17,9},{25,1},{2,26},{10... | collective-permute-start | bytes 196616 | tf_op jit(solution)/shard_map/ppermute | solution.py:295
  29.7 5.9 %collective-permute-start.12 = (bf16[16,16,128]{2,1,0:T(8,128)(2,1)S(1)}, bf16[16,16,128]{2,1,0:T(8,128)(2,1)S(1)}, u32[]{:S(2)}, u32[]{:S(2)}) collective-permute-start(bf16[16,16,128]{2,1,0:T(8,128)(2,1)S(1)} %get-tuple-element.94), channel_id=1, source_target_pairs={{0,8},{8,0},{16,24},{24,16},{1,9},{9,1},{17,25},{25,17},{2,10},{10... | collective-permute-start | bytes 196616 | tf_op jit(solution)/shard_map/ppermute | solution.py:295
  31.4 5.4 %collective-permute-start.13 = (bf16[16,16,128]{2,1,0:T(8,128)(2,1)S(1)}, bf16[16,16,128]{2,1,0:T(8,128)(2,1)S(1)}, u32[]{:S(2)}, u32[]{:S(2)}) collective-permute-start(bf16[16,16,128]{2,1,0:T(8,128)(2,1)S(1)} %get-tuple-element.95), channel_id=1, source_target_pairs={{0,16},{8,24},{16,0},{24,8},{1,17},{9,25},{17,1},{25,9},{2,18},{10... | collective-permute-start | bytes 196616 | tf_op jit(solution)/shard_map/ppermute | solution.py:295
  32.1 5.2 %collective-permute-start.14 = (bf16[16,16,128]{2,1,0:T(8,128)(2,1)S(1)}, bf16[16,16,128]{2,1,0:T(8,128)(2,1)S(1)}, u32[]{:S(2)}, u32[]{:S(2)}) collective-permute-start(bf16[16,16,128]{2,1,0:T(8,128)(2,1)S(1)} %get-tuple-element.96), channel_id=1, source_target_pairs={{0,24},{8,16},{16,8},{24,0},{1,25},{9,17},{17,9},{25,1},{2,26},{10... | collective-permute-start | bytes 196616 | tf_op jit(solution)/shard_map/ppermute | solution.py:295
  33.3 7.7 %collective-permute-start.20 = (bf16[16,32,128]{2,1,0:T(8,128)(2,1)S(1)}, bf16[16,32,128]{2,1,0:T(8,128)(2,1)S(1)}, u32[]{:S(2)}, u32[]{:S(2)}) collective-permute-start(bf16[16,32,128]{2,1,0:T(8,128)(2,1)S(1)} %get-tuple-element.102), channel_id=1, source_target_pairs={{0,8},{8,0},{16,24},{24,16},{1,9},{9,1},{17,25},{25,17},{2,10},{10... | collective-permute-start | bytes 393224 | tf_op jit(solution)/shard_map/ppermute | solution.py:295
  34.9 6.1 %collective-permute-start.21 = (bf16[16,32,128]{2,1,0:T(8,128)(2,1)S(1)}, bf16[16,32,128]{2,1,0:T(8,128)(2,1)S(1)}, u32[]{:S(2)}, u32[]{:S(2)}) collective-permute-start(bf16[16,32,128]{2,1,0:T(8,128)(2,1)S(1)} %get-tuple-element.103), channel_id=1, source_target_pairs={{0,16},{8,24},{16,0},{24,8},{1,17},{9,25},{17,1},{25,9},{2,18},{10... | collective-permute-start | bytes 393224 | tf_op jit(solution)/shard_map/ppermute | solution.py:295
  35.6 5.9 %collective-permute-start.22 = (bf16[16,32,128]{2,1,0:T(8,128)(2,1)S(1)}, bf16[16,32,128]{2,1,0:T(8,128)(2,1)S(1)}, u32[]{:S(2)}, u32[]{:S(2)}) collective-permute-start(bf16[16,32,128]{2,1,0:T(8,128)(2,1)S(1)} %get-tuple-element.104), channel_id=1, source_target_pairs={{0,24},{8,16},{16,8},{24,0},{1,25},{9,17},{17,9},{25,1},{2,26},{10... | collective-permute-start | bytes 393224 | tf_op jit(solution)/shard_map/ppermute | solution.py:295
  37.3 10.5 %collective-permute-start.16 = (bf16[16,128,128]{2,1,0:T(8,128)(2,1)S(1)}, bf16[16,128,128]{2,1,0:T(8,128)(2,1)S(1)}, u32[]{:S(2)}, u32[]{:S(2)}) collective-permute-start(bf16[16,128,128]{2,1,0:T(8,128)(2,1)S(1)} %shard_map.88.own), channel_id=1, source_target_pairs={{1,2},{2,1},{3,4},{4,3},{5,6},{6,5},{9,10},{10,9},{11,12},{12,11},... | collective-permute-start | bytes 1572872 | tf_op jit(solution)/shard_map/ppermute | solution.py:420
  39.2 8.6 %collective-permute-start.15 = (bf16[16,128,128]{2,1,0:T(8,128)(2,1)S(1)}, bf16[16,128,128]{2,1,0:T(8,128)(2,1)S(1)}, u32[]{:S(2)}, u32[]{:S(2)}) collective-permute-start(bf16[16,128,128]{2,1,0:T(8,128)(2,1)S(1)} %shard_map.88.own), channel_id=1, source_target_pairs={{0,1},{1,0},{2,3},{3,2},{4,5},{5,4},{6,7},{7,6},{8,9},{9,8},{10,11... | collective-permute-start | bytes 1572872 | tf_op jit(solution)/shard_map/ppermute | solution.py:421
  41.5 11.9 %collective-permute-start.24 = (bf16[16,128,128]{2,1,0:T(8,128)(2,1)S(1)}, bf16[16,128,128]{2,1,0:T(8,128)(2,1)S(1)}, u32[]{:S(2)}, u32[]{:S(2)}) collective-permute-start(bf16[16,128,128]{2,1,0:T(8,128)(2,1)S(1)} %shard_map.90.own), channel_id=1, source_target_pairs={{1,2},{2,1},{3,4},{4,3},{5,6},{6,5},{9,10},{10,9},{11,12},{12,11},... | collective-permute-start | bytes 1572872 | tf_op jit(solution)/shard_map/ppermute | solution.py:420
  43.4 10.0 %collective-permute-start.23 = (bf16[16,128,128]{2,1,0:T(8,128)(2,1)S(1)}, bf16[16,128,128]{2,1,0:T(8,128)(2,1)S(1)}, u32[]{:S(2)}, u32[]{:S(2)}) collective-permute-start(bf16[16,128,128]{2,1,0:T(8,128)(2,1)S(1)} %shard_map.90.own), channel_id=1, source_target_pairs={{0,1},{1,0},{2,3},{3,2},{4,5},{5,4},{6,7},{7,6},{8,9},{9,8},{10,11... | collective-permute-start | bytes 1572872 | tf_op jit(solution)/shard_map/ppermute | solution.py:421
  48.8 7.5 %collective-permute-start.17 = (bf16[32,16,128]{2,1,0:T(8,128)(2,1)S(1)}, bf16[32,16,128]{2,1,0:T(8,128)(2,1)S(1)}, u32[]{:S(2)}, u32[]{:S(2)}) collective-permute-start(bf16[32,16,128]{2,1,0:T(8,128)(2,1)S(1)} %get-tuple-element.98), channel_id=1, source_target_pairs={{0,8},{8,0},{16,24},{24,16},{1,9},{9,1},{17,25},{25,17},{2,10},{10... | collective-permute-start | bytes 393224 | tf_op jit(solution)/shard_map/ppermute | solution.py:295
  50.2 8.2 %collective-permute-start.18 = (bf16[32,16,128]{2,1,0:T(8,128)(2,1)S(1)}, bf16[32,16,128]{2,1,0:T(8,128)(2,1)S(1)}, u32[]{:S(2)}, u32[]{:S(2)}) collective-permute-start(bf16[32,16,128]{2,1,0:T(8,128)(2,1)S(1)} %get-tuple-element.99), channel_id=1, source_target_pairs={{0,16},{8,24},{16,0},{24,8},{1,17},{9,25},{17,1},{25,9},{2,18},{10... | collective-permute-start | bytes 393224 | tf_op jit(solution)/shard_map/ppermute | solution.py:295
  50.7 7.7 %collective-permute-start.19 = (bf16[32,16,128]{2,1,0:T(8,128)(2,1)S(1)}, bf16[32,16,128]{2,1,0:T(8,128)(2,1)S(1)}, u32[]{:S(2)}, u32[]{:S(2)}) collective-permute-start(bf16[32,16,128]{2,1,0:T(8,128)(2,1)S(1)} %get-tuple-element.100), channel_id=1, source_target_pairs={{0,24},{8,16},{16,8},{24,0},{1,25},{9,17},{17,9},{25,1},{2,26},{10... | collective-permute-start | bytes 393224 | tf_op jit(solution)/shard_map/ppermute | solution.py:295
  54.5 6.3 %collective-permute-start.25 = (bf16[32,16,128]{2,1,0:T(8,128)(2,1)S(1)}, bf16[32,16,128]{2,1,0:T(8,128)(2,1)S(1)}, u32[]{:S(2)}, u32[]{:S(2)}) collective-permute-start(bf16[32,16,128]{2,1,0:T(8,128)(2,1)S(1)} %get-tuple-element.106), channel_id=1, source_target_pairs={{0,8},{8,0},{16,24},{24,16},{1,9},{9,1},{17,25},{25,17},{2,10},{10... | collective-permute-start | bytes 393224 | tf_op jit(solution)/shard_map/ppermute | solution.py:295
  55.8 8.2 %collective-permute-start.26 = (bf16[32,16,128]{2,1,0:T(8,128)(2,1)S(1)}, bf16[32,16,128]{2,1,0:T(8,128)(2,1)S(1)}, u32[]{:S(2)}, u32[]{:S(2)}) collective-permute-start(bf16[32,16,128]{2,1,0:T(8,128)(2,1)S(1)} %get-tuple-element.107), channel_id=1, source_target_pairs={{0,16},{8,24},{16,0},{24,8},{1,17},{9,25},{17,1},{25,9},{2,18},{10... | collective-permute-start | bytes 393224 | tf_op jit(solution)/shard_map/ppermute | solution.py:295
  56.4 7.7 %collective-permute-start.27 = (bf16[32,16,128]{2,1,0:T(8,128)(2,1)S(1)}, bf16[32,16,128]{2,1,0:T(8,128)(2,1)S(1)}, u32[]{:S(2)}, u32[]{:S(2)}) collective-permute-start(bf16[32,16,128]{2,1,0:T(8,128)(2,1)S(1)} %get-tuple-element.108), channel_id=1, source_target_pairs={{0,24},{8,16},{16,8},{24,0},{1,25},{9,17},{17,9},{25,1},{2,26},{10... | collective-permute-start | bytes 393224 | tf_op jit(solution)/shard_map/ppermute | solution.py:295
  65.2 7.9 %collective-permute-start.31 = (bf16[24,32,128]{2,1,0:T(8,128)(2,1)S(1)}, bf16[24,32,128]{2,1,0:T(8,128)(2,1)S(1)}, u32[]{:S(2)}, u32[]{:S(2)}) collective-permute-start(bf16[24,32,128]{2,1,0:T(8,128)(2,1)S(1)} %get-tuple-element.113), channel_id=1, source_target_pairs={{0,8},{8,0},{16,24},{24,16},{1,9},{9,1},{17,25},{25,17},{2,10},{10... | collective-permute-start | bytes 589832 | tf_op jit(solution)/shard_map/ppermute | solution.py:295
  65.9 11.3 %collective-permute-start.32 = (bf16[24,32,128]{2,1,0:T(8,128)(2,1)S(1)}, bf16[24,32,128]{2,1,0:T(8,128)(2,1)S(1)}, u32[]{:S(2)}, u32[]{:S(2)}) collective-permute-start(bf16[24,32,128]{2,1,0:T(8,128)(2,1)S(1)} %get-tuple-element.114), channel_id=1, source_target_pairs={{0,16},{8,24},{16,0},{24,8},{1,17},{9,25},{17,1},{25,9},{2,18},{10... | collective-permute-start | bytes 589832 | tf_op jit(solution)/shard_map/ppermute | solution.py:295
  67.3 10.0 %collective-permute-start.33 = (bf16[24,32,128]{2,1,0:T(8,128)(2,1)S(1)}, bf16[24,32,128]{2,1,0:T(8,128)(2,1)S(1)}, u32[]{:S(2)}, u32[]{:S(2)}) collective-permute-start(bf16[24,32,128]{2,1,0:T(8,128)(2,1)S(1)} %get-tuple-element.115), channel_id=1, source_target_pairs={{0,24},{8,16},{16,8},{24,0},{1,25},{9,17},{17,9},{25,1},{2,26},{10... | collective-permute-start | bytes 589832 | tf_op jit(solution)/shard_map/ppermute | solution.py:295
  69.3 9.3 %collective-permute-start.28 = (bf16[8,32,128]{2,1,0:T(8,128)(2,1)S(1)}, bf16[8,32,128]{2,1,0:T(8,128)(2,1)S(1)}, u32[]{:S(2)}, u32[]{:S(2)}) collective-permute-start(bf16[8,32,128]{2,1,0:T(8,128)(2,1)S(1)} %get-tuple-element.109), channel_id=1, source_target_pairs={{0,8},{8,0},{16,24},{24,16},{1,9},{9,1},{17,25},{25,17},{2,10},{10... | collective-permute-start | bytes 196616 | tf_op jit(solution)/shard_map/ppermute | solution.py:295
  70.0 8.6 %collective-permute-start.29 = (bf16[8,32,128]{2,1,0:T(8,128)(2,1)S(1)}, bf16[8,32,128]{2,1,0:T(8,128)(2,1)S(1)}, u32[]{:S(2)}, u32[]{:S(2)}) collective-permute-start(bf16[8,32,128]{2,1,0:T(8,128)(2,1)S(1)} %get-tuple-element.110), channel_id=1, source_target_pairs={{0,16},{8,24},{16,0},{24,8},{1,17},{9,25},{17,1},{25,9},{2,18},{10... | collective-permute-start | bytes 196616 | tf_op jit(solution)/shard_map/ppermute | solution.py:295
  73.1 5.6 %collective-permute-start.30 = (bf16[8,32,128]{2,1,0:T(8,128)(2,1)S(1)}, bf16[8,32,128]{2,1,0:T(8,128)(2,1)S(1)}, u32[]{:S(2)}, u32[]{:S(2)}) collective-permute-start(bf16[8,32,128]{2,1,0:T(8,128)(2,1)S(1)} %get-tuple-element.111), channel_id=1, source_target_pairs={{0,24},{8,16},{16,8},{24,0},{1,25},{9,17},{17,9},{25,1},{2,26},{10... | collective-permute-start | bytes 196616 | tf_op jit(solution)/shard_map/ppermute | solution.py:295

commit v8 on v7

--- a/solution.py
+++ b/solution.py
@@ -48,7 +48,7 @@
 
 
 def params():
-    return pltpu.CompilerParams(vmem_limit_bytes=12 * 1024 * 1024)
+    return pltpu.CompilerParams(vmem_limit_bytes=16 * 1024 * 1024)
 
 
 def vmem():
@@ -365,7 +365,7 @@
         scratch=[
             pltpu.VMEM((e_dev, orbitals, orbitals), BF16),
             pltpu.VMEM((orbitals * e_dev, orbitals), F32),
-            pltpu.SemaphoreType.DMA((4,)),
+            pltpu.SemaphoreType.DMA((8,)),
         ],
     )
     great = [exchange(parts[:groups])]

time: 79.9 us -> 79.6 us (level)
  transfers between devices with their start and end apart: 34 -> 34, of which waited for: 14 -> 13; matrix products, arithmetic and copies ran while one was open for 0% -> 0% of each run, Pallas kernels for 15% -> 15%
where the time goes in v8:
time: 79.6 us; the launch traced here: 79.4 us
  starting transfers between devices  46 us (58%)
  waiting for transfers between devices  18.1 us (23%)
  Pallas kernels  15.2 us (19%)
    ppermute x30, starting transfers between devices, exchange(): lax.ppermute(parts[d], 'energy', [(i, i ^ d) for i in range(groups)])  38.6 us
    pallas_call x14, Pallas kernels, call(): pl.pallas_call(kernel, out_shape=out_shape, in_specs=specs, scratch_shape...  15.2 us
    ppermute x30, waiting for transfers between devices, exchange(): lax.ppermute(parts[d], 'energy', [(i, i ^ d) for i in range(groups)])  14.5 us
    ppermute x2, starting transfers between devices, shards(): far = lax.ppermute(own, 'block', far_pairs)  3.84 us
    ppermute x2, waiting for transfers between devices, shards(): far = lax.ppermute(own, 'block', far_pairs)  3.67 us
    ppermute x2, starting transfers between devices, shards(): near = lax.ppermute(own, 'block', near_pairs)  3.49 us
  transfers between devices with their start and end apart: 34, of which 13 were waited for; matrix products, arithmetic and copies ran while one was open for 0% of the time, Pallas kernels for 15%

profile of v8, /device:TPU:16, one launch (start us, length us, event | category | flops | bytes accessed | tf_op | source)
XLA Modules:
  0.0 79.4 jit_solution(389319502318594235)
XLA Ops:
  0.0 1.3 %shard_map.84 = (bf16[32,32,128]{2,1,0:T(8,128)(2,1)S(1)}, bf16[32,32,128]{2,1,0:T(8,128)(2,1)S(1)}, bf16[32,32,128]{2,1,0:T(8,128)(2,1)S(1)}, bf16[32,32,128]{2,1,0:T(8,128)(2,1)S(1)}) custom-call(s32[1]{0:T(128)} %bitcast.me_ref, bf16[32,128,128]{2,1,0:T(8,128)(2,1)} %bitcast.11), custom_call_target="tpu_custom_call" | custom-call | tf_op jit(solution)/shard_map/pallas_call | solution.py:300
  1.3 1.6 %collective-permute-start = (bf16[32,32,128]{2,1,0:T(8,128)(2,1)S(1)}, bf16[32,32,128]{2,1,0:T(8,128)(2,1)S(1)}, u32[]{:S(2)}, u32[]{:S(2)}) collective-permute-start(bf16[32,32,128]{2,1,0:T(8,128)(2,1)S(1)} %get-tuple-element.69), channel_id=1, source_target_pairs={{0,8},{8,0},{16,24},{24,16},{1,9},{9,1},{17,25},{25,17},{2,10},{10... | collective-permute-start | bytes 786440 | tf_op jit(solution)/shard_map/ppermute | solution.py:295
  2.8 1.5 %collective-permute-start.1 = (bf16[32,32,128]{2,1,0:T(8,128)(2,1)S(1)}, bf16[32,32,128]{2,1,0:T(8,128)(2,1)S(1)}, u32[]{:S(2)}, u32[]{:S(2)}) collective-permute-start(bf16[32,32,128]{2,1,0:T(8,128)(2,1)S(1)} %get-tuple-element.70), channel_id=1, source_target_pairs={{0,16},{8,24},{16,0},{24,8},{1,17},{9,25},{17,1},{25,9},{2,18},{10... | collective-permute-start | bytes 786440 | tf_op jit(solution)/shard_map/ppermute | solution.py:295
  4.8 2.7 %shard_map.83 = (bf16[16,32,128]{2,1,0:T(8,128)(2,1)S(1)}, bf16[16,32,128]{2,1,0:T(8,128)(2,1)S(1)}, bf16[16,32,128]{2,1,0:T(8,128)(2,1)S(1)}, bf16[16,32,128]{2...) custom-call(s32[1]{0:T(128)} %bitcast.me_ref, ...), custom_call_target="tpu_custom_call" | custom-call | tf_op jit(solution)/shard_map/pallas_call | solution.py:300
  7.6 1.6 %collective-permute-start.3 = (bf16[16,32,128]{2,1,0:T(8,128)(2,1)S(1)}, bf16[16,32,128]{2,1,0:T(8,128)(2,1)S(1)}, u32[]{:S(2)}, u32[]{:S(2)}) collective-permute-start(bf16[16,32,128]{2,1,0:T(8,128)(2,1)S(1)} %get-tuple-element.78), channel_id=1, source_target_pairs={{0,8},{8,0},{16,24},{24,16},{1,9},{9,1},{17,25},{25,17},{2,10},{10... | collective-permute-start | bytes 393224 | tf_op jit(solution)/shard_map/ppermute | solution.py:295
  9.1 1.5 %collective-permute-start.4 = (bf16[16,32,128]{2,1,0:T(8,128)(2,1)S(1)}, bf16[16,32,128]{2,1,0:T(8,128)(2,1)S(1)}, u32[]{:S(2)}, u32[]{:S(2)}) collective-permute-start(bf16[16,32,128]{2,1,0:T(8,128)(2,1)S(1)} %get-tuple-element.79), channel_id=1, source_target_pairs={{0,16},{8,24},{16,0},{24,8},{1,17},{9,25},{17,1},{25,9},{2,18},{10... | collective-permute-start | bytes 393224 | tf_op jit(solution)/shard_map/ppermute | solution.py:295
  10.7 2.3 %collective-permute-start.5 = (bf16[16,32,128]{2,1,0:T(8,128)(2,1)S(1)}, bf16[16,32,128]{2,1,0:T(8,128)(2,1)S(1)}, u32[]{:S(2)}, u32[]{:S(2)}) collective-permute-start(bf16[16,32,128]{2,1,0:T(8,128)(2,1)S(1)} %get-tuple-element.80), channel_id=1, source_target_pairs={{0,24},{8,16},{16,8},{24,0},{1,25},{9,17},{17,9},{25,1},{2,26},{10... | collective-permute-start | bytes 393224 | tf_op jit(solution)/shard_map/ppermute | solution.py:295
  13.0 1.8 %shard_map.82 = (bf16[192,256]{1,0:T(8,128)(2,1)S(1)}, bf16[192,256]{1,0:T(8,128)(2,1)S(1)}, bf16[256,192]{1,0:T(8,128)(2,1)S(1)}, bf16[256,192]{1,0:T(8,128)(2,...) custom-call(s32[1]{0:T(128)} %bitcast.me_ref, s32[1]{0:T(128)} %bitcast.1.odd_ref, ...), custom_call_target="tpu_custom_call" | custom-call | tf_op jit(solution)/shard_map/pallas_call | solution.py:300
  14.7 2.0 %collective-permute-done.1.refs_2_ = bf16[32,32,128]{2,1,0:T(8,128)(2,1)S(1)} collective-permute-done((bf16[32,32,128]{2,1,0:T(8,128)(2,1)S(1)}, bf16[32,32,128]{2,1,0:T(8,128)(2,1)S(1)}, u32[]{:S(2)}, u32[]{:S(2)}) %collective-permute-start.1) | collective-permute-done | bytes 262176 | tf_op jit(solution)/shard_map/ppermute | solution.py:295
  17.2 1.7 %shard_map.85.less_ref = f32[192,4096]{1,0:T(8,128)S(1)} custom-call(bf16[192,256]{1,0:T(8,128)(2,1)S(1)} %get-tuple-element.67.fwd_ref, bf16[32,32,128]{2,1,0:T(8,128)(2,1)S(1)} %get-tuple-element.68.refs_0_, bf16[32,32,128]{2,1,0:T(8,128)(2,1)S(1)} %collective-permute-done.refs_1_, bf16[32,32,128]{2,1,0:T(8,128)(2,1)S(1)} %collective-permute-done.1.refs_2_, ...), custom_call_target="tpu_custom_call" | custom-call | tf_op jit(solution)/shard_map/pallas_call | solution.py:300
  18.9 1.6 %collective-permute-start.9 = (bf16[16,32,128]{2,1,0:T(8,128)(2,1)S(1)}, bf16[16,32,128]{2,1,0:T(8,128)(2,1)S(1)}, u32[]{:S(2)}, u32[]{:S(2)}) collective-permute-start(bf16[16,32,128]{2,1,0:T(8,128)(2,1)S(1)} %get-tuple-element.86), channel_id=1, source_target_pairs={{0,8},{8,0},{16,24},{24,16},{1,9},{9,1},{17,25},{25,17},{2,10},{10... | collective-permute-start | bytes 393224 | tf_op jit(solution)/shard_map/ppermute | solution.py:295
  20.4 1.2 %collective-permute-start.10 = (bf16[16,32,128]{2,1,0:T(8,128)(2,1)S(1)}, bf16[16,32,128]{2,1,0:T(8,128)(2,1)S(1)}, u32[]{:S(2)}, u32[]{:S(2)}) collective-permute-start(bf16[16,32,128]{2,1,0:T(8,128)(2,1)S(1)} %get-tuple-element.87), channel_id=1, source_target_pairs={{0,16},{8,24},{16,0},{24,8},{1,17},{9,25},{17,1},{25,9},{2,18},{10... | collective-permute-start | bytes 393224 | tf_op jit(solution)/shard_map/ppermute | solution.py:295
  21.6 1.4 %collective-permute-start.11 = (bf16[16,32,128]{2,1,0:T(8,128)(2,1)S(1)}, bf16[16,32,128]{2,1,0:T(8,128)(2,1)S(1)}, u32[]{:S(2)}, u32[]{:S(2)}) collective-permute-start(bf16[16,32,128]{2,1,0:T(8,128)(2,1)S(1)} %get-tuple-element.88), channel_id=1, source_target_pairs={{0,24},{8,16},{16,8},{24,0},{1,25},{9,17},{17,9},{25,1},{2,26},{10... | collective-permute-start | bytes 393224 | tf_op jit(solution)/shard_map/ppermute | solution.py:295
  23.0 0.9 %shard_map.86 = (bf16[16,16,128]{2,1,0:T(8,128)(2,1)S(1)}, bf16[16,16,128]{2,1,0:T(8,128)(2,1)S(1)}, bf16[16,16,128]{2,1,0:T(8,128)(2,1)S(1)}, bf16[16,16,128]{2...) custom-call(bf16[192,256]{1,0:T(8,128)(2,1)S(1)} %get-tuple-element., ...), custom_call_target="tpu_custom_call" | custom-call | tf_op jit(solution)/shard_map/pallas_call | solution.py:300
  23.9 1.3 %collective-permute-start.6 = (bf16[16,16,128]{2,1,0:T(8,128)(2,1)S(1)}, bf16[16,16,128]{2,1,0:T(8,128)(2,1)S(1)}, u32[]{:S(2)}, u32[]{:S(2)}) collective-permute-start(bf16[16,16,128]{2,1,0:T(8,128)(2,1)S(1)} %get-tuple-element.82), channel_id=1, source_target_pairs={{0,8},{8,0},{16,24},{24,16},{1,9},{9,1},{17,25},{25,17},{2,10},{10... | collective-permute-start | bytes 196616 | tf_op jit(solution)/shard_map/ppermute | solution.py:295
  25.2 1.6 %collective-permute-start.7 = (bf16[16,16,128]{2,1,0:T(8,128)(2,1)S(1)}, bf16[16,16,128]{2,1,0:T(8,128)(2,1)S(1)}, u32[]{:S(2)}, u32[]{:S(2)}) collective-permute-start(bf16[16,16,128]{2,1,0:T(8,128)(2,1)S(1)} %get-tuple-element.83), channel_id=1, source_target_pairs={{0,16},{8,24},{16,0},{24,8},{1,17},{9,25},{17,1},{25,9},{2,18},{10... | collective-permute-start | bytes 196616 | tf_op jit(solution)/shard_map/ppermute | solution.py:295
  26.9 1.4 %collective-permute-start.8 = (bf16[16,16,128]{2,1,0:T(8,128)(2,1)S(1)}, bf16[16,16,128]{2,1,0:T(8,128)(2,1)S(1)}, u32[]{:S(2)}, u32[]{:S(2)}) collective-permute-start(bf16[16,16,128]{2,1,0:T(8,128)(2,1)S(1)} %get-tuple-element.84), channel_id=1, source_target_pairs={{0,24},{8,16},{16,8},{24,0},{1,25},{9,17},{17,9},{25,1},{2,26},{10... | collective-permute-start | bytes 196616 | tf_op jit(solution)/shard_map/ppermute | solution.py:295
  28.8 0.9 %shard_map.87 = (bf16[16,16,128]{2,1,0:T(8,128)(2,1)S(1)}, bf16[16,16,128]{2,1,0:T(8,128)(2,1)S(1)}, bf16[16,16,128]{2,1,0:T(8,128)(2,1)S(1)}, bf16[16,16,128]{2...) custom-call(bf16[192,256]{1,0:T(8,128)(2,1)S(1)} %get-tuple-element., ...), custom_call_target="tpu_custom_call" | custom-call | tf_op jit(solution)/shard_map/pallas_call | solution.py:300
  29.7 1.7 %collective-permute-start.12 = (bf16[16,16,128]{2,1,0:T(8,128)(2,1)S(1)}, bf16[16,16,128]{2,1,0:T(8,128)(2,1)S(1)}, u32[]{:S(2)}, u32[]{:S(2)}) collective-permute-start(bf16[16,16,128]{2,1,0:T(8,128)(2,1)S(1)} %get-tuple-element.94), channel_id=1, source_target_pairs={{0,8},{8,0},{16,24},{24,16},{1,9},{9,1},{17,25},{25,17},{2,10},{10... | collective-permute-start | bytes 196616 | tf_op jit(solution)/shard_map/ppermute | solution.py:295
  32.1 1.2 %collective-permute-start.14 = (bf16[16,16,128]{2,1,0:T(8,128)(2,1)S(1)}, bf16[16,16,128]{2,1,0:T(8,128)(2,1)S(1)}, u32[]{:S(2)}, u32[]{:S(2)}) collective-permute-start(bf16[16,16,128]{2,1,0:T(8,128)(2,1)S(1)} %get-tuple-element.96), channel_id=1, source_target_pairs={{0,24},{8,16},{16,8},{24,0},{1,25},{9,17},{17,9},{25,1},{2,26},{10... | collective-permute-start | bytes 196616 | tf_op jit(solution)/shard_map/ppermute | solution.py:295
  33.3 1.6 %collective-permute-start.20 = (bf16[16,32,128]{2,1,0:T(8,128)(2,1)S(1)}, bf16[16,32,128]{2,1,0:T(8,128)(2,1)S(1)}, u32[]{:S(2)}, u32[]{:S(2)}) collective-permute-start(bf16[16,32,128]{2,1,0:T(8,128)(2,1)S(1)} %get-tuple-element.102), channel_id=1, source_target_pairs={{0,8},{8,0},{16,24},{24,16},{1,9},{9,1},{17,25},{25,17},{2,10},{10... | collective-permute-start | bytes 393224 | tf_op jit(solution)/shard_map/ppermute | solution.py:295
  34.9 0.7 collective-permute-start.21
  35.6 1.2 %collective-permute-start.22 = (bf16[16,32,128]{2,1,0:T(8,128)(2,1)S(1)}, bf16[16,32,128]{2,1,0:T(8,128)(2,1)S(1)}, u32[]{:S(2)}, u32[]{:S(2)}) collective-permute-start(bf16[16,32,128]{2,1,0:T(8,128)(2,1)S(1)} %get-tuple-element.104), channel_id=1, source_target_pairs={{0,24},{8,16},{16,8},{24,0},{1,25},{9,17},{17,9},{25,1},{2,26},{10... | collective-permute-start | bytes 393224 | tf_op jit(solution)/shard_map/ppermute | solution.py:295
  37.3 1.9 %collective-permute-start.16 = (bf16[16,128,128]{2,1,0:T(8,128)(2,1)S(1)}, bf16[16,128,128]{2,1,0:T(8,128)(2,1)S(1)}, u32[]{:S(2)}, u32[]{:S(2)}) collective-permute-start(bf16[16,128,128]{2,1,0:T(8,128)(2,1)S(1)} %shard_map.88.own), channel_id=1, source_target_pairs={{1,2},{2,1},{3,4},{4,3},{5,6},{6,5},{9,10},{10,9},{11,12},{12,11},... | collective-permute-start | bytes 1572872 | tf_op jit(solution)/shard_map/ppermute | solution.py:420
  39.2 1.7 %collective-permute-start.15 = (bf16[16,128,128]{2,1,0:T(8,128)(2,1)S(1)}, bf16[16,128,128]{2,1,0:T(8,128)(2,1)S(1)}, u32[]{:S(2)}, u32[]{:S(2)}) collective-permute-start(bf16[16,128,128]{2,1,0:T(8,128)(2,1)S(1)} %shard_map.88.own), channel_id=1, source_target_pairs={{0,1},{1,0},{2,3},{3,2},{4,5},{5,4},{6,7},{7,6},{8,9},{9,8},{10,11... | collective-permute-start | bytes 1572872 | tf_op jit(solution)/shard_map/ppermute | solution.py:421
  41.5 1.9 %collective-permute-start.24 = (bf16[16,128,128]{2,1,0:T(8,128)(2,1)S(1)}, bf16[16,128,128]{2,1,0:T(8,128)(2,1)S(1)}, u32[]{:S(2)}, u32[]{:S(2)}) collective-permute-start(bf16[16,128,128]{2,1,0:T(8,128)(2,1)S(1)} %shard_map.90.own), channel_id=1, source_target_pairs={{1,2},{2,1},{3,4},{4,3},{5,6},{6,5},{9,10},{10,9},{11,12},{12,11},... | collective-permute-start | bytes 1572872 | tf_op jit(solution)/shard_map/ppermute | solution.py:420
  43.4 1.7 %collective-permute-start.23 = (bf16[16,128,128]{2,1,0:T(8,128)(2,1)S(1)}, bf16[16,128,128]{2,1,0:T(8,128)(2,1)S(1)}, u32[]{:S(2)}, u32[]{:S(2)}) collective-permute-start(bf16[16,128,128]{2,1,0:T(8,128)(2,1)S(1)} %shard_map.90.own), channel_id=1, source_target_pairs={{0,1},{1,0},{2,3},{3,2},{4,5},{5,4},{6,7},{7,6},{8,9},{9,8},{10,11... | collective-permute-start | bytes 1572872 | tf_op jit(solution)/shard_map/ppermute | solution.py:421
  45.2 2.6 %collective-permute-done.16.far = bf16[16,128,128]{2,1,0:T(8,128)(2,1)S(1)} collective-permute-done((bf16[16,128,128]{2,1,0:T(8,128)(2,1)S(1)}, bf16[16,128,128]{2,1,0:T(8,128)(2,1)S(1)}, u32[]{:S(2)}, u32[]{:S(2)}) %collective-permute-start.16) | collective-permute-done | bytes 524320 | tf_op jit(solution)/shard_map/ppermute | solution.py:420
  47.8 1.0 %shard_map.89 = (bf16[32,16,128]{2,1,0:T(8,128)(2,1)S(1)}, bf16[32,16,128]{2,1,0:T(8,128)(2,1)S(1)}, bf16[32,16,128]{2,1,0:T(8,128)(2,1)S(1)}, bf16[32,16,128]{2,1,0:T(8,128)(2,1)S(1)}) custom-call(s32[1]{0:T(128)} %bitcast.me_ref, bf16[128,384]{1,0:T(8,128)(2,1)S(1)} %get-tuple-element.73.left, bf16[256,256]{1,0:T(8,128)(2,1)S(1)} %get-tuple-element.74.pair_right, ...), custom_call_target="tpu_custom_call" | custom-call | tf_op jit(solution)/shard_map/pallas_call | solution.py:300
  48.8 1.4 %collective-permute-start.17 = (bf16[32,16,128]{2,1,0:T(8,128)(2,1)S(1)}, bf16[32,16,128]{2,1,0:T(8,128)(2,1)S(1)}, u32[]{:S(2)}, u32[]{:S(2)}) collective-permute-start(bf16[32,16,128]{2,1,0:T(8,128)(2,1)S(1)} %get-tuple-element.98), channel_id=1, source_target_pairs={{0,8},{8,0},{16,24},{24,16},{1,9},{9,1},{17,25},{25,17},{2,10},{10... | collective-permute-start | bytes 393224 | tf_op jit(solution)/shard_map/ppermute | solution.py:295
  50.9 1.5 %collective-permute-start.19 = (bf16[32,16,128]{2,1,0:T(8,128)(2,1)S(1)}, bf16[32,16,128]{2,1,0:T(8,128)(2,1)S(1)}, u32[]{:S(2)}, u32[]{:S(2)}) collective-permute-start(bf16[32,16,128]{2,1,0:T(8,128)(2,1)S(1)} %get-tuple-element.100), channel_id=1, source_target_pairs={{0,24},{8,16},{16,8},{24,0},{1,25},{9,17},{17,9},{25,1},{2,26},{10... | collective-permute-start | bytes 393224 | tf_op jit(solution)/shard_map/ppermute | solution.py:295
  52.4 1.0 %collective-permute-done.24.far = bf16[16,128,128]{2,1,0:T(8,128)(2,1)S(1)} collective-permute-done((bf16[16,128,128]{2,1,0:T(8,128)(2,1)S(1)}, bf16[16,128,128]{2,1,0:T(8,128)(2,1)S(1)}, u32[]{:S(2)}, u32[]{:S(2)}) %collective-permute-start.24) | collective-permute-done | bytes 524320 | tf_op jit(solution)/shard_map/ppermute | solution.py:420
  53.4 1.0 %shard_map.91 = (bf16[32,16,128]{2,1,0:T(8,128)(2,1)S(1)}, bf16[32,16,128]{2,1,0:T(8,128)(2,1)S(1)}, bf16[32,16,128]{2,1,0:T(8,128)(2,1)S(1)}, bf16[32,16,128]{2,1,0:T(8,128)(2,1)S(1)}) custom-call(s32[1]{0:T(128)} %bitcast.me_ref, bf16[128,384]{1,0:T(8,128)(2,1)S(1)} %get-tuple-element.73.left, bf16[256,256]{1,0:T(8,128)(2,1)S(1)} %get-tuple-element.74.pair_right, ...), custom_call_target="tpu_custom_call" | custom-call | tf_op jit(solution)/shard_map/pallas_call | solution.py:300
  54.5 1.4 %collective-permute-start.25 = (bf16[32,16,128]{2,1,0:T(8,128)(2,1)S(1)}, bf16[32,16,128]{2,1,0:T(8,128)(2,1)S(1)}, u32[]{:S(2)}, u32[]{:S(2)}) collective-permute-start(bf16[32,16,128]{2,1,0:T(8,128)(2,1)S(1)} %get-tuple-element.106), channel_id=1, source_target_pairs={{0,8},{8,0},{16,24},{24,16},{1,9},{9,1},{17,25},{25,17},{2,10},{10... | collective-permute-start | bytes 393224 | tf_op jit(solution)/shard_map/ppermute | solution.py:295
  56.5 1.5 %collective-permute-start.27 = (bf16[32,16,128]{2,1,0:T(8,128)(2,1)S(1)}, bf16[32,16,128]{2,1,0:T(8,128)(2,1)S(1)}, u32[]{:S(2)}, u32[]{:S(2)}) collective-permute-start(bf16[32,16,128]{2,1,0:T(8,128)(2,1)S(1)} %get-tuple-element.108), channel_id=1, source_target_pairs={{0,24},{8,16},{16,8},{24,0},{1,25},{9,17},{17,9},{25,1},{2,26},{10... | collective-permute-start | bytes 393224 | tf_op jit(solution)/shard_map/ppermute | solution.py:295
  58.4 2.4 %collective-permute-done.25.refs_5_ = bf16[32,16,128]{2,1,0:T(8,128)(2,1)S(1)} collective-permute-done((bf16[32,16,128]{2,1,0:T(8,128)(2,1)S(1)}, bf16[32,16,128]{2,1,0:T(8,128)(2,1)S(1)}, u32[]{:S(2)}, u32[]{:S(2)}) %collective-permute-start.25) | collective-permute-done | bytes 131104 | tf_op jit(solution)/shard_map/ppermute | solution.py:295
  60.9 3.2 %collective-permute-done.26.refs_6_ = bf16[32,16,128]{2,1,0:T(8,128)(2,1)S(1)} collective-permute-done((bf16[32,16,128]{2,1,0:T(8,128)(2,1)S(1)}, bf16[32,16,128]{2,1,0:T(8,128)(2,1)S(1)}, u32[]{:S(2)}, u32[]{:S(2)}) %collective-permute-start.26) | collective-permute-done | bytes 131104 | tf_op jit(solution)/shard_map/ppermute | solution.py:295
  64.0 1.1 %shard_map.93 = (bf16[24,32,128]{2,1,0:T(8,128)(2,1)S(1)}, bf16[24,32,128]{2,1,0:T(8,128)(2,1)S(1)}, bf16[24,32,128]{2,1,0:T(8,128)(2,1)S(1)}, bf16[24,32,128]{2,1,0:T(8,128)(2,1)S(1)}) custom-call(bf16[192,256]{1,0:T(8,128)(2,1)S(1)} %get-tuple-element.61.fwd_l_ref, bf16[256,192]{1,0:T(8,128)(2,1)S(1)} %get-tuple-element.62.back_ref, ...), custom_call_target="tpu_custom_call" | custom-call | tf_op jit(solution)/shard_map/pallas_call | solution.py:300
  65.2 0.8 collective-permute-start.31
  65.9 1.3 %collective-permute-start.32 = (bf16[24,32,128]{2,1,0:T(8,128)(2,1)S(1)}, bf16[24,32,128]{2,1,0:T(8,128)(2,1)S(1)}, u32[]{:S(2)}, u32[]{:S(2)}) collective-permute-start(bf16[24,32,128]{2,1,0:T(8,128)(2,1)S(1)} %get-tuple-element.114), channel_id=1, source_target_pairs={{0,16},{8,24},{16,0},{24,8},{1,17},{9,25},{17,1},{25,9},{2,18},{10... | collective-permute-start | bytes 589832 | tf_op jit(solution)/shard_map/ppermute | solution.py:295
  67.3 1.5 %collective-permute-start.33 = (bf16[24,32,128]{2,1,0:T(8,128)(2,1)S(1)}, bf16[24,32,128]{2,1,0:T(8,128)(2,1)S(1)}, u32[]{:S(2)}, u32[]{:S(2)}) collective-permute-start(bf16[24,32,128]{2,1,0:T(8,128)(2,1)S(1)} %get-tuple-element.115), channel_id=1, source_target_pairs={{0,24},{8,16},{16,8},{24,0},{1,25},{9,17},{17,9},{25,1},{2,26},{10... | collective-permute-start | bytes 589832 | tf_op jit(solution)/shard_map/ppermute | solution.py:295
  69.3 0.8 collective-permute-start.28
  70.0 1.3 %collective-permute-start.29 = (bf16[8,32,128]{2,1,0:T(8,128)(2,1)S(1)}, bf16[8,32,128]{2,1,0:T(8,128)(2,1)S(1)}, u32[]{:S(2)}, u32[]{:S(2)}) collective-permute-start(bf16[8,32,128]{2,1,0:T(8,128)(2,1)S(1)} %get-tuple-element.110), channel_id=1, source_target_pairs={{0,16},{8,24},{16,0},{24,8},{1,17},{9,25},{17,1},{25,9},{2,18},{10... | collective-permute-start | bytes 196616 | tf_op jit(solution)/shard_map/ppermute | solution.py:295
  71.4 1.7 %collective-permute-done.31.refs_1_ = bf16[24,32,128]{2,1,0:T(8,128)(2,1)S(1)} collective-permute-done((bf16[24,32,128]{2,1,0:T(8,128)(2,1)S(1)}, bf16[24,32,128]{2,1,0:T(8,128)(2,1)S(1)}, u32[]{:S(2)}, u32[]{:S(2)}) %collective-permute-start.31) | collective-permute-done | bytes 196640 | tf_op jit(solution)/shard_map/ppermute | solution.py:295
  73.1 1.5 %collective-permute-start.30 = (bf16[8,32,128]{2,1,0:T(8,128)(2,1)S(1)}, bf16[8,32,128]{2,1,0:T(8,128)(2,1)S(1)}, u32[]{:S(2)}, u32[]{:S(2)}) collective-permute-start(bf16[8,32,128]{2,1,0:T(8,128)(2,1)S(1)} %get-tuple-element.111), channel_id=1, source_target_pairs={{0,24},{8,16},{16,8},{24,0},{1,25},{9,17},{17,9},{25,1},{2,26},{10... | collective-permute-start | bytes 196616 | tf_op jit(solution)/shard_map/ppermute | solution.py:295
  74.5 2.7 %collective-permute-done.32.refs_2_ = bf16[24,32,128]{2,1,0:T(8,128)(2,1)S(1)} collective-permute-done((bf16[24,32,128]{2,1,0:T(8,128)(2,1)S(1)}, bf16[24,32,128]{2,1,0:T(8,128)(2,1)S(1)}, u32[]{:S(2)}, u32[]{:S(2)}) %collective-permute-start.32) | collective-permute-done | bytes 196640 | tf_op jit(solution)/shard_map/ppermute | solution.py:295
  77.2 1.3 %shard_map.94.refs_3_ = f32[32,128,128]{2,1,0:T(8,128)} custom-call(s32[1]{0:T(128)} %bitcast.me_ref, bf16[24,32,128]{2,1,0:T(8,128)(2,1)S(1)} %get-tuple-element.112.refs_0_, bf16[24,32,128]{2,1,0:T(8,128)(2,1)S(1)} %collective-permute-done.31.refs_1_, bf16[24,32,128]{2,1,0:T(8,128)(2,1)S(1)} %collective-permute-done.32.refs_2_, ...), custom_call_target="tpu_custom_call" | custom-call | tf_op jit(solution)/shard_map/pallas_call | solution.py:300
  78.6 0.8 shard_map.95
  (38 shorter events, 5.5 us)
Async XLA Ops:
  0.0 13.0 %copy-start.1 = (s32[1,2]{1,0:T(1,128)S(1)}, s32[1,2]{1,0:T(1,128)}, u32[]{:S(2)}) copy-start(s32[1,2]{1,0:T(1,128)} %param.11) | copy-start | bytes 28
  0.0 13.0 %copy-start = (bf16[1,3,128,128]{3,2,1,0:T(8,128)(2,1)S(1)}, bf16[1,3,128,128]{3,2,1,0:T(8,128)(2,1)}, u32[]{:S(2)}) copy-start(bf16[1,3,128,128]{3,2,1,0:T(8,128)(2,1)} %param.10) | copy-start | bytes 294916
  1.3 9.4 %collective-permute-start = (bf16[32,32,128]{2,1,0:T(8,128)(2,1)S(1)}, bf16[32,32,128]{2,1,0:T(8,128)(2,1)S(1)}, u32[]{:S(2)}, u32[]{:S(2)}) collective-permute-start(bf16[32,32,128]{2,1,0:T(8,128)(2,1)S(1)} %get-tuple-element.69), channel_id=1, source_target_pairs={{0,8},{8,0},{16,24},{24,16},{1,9},{9,1},{17,25},{25,17},{2,10},{10... | collective-permute-start | bytes 786440 | tf_op jit(solution)/shard_map/ppermute | solution.py:295
  2.8 13.9 %collective-permute-start.1 = (bf16[32,32,128]{2,1,0:T(8,128)(2,1)S(1)}, bf16[32,32,128]{2,1,0:T(8,128)(2,1)S(1)}, u32[]{:S(2)}, u32[]{:S(2)}) collective-permute-start(bf16[32,32,128]{2,1,0:T(8,128)(2,1)S(1)} %get-tuple-element.70), channel_id=1, source_target_pairs={{0,16},{8,24},{16,0},{24,8},{1,17},{9,25},{17,1},{25,9},{2,18},{10... | collective-permute-start | bytes 786440 | tf_op jit(solution)/shard_map/ppermute | solution.py:295
  4.3 12.8 %collective-permute-start.2 = (bf16[32,32,128]{2,1,0:T(8,128)(2,1)S(1)}, bf16[32,32,128]{2,1,0:T(8,128)(2,1)S(1)}, u32[]{:S(2)}, u32[]{:S(2)}) collective-permute-start(bf16[32,32,128]{2,1,0:T(8,128)(2,1)S(1)} %get-tuple-element.71), channel_id=1, source_target_pairs={{0,24},{8,16},{16,8},{24,0},{1,25},{9,17},{17,9},{25,1},{2,26},{10... | collective-permute-start | bytes 786440 | tf_op jit(solution)/shard_map/ppermute | solution.py:295
  7.6 14.0 %collective-permute-start.3 = (bf16[16,32,128]{2,1,0:T(8,128)(2,1)S(1)}, bf16[16,32,128]{2,1,0:T(8,128)(2,1)S(1)}, u32[]{:S(2)}, u32[]{:S(2)}) collective-permute-start(bf16[16,32,128]{2,1,0:T(8,128)(2,1)S(1)} %get-tuple-element.78), channel_id=1, source_target_pairs={{0,8},{8,0},{16,24},{24,16},{1,9},{9,1},{17,25},{25,17},{2,10},{10... | collective-permute-start | bytes 393224 | tf_op jit(solution)/shard_map/ppermute | solution.py:295
  9.1 13.9 %collective-permute-start.4 = (bf16[16,32,128]{2,1,0:T(8,128)(2,1)S(1)}, bf16[16,32,128]{2,1,0:T(8,128)(2,1)S(1)}, u32[]{:S(2)}, u32[]{:S(2)}) collective-permute-start(bf16[16,32,128]{2,1,0:T(8,128)(2,1)S(1)} %get-tuple-element.79), channel_id=1, source_target_pairs={{0,16},{8,24},{16,0},{24,8},{1,17},{9,25},{17,1},{25,9},{2,18},{10... | collective-permute-start | bytes 393224 | tf_op jit(solution)/shard_map/ppermute | solution.py:295
  10.7 12.4 %collective-permute-start.5 = (bf16[16,32,128]{2,1,0:T(8,128)(2,1)S(1)}, bf16[16,32,128]{2,1,0:T(8,128)(2,1)S(1)}, u32[]{:S(2)}, u32[]{:S(2)}) collective-permute-start(bf16[16,32,128]{2,1,0:T(8,128)(2,1)S(1)} %get-tuple-element.80), channel_id=1, source_target_pairs={{0,24},{8,16},{16,8},{24,0},{1,25},{9,17},{17,9},{25,1},{2,26},{10... | collective-permute-start | bytes 393224 | tf_op jit(solution)/shard_map/ppermute | solution.py:295
  18.9 8.0 %collective-permute-start.9 = (bf16[16,32,128]{2,1,0:T(8,128)(2,1)S(1)}, bf16[16,32,128]{2,1,0:T(8,128)(2,1)S(1)}, u32[]{:S(2)}, u32[]{:S(2)}) collective-permute-start(bf16[16,32,128]{2,1,0:T(8,128)(2,1)S(1)} %get-tuple-element.86), channel_id=1, source_target_pairs={{0,8},{8,0},{16,24},{24,16},{1,9},{9,1},{17,25},{25,17},{2,10},{10... | collective-permute-start | bytes 393224 | tf_op jit(solution)/shard_map/ppermute | solution.py:295
  20.4 8.3 %collective-permute-start.10 = (bf16[16,32,128]{2,1,0:T(8,128)(2,1)S(1)}, bf16[16,32,128]{2,1,0:T(8,128)(2,1)S(1)}, u32[]{:S(2)}, u32[]{:S(2)}) collective-permute-start(bf16[16,32,128]{2,1,0:T(8,128)(2,1)S(1)} %get-tuple-element.87), channel_id=1, source_target_pairs={{0,16},{8,24},{16,0},{24,8},{1,17},{9,25},{17,1},{25,9},{2,18},{10... | collective-permute-start | bytes 393224 | tf_op jit(solution)/shard_map/ppermute | solution.py:295
  21.6 7.2 %collective-permute-start.11 = (bf16[16,32,128]{2,1,0:T(8,128)(2,1)S(1)}, bf16[16,32,128]{2,1,0:T(8,128)(2,1)S(1)}, u32[]{:S(2)}, u32[]{:S(2)}) collective-permute-start(bf16[16,32,128]{2,1,0:T(8,128)(2,1)S(1)} %get-tuple-element.88), channel_id=1, source_target_pairs={{0,24},{8,16},{16,8},{24,0},{1,25},{9,17},{17,9},{25,1},{2,26},{10... | collective-permute-start | bytes 393224 | tf_op jit(solution)/shard_map/ppermute | solution.py:295
  23.9 8.2 %collective-permute-start.6 = (bf16[16,16,128]{2,1,0:T(8,128)(2,1)S(1)}, bf16[16,16,128]{2,1,0:T(8,128)(2,1)S(1)}, u32[]{:S(2)}, u32[]{:S(2)}) collective-permute-start(bf16[16,16,128]{2,1,0:T(8,128)(2,1)S(1)} %get-tuple-element.82), channel_id=1, source_target_pairs={{0,8},{8,0},{16,24},{24,16},{1,9},{9,1},{17,25},{25,17},{2,10},{10... | collective-permute-start | bytes 196616 | tf_op jit(solution)/shard_map/ppermute | solution.py:295
  25.2 8.0 %collective-permute-start.7 = (bf16[16,16,128]{2,1,0:T(8,128)(2,1)S(1)}, bf16[16,16,128]{2,1,0:T(8,128)(2,1)S(1)}, u32[]{:S(2)}, u32[]{:S(2)}) collective-permute-start(bf16[16,16,128]{2,1,0:T(8,128)(2,1)S(1)} %get-tuple-element.83), channel_id=1, source_target_pairs={{0,16},{8,24},{16,0},{24,8},{1,17},{9,25},{17,1},{25,9},{2,18},{10... | collective-permute-start | bytes 196616 | tf_op jit(solution)/shard_map/ppermute | solution.py:295
  26.9 8.0 %collective-permute-start.8 = (bf16[16,16,128]{2,1,0:T(8,128)(2,1)S(1)}, bf16[16,16,128]{2,1,0:T(8,128)(2,1)S(1)}, u32[]{:S(2)}, u32[]{:S(2)}) collective-permute-start(bf16[16,16,128]{2,1,0:T(8,128)(2,1)S(1)} %get-tuple-element.84), channel_id=1, source_target_pairs={{0,24},{8,16},{16,8},{24,0},{1,25},{9,17},{17,9},{25,1},{2,26},{10... | collective-permute-start | bytes 196616 | tf_op jit(solution)/shard_map/ppermute | solution.py:295
  29.7 5.9 %collective-permute-start.12 = (bf16[16,16,128]{2,1,0:T(8,128)(2,1)S(1)}, bf16[16,16,128]{2,1,0:T(8,128)(2,1)S(1)}, u32[]{:S(2)}, u32[]{:S(2)}) collective-permute-start(bf16[16,16,128]{2,1,0:T(8,128)(2,1)S(1)} %get-tuple-element.94), channel_id=1, source_target_pairs={{0,8},{8,0},{16,24},{24,16},{1,9},{9,1},{17,25},{25,17},{2,10},{10... | collective-permute-start | bytes 196616 | tf_op jit(solution)/shard_map/ppermute | solution.py:295
  31.4 5.4 %collective-permute-start.13 = (bf16[16,16,128]{2,1,0:T(8,128)(2,1)S(1)}, bf16[16,16,128]{2,1,0:T(8,128)(2,1)S(1)}, u32[]{:S(2)}, u32[]{:S(2)}) collective-permute-start(bf16[16,16,128]{2,1,0:T(8,128)(2,1)S(1)} %get-tuple-element.95), channel_id=1, source_target_pairs={{0,16},{8,24},{16,0},{24,8},{1,17},{9,25},{17,1},{25,9},{2,18},{10... | collective-permute-start | bytes 196616 | tf_op jit(solution)/shard_map/ppermute | solution.py:295
  32.1 5.2 %collective-permute-start.14 = (bf16[16,16,128]{2,1,0:T(8,128)(2,1)S(1)}, bf16[16,16,128]{2,1,0:T(8,128)(2,1)S(1)}, u32[]{:S(2)}, u32[]{:S(2)}) collective-permute-start(bf16[16,16,128]{2,1,0:T(8,128)(2,1)S(1)} %get-tuple-element.96), channel_id=1, source_target_pairs={{0,24},{8,16},{16,8},{24,0},{1,25},{9,17},{17,9},{25,1},{2,26},{10... | collective-permute-start | bytes 196616 | tf_op jit(solution)/shard_map/ppermute | solution.py:295
  33.3 7.7 %collective-permute-start.20 = (bf16[16,32,128]{2,1,0:T(8,128)(2,1)S(1)}, bf16[16,32,128]{2,1,0:T(8,128)(2,1)S(1)}, u32[]{:S(2)}, u32[]{:S(2)}) collective-permute-start(bf16[16,32,128]{2,1,0:T(8,128)(2,1)S(1)} %get-tuple-element.102), channel_id=1, source_target_pairs={{0,8},{8,0},{16,24},{24,16},{1,9},{9,1},{17,25},{25,17},{2,10},{10... | collective-permute-start | bytes 393224 | tf_op jit(solution)/shard_map/ppermute | solution.py:295
  34.9 6.1 %collective-permute-start.21 = (bf16[16,32,128]{2,1,0:T(8,128)(2,1)S(1)}, bf16[16,32,128]{2,1,0:T(8,128)(2,1)S(1)}, u32[]{:S(2)}, u32[]{:S(2)}) collective-permute-start(bf16[16,32,128]{2,1,0:T(8,128)(2,1)S(1)} %get-tuple-element.103), channel_id=1, source_target_pairs={{0,16},{8,24},{16,0},{24,8},{1,17},{9,25},{17,1},{25,9},{2,18},{10... | collective-permute-start | bytes 393224 | tf_op jit(solution)/shard_map/ppermute | solution.py:295
  35.6 5.9 %collective-permute-start.22 = (bf16[16,32,128]{2,1,0:T(8,128)(2,1)S(1)}, bf16[16,32,128]{2,1,0:T(8,128)(2,1)S(1)}, u32[]{:S(2)}, u32[]{:S(2)}) collective-permute-start(bf16[16,32,128]{2,1,0:T(8,128)(2,1)S(1)} %get-tuple-element.104), channel_id=1, source_target_pairs={{0,24},{8,16},{16,8},{24,0},{1,25},{9,17},{17,9},{25,1},{2,26},{10... | collective-permute-start | bytes 393224 | tf_op jit(solution)/shard_map/ppermute | solution.py:295
  37.3 10.5 %collective-permute-start.16 = (bf16[16,128,128]{2,1,0:T(8,128)(2,1)S(1)}, bf16[16,128,128]{2,1,0:T(8,128)(2,1)S(1)}, u32[]{:S(2)}, u32[]{:S(2)}) collective-permute-start(bf16[16,128,128]{2,1,0:T(8,128)(2,1)S(1)} %shard_map.88.own), channel_id=1, source_target_pairs={{1,2},{2,1},{3,4},{4,3},{5,6},{6,5},{9,10},{10,9},{11,12},{12,11},... | collective-permute-start | bytes 1572872 | tf_op jit(solution)/shard_map/ppermute | solution.py:420
  39.2 8.6 %collective-permute-start.15 = (bf16[16,128,128]{2,1,0:T(8,128)(2,1)S(1)}, bf16[16,128,128]{2,1,0:T(8,128)(2,1)S(1)}, u32[]{:S(2)}, u32[]{:S(2)}) collective-permute-start(bf16[16,128,128]{2,1,0:T(8,128)(2,1)S(1)} %shard_map.88.own), channel_id=1, source_target_pairs={{0,1},{1,0},{2,3},{3,2},{4,5},{5,4},{6,7},{7,6},{8,9},{9,8},{10,11... | collective-permute-start | bytes 1572872 | tf_op jit(solution)/shard_map/ppermute | solution.py:421
  41.5 11.9 %collective-permute-start.24 = (bf16[16,128,128]{2,1,0:T(8,128)(2,1)S(1)}, bf16[16,128,128]{2,1,0:T(8,128)(2,1)S(1)}, u32[]{:S(2)}, u32[]{:S(2)}) collective-permute-start(bf16[16,128,128]{2,1,0:T(8,128)(2,1)S(1)} %shard_map.90.own), channel_id=1, source_target_pairs={{1,2},{2,1},{3,4},{4,3},{5,6},{6,5},{9,10},{10,9},{11,12},{12,11},... | collective-permute-start | bytes 1572872 | tf_op jit(solution)/shard_map/ppermute | solution.py:420
  43.4 10.0 %collective-permute-start.23 = (bf16[16,128,128]{2,1,0:T(8,128)(2,1)S(1)}, bf16[16,128,128]{2,1,0:T(8,128)(2,1)S(1)}, u32[]{:S(2)}, u32[]{:S(2)}) collective-permute-start(bf16[16,128,128]{2,1,0:T(8,128)(2,1)S(1)} %shard_map.90.own), channel_id=1, source_target_pairs={{0,1},{1,0},{2,3},{3,2},{4,5},{5,4},{6,7},{7,6},{8,9},{9,8},{10,11... | collective-permute-start | bytes 1572872 | tf_op jit(solution)/shard_map/ppermute | solution.py:421
  48.8 7.7 %collective-permute-start.17 = (bf16[32,16,128]{2,1,0:T(8,128)(2,1)S(1)}, bf16[32,16,128]{2,1,0:T(8,128)(2,1)S(1)}, u32[]{:S(2)}, u32[]{:S(2)}) collective-permute-start(bf16[32,16,128]{2,1,0:T(8,128)(2,1)S(1)} %get-tuple-element.98), channel_id=1, source_target_pairs={{0,8},{8,0},{16,24},{24,16},{1,9},{9,1},{17,25},{25,17},{2,10},{10... | collective-permute-start | bytes 393224 | tf_op jit(solution)/shard_map/ppermute | solution.py:295
  50.2 8.2 %collective-permute-start.18 = (bf16[32,16,128]{2,1,0:T(8,128)(2,1)S(1)}, bf16[32,16,128]{2,1,0:T(8,128)(2,1)S(1)}, u32[]{:S(2)}, u32[]{:S(2)}) collective-permute-start(bf16[32,16,128]{2,1,0:T(8,128)(2,1)S(1)} %get-tuple-element.99), channel_id=1, source_target_pairs={{0,16},{8,24},{16,0},{24,8},{1,17},{9,25},{17,1},{25,9},{2,18},{10... | collective-permute-start | bytes 393224 | tf_op jit(solution)/shard_map/ppermute | solution.py:295
  50.9 7.5 %collective-permute-start.19 = (bf16[32,16,128]{2,1,0:T(8,128)(2,1)S(1)}, bf16[32,16,128]{2,1,0:T(8,128)(2,1)S(1)}, u32[]{:S(2)}, u32[]{:S(2)}) collective-permute-start(bf16[32,16,128]{2,1,0:T(8,128)(2,1)S(1)} %get-tuple-element.100), channel_id=1, source_target_pairs={{0,24},{8,16},{16,8},{24,0},{1,25},{9,17},{17,9},{25,1},{2,26},{10... | collective-permute-start | bytes 393224 | tf_op jit(solution)/shard_map/ppermute | solution.py:295
  54.5 6.4 %collective-permute-start.25 = (bf16[32,16,128]{2,1,0:T(8,128)(2,1)S(1)}, bf16[32,16,128]{2,1,0:T(8,128)(2,1)S(1)}, u32[]{:S(2)}, u32[]{:S(2)}) collective-permute-start(bf16[32,16,128]{2,1,0:T(8,128)(2,1)S(1)} %get-tuple-element.106), channel_id=1, source_target_pairs={{0,8},{8,0},{16,24},{24,16},{1,9},{9,1},{17,25},{25,17},{2,10},{10... | collective-permute-start | bytes 393224 | tf_op jit(solution)/shard_map/ppermute | solution.py:295
  55.8 8.2 %collective-permute-start.26 = (bf16[32,16,128]{2,1,0:T(8,128)(2,1)S(1)}, bf16[32,16,128]{2,1,0:T(8,128)(2,1)S(1)}, u32[]{:S(2)}, u32[]{:S(2)}) collective-permute-start(bf16[32,16,128]{2,1,0:T(8,128)(2,1)S(1)} %get-tuple-element.107), channel_id=1, source_target_pairs={{0,16},{8,24},{16,0},{24,8},{1,17},{9,25},{17,1},{25,9},{2,18},{10... | collective-permute-start | bytes 393224 | tf_op jit(solution)/shard_map/ppermute | solution.py:295
  56.5 7.5 %collective-permute-start.27 = (bf16[32,16,128]{2,1,0:T(8,128)(2,1)S(1)}, bf16[32,16,128]{2,1,0:T(8,128)(2,1)S(1)}, u32[]{:S(2)}, u32[]{:S(2)}) collective-permute-start(bf16[32,16,128]{2,1,0:T(8,128)(2,1)S(1)} %get-tuple-element.108), channel_id=1, source_target_pairs={{0,24},{8,16},{16,8},{24,0},{1,25},{9,17},{17,9},{25,1},{2,26},{10... | collective-permute-start | bytes 393224 | tf_op jit(solution)/shard_map/ppermute | solution.py:295
  65.2 7.9 %collective-permute-start.31 = (bf16[24,32,128]{2,1,0:T(8,128)(2,1)S(1)}, bf16[24,32,128]{2,1,0:T(8,128)(2,1)S(1)}, u32[]{:S(2)}, u32[]{:S(2)}) collective-permute-start(bf16[24,32,128]{2,1,0:T(8,128)(2,1)S(1)} %get-tuple-element.113), channel_id=1, source_target_pairs={{0,8},{8,0},{16,24},{24,16},{1,9},{9,1},{17,25},{25,17},{2,10},{10... | collective-permute-start | bytes 589832 | tf_op jit(solution)/shard_map/ppermute | solution.py:295
  65.9 11.3 %collective-permute-start.32 = (bf16[24,32,128]{2,1,0:T(8,128)(2,1)S(1)}, bf16[24,32,128]{2,1,0:T(8,128)(2,1)S(1)}, u32[]{:S(2)}, u32[]{:S(2)}) collective-permute-start(bf16[24,32,128]{2,1,0:T(8,128)(2,1)S(1)} %get-tuple-element.114), channel_id=1, source_target_pairs={{0,16},{8,24},{16,0},{24,8},{1,17},{9,25},{17,1},{25,9},{2,18},{10... | collective-permute-start | bytes 589832 | tf_op jit(solution)/shard_map/ppermute | solution.py:295
  67.3 10.0 %collective-permute-start.33 = (bf16[24,32,128]{2,1,0:T(8,128)(2,1)S(1)}, bf16[24,32,128]{2,1,0:T(8,128)(2,1)S(1)}, u32[]{:S(2)}, u32[]{:S(2)}) collective-permute-start(bf16[24,32,128]{2,1,0:T(8,128)(2,1)S(1)} %get-tuple-element.115), channel_id=1, source_target_pairs={{0,24},{8,16},{16,8},{24,0},{1,25},{9,17},{17,9},{25,1},{2,26},{10... | collective-permute-start | bytes 589832 | tf_op jit(solution)/shard_map/ppermute | solution.py:295
  69.3 9.3 %collective-permute-start.28 = (bf16[8,32,128]{2,1,0:T(8,128)(2,1)S(1)}, bf16[8,32,128]{2,1,0:T(8,128)(2,1)S(1)}, u32[]{:S(2)}, u32[]{:S(2)}) collective-permute-start(bf16[8,32,128]{2,1,0:T(8,128)(2,1)S(1)} %get-tuple-element.109), channel_id=1, source_target_pairs={{0,8},{8,0},{16,24},{24,16},{1,9},{9,1},{17,25},{25,17},{2,10},{10... | collective-permute-start | bytes 196616 | tf_op jit(solution)/shard_map/ppermute | solution.py:295
  70.0 8.6 %collective-permute-start.29 = (bf16[8,32,128]{2,1,0:T(8,128)(2,1)S(1)}, bf16[8,32,128]{2,1,0:T(8,128)(2,1)S(1)}, u32[]{:S(2)}, u32[]{:S(2)}) collective-permute-start(bf16[8,32,128]{2,1,0:T(8,128)(2,1)S(1)} %get-tuple-element.110), channel_id=1, source_target_pairs={{0,16},{8,24},{16,0},{24,8},{1,17},{9,25},{17,1},{25,9},{2,18},{10... | collective-permute-start | bytes 196616 | tf_op jit(solution)/shard_map/ppermute | solution.py:295
  73.1 5.6 %collective-permute-start.30 = (bf16[8,32,128]{2,1,0:T(8,128)(2,1)S(1)}, bf16[8,32,128]{2,1,0:T(8,128)(2,1)S(1)}, u32[]{:S(2)}, u32[]{:S(2)}) collective-permute-start(bf16[8,32,128]{2,1,0:T(8,128)(2,1)S(1)} %get-tuple-element.111), channel_id=1, source_target_pairs={{0,24},{8,16},{16,8},{24,0},{1,25},{9,17},{17,9},{25,1},{2,26},{10... | collective-permute-start | bytes 196616 | tf_op jit(solution)/shard_map/ppermute | solution.py:295
